TPU v7x, 256 devices: a whole 4x4x8 slice. The times are simulated.
256 devices in a mesh: mod: 8 (over y, x_hi), row: 32 (over z, x_lo, core).
Axes of the slice: x: 4 (x_hi: 2, x_lo: 2; x = x_hi * 2 + x_lo), y: 4, z: 8, core: 2. Of those that a mesh axis runs over, the one named last changes fastest.
Arguments:
- image: bfloat16 [6144, 1024], P('row', 'mod'), may hold values from -16 to 16
- modality: bfloat16 [8, 6144, 1024], P('mod', 'row'), may hold values from -16 to 16
- pair_index: int32 [8, 6144], P('mod'), may hold values from 0 to 6143, each once within a row
Outputs:
- image_grad: float32 [6144, 1024], P('row', 'mod')
- modality_grad: float32 [8, 6144, 1024], P('mod', 'row')
- row_loss: float32 [8, 6144], P('mod', 'row')
- col_loss: float32 [8, 6144], P('mod', 'row')
All inputs are finite; a program needn't handle non-finite values.
Results may differ from a plain program's by a relative error of at most 0.0015.
Values may be sent and summed in bfloat16 or wider, within the bound.
No kernel may reach another device: no remote copies, remote signals or barrier semaphores. Data moves between devices by JAX's collectives and lax.ppermute only.
A program may use at most 128 MiB of HBM per device.

v0:
```python
import functools
import jax
import jax.numpy as jnp
from jax import lax
from jax.experimental import pallas as pl
from jax.experimental.pallas import tpu as pltpu
from jax.sharding import Mesh, PartitionSpec as P

LAST = (((1,), (1,)), ((), ()))
FIRST = (((0,), (0,)), ((), ()))
F32, BF16, I16 = jnp.float32, jnp.bfloat16, jnp.int16
PAD = 16


def call(kernel, out, name, mib, **kw):
    return pl.pallas_call(
        kernel,
        out_shape=out,
        compiler_params=pltpu.CompilerParams(vmem_limit_bytes=mib * 2**20),
        cost_estimate=pl.CostEstimate(flops=1000, bytes_accessed=1000, transcendentals=0),
        name=name,
        **kw,
    )


def shape(s, t):
    return jax.ShapeDtypeStruct(s, t)


def eye(n):
    return lax.broadcasted_iota(jnp.int32, (n, n), 0) == lax.broadcasted_iota(jnp.int32, (n, n), 1)


def to_lanes(v):
    n = v.shape[0]
    parts = []
    for a in range(0, n, 128):
        w = min(128, n - a)
        parts.append(jnp.sum(jnp.where(eye(w), v[a : a + w], F32(0)), axis=0, keepdims=True))
    return jnp.concatenate(parts, axis=1)


def to_rows(v):
    n = v.shape[1]
    parts = []
    for a in range(0, n, 128):
        w = min(128, n - a)
        parts.append(jnp.sum(jnp.where(eye(w), v[:, a : a + w], F32(0)), axis=1, keepdims=True))
    return jnp.concatenate(parts, axis=0)


def power_of(x):
    top = jnp.max(jnp.abs(x), axis=0, keepdims=True)
    return jnp.ceil(jnp.log2(jnp.maximum(top, F32(1e-30)))) - 14.0


def fixed(x):
    return x.astype(jnp.int32).astype(I16)


def encode(x, ref):
    rows, cols = x.shape
    power = power_of(x)
    ref[:rows, :] = fixed(jnp.round(x * jnp.exp2(-power)))
    ref[rows:, :] = fixed(jnp.broadcast_to(power, (PAD, cols)))


def floats(c):
    return c.astype(jnp.int32).astype(F32)


def decode(c, tiles=1):
    f = floats(c)
    rows = c.shape[-2] - PAD
    n = rows // tiles
    parts = [f[..., i * n : (i + 1) * n, :] * jnp.exp2(f[..., rows + i : rows + i + 1, :]) for i in range(tiles)]
    return parts[0] if tiles == 1 else jnp.concatenate(parts, axis=-2)


def turn_left(v, n):
    lanes = v.shape[1]
    return pltpu.roll(jnp.broadcast_to(v, (8, lanes)), lax.rem(lanes - n, lanes), 1)[0:1]


def prep_kernel(pair_index, keys, pairs, cols, keys_out):
    keys_out[...] = keys[...]
    n_im, n_ks = pairs.shape[1], cols.shape[1]
    rows = n_ks // 8
    zl, xl, core = lax.axis_index("zl"), lax.axis_index("xl"), lax.axis_index("core")
    mine = turn_left(pair_index[...].astype(F32), ((zl * 2 + xl) * 2 + core) * rows)
    pairs[...] = jnp.concatenate([mine[:, a * n_ks : a * n_ks + rows] for a in range(n_im // rows)], axis=1)
    p = lax.broadcasted_iota(jnp.int32, (1, n_ks), 1)
    k = sum((p >= a * rows).astype(jnp.int32) for a in range(1, 8))
    block = ((zl ^ (k >> 1 & 1)) * 2 + (k & 1)) * 2 + (core ^ (k >> 2))
    cols[...] = (lax.axis_index("zh") * n_ks + (block - k) * rows + p).astype(F32)


def join_kernel(own, x, z, d, after_a, after_b, out):
    del after_a, after_b
    rows = own.shape[0]
    xl = lax.axis_index("xl")
    for k, (mine, beside) in enumerate(((own, x), (z, d))):
        out[pl.ds(pl.multiple_of((2 * k + xl) * rows, 16), rows), :] = mine[...]
        out[pl.ds(pl.multiple_of((2 * k + 1 - xl) * rows, 16), rows), :] = beside[...]


def hold_kernel(keys, after, out):
    del after
    out[...] = keys[...]


def turn_kernel(behind, ahead, half_a, half_b):
    n = half_a.shape[0]
    half_a[...] = behind[:n]
    half_b[...] = ahead[n:]


def scores_kernel(scale, tile, *refs):
    keys, (i0, i1, i3, ia, ib, pairs, cols, s_ref, im, rs, cs) = refs[:2], refs[2:]
    y = lax.axis_index("y")
    nzh, rows, width = ia.shape
    n_im = im.shape[0]
    part = keys[0].shape[0]

    def place(k, xh, ref, first):
        at = pl.multiple_of((lax.rem(y + 4 - k, 4) * 2 + xh) * width, 128)
        for j in range(nzh):
            im[j * rows : (j + 1) * rows, pl.ds(at, width)] = ref[first + j]

    for k, ref in ((0, i0), (1, i1), (3, i3)):
        for xh in range(2):
            place(k, xh, ref, xh * nzh)
    place(2, 0, ia, 0)
    place(2, 1, ib, 0)

    rows_of = [slice(r, r + tile) for r in range(0, n_im, tile)]
    col_top, col_sum, col_pick = [None] * 2, [None] * 2, [None] * 2
    row_state = [None] * len(rows_of)

    def online(s, state, axis):
        top = jnp.max(s, axis=axis, keepdims=True)
        if state is None:
            return top, jnp.sum(jnp.exp(s - top), axis=axis, keepdims=True)
        new = jnp.maximum(state[0], top)
        return new, state[1] * jnp.exp(state[0] - new) + jnp.sum(jnp.exp(s - new), axis=axis, keepdims=True)

    def stats(h, r):
        lanes = slice(h * part, (h + 1) * part)
        s = s_ref[rows_of[r], lanes]
        picked = jnp.where(to_rows(pairs[:, rows_of[r]]) == cols[:, lanes], s, F32(0))
        old = row_state[r]
        top, total = online(s, old and old[:2], 1)
        pick = jnp.sum(picked, axis=1, keepdims=True)
        row_state[r] = (top, total, pick if old is None else old[2] + pick)
        state = None if col_top[h] is None else (col_top[h], col_sum[h])
        col_top[h], col_sum[h] = online(s, state, 0)
        pick = jnp.sum(picked, axis=0, keepdims=True)
        col_pick[h] = pick if col_pick[h] is None else col_pick[h] + pick

    before = None
    for h, ks in enumerate(keys):
        for r in range(len(rows_of)):
            s = lax.dot_general(im[rows_of[r], :], ks[...], LAST, preferred_element_type=F32)
            s_ref[rows_of[r], h * part : (h + 1) * part] = s * scale
            if before:
                stats(*before)
            before = (h, r)
    stats(*before)
    for r, (top, total, pick) in enumerate(row_state):
        rs[0:1, rows_of[r]] = to_lanes(top + jnp.log(total))
        rs[1:2, rows_of[r]] = to_lanes(pick)
    for h in range(2):
        cs[0:1, h * part : (h + 1) * part] = col_top[h] + jnp.log(col_sum[h])
        cs[1:2, h * part : (h + 1) * part] = col_pick[h]


def merge(parts):
    top = functools.reduce(jnp.maximum, parts)
    return top + jnp.log(sum(jnp.exp(p - top) for p in parts))


def meet(parts):
    return jnp.concatenate([merge([p[0:1] for p in parts]), sum(p[1:2] for p in parts)], axis=0)


def turned(c, n):
    return jnp.concatenate([c[:, (k ^ 1) * n : ((k ^ 1) + 1) * n] for k in range(c.shape[1] // n)], axis=1)


def meet_kernel(c, c_other, out):
    out[...] = meet([c[...], turned(c_other[...], c.shape[1] // 2)])


def weights_kernel(scale, tile, *refs):
    rparts, cparts = refs[:4], refs[4:8]
    pairs, cols, s_ref, k0, k1, im, own, p1, p3, o2a, o2b, mine, sent, rl, cl, w_ref, total = refs[8:]
    n_im, n_ks = s_ref.shape
    keys = (k0, k1)
    half, part = n_ks // 2, n_ks // 4
    width = own.shape[1]
    cstat = meet([turned(c[...], part) if k >= 2 else c[...] for k, c in enumerate(cparts)])
    lse_col = cstat[0:1]
    rows = cl.shape[1]
    cl[...] = turn_left(lse_col - cstat[1:2], lax.axis_index("xl") * rows)[:, :rows]
    rstat = meet([r[...] for r in rparts])
    lse_row = rstat[0:1]
    rl[...] = turn_left(lse_row - rstat[1:2], lax.axis_index("zh") * rows)[:, :rows]

    def weigh(a):
        rows = slice(a, a + tile)
        s = s_ref[rows, :]
        two = jnp.where(to_rows(pairs[:, rows]) == cols[...], F32(2), F32(0))
        w = jnp.exp(s - to_rows(lse_row[:, rows])) + jnp.exp(s - lse_col) - two
        w_ref[rows, :] = w.astype(BF16)

    def term(a):
        rows = slice(a, a + tile)
        x = sum(
            jnp.dot(w_ref[rows, k * half : (k + 1) * half], keys[k][...], preferred_element_type=F32) for k in range(2)
        )
        total[rows, :] = x * scale

    tiles = range(0, n_im, tile)
    weigh(0)
    for a in tiles:
        if a + tile < n_im:
            weigh(a + tile)
        term(a)
    for k, out in ((2, None), (1, p1), (3, p3), (0, own)):
        lanes = pl.ds(pl.multiple_of(lax.rem(lax.axis_index("y") + k, 4) * width, 128), width)
        if k == 2:
            encode(total[: n_im // 2, lanes], o2a)
            encode(total[n_im // 2 :, lanes], o2b)
        else:
            out[...] = total[:, lanes]
    other = lax.dot_general(w_ref[:, half:], im[...], FIRST, preferred_element_type=F32) * scale
    for p in range(4):
        encode(other[p * rows : (p + 1) * rows, :], sent.at[p])
    mine[...] = lax.dot_general(w_ref[:, :half], im[...], FIRST, preferred_element_type=F32) * scale


def relay_kernel(p1, p3, got_a, got_b, o1, o3):
    n = p1.shape[0] // 2
    encode(jnp.concatenate([p1[:n, :] + decode(got_a[...]), p1[n:, :]], axis=0), o1)
    encode(jnp.concatenate([p3[:n, :], p3[n:, :] + decode(got_b[...])], axis=0), o3)


def key_sum_kernel(mine, got, own, keep_x, keep_z, to_x, to_z):
    rows, d = own.shape
    n = d // 2
    xl = lax.axis_index("xl")

    def piece(k):
        p = xl ^ k
        return mine[pl.ds(pl.multiple_of(p * rows, 16), rows), :] + decode(got[p])

    x, z, both = piece(1), piece(2), piece(3)
    encode(x[:, :n], to_x.at[0])
    encode(both[:, :n], to_x.at[1])
    encode(z[:, n:], to_z.at[0])
    encode(both[:, n:], to_z.at[1])
    keep_x[...] = x[:, n:]
    keep_z[...] = z[:, :n]
    own[...] = piece(0)


def key_relay_kernel(after, own, keep_x, keep_z, from_x, from_z, total, to_x, to_z):
    del after
    n = keep_x.shape[1]
    total[:, :n] = own[:, :n] + decode(from_x[0])
    total[:, n:] = own[:, n:] + decode(from_z[0])
    encode(keep_z[...] + decode(from_x[1]), to_z)
    encode(keep_x[...] + decode(from_z[1]), to_x)


def last_kernel(own_key, from_x, from_z, own, twin, key_out, image_out):
    n = own_key.shape[1] // 2
    key_out[:, :n] = own_key[:, :n] + decode(from_z[...])
    key_out[:, n:] = own_key[:, n:] + decode(from_x[...])
    image_out[...] = own[...] + decode(twin[...])


def image_sum_kernel(after, own, got1, got3, keep, to_a, to_b, total):
    del after
    zh, xh = lax.axis_index("zh"), lax.axis_index("xh")
    rows, width = keep.shape[1:]
    n = own.shape[0] // rows
    total[...] = own[...] + decode(got1[...]) + decode(got3[...])

    def piece(o, j):
        row = pl.multiple_of(lax.rem(zh + j, n) * rows, 16)
        return total[pl.ds(row, rows), pl.ds(pl.multiple_of((xh ^ o) * width, 128), width)]

    encode(piece(0, 2), to_a)
    encode(piece(1, 2), to_b)
    for o in range(2):
        for at, j in enumerate((0, 1, n - 1)):
            keep[3 * o + at] = piece(o, j)


def image_relay_kernel(after, keep, got_a, got_b, up, down):
    del after
    encode(keep[1] + decode(got_a[...]), up.at[0])
    encode(keep[4], up.at[1])
    encode(keep[2], down.at[0])
    encode(keep[5] + decode(got_b[...]), down.at[1])


def image_twin_kernel(keep, up, down, own, to_twin):
    own[...] = keep[0] + decode(up[0]) + decode(down[0])
    encode(keep[3] + decode(up[1]) + decode(down[1]), to_twin)


def shift(x, axis, n, k):
    return lax.ppermute(x, axis, [(i, (i + k) % n) for i in range(n)])


def flip(x, axis, n, d):
    return lax.ppermute(x, axis, [(i, i ^ d) for i in range(n)])


def on_device(image, modality, pair_index):
    keys = modality[0]
    rows, d = keys.shape
    width = image.shape[1]
    scale = d ** (-0.5)
    nzh = lax.axis_size("zh")
    n_im, n_ks = nzh * rows, 8 * rows
    half = n_ks // 2
    vmem = pl.BlockSpec(memory_space=pltpu.VMEM)
    pairs, cols, held = call(
        prep_kernel,
        [shape((1, n_im), F32), shape((1, n_ks), F32), shape((rows, d), BF16)],
        "prep",
        8,
        in_specs=[vmem] * 2,
    )(pair_index, keys)
    i0 = lax.all_to_all(jnp.broadcast_to(image, (2 * nzh, rows, width)), ("xh", "zh"), 0, 0)
    i1, i3 = shift(i0, "y", 4, 1), shift(i0, "y", 4, 3)
    held = call(hold_kernel, shape((rows, d), BF16), "hold", 8, in_specs=[vmem] * 2)(held, i0)
    key_x = flip(held, "xl", 2, 1)
    key_z = flip(held, "zl", 2, 1)
    key_d = lax.ppermute(held, ("zl", "xl"), [(i, 3 - i) for i in range(4)])
    half_block = shape((nzh, rows, width), BF16)
    ia, ib = call(turn_kernel, [half_block] * 2, "turn", 12, in_specs=[vmem] * 2)(i1, i3)
    ia, ib = shift(ia, "y", 4, 1), shift(ib, "y", 4, 3)
    k0 = call(join_kernel, shape((half, d), BF16), "join", 12, in_specs=[vmem] * 6)(held, key_x, key_z, key_d, ia, ib)
    ks = [k0, flip(k0, "core", 2, 1)]

    tile = min(256, n_im)
    scores, im, rs, cs = call(
        functools.partial(scores_kernel, scale, tile),
        [shape((n_im, n_ks), F32), shape((n_im, d), BF16), shape((2, n_im), F32), shape((2, n_ks), F32)],
        "scores",
        28,
        in_specs=[vmem] * 9,
    )(*ks, i0, i1, i3, ia, ib, pairs, cols)
    rstats = [rs] + [shift(rs, "zh", 4, k) for k in (1, 2, 3)]
    cs = call(meet_kernel, shape((2, n_ks), F32), "meet", 4, in_specs=[vmem] * 2)(cs, flip(cs, "core", 2, 1))
    cstats = [cs] + [lax.ppermute(cs, ("zl", "xl"), [(i, i ^ k) for i in range(4)]) for k in (1, 2, 3)]
    outs = [shape((n_im, 2 * width), F32)] * 3 + [shape((n_im // 2 + PAD, 2 * width), I16)] * 2
    outs += [shape((half, d), F32), shape((4, rows + PAD, d), I16)] + [shape((1, rows), F32)] * 2
    own, p1, p3, q2a, q2b, mine, sent, row_loss, col_loss = call(
        functools.partial(weights_kernel, scale, tile),
        outs,
        "weights",
        36,
        in_specs=[vmem] * 14,
        scratch_shapes=[pltpu.VMEM((n_im, n_ks), BF16), pltpu.VMEM((n_im, d), F32)],
    )(*rstats, *cstats, pairs, cols, scores, *ks, im)
    q1, q3 = call(
        relay_kernel, [shape((n_im + PAD, 2 * width), I16)] * 2, "relay", 12, in_specs=[vmem] * 4
    )(p1, p3, shift(q2a, "y", 4, 1), shift(q2b, "y", 4, 3))
    q1, q3 = shift(q1, "y", 4, 1), shift(q3, "y", 4, 3)
    own_key, keep_x, keep_z, to_x, to_z = call(
        key_sum_kernel,
        [shape((rows, d), F32)] + [shape((rows, d // 2), F32)] * 2 + [shape((2, rows + PAD, d // 2), I16)] * 2,
        "key_sum",
        16,
        in_specs=[vmem] * 2,
    )(mine, flip(sent, "core", 2, 1))
    from_x, from_z = flip(to_x, "xl", 2, 1), flip(to_z, "zl", 2, 1)
    coded = shape((rows + PAD, width), I16)
    coded2 = shape((2, rows + PAD, width), I16)
    keep, to_a, to_b = call(
        image_sum_kernel,
        [shape((6, rows, width), F32), coded, coded],
        "image_sum",
        12,
        in_specs=[vmem] * 4,
        scratch_shapes=[pltpu.VMEM((n_im, 2 * width), F32)],
    )(keep_z, own, q1, q3)
    own_key, to_x, to_z = call(
        key_relay_kernel,
        [shape((rows, d), F32)] + [shape((rows + PAD, d // 2), I16)] * 2,
        "key_relay",
        12,
        in_specs=[vmem] * 6,
    )(to_a, own_key, keep_x, keep_z, from_x, from_z)
    up, down = call(image_relay_kernel, [coded2] * 2, "image_relay", 8, in_specs=[vmem] * 4)(
        to_x, keep, shift(to_a, "zh", 4, 1), shift(to_b, "zh", 4, 3)
    )
    own, to_twin = call(image_twin_kernel, [shape((rows, width), F32), coded], "image_twin", 8, in_specs=[vmem] * 3)(
        keep, shift(up, "zh", 4, 1), shift(down, "zh", 4, 3)
    )
    modality_grad, image_grad = call(
        last_kernel, [shape((rows, d), F32), shape((rows, width), F32)], "last", 8, in_specs=[vmem] * 5
    )(own_key, flip(to_x, "xl", 2, 1), flip(to_z, "zl", 2, 1), own, flip(to_twin, "xh", 2, 1))
    return (image_grad, modality_grad[None], row_loss, col_loss)


def solution(mesh):
    ny = mesh.devices.shape[0] // 2
    nzh = mesh.devices.shape[1] // 8
    names = ("y", "xh", "zh", "zl", "xl", "core")
    fine = Mesh(mesh.devices.reshape(ny, 2, nzh, 2, 2, 2), names)
    mod, rows = names[:2], names[2:]
    in_specs = (P(rows, mod), P(mod, rows, None), P(mod, None))
    out_specs = (P(rows, mod), P(mod, rows, None), P(mod, rows), P(mod, rows))
    return jax.shard_map(
        on_device, mesh=fine, in_specs=in_specs, out_specs=out_specs, check_vma=False
    )
```

profile of v0, /device:TPU:4, one launch (start us, length us, event | category | flops | bytes accessed | tf_op | source)
XLA Modules:
  0.0 124.8 jit_solution(5892379607530352869)
XLA Ops:
  1.5 24.5 %all_to_all.5.after.refs_2_ = bf16[8,192,128]{2,1,0:T(8,128)(2,1)S(1)} all-to-all(bf16[8,192,128]{2,1,0:T(8,128)(2,1)S(1)} %broadcast_in_dim.6), channel_id=1, replica_groups=mesh['y'=4,'xh'=2,'zh'=4,'zl'=2,'xl'=2,'core'=2] {'xh','zh'}, dimensions={0} | all-to-all | bytes 786432 | tf_op jit(solution)/shard_map/all_to_all | solution.py:338
  25.9 3.0 %collective-permute-start.4 = (bf16[8,192,128]{2,1,0:T(8,128)(2,1)S(1)}, bf16[8,192,128]{2,1,0:T(8,128)(2,1)S(1)}, u32[]{:S(2)}, u32[]{:S(2)}) collective-permute-start(bf16[8,192,128]{2,1,0:T(8,128)(2,1)S(1)} %all_to_all.5.after.refs_2_), channel_id=1, source_target_pairs={{0,192},{64,0},{128,64},{192,128},{1,193},{65,1},{129,65},{193,129... | collective-permute-start | bytes 1179656 | tf_op jit(solution)/shard_map/ppermute | solution.py:315
  29.0 1.0 copy-done
  30.9 1.8 %collective-permute-start.2 = (bf16[192,1024]{1,0:T(8,128)(2,1)S(1)}, bf16[192,1024]{1,0:T(8,128)(2,1)S(1)}, u32[]{:S(2)}, u32[]{:S(2)}) collective-permute-start(bf16[192,1024]{1,0:T(8,128)(2,1)S(1)} %hold.1.own), channel_id=1, source_target_pairs={{0,6},{2,4},{4,2},{6,0},{1,7},{3,5},{5,3},{7,1},{8,14},{10,12},{12... | collective-permute-start | bytes 1179656 | tf_op jit(solution)/shard_map/ppermute | solution.py:343
  35.2 3.4 %collective-permute-done.3.behind.refs_3_ = bf16[8,192,128]{2,1,0:T(8,128)(2,1)S(1)} collective-permute-done((bf16[8,192,128]{2,1,0:T(8,128)(2,1)S(1)}, bf16[8,192,128]{2,1,0:T(8,128)(2,1)S(1)}, u32[]{:S(2)}, u32[]{:S(2)}) %collective-permute-start.3) | collective-permute-done | bytes 393248 | tf_op jit(solution)/shard_map/ppermute | solution.py:315
  38.7 3.2 %collective-permute-start.6 = (bf16[4,192,128]{2,1,0:T(8,128)(2,1)S(1)}, bf16[4,192,128]{2,1,0:T(8,128)(2,1)S(1)}, u32[]{:S(2)}, u32[]{:S(2)}) collective-permute-start(bf16[4,192,128]{2,1,0:T(8,128)(2,1)S(1)} %get-tuple-element.43), channel_id=1, source_target_pairs={{0,192},{64,0},{128,64},{192,128},{1,193},{65,1},{129,65},{193,129... | collective-permute-start | bytes 589832 | tf_op jit(solution)/shard_map/ppermute | solution.py:315
  41.9 2.1 %collective-permute-done.2.d = bf16[192,1024]{1,0:T(8,128)(2,1)S(1)} collective-permute-done((bf16[192,1024]{1,0:T(8,128)(2,1)S(1)}, bf16[192,1024]{1,0:T(8,128)(2,1)S(1)}, u32[]{:S(2)}, u32[]{:S(2)}) %collective-permute-start.2) | collective-permute-done | bytes 393248 | tf_op jit(solution)/shard_map/ppermute | solution.py:343
  44.0 4.6 %collective-permute-done.1.z = bf16[192,1024]{1,0:T(8,128)(2,1)S(1)} collective-permute-done((bf16[192,1024]{1,0:T(8,128)(2,1)S(1)}, bf16[192,1024]{1,0:T(8,128)(2,1)S(1)}, u32[]{:S(2)}, u32[]{:S(2)}) %collective-permute-start.1) | collective-permute-done | bytes 393248 | tf_op jit(solution)/shard_map/ppermute | solution.py:319
  49.0 3.4 %collective-permute-done.7.refs_1_.refs_12_ = bf16[768,1024]{1,0:T(8,128)(2,1)S(1)} collective-permute-done((bf16[768,1024]{1,0:T(8,128)(2,1)S(1)}, bf16[768,1024]{1,0:T(8,128)(2,1)S(1)}, u32[]{:S(2)}, u32[]{:S(2)}) %collective-permute-start.7) | collective-permute-done | bytes 1572896 | tf_op jit(solution)/shard_map/ppermute | solution.py:319
  52.4 5.1 %scores.1 = (f32[768,1536]{1,0:T(8,128)S(1)}, bf16[768,1024]{1,0:T(8,128)(2,1)S(1)}, f32[2,768]{1,0:T(2,128)S(1)}, f32[2,1536]{1,0:T(2,128)S(1)}) custom-call(bf16[768,1024]{1,0:T(8,128)(2,1)S(1)} %join.1.refs_0_.refs_11_, bf16[768,1024]{1,0:T(8,128)(2,1)S(1)} %collective-permute-done.7.refs_1_.refs_12_, bf16[8,192,128]{2,1,0:T(8,128)(2,1)S(1)} %all_to_all.5.after.refs_2_, ...), custom_call_target="tpu_custom_call" | custom-call | flops 1000 | bytes 1000 | tf_op jit(solution)/shard_map/scores/pallas_call | solution.py:351
  57.7 1.9 %collective-permute-start.10 = (f32[2,768]{1,0:T(2,128)S(1)}, f32[2,768]{1,0:T(2,128)S(1)}, u32[]{:S(2)}, u32[]{:S(2)}) collective-permute-start(f32[2,768]{1,0:T(2,128)S(1)} %get-tuple-element.46.refs_0_), channel_id=1, source_target_pairs={{0,24},{8,0},{16,8},{24,16},{1,25},{9,1},{17,9},{25,17},{2,26},{10... | collective-permute-start | bytes 18440 | tf_op jit(solution)/shard_map/ppermute | solution.py:315
  59.6 1.3 %collective-permute-start.14 = (f32[2,1536]{1,0:T(2,128)S(1)}, f32[2,1536]{1,0:T(2,128)S(1)}, u32[]{:S(2)}, u32[]{:S(2)}) collective-permute-start(f32[2,1536]{1,0:T(2,128)S(1)} %meet.1.refs_4_), channel_id=1, source_target_pairs={{0,6},{2,4},{4,2},{6,0},{1,7},{3,5},{5,3},{7,1},{8,14},{10,12},{12... | collective-permute-start | bytes 36872 | tf_op jit(solution)/shard_map/ppermute | solution.py:360
  60.9 1.7 %collective-permute-start.13 = (f32[2,1536]{1,0:T(2,128)S(1)}, f32[2,1536]{1,0:T(2,128)S(1)}, u32[]{:S(2)}, u32[]{:S(2)}) collective-permute-start(f32[2,1536]{1,0:T(2,128)S(1)} %meet.1.refs_4_), channel_id=1, source_target_pairs={{0,4},{2,6},{4,0},{6,2},{1,5},{3,7},{5,1},{7,3},{8,12},{10,14},{12... | collective-permute-start | bytes 36872 | tf_op jit(solution)/shard_map/ppermute | solution.py:360
  63.4 2.8 %collective-permute-start.9 = (f32[2,768]{1,0:T(2,128)S(1)}, f32[2,768]{1,0:T(2,128)S(1)}, u32[]{:S(2)}, u32[]{:S(2)}) collective-permute-start(f32[2,768]{1,0:T(2,128)S(1)} %get-tuple-element.46.refs_0_), channel_id=1, source_target_pairs={{0,16},{8,24},{16,0},{24,8},{1,17},{9,25},{17,1},{25,9},{2,18},{10... | collective-permute-start | bytes 18440 | tf_op jit(solution)/shard_map/ppermute | solution.py:315
  66.8 4.1 %collective-permute-done.9.refs_2_ = f32[2,768]{1,0:T(2,128)S(1)} collective-permute-done((f32[2,768]{1,0:T(2,128)S(1)}, f32[2,768]{1,0:T(2,128)S(1)}, u32[]{:S(2)}, u32[]{:S(2)}) %collective-permute-start.9) | collective-permute-done | bytes 6176 | tf_op jit(solution)/shard_map/ppermute | solution.py:315
  70.9 1.1 collective-permute-done.8.refs_1_
  72.0 7.9 %weights.1 = (f32[768,256]{1,0:T(8,128)S(1)}, f32[768,256]{1,0:T(8,128)S(1)}, f32[768,256]{1,0:T(8,128)S(1)}, s16[400,256]{1,0:T(8,128)(2,1)S(1)}, s16[400,256]{...) custom-call(f32[2,768]{1,0:T(2,128)S(1)} %get-tuple-element.46.refs_, ...), custom_call_target="tpu_custom_call" | custom-call | flops 1000 | bytes 1000 | tf_op jit(solution)/shard_map/weights/pallas_call | solution.py:363
  80.2 2.9 %collective-permute-start.17 = (s16[400,256]{1,0:T(8,128)(2,1)S(1)}, s16[400,256]{1,0:T(8,128)(2,1)S(1)}, u32[]{:S(2)}, u32[]{:S(2)}) collective-permute-start(s16[400,256]{1,0:T(8,128)(2,1)S(1)} %get-tuple-element.57), channel_id=1, source_target_pairs={{0,192},{64,0},{128,64},{192,128},{1,193},{65,1},{129,65},{193,129... | collective-permute-start | bytes 614408 | tf_op jit(solution)/shard_map/ppermute | solution.py:315
  84.4 1.3 %collective-permute-start.20 = (s16[2,208,512]{2,1,0:T(8,128)(2,1)S(1)}, s16[2,208,512]{2,1,0:T(8,128)(2,1)S(1)}, u32[]{:S(2)}, u32[]{:S(2)}) collective-permute-start(s16[2,208,512]{2,1,0:T(8,128)(2,1)S(1)} %get-tuple-element.63), channel_id=1, source_target_pairs={{0,2},{2,0},{1,3},{3,1},{4,6},{6,4},{5,7},{7,5},{8,10},{10,8},{9,1... | collective-permute-start | bytes 1277960 | tf_op jit(solution)/shard_map/ppermute | solution.py:319
  85.7 2.0 %collective-permute-start.21 = (s16[2,208,512]{2,1,0:T(8,128)(2,1)S(1)}, s16[2,208,512]{2,1,0:T(8,128)(2,1)S(1)}, u32[]{:S(2)}, u32[]{:S(2)}) collective-permute-start(s16[2,208,512]{2,1,0:T(8,128)(2,1)S(1)} %get-tuple-element.64), channel_id=1, source_target_pairs={{0,4},{4,0},{1,5},{5,1},{2,6},{6,2},{3,7},{7,3},{8,12},{12,8},{9,1... | collective-permute-start | bytes 1277960 | tf_op jit(solution)/shard_map/ppermute | solution.py:319
  89.0 1.2 collective-permute-start.18
  90.2 2.1 %collective-permute-start.19 = (s16[784,256]{1,0:T(8,128)(2,1)S(1)}, s16[784,256]{1,0:T(8,128)(2,1)S(1)}, u32[]{:S(2)}, u32[]{:S(2)}) collective-permute-start(s16[784,256]{1,0:T(8,128)(2,1)S(1)} %get-tuple-element.59), channel_id=1, source_target_pairs={{0,192},{64,0},{128,64},{192,128},{1,193},{65,1},{129,65},{193,129... | collective-permute-start | bytes 1204232 | tf_op jit(solution)/shard_map/ppermute | solution.py:315
  92.3 8.9 %collective-permute-done.18.got1 = s16[784,256]{1,0:T(8,128)(2,1)S(1)} collective-permute-done((s16[784,256]{1,0:T(8,128)(2,1)S(1)}, s16[784,256]{1,0:T(8,128)(2,1)S(1)}, u32[]{:S(2)}, u32[]{:S(2)}) %collective-permute-start.18) | collective-permute-done | bytes 401440 | tf_op jit(solution)/shard_map/ppermute | solution.py:315
  102.4 2.3 %collective-permute-start.24 = (s16[208,128]{1,0:T(8,128)(2,1)S(1)}, s16[208,128]{1,0:T(8,128)(2,1)S(1)}, u32[]{:S(2)}, u32[]{:S(2)}) collective-permute-start(s16[208,128]{1,0:T(8,128)(2,1)S(1)} %get-tuple-element.60.after), channel_id=1, source_target_pairs={{0,8},{8,16},{16,24},{24,0},{1,9},{9,17},{17,25},{25,1},{2,10},{10... | collective-permute-start | bytes 159752 | tf_op jit(solution)/shard_map/ppermute | solution.py:315
  105.2 2.1 %collective-permute-start.23 = (s16[208,512]{1,0:T(8,128)(2,1)S(1)}, s16[208,512]{1,0:T(8,128)(2,1)S(1)}, u32[]{:S(2)}, u32[]{:S(2)}) collective-permute-start(s16[208,512]{1,0:T(8,128)(2,1)S(1)} %get-tuple-element.67), channel_id=1, source_target_pairs={{0,4},{4,0},{1,5},{5,1},{2,6},{6,2},{3,7},{7,3},{8,12},{12,8},{9,1... | collective-permute-start | bytes 638984 | tf_op jit(solution)/shard_map/ppermute | solution.py:319
  107.2 1.2 collective-permute-start.22
  108.5 1.2 collective-permute-done.24.got_a
  110.5 3.5 %collective-permute-start.27 = (s16[2,208,128]{2,1,0:T(8,128)(2,1)S(1)}, s16[2,208,128]{2,1,0:T(8,128)(2,1)S(1)}, u32[]{:S(2)}, u32[]{:S(2)}) collective-permute-start(s16[2,208,128]{2,1,0:T(8,128)(2,1)S(1)} %get-tuple-element.71), channel_id=1, source_target_pairs={{0,24},{8,0},{16,8},{24,16},{1,25},{9,1},{17,9},{25,17},{2,26},{10... | collective-permute-start | bytes 319496 | tf_op jit(solution)/shard_map/ppermute | solution.py:315
  114.0 4.0 %collective-permute-done.26.up = s16[2,208,128]{2,1,0:T(8,128)(2,1)S(1)} collective-permute-done((s16[2,208,128]{2,1,0:T(8,128)(2,1)S(1)}, s16[2,208,128]{2,1,0:T(8,128)(2,1)S(1)}, u32[]{:S(2)}, u32[]{:S(2)}) %collective-permute-start.26) | collective-permute-done | bytes 106528 | tf_op jit(solution)/shard_map/ppermute | solution.py:315
  118.1 2.8 %collective-permute-start.28 = (s16[208,128]{1,0:T(8,128)(2,1)S(1)}, s16[208,128]{1,0:T(8,128)(2,1)S(1)}, u32[]{:S(2)}, u32[]{:S(2)}) collective-permute-start(s16[208,128]{1,0:T(8,128)(2,1)S(1)} %get-tuple-element.73), channel_id=1, source_target_pairs={{0,32},{32,0},{1,33},{33,1},{2,34},{34,2},{3,35},{35,3},{4,36},{36... | collective-permute-start | bytes 159752 | tf_op jit(solution)/shard_map/ppermute | solution.py:319
  120.9 2.9 %collective-permute-done.28.twin = s16[208,128]{1,0:T(8,128)(2,1)S(1)} collective-permute-done((s16[208,128]{1,0:T(8,128)(2,1)S(1)}, s16[208,128]{1,0:T(8,128)(2,1)S(1)}, u32[]{:S(2)}, u32[]{:S(2)}) %collective-permute-start.28) | collective-permute-done | bytes 53280 | tf_op jit(solution)/shard_map/ppermute | solution.py:319
  123.8 1.0 last.1
  (46 shorter events, 11.9 us)
Async XLA Ops:
  25.9 9.2 %collective-permute-start.4 = (bf16[8,192,128]{2,1,0:T(8,128)(2,1)S(1)}, bf16[8,192,128]{2,1,0:T(8,128)(2,1)S(1)}, u32[]{:S(2)}, u32[]{:S(2)}) collective-permute-start(bf16[8,192,128]{2,1,0:T(8,128)(2,1)S(1)} %all_to_all.5.after.refs_2_), channel_id=1, source_target_pairs={{0,192},{64,0},{128,64},{192,128},{1,193},{65,1},{129,65},{193,129... | collective-permute-start | bytes 1179656 | tf_op jit(solution)/shard_map/ppermute | solution.py:315
  29.0 9.6 %collective-permute-start.3 = (bf16[8,192,128]{2,1,0:T(8,128)(2,1)S(1)}, bf16[8,192,128]{2,1,0:T(8,128)(2,1)S(1)}, u32[]{:S(2)}, u32[]{:S(2)}) collective-permute-start(bf16[8,192,128]{2,1,0:T(8,128)(2,1)S(1)} %all_to_all.5.after.refs_2_), channel_id=1, source_target_pairs={{0,64},{64,128},{128,192},{192,0},{1,65},{65,129},{129,193},{193,1... | collective-permute-start | bytes 1179656 | tf_op jit(solution)/shard_map/ppermute | solution.py:315
  29.0 1.0 copy-start
  30.0 0.7 copy-start.1
  30.9 13.0 %collective-permute-start.2 = (bf16[192,1024]{1,0:T(8,128)(2,1)S(1)}, bf16[192,1024]{1,0:T(8,128)(2,1)S(1)}, u32[]{:S(2)}, u32[]{:S(2)}) collective-permute-start(bf16[192,1024]{1,0:T(8,128)(2,1)S(1)} %hold.1.own), channel_id=1, source_target_pairs={{0,6},{2,4},{4,2},{6,0},{1,7},{3,5},{5,3},{7,1},{8,14},{10,12},{12... | collective-permute-start | bytes 1179656 | tf_op jit(solution)/shard_map/ppermute | solution.py:343
  32.8 15.8 %collective-permute-start.1 = (bf16[192,1024]{1,0:T(8,128)(2,1)S(1)}, bf16[192,1024]{1,0:T(8,128)(2,1)S(1)}, u32[]{:S(2)}, u32[]{:S(2)}) collective-permute-start(bf16[192,1024]{1,0:T(8,128)(2,1)S(1)} %hold.1.own), channel_id=1, source_target_pairs={{0,4},{4,0},{1,5},{5,1},{2,6},{6,2},{3,7},{7,3},{8,12},{12,8},{9,1... | collective-permute-start | bytes 1179656 | tf_op jit(solution)/shard_map/ppermute | solution.py:319
  33.7 15.1 %collective-permute-start = (bf16[192,1024]{1,0:T(8,128)(2,1)S(1)}, bf16[192,1024]{1,0:T(8,128)(2,1)S(1)}, u32[]{:S(2)}, u32[]{:S(2)}) collective-permute-start(bf16[192,1024]{1,0:T(8,128)(2,1)S(1)} %hold.1.own), channel_id=1, source_target_pairs={{0,2},{2,0},{1,3},{3,1},{4,6},{6,4},{5,7},{7,5},{8,10},{10,8},{9,1... | collective-permute-start | bytes 1179656 | tf_op jit(solution)/shard_map/ppermute | solution.py:319
  38.6 10.2 %collective-permute-start.5 = (bf16[4,192,128]{2,1,0:T(8,128)(2,1)S(1)}, bf16[4,192,128]{2,1,0:T(8,128)(2,1)S(1)}, u32[]{:S(2)}, u32[]{:S(2)}) collective-permute-start(bf16[4,192,128]{2,1,0:T(8,128)(2,1)S(1)} %get-tuple-element.42), channel_id=1, source_target_pairs={{0,64},{64,128},{128,192},{192,0},{1,65},{65,129},{129,193},{193,1... | collective-permute-start | bytes 589832 | tf_op jit(solution)/shard_map/ppermute | solution.py:315
  38.7 10.1 %collective-permute-start.6 = (bf16[4,192,128]{2,1,0:T(8,128)(2,1)S(1)}, bf16[4,192,128]{2,1,0:T(8,128)(2,1)S(1)}, u32[]{:S(2)}, u32[]{:S(2)}) collective-permute-start(bf16[4,192,128]{2,1,0:T(8,128)(2,1)S(1)} %get-tuple-element.43), channel_id=1, source_target_pairs={{0,192},{64,0},{128,64},{192,128},{1,193},{65,1},{129,65},{193,129... | collective-permute-start | bytes 589832 | tf_op jit(solution)/shard_map/ppermute | solution.py:315
  48.9 3.5 %collective-permute-start.7 = (bf16[768,1024]{1,0:T(8,128)(2,1)S(1)}, bf16[768,1024]{1,0:T(8,128)(2,1)S(1)}, u32[]{:S(2)}, u32[]{:S(2)}) collective-permute-start(bf16[768,1024]{1,0:T(8,128)(2,1)S(1)} %join.1.refs_0_.refs_11_), channel_id=1, source_target_pairs={{0,1},{1,0},{2,3},{3,2},{4,5},{5,4},{6,7},{7,6},{8,9},{9,8},{10,11... | collective-permute-start | bytes 4718600 | tf_op jit(solution)/shard_map/ppermute | solution.py:319
  57.5 2.1 %collective-permute-start.11 = (f32[2,1536]{1,0:T(2,128)S(1)}, f32[2,1536]{1,0:T(2,128)S(1)}, u32[]{:S(2)}, u32[]{:S(2)}) collective-permute-start(f32[2,1536]{1,0:T(2,128)S(1)} %get-tuple-element.47.c), channel_id=1, source_target_pairs={{0,1},{1,0},{2,3},{3,2},{4,5},{5,4},{6,7},{7,6},{8,9},{9,8},{10,11... | collective-permute-start | bytes 36872 | tf_op jit(solution)/shard_map/ppermute | solution.py:319
  57.7 8.5 %collective-permute-start.10 = (f32[2,768]{1,0:T(2,128)S(1)}, f32[2,768]{1,0:T(2,128)S(1)}, u32[]{:S(2)}, u32[]{:S(2)}) collective-permute-start(f32[2,768]{1,0:T(2,128)S(1)} %get-tuple-element.46.refs_0_), channel_id=1, source_target_pairs={{0,24},{8,0},{16,8},{24,16},{1,25},{9,1},{17,9},{25,17},{2,26},{10... | collective-permute-start | bytes 18440 | tf_op jit(solution)/shard_map/ppermute | solution.py:315
  59.6 12.3 %collective-permute-start.14 = (f32[2,1536]{1,0:T(2,128)S(1)}, f32[2,1536]{1,0:T(2,128)S(1)}, u32[]{:S(2)}, u32[]{:S(2)}) collective-permute-start(f32[2,1536]{1,0:T(2,128)S(1)} %meet.1.refs_4_), channel_id=1, source_target_pairs={{0,6},{2,4},{4,2},{6,0},{1,7},{3,5},{5,3},{7,1},{8,14},{10,12},{12... | collective-permute-start | bytes 36872 | tf_op jit(solution)/shard_map/ppermute | solution.py:360
  60.9 11.1 %collective-permute-start.13 = (f32[2,1536]{1,0:T(2,128)S(1)}, f32[2,1536]{1,0:T(2,128)S(1)}, u32[]{:S(2)}, u32[]{:S(2)}) collective-permute-start(f32[2,1536]{1,0:T(2,128)S(1)} %meet.1.refs_4_), channel_id=1, source_target_pairs={{0,4},{2,6},{4,0},{6,2},{1,5},{3,7},{5,1},{7,3},{8,12},{10,14},{12... | collective-permute-start | bytes 36872 | tf_op jit(solution)/shard_map/ppermute | solution.py:360
  62.5 9.4 %collective-permute-start.12 = (f32[2,1536]{1,0:T(2,128)S(1)}, f32[2,1536]{1,0:T(2,128)S(1)}, u32[]{:S(2)}, u32[]{:S(2)}) collective-permute-start(f32[2,1536]{1,0:T(2,128)S(1)} %meet.1.refs_4_), channel_id=1, source_target_pairs={{0,2},{2,0},{4,6},{6,4},{1,3},{3,1},{5,7},{7,5},{8,10},{10,8},{12,... | collective-permute-start | bytes 36872 | tf_op jit(solution)/shard_map/ppermute | solution.py:360
  63.4 7.5 %collective-permute-start.9 = (f32[2,768]{1,0:T(2,128)S(1)}, f32[2,768]{1,0:T(2,128)S(1)}, u32[]{:S(2)}, u32[]{:S(2)}) collective-permute-start(f32[2,768]{1,0:T(2,128)S(1)} %get-tuple-element.46.refs_0_), channel_id=1, source_target_pairs={{0,16},{8,24},{16,0},{24,8},{1,17},{9,25},{17,1},{25,9},{2,18},{10... | collective-permute-start | bytes 18440 | tf_op jit(solution)/shard_map/ppermute | solution.py:315
  66.2 5.7 %collective-permute-start.8 = (f32[2,768]{1,0:T(2,128)S(1)}, f32[2,768]{1,0:T(2,128)S(1)}, u32[]{:S(2)}, u32[]{:S(2)}) collective-permute-start(f32[2,768]{1,0:T(2,128)S(1)} %get-tuple-element.46.refs_0_), channel_id=1, source_target_pairs={{0,8},{8,16},{16,24},{24,0},{1,9},{9,17},{17,25},{25,1},{2,10},{10... | collective-permute-start | bytes 18440 | tf_op jit(solution)/shard_map/ppermute | solution.py:315
  79.9 3.6 %collective-permute-start.15 = (s16[4,208,1024]{2,1,0:T(8,128)(2,1)S(1)}, s16[4,208,1024]{2,1,0:T(8,128)(2,1)S(1)}, u32[]{:S(2)}, u32[]{:S(2)}) collective-permute-start(s16[4,208,1024]{2,1,0:T(8,128)(2,1)S(1)} %get-tuple-element.51), channel_id=1, source_target_pairs={{0,1},{1,0},{2,3},{3,2},{4,5},{5,4},{6,7},{7,6},{8,9},{9,8},{10,11... | collective-permute-start | bytes 5111816 | tf_op jit(solution)/shard_map/ppermute | solution.py:319
  79.9 8.7 %collective-permute-start.16 = (s16[400,256]{1,0:T(8,128)(2,1)S(1)}, s16[400,256]{1,0:T(8,128)(2,1)S(1)}, u32[]{:S(2)}, u32[]{:S(2)}) collective-permute-start(s16[400,256]{1,0:T(8,128)(2,1)S(1)} %get-tuple-element.56), channel_id=1, source_target_pairs={{0,64},{64,128},{128,192},{192,0},{1,65},{65,129},{129,193},{193,1... | collective-permute-start | bytes 614408 | tf_op jit(solution)/shard_map/ppermute | solution.py:315
  80.2 8.4 %collective-permute-start.17 = (s16[400,256]{1,0:T(8,128)(2,1)S(1)}, s16[400,256]{1,0:T(8,128)(2,1)S(1)}, u32[]{:S(2)}, u32[]{:S(2)}) collective-permute-start(s16[400,256]{1,0:T(8,128)(2,1)S(1)} %get-tuple-element.57), channel_id=1, source_target_pairs={{0,192},{64,0},{128,64},{192,128},{1,193},{65,1},{129,65},{193,129... | collective-permute-start | bytes 614408 | tf_op jit(solution)/shard_map/ppermute | solution.py:315
  84.4 20.3 %collective-permute-start.20 = (s16[2,208,512]{2,1,0:T(8,128)(2,1)S(1)}, s16[2,208,512]{2,1,0:T(8,128)(2,1)S(1)}, u32[]{:S(2)}, u32[]{:S(2)}) collective-permute-start(s16[2,208,512]{2,1,0:T(8,128)(2,1)S(1)} %get-tuple-element.63), channel_id=1, source_target_pairs={{0,2},{2,0},{1,3},{3,1},{4,6},{6,4},{5,7},{7,5},{8,10},{10,8},{9,1... | collective-permute-start | bytes 1277960 | tf_op jit(solution)/shard_map/ppermute | solution.py:319
  85.7 19.0 %collective-permute-start.21 = (s16[2,208,512]{2,1,0:T(8,128)(2,1)S(1)}, s16[2,208,512]{2,1,0:T(8,128)(2,1)S(1)}, u32[]{:S(2)}, u32[]{:S(2)}) collective-permute-start(s16[2,208,512]{2,1,0:T(8,128)(2,1)S(1)} %get-tuple-element.64), channel_id=1, source_target_pairs={{0,4},{4,0},{1,5},{5,1},{2,6},{6,2},{3,7},{7,3},{8,12},{12,8},{9,1... | collective-permute-start | bytes 1277960 | tf_op jit(solution)/shard_map/ppermute | solution.py:319
  89.0 12.2 %collective-permute-start.18 = (s16[784,256]{1,0:T(8,128)(2,1)S(1)}, s16[784,256]{1,0:T(8,128)(2,1)S(1)}, u32[]{:S(2)}, u32[]{:S(2)}) collective-permute-start(s16[784,256]{1,0:T(8,128)(2,1)S(1)} %get-tuple-element.58), channel_id=1, source_target_pairs={{0,64},{64,128},{128,192},{192,0},{1,65},{65,129},{129,193},{193,1... | collective-permute-start | bytes 1204232 | tf_op jit(solution)/shard_map/ppermute | solution.py:315
  90.2 11.0 %collective-permute-start.19 = (s16[784,256]{1,0:T(8,128)(2,1)S(1)}, s16[784,256]{1,0:T(8,128)(2,1)S(1)}, u32[]{:S(2)}, u32[]{:S(2)}) collective-permute-start(s16[784,256]{1,0:T(8,128)(2,1)S(1)} %get-tuple-element.59), channel_id=1, source_target_pairs={{0,192},{64,0},{128,64},{192,128},{1,193},{65,1},{129,65},{193,129... | collective-permute-start | bytes 1204232 | tf_op jit(solution)/shard_map/ppermute | solution.py:315
  101.7 6.7 %collective-permute-start.25 = (s16[208,128]{1,0:T(8,128)(2,1)S(1)}, s16[208,128]{1,0:T(8,128)(2,1)S(1)}, u32[]{:S(2)}, u32[]{:S(2)}) collective-permute-start(s16[208,128]{1,0:T(8,128)(2,1)S(1)} %get-tuple-element.69), channel_id=1, source_target_pairs={{0,24},{8,0},{16,8},{24,16},{1,25},{9,1},{17,9},{25,17},{2,26},{10... | collective-permute-start | bytes 159752 | tf_op jit(solution)/shard_map/ppermute | solution.py:315
  102.4 7.3 %collective-permute-start.24 = (s16[208,128]{1,0:T(8,128)(2,1)S(1)}, s16[208,128]{1,0:T(8,128)(2,1)S(1)}, u32[]{:S(2)}, u32[]{:S(2)}) collective-permute-start(s16[208,128]{1,0:T(8,128)(2,1)S(1)} %get-tuple-element.60.after), channel_id=1, source_target_pairs={{0,8},{8,16},{16,24},{24,0},{1,9},{9,17},{17,25},{25,1},{2,10},{10... | collective-permute-start | bytes 159752 | tf_op jit(solution)/shard_map/ppermute | solution.py:315
  105.2 18.6 %collective-permute-start.23 = (s16[208,512]{1,0:T(8,128)(2,1)S(1)}, s16[208,512]{1,0:T(8,128)(2,1)S(1)}, u32[]{:S(2)}, u32[]{:S(2)}) collective-permute-start(s16[208,512]{1,0:T(8,128)(2,1)S(1)} %get-tuple-element.67), channel_id=1, source_target_pairs={{0,4},{4,0},{1,5},{5,1},{2,6},{6,2},{3,7},{7,3},{8,12},{12,8},{9,1... | collective-permute-start | bytes 638984 | tf_op jit(solution)/shard_map/ppermute | solution.py:319
  107.2 16.5 %collective-permute-start.22 = (s16[208,512]{1,0:T(8,128)(2,1)S(1)}, s16[208,512]{1,0:T(8,128)(2,1)S(1)}, u32[]{:S(2)}, u32[]{:S(2)}) collective-permute-start(s16[208,512]{1,0:T(8,128)(2,1)S(1)} %get-tuple-element.66.after), channel_id=1, source_target_pairs={{0,2},{2,0},{1,3},{3,1},{4,6},{6,4},{5,7},{7,5},{8,10},{10,8},{9,1... | collective-permute-start | bytes 638984 | tf_op jit(solution)/shard_map/ppermute | solution.py:319
  109.8 8.2 %collective-permute-start.26 = (s16[2,208,128]{2,1,0:T(8,128)(2,1)S(1)}, s16[2,208,128]{2,1,0:T(8,128)(2,1)S(1)}, u32[]{:S(2)}, u32[]{:S(2)}) collective-permute-start(s16[2,208,128]{2,1,0:T(8,128)(2,1)S(1)} %get-tuple-element.70), channel_id=1, source_target_pairs={{0,8},{8,16},{16,24},{24,0},{1,9},{9,17},{17,25},{25,1},{2,10},{10... | collective-permute-start | bytes 319496 | tf_op jit(solution)/shard_map/ppermute | solution.py:315
  110.5 7.4 %collective-permute-start.27 = (s16[2,208,128]{2,1,0:T(8,128)(2,1)S(1)}, s16[2,208,128]{2,1,0:T(8,128)(2,1)S(1)}, u32[]{:S(2)}, u32[]{:S(2)}) collective-permute-start(s16[2,208,128]{2,1,0:T(8,128)(2,1)S(1)} %get-tuple-element.71), channel_id=1, source_target_pairs={{0,24},{8,0},{16,8},{24,16},{1,25},{9,1},{17,9},{25,17},{2,26},{10... | collective-permute-start | bytes 319496 | tf_op jit(solution)/shard_map/ppermute | solution.py:315
  118.1 5.7 %collective-permute-start.28 = (s16[208,128]{1,0:T(8,128)(2,1)S(1)}, s16[208,128]{1,0:T(8,128)(2,1)S(1)}, u32[]{:S(2)}, u32[]{:S(2)}) collective-permute-start(s16[208,128]{1,0:T(8,128)(2,1)S(1)} %get-tuple-element.73), channel_id=1, source_target_pairs={{0,32},{32,0},{1,33},{33,1},{2,34},{34,2},{3,35},{35,3},{4,36},{36... | collective-permute-start | bytes 159752 | tf_op jit(solution)/shard_map/ppermute | solution.py:319
where the time goes:
time: 127 us; the launch traced here: 125 us
  starting transfers between devices  42.4 us (33%)
  waiting for transfers between devices  37.8 us (30%)
  blocking collectives  24.5 us (19%)
  Pallas kernels  16.9 us (13%)
  local copies, waits for them, and re-layouts  2.58 us (2%)
    ppermute x15, starting transfers between devices, shift(): return lax.ppermute(x, axis, [(i, (i + k) % n) for i in range(n)])  25.3 us
    all_to_all x1, blocking collectives, on_device(): lax.all_to_all(jnp.broadcast_to(image, (2 * nzh, rows, width)), ('xh', 'z...  24.5 us
    ppermute x15, waiting for transfers between devices, shift(): return lax.ppermute(x, axis, [(i, (i + k) % n) for i in range(n)])  24.3 us
    ppermute x10, starting transfers between devices, flip(): return lax.ppermute(x, axis, [(i, i ^ d) for i in range(n)])  11.5 us
    ppermute x10, waiting for transfers between devices, flip(): return lax.ppermute(x, axis, [(i, i ^ d) for i in range(n)])  11.4 us
    pallas_call x1, Pallas kernels, on_device(): call(functools.partial(weights_kernel, scale, tile), outs, 'weights', 36,...  7.93 us
    pallas_call x1, Pallas kernels, on_device(): call(functools.partial(scores_kernel, scale, tile), [shape((n_im, n_ks),...  5.06 us
    ppermute x3, starting transfers between devices, on_device(): lax.ppermute(cs, ('zl', 'xl'), [(i, i ^ k) for i in range(4)])  3.76 us
  transfers between devices with their start and end apart: 29, of which 14 were waited for; matrix products, arithmetic and copies ran while one was open for 0% of the time, Pallas kernels for 2%

commit v1 on v0

--- a/solution.py
+++ b/solution.py
@@ -95,18 +95,23 @@
     cols[...] = (lax.axis_index("zh") * n_ks + (block - k) * rows + p).astype(F32)
 
 
-def join_kernel(own, x, z, d, after_a, after_b, out):
+def join_kernel(own, x, z, d_top, d_low, after_a, after_b, out):
     del after_a, after_b
     rows = own.shape[0]
     xl = lax.axis_index("xl")
-    for k, (mine, beside) in enumerate(((own, x), (z, d))):
-        out[pl.ds(pl.multiple_of((2 * k + xl) * rows, 16), rows), :] = mine[...]
-        out[pl.ds(pl.multiple_of((2 * k + 1 - xl) * rows, 16), rows), :] = beside[...]
-
-
-def hold_kernel(keys, after, out):
+    for k, parts in enumerate(((own,), (x,), (z,), (d_top, d_low))):
+        at = (k // 2 * 2 + (xl ^ (k % 2))) * rows
+        for part in parts:
+            n = part.shape[0]
+            out[pl.ds(pl.multiple_of(at, 16), n), :] = part[...]
+            at += n
+
+
+def hold_kernel(x, z, after, z_top, x_low):
     del after
-    out[...] = keys[...]
+    n = z_top.shape[0]
+    z_top[...] = z[:n, :]
+    x_low[...] = x[n:, :]
 
 
 def turn_kernel(behind, ahead, half_a, half_b):
@@ -115,7 +120,7 @@
     half_b[...] = ahead[n:]
 
 
-def scores_kernel(scale, tile, *refs):
+def scores_kernel(scale, *refs):
     keys, (i0, i1, i3, ia, ib, pairs, cols, s_ref, im, rs, cs) = refs[:2], refs[2:]
     y = lax.axis_index("y")
     nzh, rows, width = ia.shape
@@ -133,45 +138,36 @@
     place(2, 0, ia, 0)
     place(2, 1, ib, 0)
 
-    rows_of = [slice(r, r + tile) for r in range(0, n_im, tile)]
-    col_top, col_sum, col_pick = [None] * 2, [None] * 2, [None] * 2
-    row_state = [None] * len(rows_of)
-
-    def online(s, state, axis):
-        top = jnp.max(s, axis=axis, keepdims=True)
-        if state is None:
-            return top, jnp.sum(jnp.exp(s - top), axis=axis, keepdims=True)
-        new = jnp.maximum(state[0], top)
-        return new, state[1] * jnp.exp(state[0] - new) + jnp.sum(jnp.exp(s - new), axis=axis, keepdims=True)
-
-    def stats(h, r):
-        lanes = slice(h * part, (h + 1) * part)
-        s = s_ref[rows_of[r], lanes]
-        picked = jnp.where(to_rows(pairs[:, rows_of[r]]) == cols[:, lanes], s, F32(0))
-        old = row_state[r]
-        top, total = online(s, old and old[:2], 1)
+    chunk = min(256, part)
+    row = [None]
+
+    def stats(c):
+        s = s_ref[:, c : c + chunk]
+        picked = jnp.where(targets == cols[:, c : c + chunk], s, F32(0))
+        top = jnp.max(s, axis=0, keepdims=True)
+        cs[0:1, c : c + chunk] = top + jnp.log(jnp.sum(jnp.exp(s - top), axis=0, keepdims=True))
+        cs[1:2, c : c + chunk] = jnp.sum(picked, axis=0, keepdims=True)
+        top = jnp.max(s, axis=1, keepdims=True)
         pick = jnp.sum(picked, axis=1, keepdims=True)
-        row_state[r] = (top, total, pick if old is None else old[2] + pick)
-        state = None if col_top[h] is None else (col_top[h], col_sum[h])
-        col_top[h], col_sum[h] = online(s, state, 0)
-        pick = jnp.sum(picked, axis=0, keepdims=True)
-        col_pick[h] = pick if col_pick[h] is None else col_pick[h] + pick
-
-    before = None
-    for h, ks in enumerate(keys):
-        for r in range(len(rows_of)):
-            s = lax.dot_general(im[rows_of[r], :], ks[...], LAST, preferred_element_type=F32)
-            s_ref[rows_of[r], h * part : (h + 1) * part] = s * scale
-            if before:
-                stats(*before)
-            before = (h, r)
-    stats(*before)
-    for r, (top, total, pick) in enumerate(row_state):
-        rs[0:1, rows_of[r]] = to_lanes(top + jnp.log(total))
-        rs[1:2, rows_of[r]] = to_lanes(pick)
-    for h in range(2):
-        cs[0:1, h * part : (h + 1) * part] = col_top[h] + jnp.log(col_sum[h])
-        cs[1:2, h * part : (h + 1) * part] = col_pick[h]
+        if row[0] is None:
+            row[0] = (top, jnp.sum(jnp.exp(s - top), axis=1, keepdims=True), pick)
+        else:
+            old, total, before = row[0]
+            new = jnp.maximum(old, top)
+            total = total * jnp.exp(old - new) + jnp.sum(jnp.exp(s - new), axis=1, keepdims=True)
+            row[0] = (new, total, before + pick)
+
+    targets = to_rows(pairs[...])
+    for c in range(0, 2 * part, chunk):
+        at = c % part
+        s = lax.dot_general(im[...], keys[c // part][at : at + chunk, :], LAST, preferred_element_type=F32)
+        s_ref[:, c : c + chunk] = s * scale
+        if c:
+            stats(c - chunk)
+    stats(2 * part - chunk)
+    top, total, pick = row[0]
+    rs[0:1, :] = to_lanes(top + jnp.log(total))
+    rs[1:2, :] = to_lanes(pick)
 
 
 def merge(parts):
@@ -337,19 +333,22 @@
     )(pair_index, keys)
     i0 = lax.all_to_all(jnp.broadcast_to(image, (2 * nzh, rows, width)), ("xh", "zh"), 0, 0)
     i1, i3 = shift(i0, "y", 4, 1), shift(i0, "y", 4, 3)
-    held = call(hold_kernel, shape((rows, d), BF16), "hold", 8, in_specs=[vmem] * 2)(held, i0)
-    key_x = flip(held, "xl", 2, 1)
-    key_z = flip(held, "zl", 2, 1)
-    key_d = lax.ppermute(held, ("zl", "xl"), [(i, 3 - i) for i in range(4)])
+    key_x = flip(keys, "xl", 2, 1)
+    key_z = flip(keys, "zl", 2, 1)
+    quarter = shape((rows // 2, d), BF16)
+    d_top, d_low = call(hold_kernel, [quarter] * 2, "hold", 8, in_specs=[vmem] * 3)(key_x, key_z, i0)
+    d_top, d_low = flip(d_top, "xl", 2, 1), flip(d_low, "zl", 2, 1)
     half_block = shape((nzh, rows, width), BF16)
     ia, ib = call(turn_kernel, [half_block] * 2, "turn", 12, in_specs=[vmem] * 2)(i1, i3)
     ia, ib = shift(ia, "y", 4, 1), shift(ib, "y", 4, 3)
-    k0 = call(join_kernel, shape((half, d), BF16), "join", 12, in_specs=[vmem] * 6)(held, key_x, key_z, key_d, ia, ib)
+    k0 = call(join_kernel, shape((half, d), BF16), "join", 12, in_specs=[vmem] * 7)(
+        held, key_x, key_z, d_top, d_low, ia, ib
+    )
     ks = [k0, flip(k0, "core", 2, 1)]
 
-    tile = min(256, n_im)
+    tile = min(384, n_im)
     scores, im, rs, cs = call(
-        functools.partial(scores_kernel, scale, tile),
+        functools.partial(scores_kernel, scale),
         [shape((n_im, n_ks), F32), shape((n_im, d), BF16), shape((2, n_im), F32), shape((2, n_ks), F32)],
         "scores",
         28,

time: 127 us -> 127 us (level)
  blocking collectives: 24.5 us -> 0 us
  waiting for transfers between devices: 37.8 us -> 53.7 us
  starting transfers between devices: 42.4 us -> 52.7 us
    all_to_all x1 -> x0, blocking collectives: 24.5 us -> none  [on_device(): lax.all_to_all(jnp.broadcast_to(image, (2 * nzh, rows, width)), ('xh', 'z...]
    all_to_all x0 -> x1, waiting for transfers between devices: none -> 11.6 us  [on_device(): lax.all_to_all(jnp.broadcast_to(image, (2 * nzh, rows, width)), ('xh', 'z...]
    all_to_all x0 -> x1, starting transfers between devices: none -> 11.4 us  [on_device(): lax.all_to_all(jnp.broadcast_to(image, (2 * nzh, rows, width)), ('xh', 'z...]
    ppermute x15, waiting for transfers between devices: 24.3 us -> 32.9 us  [shift(): return lax.ppermute(x, axis, [(i, (i + k) % n) for i in range(n)])]
    ppermute x10 -> x12, starting transfers between devices: 11.5 us -> 14 us  [flip(): return lax.ppermute(x, axis, [(i, i ^ d) for i in range(n)])]
    ppermute x10 -> x12, waiting for transfers between devices: 11.4 us -> 9.28 us  [flip(): return lax.ppermute(x, axis, [(i, i ^ d) for i in range(n)])]
    ppermute x1 -> x0, waiting for transfers between devices: 2.05 us -> none  [on_device(): key_d = lax.ppermute(held, ('zl', 'xl'), [(i, 3 - i) for i in range(4)])]
    ppermute x15, starting transfers between devices: 25.3 us -> 23.4 us  [shift(): return lax.ppermute(x, axis, [(i, (i + k) % n) for i in range(n)])]
  transfers between devices with their start and end apart: 29 -> 31, of which waited for: 14 -> 14; matrix products, arithmetic and copies ran while one was open for 0% -> 0% of each run, Pallas kernels for 2% -> 2%
where the time goes in v1:
time: 127 us; the launch traced here: 125 us
  waiting for transfers between devices  53.7 us (42%)
  starting transfers between devices  52.7 us (41%)
  Pallas kernels  16.4 us (13%)
  local copies, waits for them, and re-layouts  1.65 us (1%)
    ppermute x15, waiting for transfers between devices, shift(): return lax.ppermute(x, axis, [(i, (i + k) % n) for i in range(n)])  32.9 us
    ppermute x15, starting transfers between devices, shift(): return lax.ppermute(x, axis, [(i, (i + k) % n) for i in range(n)])  23.4 us
    ppermute x12, starting transfers between devices, flip(): return lax.ppermute(x, axis, [(i, i ^ d) for i in range(n)])  14 us
    all_to_all x1, waiting for transfers between devices, on_device(): lax.all_to_all(jnp.broadcast_to(image, (2 * nzh, rows, width)), ('xh', 'z...  11.6 us
    all_to_all x1, starting transfers between devices, on_device(): lax.all_to_all(jnp.broadcast_to(image, (2 * nzh, rows, width)), ('xh', 'z...  11.4 us
    ppermute x12, waiting for transfers between devices, flip(): return lax.ppermute(x, axis, [(i, i ^ d) for i in range(n)])  9.28 us
    pallas_call x1, Pallas kernels, on_device(): call(functools.partial(weights_kernel, scale, tile), outs, 'weights', 36,...  7.85 us
    pallas_call x1, Pallas kernels, on_device(): call(functools.partial(scores_kernel, scale), [shape((n_im, n_ks), F32),...  4.7 us
  transfers between devices with their start and end apart: 31, of which 14 were waited for; matrix products, arithmetic and copies ran while one was open for 0% of the time, Pallas kernels for 2%

profile of v1, /device:TPU:4, one launch (start us, length us, event | category | flops | bytes accessed | tf_op | source)
XLA Modules:
  0.0 125.2 jit_solution(1116021998161830604)
XLA Ops:
  0.7 1.6 %broadcast_in_dim.6 = bf16[8,192,128]{2,1,0:T(8,128)(2,1)} broadcast(bf16[192,128]{1,0:T(8,128)(2,1)} %param.3), dimensions={1,2} | broadcast | bytes 442368 | tf_op jit(solution)/shard_map/broadcast_in_dim | solution.py:334
  2.3 11.4 %all-to-all-start = ((bf16[8,192,128]{2,1,0:T(8,128)(2,1)}), bf16[8,192,128]{2,1,0:T(8,128)(2,1)S(1)}, u32[]{:S(2)}, u32[]{:S(2)}) async-start(bf16[8,192,128]{2,1,0:T(8,128)(2,1)} %broadcast_in_dim.6), calls=%async_computation | async-start | bytes 786432 | tf_op jit(solution)/shard_map/all_to_all | solution.py:334
  14.7 1.2 collective-permute-start
  15.9 11.6 %all-to-all-done.after.refs_2_ = bf16[8,192,128]{2,1,0:T(8,128)(2,1)S(1)} async-done(((bf16[8,192,128]{2,1,0:T(8,128)(2,1)}), bf16[8,192,128]{2,1,0:T(8,128)(2,1)S(1)}, u32[]{:S(2)}, u32[]{:S(2)}) %all-to-all-start) | async-done | bytes 393248 | tf_op jit(solution)/shard_map/all_to_all | solution.py:334
  27.5 3.0 %collective-permute-start.5 = (bf16[8,192,128]{2,1,0:T(8,128)(2,1)S(1)}, bf16[8,192,128]{2,1,0:T(8,128)(2,1)S(1)}, u32[]{:S(2)}, u32[]{:S(2)}) collective-permute-start(bf16[8,192,128]{2,1,0:T(8,128)(2,1)S(1)} %all-to-all-done.after.refs_2_), channel_id=1, source_target_pairs={{0,192},{64,0},{128,64},{192,128},{1,193},{65,1},{129,65},{193,129... | collective-permute-start | bytes 1179656 | tf_op jit(solution)/shard_map/ppermute | solution.py:311
  30.5 1.4 %collective-permute-done.1.z = bf16[192,1024]{1,0:T(8,128)(2,1)S(1)} collective-permute-done((bf16[192,1024]{1,0:T(8,128)(2,1)}, bf16[192,1024]{1,0:T(8,128)(2,1)S(1)}, u32[]{:S(2)}, u32[]{:S(2)}) %collective-permute-start.1) | collective-permute-done | bytes 393248 | tf_op jit(solution)/shard_map/ppermute | solution.py:315
  32.0 1.3 %collective-permute-start.2 = (bf16[96,1024]{1,0:T(8,128)(2,1)S(1)}, bf16[96,1024]{1,0:T(8,128)(2,1)S(1)}, u32[]{:S(2)}, u32[]{:S(2)}) collective-permute-start(bf16[96,1024]{1,0:T(8,128)(2,1)S(1)} %get-tuple-element.44), channel_id=1, source_target_pairs={{0,2},{2,0},{1,3},{3,1},{4,6},{6,4},{5,7},{7,5},{8,10},{10,8},{9,1... | collective-permute-start | bytes 589832 | tf_op jit(solution)/shard_map/ppermute | solution.py:315
  34.3 1.5 %collective-permute-done.5.ahead.refs_4_ = bf16[8,192,128]{2,1,0:T(8,128)(2,1)S(1)} collective-permute-done((bf16[8,192,128]{2,1,0:T(8,128)(2,1)S(1)}, bf16[8,192,128]{2,1,0:T(8,128)(2,1)S(1)}, u32[]{:S(2)}, u32[]{:S(2)}) %collective-permute-start.5) | collective-permute-done | bytes 393248 | tf_op jit(solution)/shard_map/ppermute | solution.py:311
  35.8 5.7 %collective-permute-done.4.behind.refs_3_ = bf16[8,192,128]{2,1,0:T(8,128)(2,1)S(1)} collective-permute-done((bf16[8,192,128]{2,1,0:T(8,128)(2,1)S(1)}, bf16[8,192,128]{2,1,0:T(8,128)(2,1)S(1)}, u32[]{:S(2)}, u32[]{:S(2)}) %collective-permute-start.4) | collective-permute-done | bytes 393248 | tf_op jit(solution)/shard_map/ppermute | solution.py:311
  41.7 3.2 %collective-permute-start.7 = (bf16[4,192,128]{2,1,0:T(8,128)(2,1)S(1)}, bf16[4,192,128]{2,1,0:T(8,128)(2,1)S(1)}, u32[]{:S(2)}, u32[]{:S(2)}) collective-permute-start(bf16[4,192,128]{2,1,0:T(8,128)(2,1)S(1)} %get-tuple-element.47), channel_id=1, source_target_pairs={{0,192},{64,0},{128,64},{192,128},{1,193},{65,1},{129,65},{193,129... | collective-permute-start | bytes 589832 | tf_op jit(solution)/shard_map/ppermute | solution.py:311
  45.1 3.4 %collective-permute-done.6.after_a.refs_5_ = bf16[4,192,128]{2,1,0:T(8,128)(2,1)S(1)} collective-permute-done((bf16[4,192,128]{2,1,0:T(8,128)(2,1)S(1)}, bf16[4,192,128]{2,1,0:T(8,128)(2,1)S(1)}, u32[]{:S(2)}, u32[]{:S(2)}) %collective-permute-start.6) | collective-permute-done | bytes 196640 | tf_op jit(solution)/shard_map/ppermute | solution.py:311
  48.8 3.4 %collective-permute-done.8.refs_1_.refs_12_ = bf16[768,1024]{1,0:T(8,128)(2,1)S(1)} collective-permute-done((bf16[768,1024]{1,0:T(8,128)(2,1)S(1)}, bf16[768,1024]{1,0:T(8,128)(2,1)S(1)}, u32[]{:S(2)}, u32[]{:S(2)}) %collective-permute-start.8) | collective-permute-done | bytes 1572896 | tf_op jit(solution)/shard_map/ppermute | solution.py:315
  52.2 4.7 %scores.1 = (f32[768,1536]{1,0:T(8,128)S(1)}, bf16[768,1024]{1,0:T(8,128)(2,1)S(1)}, f32[2,768]{1,0:T(2,128)S(1)}, f32[2,1536]{1,0:T(2,128)S(1)}) custom-call(bf16[768,1024]{1,0:T(8,128)(2,1)S(1)} %join.1.refs_0_.refs_11_, bf16[768,1024]{1,0:T(8,128)(2,1)S(1)} %collective-permute-done.8.refs_1_.refs_12_, ...), custom_call_target="tpu_custom_call" | custom-call | flops 1000 | bytes 1000 | tf_op jit(solution)/shard_map/scores/pallas_call | solution.py:350
  58.2 3.1 %collective-permute-start.15 = (f32[2,1536]{1,0:T(2,128)S(1)}, f32[2,1536]{1,0:T(2,128)S(1)}, u32[]{:S(2)}, u32[]{:S(2)}) collective-permute-start(f32[2,1536]{1,0:T(2,128)S(1)} %meet.1.refs_4_), channel_id=1, source_target_pairs={{0,6},{2,4},{4,2},{6,0},{1,7},{3,5},{5,3},{7,1},{8,14},{10,12},{12... | collective-permute-start | bytes 36872 | tf_op jit(solution)/shard_map/ppermute | solution.py:359
  62.1 1.5 %collective-permute-start.10 = (f32[2,768]{1,0:T(2,128)S(1)}, f32[2,768]{1,0:T(2,128)S(1)}, u32[]{:S(2)}, u32[]{:S(2)}) collective-permute-start(f32[2,768]{1,0:T(2,128)S(1)} %get-tuple-element.50.refs_0_), channel_id=1, source_target_pairs={{0,16},{8,24},{16,0},{24,8},{1,17},{9,25},{17,1},{25,9},{2,18},{10... | collective-permute-start | bytes 18440 | tf_op jit(solution)/shard_map/ppermute | solution.py:311
  63.6 1.5 %collective-permute-start.9 = (f32[2,768]{1,0:T(2,128)S(1)}, f32[2,768]{1,0:T(2,128)S(1)}, u32[]{:S(2)}, u32[]{:S(2)}) collective-permute-start(f32[2,768]{1,0:T(2,128)S(1)} %get-tuple-element.50.refs_0_), channel_id=1, source_target_pairs={{0,8},{8,16},{16,24},{24,0},{1,9},{9,17},{17,25},{25,1},{2,10},{10... | collective-permute-start | bytes 18440 | tf_op jit(solution)/shard_map/ppermute | solution.py:311
  65.0 4.6 %collective-permute-done.10.refs_2_ = f32[2,768]{1,0:T(2,128)S(1)} collective-permute-done((f32[2,768]{1,0:T(2,128)S(1)}, f32[2,768]{1,0:T(2,128)S(1)}, u32[]{:S(2)}, u32[]{:S(2)}) %collective-permute-start.10) | collective-permute-done | bytes 6176 | tf_op jit(solution)/shard_map/ppermute | solution.py:311
  69.6 7.9 %weights.1 = (f32[768,256]{1,0:T(8,128)S(1)}, f32[768,256]{1,0:T(8,128)S(1)}, f32[768,256]{1,0:T(8,128)S(1)}, s16[400,256]{1,0:T(8,128)(2,1)S(1)}, s16[400,256]{...) custom-call(f32[2,768]{1,0:T(2,128)S(1)} %get-tuple-element.50.refs_, ...), custom_call_target="tpu_custom_call" | custom-call | flops 1000 | bytes 1000 | tf_op jit(solution)/shard_map/weights/pallas_call | solution.py:362
  77.5 3.3 %collective-permute-start.18 = (s16[400,256]{1,0:T(8,128)(2,1)S(1)}, s16[400,256]{1,0:T(8,128)(2,1)S(1)}, u32[]{:S(2)}, u32[]{:S(2)}) collective-permute-start(s16[400,256]{1,0:T(8,128)(2,1)S(1)} %get-tuple-element.61), channel_id=1, source_target_pairs={{0,192},{64,0},{128,64},{192,128},{1,193},{65,1},{129,65},{193,129... | collective-permute-start | bytes 614408 | tf_op jit(solution)/shard_map/ppermute | solution.py:311
  82.0 1.5 %collective-permute-start.21 = (s16[2,208,512]{2,1,0:T(8,128)(2,1)S(1)}, s16[2,208,512]{2,1,0:T(8,128)(2,1)S(1)}, u32[]{:S(2)}, u32[]{:S(2)}) collective-permute-start(s16[2,208,512]{2,1,0:T(8,128)(2,1)S(1)} %get-tuple-element.67), channel_id=1, source_target_pairs={{0,2},{2,0},{1,3},{3,1},{4,6},{6,4},{5,7},{7,5},{8,10},{10,8},{9,1... | collective-permute-start | bytes 1277960 | tf_op jit(solution)/shard_map/ppermute | solution.py:315
  83.5 2.0 %collective-permute-start.22 = (s16[2,208,512]{2,1,0:T(8,128)(2,1)S(1)}, s16[2,208,512]{2,1,0:T(8,128)(2,1)S(1)}, u32[]{:S(2)}, u32[]{:S(2)}) collective-permute-start(s16[2,208,512]{2,1,0:T(8,128)(2,1)S(1)} %get-tuple-element.68), channel_id=1, source_target_pairs={{0,4},{4,0},{1,5},{5,1},{2,6},{6,2},{3,7},{7,3},{8,12},{12,8},{9,1... | collective-permute-start | bytes 1277960 | tf_op jit(solution)/shard_map/ppermute | solution.py:315
  86.8 1.2 collective-permute-start.19
  88.1 2.1 %collective-permute-start.20 = (s16[784,256]{1,0:T(8,128)(2,1)S(1)}, s16[784,256]{1,0:T(8,128)(2,1)S(1)}, u32[]{:S(2)}, u32[]{:S(2)}) collective-permute-start(s16[784,256]{1,0:T(8,128)(2,1)S(1)} %get-tuple-element.63), channel_id=1, source_target_pairs={{0,192},{64,0},{128,64},{192,128},{1,193},{65,1},{129,65},{193,129... | collective-permute-start | bytes 1204232 | tf_op jit(solution)/shard_map/ppermute | solution.py:311
  90.2 9.1 %collective-permute-done.19.got1 = s16[784,256]{1,0:T(8,128)(2,1)S(1)} collective-permute-done((s16[784,256]{1,0:T(8,128)(2,1)S(1)}, s16[784,256]{1,0:T(8,128)(2,1)S(1)}, u32[]{:S(2)}, u32[]{:S(2)}) %collective-permute-start.19) | collective-permute-done | bytes 401440 | tf_op jit(solution)/shard_map/ppermute | solution.py:311
  99.8 2.7 %collective-permute-start.26 = (s16[208,128]{1,0:T(8,128)(2,1)S(1)}, s16[208,128]{1,0:T(8,128)(2,1)S(1)}, u32[]{:S(2)}, u32[]{:S(2)}) collective-permute-start(s16[208,128]{1,0:T(8,128)(2,1)S(1)} %get-tuple-element.73), channel_id=1, source_target_pairs={{0,24},{8,0},{16,8},{24,16},{1,25},{9,1},{17,9},{25,17},{2,26},{10... | collective-permute-start | bytes 159752 | tf_op jit(solution)/shard_map/ppermute | solution.py:311
  103.2 2.1 %collective-permute-start.24 = (s16[208,512]{1,0:T(8,128)(2,1)S(1)}, s16[208,512]{1,0:T(8,128)(2,1)S(1)}, u32[]{:S(2)}, u32[]{:S(2)}) collective-permute-start(s16[208,512]{1,0:T(8,128)(2,1)S(1)} %get-tuple-element.71), channel_id=1, source_target_pairs={{0,4},{4,0},{1,5},{5,1},{2,6},{6,2},{3,7},{7,3},{8,12},{12,8},{9,1... | collective-permute-start | bytes 638984 | tf_op jit(solution)/shard_map/ppermute | solution.py:315
  105.3 1.2 collective-permute-start.23
  106.5 2.8 %collective-permute-done.25.got_a = s16[208,128]{1,0:T(8,128)(2,1)S(1)} collective-permute-done((s16[208,128]{1,0:T(8,128)(2,1)S(1)}, s16[208,128]{1,0:T(8,128)(2,1)S(1)}, u32[]{:S(2)}, u32[]{:S(2)}) %collective-permute-start.25) | collective-permute-done | bytes 53280 | tf_op jit(solution)/shard_map/ppermute | solution.py:311
  109.9 3.7 %collective-permute-start.28 = (s16[2,208,128]{2,1,0:T(8,128)(2,1)S(1)}, s16[2,208,128]{2,1,0:T(8,128)(2,1)S(1)}, u32[]{:S(2)}, u32[]{:S(2)}) collective-permute-start(s16[2,208,128]{2,1,0:T(8,128)(2,1)S(1)} %get-tuple-element.75), channel_id=1, source_target_pairs={{0,24},{8,0},{16,8},{24,16},{1,25},{9,1},{17,9},{25,17},{2,26},{10... | collective-permute-start | bytes 319496 | tf_op jit(solution)/shard_map/ppermute | solution.py:311
  113.7 4.7 %collective-permute-done.27.up = s16[2,208,128]{2,1,0:T(8,128)(2,1)S(1)} collective-permute-done((s16[2,208,128]{2,1,0:T(8,128)(2,1)S(1)}, s16[2,208,128]{2,1,0:T(8,128)(2,1)S(1)}, u32[]{:S(2)}, u32[]{:S(2)}) %collective-permute-start.27) | collective-permute-done | bytes 106528 | tf_op jit(solution)/shard_map/ppermute | solution.py:311
  118.5 2.4 %collective-permute-start.29 = (s16[208,128]{1,0:T(8,128)(2,1)S(1)}, s16[208,128]{1,0:T(8,128)(2,1)S(1)}, u32[]{:S(2)}, u32[]{:S(2)}) collective-permute-start(s16[208,128]{1,0:T(8,128)(2,1)S(1)} %get-tuple-element.77), channel_id=1, source_target_pairs={{0,32},{32,0},{1,33},{33,1},{2,34},{34,2},{3,35},{35,3},{4,36},{36... | collective-permute-start | bytes 159752 | tf_op jit(solution)/shard_map/ppermute | solution.py:315
  120.9 3.3 %collective-permute-done.29.twin = s16[208,128]{1,0:T(8,128)(2,1)S(1)} collective-permute-done((s16[208,128]{1,0:T(8,128)(2,1)S(1)}, s16[208,128]{1,0:T(8,128)(2,1)S(1)}, u32[]{:S(2)}, u32[]{:S(2)}) %collective-permute-start.29) | collective-permute-done | bytes 53280 | tf_op jit(solution)/shard_map/ppermute | solution.py:315
  (49 shorter events, 10.3 us)
Async XLA Ops:
  0.6 44.3 %copy-start = (bf16[1,192,1024]{2,1,0:T(8,128)(2,1)S(1)}, bf16[1,192,1024]{2,1,0:T(8,128)(2,1)}, u32[]{:S(2)}) copy-start(bf16[1,192,1024]{2,1,0:T(8,128)(2,1)} %param.4) | copy-start | bytes 1179652
  2.3 25.2 %all-to-all-start = ((bf16[8,192,128]{2,1,0:T(8,128)(2,1)}), bf16[8,192,128]{2,1,0:T(8,128)(2,1)S(1)}, u32[]{:S(2)}, u32[]{:S(2)}) async-start(bf16[8,192,128]{2,1,0:T(8,128)(2,1)} %broadcast_in_dim.6), calls=%async_computation | async-start | bytes 786432 | tf_op jit(solution)/shard_map/all_to_all | solution.py:334
  13.7 18.2 %collective-permute-start.1 = (bf16[192,1024]{1,0:T(8,128)(2,1)}, bf16[192,1024]{1,0:T(8,128)(2,1)S(1)}, u32[]{:S(2)}, u32[]{:S(2)}) collective-permute-start(bf16[192,1024]{1,0:T(8,128)(2,1)} %bitcast.2), channel_id=1, source_target_pairs={{0,4},{4,0},{1,5},{5,1},{2,6},{6,2},{3,7},{7,3},{8,12},{12,8},{9,1... | collective-permute-start | bytes 1179656 | tf_op jit(solution)/shard_map/ppermute | solution.py:315
  14.7 17.2 %collective-permute-start = (bf16[192,1024]{1,0:T(8,128)(2,1)}, bf16[192,1024]{1,0:T(8,128)(2,1)S(1)}, u32[]{:S(2)}, u32[]{:S(2)}) collective-permute-start(bf16[192,1024]{1,0:T(8,128)(2,1)} %bitcast.3), channel_id=1, source_target_pairs={{0,2},{2,0},{1,3},{3,1},{4,6},{6,4},{5,7},{7,5},{8,10},{10,8},{9,1... | collective-permute-start | bytes 1179656 | tf_op jit(solution)/shard_map/ppermute | solution.py:315
  27.5 8.3 %collective-permute-start.5 = (bf16[8,192,128]{2,1,0:T(8,128)(2,1)S(1)}, bf16[8,192,128]{2,1,0:T(8,128)(2,1)S(1)}, u32[]{:S(2)}, u32[]{:S(2)}) collective-permute-start(bf16[8,192,128]{2,1,0:T(8,128)(2,1)S(1)} %all-to-all-done.after.refs_2_), channel_id=1, source_target_pairs={{0,192},{64,0},{128,64},{192,128},{1,193},{65,1},{129,65},{193,129... | collective-permute-start | bytes 1179656 | tf_op jit(solution)/shard_map/ppermute | solution.py:311
  30.5 11.0 %collective-permute-start.4 = (bf16[8,192,128]{2,1,0:T(8,128)(2,1)S(1)}, bf16[8,192,128]{2,1,0:T(8,128)(2,1)S(1)}, u32[]{:S(2)}, u32[]{:S(2)}) collective-permute-start(bf16[8,192,128]{2,1,0:T(8,128)(2,1)S(1)} %all-to-all-done.after.refs_2_), channel_id=1, source_target_pairs={{0,64},{64,128},{128,192},{192,0},{1,65},{65,129},{129,193},{193,1... | collective-permute-start | bytes 1179656 | tf_op jit(solution)/shard_map/ppermute | solution.py:311
  32.0 13.1 %collective-permute-start.2 = (bf16[96,1024]{1,0:T(8,128)(2,1)S(1)}, bf16[96,1024]{1,0:T(8,128)(2,1)S(1)}, u32[]{:S(2)}, u32[]{:S(2)}) collective-permute-start(bf16[96,1024]{1,0:T(8,128)(2,1)S(1)} %get-tuple-element.44), channel_id=1, source_target_pairs={{0,2},{2,0},{1,3},{3,1},{4,6},{6,4},{5,7},{7,5},{8,10},{10,8},{9,1... | collective-permute-start | bytes 589832 | tf_op jit(solution)/shard_map/ppermute | solution.py:315
  33.3 11.8 %collective-permute-start.3 = (bf16[96,1024]{1,0:T(8,128)(2,1)S(1)}, bf16[96,1024]{1,0:T(8,128)(2,1)S(1)}, u32[]{:S(2)}, u32[]{:S(2)}) collective-permute-start(bf16[96,1024]{1,0:T(8,128)(2,1)S(1)} %get-tuple-element.45), channel_id=1, source_target_pairs={{0,4},{4,0},{1,5},{5,1},{2,6},{6,2},{3,7},{7,3},{8,12},{12,8},{9,1... | collective-permute-start | bytes 589832 | tf_op jit(solution)/shard_map/ppermute | solution.py:315
  41.6 7.0 %collective-permute-start.6 = (bf16[4,192,128]{2,1,0:T(8,128)(2,1)S(1)}, bf16[4,192,128]{2,1,0:T(8,128)(2,1)S(1)}, u32[]{:S(2)}, u32[]{:S(2)}) collective-permute-start(bf16[4,192,128]{2,1,0:T(8,128)(2,1)S(1)} %get-tuple-element.46), channel_id=1, source_target_pairs={{0,64},{64,128},{128,192},{192,0},{1,65},{65,129},{129,193},{193,1... | collective-permute-start | bytes 589832 | tf_op jit(solution)/shard_map/ppermute | solution.py:311
  41.7 6.9 %collective-permute-start.7 = (bf16[4,192,128]{2,1,0:T(8,128)(2,1)S(1)}, bf16[4,192,128]{2,1,0:T(8,128)(2,1)S(1)}, u32[]{:S(2)}, u32[]{:S(2)}) collective-permute-start(bf16[4,192,128]{2,1,0:T(8,128)(2,1)S(1)} %get-tuple-element.47), channel_id=1, source_target_pairs={{0,192},{64,0},{128,64},{192,128},{1,193},{65,1},{129,65},{193,129... | collective-permute-start | bytes 589832 | tf_op jit(solution)/shard_map/ppermute | solution.py:311
  48.7 3.5 %collective-permute-start.8 = (bf16[768,1024]{1,0:T(8,128)(2,1)S(1)}, bf16[768,1024]{1,0:T(8,128)(2,1)S(1)}, u32[]{:S(2)}, u32[]{:S(2)}) collective-permute-start(bf16[768,1024]{1,0:T(8,128)(2,1)S(1)} %join.1.refs_0_.refs_11_), channel_id=1, source_target_pairs={{0,1},{1,0},{2,3},{3,2},{4,5},{5,4},{6,7},{7,6},{8,9},{9,8},{10,11... | collective-permute-start | bytes 4718600 | tf_op jit(solution)/shard_map/ppermute | solution.py:315
  56.9 1.3 %collective-permute-start.12 = (f32[2,1536]{1,0:T(2,128)S(1)}, f32[2,1536]{1,0:T(2,128)S(1)}, u32[]{:S(2)}, u32[]{:S(2)}) collective-permute-start(f32[2,1536]{1,0:T(2,128)S(1)} %get-tuple-element.51.c), channel_id=1, source_target_pairs={{0,1},{1,0},{2,3},{3,2},{4,5},{5,4},{6,7},{7,6},{8,9},{9,8},{10,11... | collective-permute-start | bytes 36872 | tf_op jit(solution)/shard_map/ppermute | solution.py:315
  57.1 6.5 %collective-permute-start.11 = (f32[2,768]{1,0:T(2,128)S(1)}, f32[2,768]{1,0:T(2,128)S(1)}, u32[]{:S(2)}, u32[]{:S(2)}) collective-permute-start(f32[2,768]{1,0:T(2,128)S(1)} %get-tuple-element.50.refs_0_), channel_id=1, source_target_pairs={{0,24},{8,0},{16,8},{24,16},{1,25},{9,1},{17,9},{25,17},{2,26},{10... | collective-permute-start | bytes 18440 | tf_op jit(solution)/shard_map/ppermute | solution.py:311
  58.2 11.4 %collective-permute-start.15 = (f32[2,1536]{1,0:T(2,128)S(1)}, f32[2,1536]{1,0:T(2,128)S(1)}, u32[]{:S(2)}, u32[]{:S(2)}) collective-permute-start(f32[2,1536]{1,0:T(2,128)S(1)} %meet.1.refs_4_), channel_id=1, source_target_pairs={{0,6},{2,4},{4,2},{6,0},{1,7},{3,5},{5,3},{7,1},{8,14},{10,12},{12... | collective-permute-start | bytes 36872 | tf_op jit(solution)/shard_map/ppermute | solution.py:359
  61.2 8.4 %collective-permute-start.14 = (f32[2,1536]{1,0:T(2,128)S(1)}, f32[2,1536]{1,0:T(2,128)S(1)}, u32[]{:S(2)}, u32[]{:S(2)}) collective-permute-start(f32[2,1536]{1,0:T(2,128)S(1)} %meet.1.refs_4_), channel_id=1, source_target_pairs={{0,4},{2,6},{4,0},{6,2},{1,5},{3,7},{5,1},{7,3},{8,12},{10,14},{12... | collective-permute-start | bytes 36872 | tf_op jit(solution)/shard_map/ppermute | solution.py:359
  61.2 8.4 %collective-permute-start.13 = (f32[2,1536]{1,0:T(2,128)S(1)}, f32[2,1536]{1,0:T(2,128)S(1)}, u32[]{:S(2)}, u32[]{:S(2)}) collective-permute-start(f32[2,1536]{1,0:T(2,128)S(1)} %meet.1.refs_4_), channel_id=1, source_target_pairs={{0,2},{2,0},{4,6},{6,4},{1,3},{3,1},{5,7},{7,5},{8,10},{10,8},{12,... | collective-permute-start | bytes 36872 | tf_op jit(solution)/shard_map/ppermute | solution.py:359
  62.1 7.5 %collective-permute-start.10 = (f32[2,768]{1,0:T(2,128)S(1)}, f32[2,768]{1,0:T(2,128)S(1)}, u32[]{:S(2)}, u32[]{:S(2)}) collective-permute-start(f32[2,768]{1,0:T(2,128)S(1)} %get-tuple-element.50.refs_0_), channel_id=1, source_target_pairs={{0,16},{8,24},{16,0},{24,8},{1,17},{9,25},{17,1},{25,9},{2,18},{10... | collective-permute-start | bytes 18440 | tf_op jit(solution)/shard_map/ppermute | solution.py:311
  63.6 6.1 %collective-permute-start.9 = (f32[2,768]{1,0:T(2,128)S(1)}, f32[2,768]{1,0:T(2,128)S(1)}, u32[]{:S(2)}, u32[]{:S(2)}) collective-permute-start(f32[2,768]{1,0:T(2,128)S(1)} %get-tuple-element.50.refs_0_), channel_id=1, source_target_pairs={{0,8},{8,16},{16,24},{24,0},{1,9},{9,17},{17,25},{25,1},{2,10},{10... | collective-permute-start | bytes 18440 | tf_op jit(solution)/shard_map/ppermute | solution.py:311
  77.5 3.6 %collective-permute-start.16 = (s16[4,208,1024]{2,1,0:T(8,128)(2,1)S(1)}, s16[4,208,1024]{2,1,0:T(8,128)(2,1)S(1)}, u32[]{:S(2)}, u32[]{:S(2)}) collective-permute-start(s16[4,208,1024]{2,1,0:T(8,128)(2,1)S(1)} %get-tuple-element.55), channel_id=1, source_target_pairs={{0,1},{1,0},{2,3},{3,2},{4,5},{5,4},{6,7},{7,6},{8,9},{9,8},{10,11... | collective-permute-start | bytes 5111816 | tf_op jit(solution)/shard_map/ppermute | solution.py:315
  77.5 9.0 %collective-permute-start.17 = (s16[400,256]{1,0:T(8,128)(2,1)S(1)}, s16[400,256]{1,0:T(8,128)(2,1)S(1)}, u32[]{:S(2)}, u32[]{:S(2)}) collective-permute-start(s16[400,256]{1,0:T(8,128)(2,1)S(1)} %get-tuple-element.60), channel_id=1, source_target_pairs={{0,64},{64,128},{128,192},{192,0},{1,65},{65,129},{129,193},{193,1... | collective-permute-start | bytes 614408 | tf_op jit(solution)/shard_map/ppermute | solution.py:311
  77.5 9.0 %collective-permute-start.18 = (s16[400,256]{1,0:T(8,128)(2,1)S(1)}, s16[400,256]{1,0:T(8,128)(2,1)S(1)}, u32[]{:S(2)}, u32[]{:S(2)}) collective-permute-start(s16[400,256]{1,0:T(8,128)(2,1)S(1)} %get-tuple-element.61), channel_id=1, source_target_pairs={{0,192},{64,0},{128,64},{192,128},{1,193},{65,1},{129,65},{193,129... | collective-permute-start | bytes 614408 | tf_op jit(solution)/shard_map/ppermute | solution.py:311
  82.0 20.8 %collective-permute-start.21 = (s16[2,208,512]{2,1,0:T(8,128)(2,1)S(1)}, s16[2,208,512]{2,1,0:T(8,128)(2,1)S(1)}, u32[]{:S(2)}, u32[]{:S(2)}) collective-permute-start(s16[2,208,512]{2,1,0:T(8,128)(2,1)S(1)} %get-tuple-element.67), channel_id=1, source_target_pairs={{0,2},{2,0},{1,3},{3,1},{4,6},{6,4},{5,7},{7,5},{8,10},{10,8},{9,1... | collective-permute-start | bytes 1277960 | tf_op jit(solution)/shard_map/ppermute | solution.py:315
  83.5 19.3 %collective-permute-start.22 = (s16[2,208,512]{2,1,0:T(8,128)(2,1)S(1)}, s16[2,208,512]{2,1,0:T(8,128)(2,1)S(1)}, u32[]{:S(2)}, u32[]{:S(2)}) collective-permute-start(s16[2,208,512]{2,1,0:T(8,128)(2,1)S(1)} %get-tuple-element.68), channel_id=1, source_target_pairs={{0,4},{4,0},{1,5},{5,1},{2,6},{6,2},{3,7},{7,3},{8,12},{12,8},{9,1... | collective-permute-start | bytes 1277960 | tf_op jit(solution)/shard_map/ppermute | solution.py:315
  86.8 12.4 %collective-permute-start.19 = (s16[784,256]{1,0:T(8,128)(2,1)S(1)}, s16[784,256]{1,0:T(8,128)(2,1)S(1)}, u32[]{:S(2)}, u32[]{:S(2)}) collective-permute-start(s16[784,256]{1,0:T(8,128)(2,1)S(1)} %get-tuple-element.62), channel_id=1, source_target_pairs={{0,64},{64,128},{128,192},{192,0},{1,65},{65,129},{129,193},{193,1... | collective-permute-start | bytes 1204232 | tf_op jit(solution)/shard_map/ppermute | solution.py:311
  88.1 11.2 %collective-permute-start.20 = (s16[784,256]{1,0:T(8,128)(2,1)S(1)}, s16[784,256]{1,0:T(8,128)(2,1)S(1)}, u32[]{:S(2)}, u32[]{:S(2)}) collective-permute-start(s16[784,256]{1,0:T(8,128)(2,1)S(1)} %get-tuple-element.63), channel_id=1, source_target_pairs={{0,192},{64,0},{128,64},{192,128},{1,193},{65,1},{129,65},{193,129... | collective-permute-start | bytes 1204232 | tf_op jit(solution)/shard_map/ppermute | solution.py:311
  99.8 6.7 %collective-permute-start.26 = (s16[208,128]{1,0:T(8,128)(2,1)S(1)}, s16[208,128]{1,0:T(8,128)(2,1)S(1)}, u32[]{:S(2)}, u32[]{:S(2)}) collective-permute-start(s16[208,128]{1,0:T(8,128)(2,1)S(1)} %get-tuple-element.73), channel_id=1, source_target_pairs={{0,24},{8,0},{16,8},{24,16},{1,25},{9,1},{17,9},{25,17},{2,26},{10... | collective-permute-start | bytes 159752 | tf_op jit(solution)/shard_map/ppermute | solution.py:311
  102.4 6.9 %collective-permute-start.25 = (s16[208,128]{1,0:T(8,128)(2,1)S(1)}, s16[208,128]{1,0:T(8,128)(2,1)S(1)}, u32[]{:S(2)}, u32[]{:S(2)}) collective-permute-start(s16[208,128]{1,0:T(8,128)(2,1)S(1)} %get-tuple-element.64.after), channel_id=1, source_target_pairs={{0,8},{8,16},{16,24},{24,0},{1,9},{9,17},{17,25},{25,1},{2,10},{10... | collective-permute-start | bytes 159752 | tf_op jit(solution)/shard_map/ppermute | solution.py:311
  103.2 21.0 %collective-permute-start.24 = (s16[208,512]{1,0:T(8,128)(2,1)S(1)}, s16[208,512]{1,0:T(8,128)(2,1)S(1)}, u32[]{:S(2)}, u32[]{:S(2)}) collective-permute-start(s16[208,512]{1,0:T(8,128)(2,1)S(1)} %get-tuple-element.71), channel_id=1, source_target_pairs={{0,4},{4,0},{1,5},{5,1},{2,6},{6,2},{3,7},{7,3},{8,12},{12,8},{9,1... | collective-permute-start | bytes 638984 | tf_op jit(solution)/shard_map/ppermute | solution.py:315
  105.3 18.9 %collective-permute-start.23 = (s16[208,512]{1,0:T(8,128)(2,1)S(1)}, s16[208,512]{1,0:T(8,128)(2,1)S(1)}, u32[]{:S(2)}, u32[]{:S(2)}) collective-permute-start(s16[208,512]{1,0:T(8,128)(2,1)S(1)} %get-tuple-element.70.after), channel_id=1, source_target_pairs={{0,2},{2,0},{1,3},{3,1},{4,6},{6,4},{5,7},{7,5},{8,10},{10,8},{9,1... | collective-permute-start | bytes 638984 | tf_op jit(solution)/shard_map/ppermute | solution.py:315
  109.5 8.9 %collective-permute-start.27 = (s16[2,208,128]{2,1,0:T(8,128)(2,1)S(1)}, s16[2,208,128]{2,1,0:T(8,128)(2,1)S(1)}, u32[]{:S(2)}, u32[]{:S(2)}) collective-permute-start(s16[2,208,128]{2,1,0:T(8,128)(2,1)S(1)} %get-tuple-element.74), channel_id=1, source_target_pairs={{0,8},{8,16},{16,24},{24,0},{1,9},{9,17},{17,25},{25,1},{2,10},{10... | collective-permute-start | bytes 319496 | tf_op jit(solution)/shard_map/ppermute | solution.py:311
  109.9 8.4 %collective-permute-start.28 = (s16[2,208,128]{2,1,0:T(8,128)(2,1)S(1)}, s16[2,208,128]{2,1,0:T(8,128)(2,1)S(1)}, u32[]{:S(2)}, u32[]{:S(2)}) collective-permute-start(s16[2,208,128]{2,1,0:T(8,128)(2,1)S(1)} %get-tuple-element.75), channel_id=1, source_target_pairs={{0,24},{8,0},{16,8},{24,16},{1,25},{9,1},{17,9},{25,17},{2,26},{10... | collective-permute-start | bytes 319496 | tf_op jit(solution)/shard_map/ppermute | solution.py:311
  118.5 5.7 %collective-permute-start.29 = (s16[208,128]{1,0:T(8,128)(2,1)S(1)}, s16[208,128]{1,0:T(8,128)(2,1)S(1)}, u32[]{:S(2)}, u32[]{:S(2)}) collective-permute-start(s16[208,128]{1,0:T(8,128)(2,1)S(1)} %get-tuple-element.77), channel_id=1, source_target_pairs={{0,32},{32,0},{1,33},{33,1},{2,34},{34,2},{3,35},{35,3},{4,36},{36... | collective-permute-start | bytes 159752 | tf_op jit(solution)/shard_map/ppermute | solution.py:315
  (1 other events, 44.3 us)

commit v2 on v1

--- a/solution.py
+++ b/solution.py
@@ -80,6 +80,12 @@
 def turn_left(v, n):
     lanes = v.shape[1]
     return pltpu.roll(jnp.broadcast_to(v, (8, lanes)), lax.rem(lanes - n, lanes), 1)[0:1]
+
+
+def pair_kernel(image, twin, both):
+    xh = lax.axis_index("xh")
+    both[pl.ds(xh, 1)] = image[...][None]
+    both[pl.ds(1 - xh, 1)] = twin[...][None]
 
 
 def prep_kernel(pair_index, keys, pairs, cols, keys_out):
@@ -105,6 +111,14 @@
             n = part.shape[0]
             out[pl.ds(pl.multiple_of(at, 16), n), :] = part[...]
             at += n
+
+
+def stack_kernel(both, b1, b2, b3, keys, out, held):
+    zh = lax.axis_index("zh")
+    for k, ref in enumerate((both, b1, b2, b3)):
+        for xh in range(2):
+            out[pl.ds(4 * xh + lax.rem(zh + 4 - k, 4), 1)] = ref[xh : xh + 1]
+    held[...] = keys[...]
 
 
 def hold_kernel(x, z, after, z_top, x_low):
@@ -241,70 +255,41 @@
     encode(jnp.concatenate([p3[:n, :], p3[n:, :] + decode(got_b[...])], axis=0), o3)
 
 
-def key_sum_kernel(mine, got, own, keep_x, keep_z, to_x, to_z):
-    rows, d = own.shape
-    n = d // 2
+def key_sum_kernel(mine, got, own, *outs):
+    rows = own.shape[0]
     xl = lax.axis_index("xl")
-
-    def piece(k):
+    for k in (3, 1, 2, 0):
         p = xl ^ k
-        return mine[pl.ds(pl.multiple_of(p * rows, 16), rows), :] + decode(got[p])
-
-    x, z, both = piece(1), piece(2), piece(3)
-    encode(x[:, :n], to_x.at[0])
-    encode(both[:, :n], to_x.at[1])
-    encode(z[:, n:], to_z.at[0])
-    encode(both[:, n:], to_z.at[1])
-    keep_x[...] = x[:, n:]
-    keep_z[...] = z[:, :n]
-    own[...] = piece(0)
-
-
-def key_relay_kernel(after, own, keep_x, keep_z, from_x, from_z, total, to_x, to_z):
-    del after
-    n = keep_x.shape[1]
-    total[:, :n] = own[:, :n] + decode(from_x[0])
-    total[:, n:] = own[:, n:] + decode(from_z[0])
-    encode(keep_z[...] + decode(from_x[1]), to_z)
-    encode(keep_x[...] + decode(from_z[1]), to_x)
-
-
-def last_kernel(own_key, from_x, from_z, own, twin, key_out, image_out):
-    n = own_key.shape[1] // 2
-    key_out[:, :n] = own_key[:, :n] + decode(from_z[...])
-    key_out[:, n:] = own_key[:, n:] + decode(from_x[...])
+        x = mine[pl.ds(pl.multiple_of(p * rows, 16), rows), :] + decode(got[p])
+        if k:
+            encode(x, outs[k - 1])
+        else:
+            own[...] = x
+
+
+def last_kernel(own_key, from_x, from_z, from_both, own, twin, key_out, image_out):
+    key_out[...] = own_key[...] + decode(from_x[...]) + decode(from_z[...]) + decode(from_both[...])
     image_out[...] = own[...] + decode(twin[...])
 
 
-def image_sum_kernel(after, own, got1, got3, keep, to_a, to_b, total):
-    del after
+def image_sum_kernel(after_x, after_z, after_both, own, got1, got3, keep, to1, to2, to3, total):
+    del after_x, after_z, after_both
     zh, xh = lax.axis_index("zh"), lax.axis_index("xh")
     rows, width = keep.shape[1:]
-    n = own.shape[0] // rows
     total[...] = own[...] + decode(got1[...]) + decode(got3[...])
-
-    def piece(o, j):
-        row = pl.multiple_of(lax.rem(zh + j, n) * rows, 16)
-        return total[pl.ds(row, rows), pl.ds(pl.multiple_of((xh ^ o) * width, 128), width)]
-
-    encode(piece(0, 2), to_a)
-    encode(piece(1, 2), to_b)
-    for o in range(2):
-        for at, j in enumerate((0, 1, n - 1)):
-            keep[3 * o + at] = piece(o, j)
-
-
-def image_relay_kernel(after, keep, got_a, got_b, up, down):
-    del after
-    encode(keep[1] + decode(got_a[...]), up.at[0])
-    encode(keep[4], up.at[1])
-    encode(keep[2], down.at[0])
-    encode(keep[5] + decode(got_b[...]), down.at[1])
-
-
-def image_twin_kernel(keep, up, down, own, to_twin):
-    own[...] = keep[0] + decode(up[0]) + decode(down[0])
-    encode(keep[3] + decode(up[1]) + decode(down[1]), to_twin)
+    for k, out in ((2, to2), (1, to1), (3, to3), (0, keep)):
+        row = pl.multiple_of(lax.rem(zh + k, 4) * rows, 16)
+        for o in range(2):
+            x = total[pl.ds(row, rows), pl.ds(pl.multiple_of((xh ^ o) * width, 128), width)]
+            if k:
+                encode(x, out.at[o])
+            else:
+                out[o] = x
+
+
+def image_twin_kernel(keep, got1, got2, got3, own, to_twin):
+    own[...] = keep[0] + decode(got1[0]) + decode(got2[0]) + decode(got3[0])
+    encode(keep[1] + decode(got1[1]) + decode(got2[1]) + decode(got3[1]), to_twin)
 
 
 def shift(x, axis, n, k):
@@ -324,17 +309,17 @@
     n_im, n_ks = nzh * rows, 8 * rows
     half = n_ks // 2
     vmem = pl.BlockSpec(memory_space=pltpu.VMEM)
+    key_block = shape((rows, d), BF16)
+    both = call(pair_kernel, shape((2, rows, width), BF16), "pair", 4, in_specs=[vmem] * 2)(image, flip(image, "xh", 2, 1))
     pairs, cols, held = call(
-        prep_kernel,
-        [shape((1, n_im), F32), shape((1, n_ks), F32), shape((rows, d), BF16)],
-        "prep",
-        8,
-        in_specs=[vmem] * 2,
+        prep_kernel, [shape((1, n_im), F32), shape((1, n_ks), F32), key_block], "prep", 8, in_specs=[vmem] * 2
     )(pair_index, keys)
-    i0 = lax.all_to_all(jnp.broadcast_to(image, (2 * nzh, rows, width)), ("xh", "zh"), 0, 0)
+    i0, held = call(stack_kernel, [shape((8, rows, width), BF16), key_block], "stack", 8, in_specs=[vmem] * 5)(
+        both, *[shift(both, "zh", 4, k) for k in (1, 2, 3)], held
+    )
     i1, i3 = shift(i0, "y", 4, 1), shift(i0, "y", 4, 3)
-    key_x = flip(keys, "xl", 2, 1)
-    key_z = flip(keys, "zl", 2, 1)
+    key_x = flip(held, "xl", 2, 1)
+    key_z = flip(held, "zl", 2, 1)
     quarter = shape((rows // 2, d), BF16)
     d_top, d_low = call(hold_kernel, [quarter] * 2, "hold", 8, in_specs=[vmem] * 3)(key_x, key_z, i0)
     d_top, d_low = flip(d_top, "xl", 2, 1), flip(d_low, "zl", 2, 1)
@@ -371,40 +356,35 @@
         relay_kernel, [shape((n_im + PAD, 2 * width), I16)] * 2, "relay", 12, in_specs=[vmem] * 4
     )(p1, p3, shift(q2a, "y", 4, 1), shift(q2b, "y", 4, 3))
     q1, q3 = shift(q1, "y", 4, 1), shift(q3, "y", 4, 3)
-    own_key, keep_x, keep_z, to_x, to_z = call(
+    own_key, to_x, to_z, to_both = call(
         key_sum_kernel,
-        [shape((rows, d), F32)] + [shape((rows, d // 2), F32)] * 2 + [shape((2, rows + PAD, d // 2), I16)] * 2,
+        [shape((rows, d), F32)] + [shape((rows + PAD, d), I16)] * 3,
         "key_sum",
         16,
         in_specs=[vmem] * 2,
     )(mine, flip(sent, "core", 2, 1))
-    from_x, from_z = flip(to_x, "xl", 2, 1), flip(to_z, "zl", 2, 1)
-    coded = shape((rows + PAD, width), I16)
-    coded2 = shape((2, rows + PAD, width), I16)
-    keep, to_a, to_b = call(
+    to_both = lax.ppermute(to_both, ("zl", "xl"), [(i, 3 - i) for i in range(4)])
+    pieces = [flip(to_x, "xl", 2, 1), flip(to_z, "zl", 2, 1), to_both]
+    coded = shape((2, rows + PAD, width), I16)
+    keep, to1, to2, to3 = call(
         image_sum_kernel,
-        [shape((6, rows, width), F32), coded, coded],
+        [shape((2, rows, width), F32), coded, coded, coded],
         "image_sum",
         12,
+        in_specs=[vmem] * 6,
+        scratch_shapes=[pltpu.VMEM((n_im, 2 * width), F32)],
+    )(*pieces, own, q1, q3)
+    to2, to1, to3 = shift(to2, "zh", 4, 2), shift(to1, "zh", 4, 1), shift(to3, "zh", 4, 3)
+    own, to_twin = call(
+        image_twin_kernel,
+        [shape((rows, width), F32), shape((rows + PAD, width), I16)],
+        "image_twin",
+        8,
         in_specs=[vmem] * 4,
-        scratch_shapes=[pltpu.VMEM((n_im, 2 * width), F32)],
-    )(keep_z, own, q1, q3)
-    own_key, to_x, to_z = call(
-        key_relay_kernel,
-        [shape((rows, d), F32)] + [shape((rows + PAD, d // 2), I16)] * 2,
-        "key_relay",
-        12,
-        in_specs=[vmem] * 6,
-    )(to_a, own_key, keep_x, keep_z, from_x, from_z)
-    up, down = call(image_relay_kernel, [coded2] * 2, "image_relay", 8, in_specs=[vmem] * 4)(
-        to_x, keep, shift(to_a, "zh", 4, 1), shift(to_b, "zh", 4, 3)
-    )
-    own, to_twin = call(image_twin_kernel, [shape((rows, width), F32), coded], "image_twin", 8, in_specs=[vmem] * 3)(
-        keep, shift(up, "zh", 4, 1), shift(down, "zh", 4, 3)
-    )
+    )(keep, to1, to2, to3)
     modality_grad, image_grad = call(
-        last_kernel, [shape((rows, d), F32), shape((rows, width), F32)], "last", 8, in_specs=[vmem] * 5
-    )(own_key, flip(to_x, "xl", 2, 1), flip(to_z, "zl", 2, 1), own, flip(to_twin, "xh", 2, 1))
+        last_kernel, [shape((rows, d), F32), shape((rows, width), F32)], "last", 8, in_specs=[vmem] * 6
+    )(own_key, *pieces, own, flip(to_twin, "xh", 2, 1))
     return (image_grad, modality_grad[None], row_loss, col_loss)
 
 

time: 127 us -> 129 us (1.016)
    ppermute x15 -> x17, starting transfers between devices: 23.4 us -> 39.1 us  [shift(): return lax.ppermute(x, axis, [(i, (i + k) % n) for i in range(n)])]
    all_to_all x1 -> x0, waiting for transfers between devices: 11.6 us -> none  [on_device(): lax.all_to_all(jnp.broadcast_to(image, (2 * nzh, rows, width)), ('xh', 'z...]
    all_to_all x1 -> x0, starting transfers between devices: 11.4 us -> none  [on_device(): lax.all_to_all(jnp.broadcast_to(image, (2 * nzh, rows, width)), ('xh', 'z...]
    ppermute x12 -> x11, waiting for transfers between devices: 9.28 us -> 17.8 us  [flip(): return lax.ppermute(x, axis, [(i, i ^ d) for i in range(n)])]
    ppermute x12 -> x11, starting transfers between devices: 14 us -> 8.8 us  [flip(): return lax.ppermute(x, axis, [(i, i ^ d) for i in range(n)])]
    ppermute x0 -> x1, waiting for transfers between devices: none -> 5.07 us  [on_device(): lax.ppermute(to_both, ('zl', 'xl'), [(i, 3 - i) for i in range(4)])]
    unnamed x4 -> x6, local copies, waits for them, and re-layouts: 0.01 us -> 2.53 us
    ppermute x0 -> x1, starting transfers between devices: none -> 2.29 us  [on_device(): lax.ppermute(to_both, ('zl', 'xl'), [(i, 3 - i) for i in range(4)])]
  transfers between devices with their start and end apart: 31 -> 32, of which waited for: 14 -> 16; matrix products, arithmetic and copies ran while one was open for 0% -> 0% of each run, Pallas kernels for 2% -> 1%
where the time goes in v2:
time: 129 us; the launch traced here: 128 us
  waiting for transfers between devices  54.7 us (42%)
  starting transfers between devices  53.7 us (42%)
  Pallas kernels  16.3 us (13%)
  local copies, waits for them, and re-layouts  2.53 us (2%)
    ppermute x17, starting transfers between devices, shift(): return lax.ppermute(x, axis, [(i, (i + k) % n) for i in range(n)])  39.1 us
    ppermute x17, waiting for transfers between devices, shift(): return lax.ppermute(x, axis, [(i, (i + k) % n) for i in range(n)])  31.8 us
    ppermute x11, waiting for transfers between devices, flip(): return lax.ppermute(x, axis, [(i, i ^ d) for i in range(n)])  17.8 us
    ppermute x11, starting transfers between devices, flip(): return lax.ppermute(x, axis, [(i, i ^ d) for i in range(n)])  8.8 us
    pallas_call x1, Pallas kernels, on_device(): call(functools.partial(weights_kernel, scale, tile), outs, 'weights', 36,...  7.85 us
    ppermute x1, waiting for transfers between devices, on_device(): lax.ppermute(to_both, ('zl', 'xl'), [(i, 3 - i) for i in range(4)])  5.07 us
    pallas_call x1, Pallas kernels, on_device(): call(functools.partial(scores_kernel, scale), [shape((n_im, n_ks), F32),...  4.72 us
    ppermute x3, starting transfers between devices, on_device(): lax.ppermute(cs, ('zl', 'xl'), [(i, i ^ k) for i in range(4)])  3.58 us
  transfers between devices with their start and end apart: 32, of which 16 were waited for; matrix products, arithmetic and copies ran while one was open for 0% of the time, Pallas kernels for 1%

profile of v2, /device:TPU:4, one launch (start us, length us, event | category | flops | bytes accessed | tf_op | source)
XLA Modules:
  0.0 128.0 jit_solution(18442596594371153006)
XLA Ops:
  0.6 2.3 %collective-permute-start = (bf16[192,128]{1,0:T(8,128)(2,1)}, bf16[192,128]{1,0:T(8,128)(2,1)S(1)}, u32[]{:S(2)}, u32[]{:S(2)}) collective-permute-start(bf16[192,128]{1,0:T(8,128)(2,1)} %image.1), channel_id=1, source_target_pairs={{0,32},{32,0},{1,33},{33,1},{2,34},{34,2},{3,35},{35,3},{4,36},{36... | collective-permute-start | bytes 147464 | tf_op jit(solution)/shard_map/ppermute | solution.py:300
  3.0 3.6 %collective-permute-done.twin = bf16[192,128]{1,0:T(8,128)(2,1)S(1)} collective-permute-done((bf16[192,128]{1,0:T(8,128)(2,1)}, bf16[192,128]{1,0:T(8,128)(2,1)S(1)}, u32[]{:S(2)}, u32[]{:S(2)}) %collective-permute-start) | collective-permute-done | bytes 49184 | tf_op jit(solution)/shard_map/ppermute | solution.py:300
  7.3 6.4 %collective-permute-start.3 = (bf16[2,192,128]{2,1,0:T(8,128)(2,1)S(1)}, bf16[2,192,128]{2,1,0:T(8,128)(2,1)S(1)}, u32[]{:S(2)}, u32[]{:S(2)}) collective-permute-start(bf16[2,192,128]{2,1,0:T(8,128)(2,1)S(1)} %pair.1.both), channel_id=1, source_target_pairs={{0,24},{8,0},{16,8},{24,16},{1,25},{9,1},{17,9},{25,17},{2,26},{10... | collective-permute-start | bytes 294920 | tf_op jit(solution)/shard_map/ppermute | solution.py:296
  14.7 2.8 %collective-permute-start.1 = (bf16[2,192,128]{2,1,0:T(8,128)(2,1)S(1)}, bf16[2,192,128]{2,1,0:T(8,128)(2,1)S(1)}, u32[]{:S(2)}, u32[]{:S(2)}) collective-permute-start(bf16[2,192,128]{2,1,0:T(8,128)(2,1)S(1)} %pair.1.both), channel_id=1, source_target_pairs={{0,8},{8,16},{16,24},{24,0},{1,9},{9,17},{17,25},{25,1},{2,10},{10... | collective-permute-start | bytes 294920 | tf_op jit(solution)/shard_map/ppermute | solution.py:296
  19.5 1.5 %collective-permute-done.3.b3 = bf16[2,192,128]{2,1,0:T(8,128)(2,1)S(1)} collective-permute-done((bf16[2,192,128]{2,1,0:T(8,128)(2,1)S(1)}, bf16[2,192,128]{2,1,0:T(8,128)(2,1)S(1)}, u32[]{:S(2)}, u32[]{:S(2)}) %collective-permute-start.3) | collective-permute-done | bytes 98336 | tf_op jit(solution)/shard_map/ppermute | solution.py:296
  21.0 3.3 %collective-permute-done.2.b2 = bf16[2,192,128]{2,1,0:T(8,128)(2,1)S(1)} collective-permute-done((bf16[2,192,128]{2,1,0:T(8,128)(2,1)S(1)}, bf16[2,192,128]{2,1,0:T(8,128)(2,1)S(1)}, u32[]{:S(2)}, u32[]{:S(2)}) %collective-permute-start.2) | collective-permute-done | bytes 98336 | tf_op jit(solution)/shard_map/ppermute | solution.py:296
  26.5 3.0 %collective-permute-start.9 = (bf16[8,192,128]{2,1,0:T(8,128)(2,1)S(1)}, bf16[8,192,128]{2,1,0:T(8,128)(2,1)S(1)}, u32[]{:S(2)}, u32[]{:S(2)}) collective-permute-start(bf16[8,192,128]{2,1,0:T(8,128)(2,1)S(1)} %get-tuple-element.42.after.refs_2_), channel_id=1, source_target_pairs={{0,192},{64,0},{128,64},{192,128},{1,193},{65,1},{129,65},{193,129... | collective-permute-start | bytes 1179656 | tf_op jit(solution)/shard_map/ppermute | solution.py:296
  29.5 4.2 %collective-permute-done.5.z = bf16[192,1024]{1,0:T(8,128)(2,1)S(1)} collective-permute-done((bf16[192,1024]{1,0:T(8,128)(2,1)S(1)}, bf16[192,1024]{1,0:T(8,128)(2,1)S(1)}, u32[]{:S(2)}, u32[]{:S(2)}) %collective-permute-start.5) | collective-permute-done | bytes 393248 | tf_op jit(solution)/shard_map/ppermute | solution.py:300
  33.7 1.5 %collective-permute-done.4.x = bf16[192,1024]{1,0:T(8,128)(2,1)S(1)} collective-permute-done((bf16[192,1024]{1,0:T(8,128)(2,1)S(1)}, bf16[192,1024]{1,0:T(8,128)(2,1)S(1)}, u32[]{:S(2)}, u32[]{:S(2)}) %collective-permute-start.4) | collective-permute-done | bytes 393248 | tf_op jit(solution)/shard_map/ppermute | solution.py:300
  35.2 1.3 %collective-permute-start.6 = (bf16[96,1024]{1,0:T(8,128)(2,1)S(1)}, bf16[96,1024]{1,0:T(8,128)(2,1)S(1)}, u32[]{:S(2)}, u32[]{:S(2)}) collective-permute-start(bf16[96,1024]{1,0:T(8,128)(2,1)S(1)} %get-tuple-element.43), channel_id=1, source_target_pairs={{0,2},{2,0},{1,3},{3,1},{4,6},{6,4},{5,7},{7,5},{8,10},{10,8},{9,1... | collective-permute-start | bytes 589832 | tf_op jit(solution)/shard_map/ppermute | solution.py:300
  36.9 3.2 %collective-permute-done.8.behind.refs_3_ = bf16[8,192,128]{2,1,0:T(8,128)(2,1)S(1)} collective-permute-done((bf16[8,192,128]{2,1,0:T(8,128)(2,1)S(1)}, bf16[8,192,128]{2,1,0:T(8,128)(2,1)S(1)}, u32[]{:S(2)}, u32[]{:S(2)}) %collective-permute-start.8) | collective-permute-done | bytes 393248 | tf_op jit(solution)/shard_map/ppermute | solution.py:296
  40.2 3.2 %collective-permute-start.11 = (bf16[4,192,128]{2,1,0:T(8,128)(2,1)S(1)}, bf16[4,192,128]{2,1,0:T(8,128)(2,1)S(1)}, u32[]{:S(2)}, u32[]{:S(2)}) collective-permute-start(bf16[4,192,128]{2,1,0:T(8,128)(2,1)S(1)} %get-tuple-element.46), channel_id=1, source_target_pairs={{0,192},{64,0},{128,64},{192,128},{1,193},{65,1},{129,65},{193,129... | collective-permute-start | bytes 589832 | tf_op jit(solution)/shard_map/ppermute | solution.py:296
  43.4 3.6 %collective-permute-done.10.after_a.refs_5_ = bf16[4,192,128]{2,1,0:T(8,128)(2,1)S(1)} collective-permute-done((bf16[4,192,128]{2,1,0:T(8,128)(2,1)S(1)}, bf16[4,192,128]{2,1,0:T(8,128)(2,1)S(1)}, u32[]{:S(2)}, u32[]{:S(2)}) %collective-permute-start.10) | collective-permute-done | bytes 196640 | tf_op jit(solution)/shard_map/ppermute | solution.py:296
  47.4 3.4 %collective-permute-done.12.refs_1_.refs_12_ = bf16[768,1024]{1,0:T(8,128)(2,1)S(1)} collective-permute-done((bf16[768,1024]{1,0:T(8,128)(2,1)S(1)}, bf16[768,1024]{1,0:T(8,128)(2,1)S(1)}, u32[]{:S(2)}, u32[]{:S(2)}) %collective-permute-start.12) | collective-permute-done | bytes 1572896 | tf_op jit(solution)/shard_map/ppermute | solution.py:300
  50.8 4.7 %scores.1 = (f32[768,1536]{1,0:T(8,128)S(1)}, bf16[768,1024]{1,0:T(8,128)(2,1)S(1)}, f32[2,768]{1,0:T(2,128)S(1)}, f32[2,1536]{1,0:T(2,128)S(1)}) custom-call(bf16[768,1024]{1,0:T(8,128)(2,1)S(1)} %join.1.refs_0_.refs_11_, bf16[768,1024]{1,0:T(8,128)(2,1)S(1)} %collective-permute-done.12.refs_1_.refs_12_, ...), custom_call_target="tpu_custom_call" | custom-call | flops 1000 | bytes 1000 | tf_op jit(solution)/shard_map/scores/pallas_call | solution.py:335
  55.8 3.9 %collective-permute-start.15 = (f32[2,768]{1,0:T(2,128)S(1)}, f32[2,768]{1,0:T(2,128)S(1)}, u32[]{:S(2)}, u32[]{:S(2)}) collective-permute-start(f32[2,768]{1,0:T(2,128)S(1)} %get-tuple-element.49.refs_0_), channel_id=1, source_target_pairs={{0,24},{8,0},{16,8},{24,16},{1,25},{9,1},{17,9},{25,17},{2,26},{10... | collective-permute-start | bytes 18440 | tf_op jit(solution)/shard_map/ppermute | solution.py:296
  60.5 1.6 %collective-permute-start.18 = (f32[2,1536]{1,0:T(2,128)S(1)}, f32[2,1536]{1,0:T(2,128)S(1)}, u32[]{:S(2)}, u32[]{:S(2)}) collective-permute-start(f32[2,1536]{1,0:T(2,128)S(1)} %meet.1.refs_4_), channel_id=1, source_target_pairs={{0,4},{2,6},{4,0},{6,2},{1,5},{3,7},{5,1},{7,3},{8,12},{10,14},{12... | collective-permute-start | bytes 36872 | tf_op jit(solution)/shard_map/ppermute | solution.py:344
  63.3 1.7 %collective-permute-start.14 = (f32[2,768]{1,0:T(2,128)S(1)}, f32[2,768]{1,0:T(2,128)S(1)}, u32[]{:S(2)}, u32[]{:S(2)}) collective-permute-start(f32[2,768]{1,0:T(2,128)S(1)} %get-tuple-element.49.refs_0_), channel_id=1, source_target_pairs={{0,16},{8,24},{16,0},{24,8},{1,17},{9,25},{17,1},{25,9},{2,18},{10... | collective-permute-start | bytes 18440 | tf_op jit(solution)/shard_map/ppermute | solution.py:296
  65.0 1.9 %collective-permute-start.13 = (f32[2,768]{1,0:T(2,128)S(1)}, f32[2,768]{1,0:T(2,128)S(1)}, u32[]{:S(2)}, u32[]{:S(2)}) collective-permute-start(f32[2,768]{1,0:T(2,128)S(1)} %get-tuple-element.49.refs_0_), channel_id=1, source_target_pairs={{0,8},{8,16},{16,24},{24,0},{1,9},{9,17},{17,25},{25,1},{2,10},{10... | collective-permute-start | bytes 18440 | tf_op jit(solution)/shard_map/ppermute | solution.py:296
  66.9 3.9 %collective-permute-done.14.refs_2_ = f32[2,768]{1,0:T(2,128)S(1)} collective-permute-done((f32[2,768]{1,0:T(2,128)S(1)}, f32[2,768]{1,0:T(2,128)S(1)}, u32[]{:S(2)}, u32[]{:S(2)}) %collective-permute-start.14) | collective-permute-done | bytes 6176 | tf_op jit(solution)/shard_map/ppermute | solution.py:296
  70.9 7.9 %weights.1 = (f32[768,256]{1,0:T(8,128)S(1)}, f32[768,256]{1,0:T(8,128)S(1)}, f32[768,256]{1,0:T(8,128)S(1)}, s16[400,256]{1,0:T(8,128)(2,1)S(1)}, s16[400,256]{...) custom-call(f32[2,768]{1,0:T(2,128)S(1)} %get-tuple-element.49.refs_, ...), custom_call_target="tpu_custom_call" | custom-call | flops 1000 | bytes 1000 | tf_op jit(solution)/shard_map/weights/pallas_call | solution.py:347
  78.7 3.3 %collective-permute-start.25 = (s16[400,256]{1,0:T(8,128)(2,1)S(1)}, s16[400,256]{1,0:T(8,128)(2,1)S(1)}, u32[]{:S(2)}, u32[]{:S(2)}) collective-permute-start(s16[400,256]{1,0:T(8,128)(2,1)S(1)} %get-tuple-element.63), channel_id=1, source_target_pairs={{0,192},{64,0},{128,64},{192,128},{1,193},{65,1},{129,65},{193,129... | collective-permute-start | bytes 614408 | tf_op jit(solution)/shard_map/ppermute | solution.py:296
  84.6 2.3 %collective-permute-start.23 = (s16[208,1024]{1,0:T(8,128)(2,1)S(1)}, s16[208,1024]{1,0:T(8,128)(2,1)S(1)}, u32[]{:S(2)}, u32[]{:S(2)}) collective-permute-start(s16[208,1024]{1,0:T(8,128)(2,1)S(1)} %get-tuple-element.58), channel_id=1, source_target_pairs={{0,6},{2,4},{4,2},{6,0},{1,7},{3,5},{5,3},{7,1},{8,14},{10,12},{12... | collective-permute-start | bytes 1277960 | tf_op jit(solution)/shard_map/ppermute | solution.py:366
  89.3 2.2 %collective-permute-start.27 = (s16[784,256]{1,0:T(8,128)(2,1)S(1)}, s16[784,256]{1,0:T(8,128)(2,1)S(1)}, u32[]{:S(2)}, u32[]{:S(2)}) collective-permute-start(s16[784,256]{1,0:T(8,128)(2,1)S(1)} %get-tuple-element.65), channel_id=1, source_target_pairs={{0,192},{64,0},{128,64},{192,128},{1,193},{65,1},{129,65},{193,129... | collective-permute-start | bytes 1204232 | tf_op jit(solution)/shard_map/ppermute | solution.py:296
  91.4 9.0 %collective-permute-done.26.got1 = s16[784,256]{1,0:T(8,128)(2,1)S(1)} collective-permute-done((s16[784,256]{1,0:T(8,128)(2,1)S(1)}, s16[784,256]{1,0:T(8,128)(2,1)S(1)}, u32[]{:S(2)}, u32[]{:S(2)}) %collective-permute-start.26) | collective-permute-done | bytes 401440 | tf_op jit(solution)/shard_map/ppermute | solution.py:296
  100.5 5.1 %collective-permute-done.23.after_both.from_both = s16[208,1024]{1,0:T(8,128)(2,1)S(1)} collective-permute-done((s16[208,1024]{1,0:T(8,128)(2,1)S(1)}, s16[208,1024]{1,0:T(8,128)(2,1)S(1)}, u32[]{:S(2)}, u32[]{:S(2)}) %collective-permute-start.23) | collective-permute-done | bytes 426016 | tf_op jit(solution)/shard_map/ppermute | solution.py:366
  106.8 3.6 %collective-permute-start.29 = (s16[2,208,128]{2,1,0:T(8,128)(2,1)S(1)}, s16[2,208,128]{2,1,0:T(8,128)(2,1)S(1)}, u32[]{:S(2)}, u32[]{:S(2)}) collective-permute-start(s16[2,208,128]{2,1,0:T(8,128)(2,1)S(1)} %get-tuple-element.68), channel_id=1, source_target_pairs={{0,16},{8,24},{16,0},{24,8},{1,17},{9,25},{17,1},{25,9},{2,18},{10... | collective-permute-start | bytes 319496 | tf_op jit(solution)/shard_map/ppermute | solution.py:296
  110.4 4.0 %collective-permute-start.30 = (s16[2,208,128]{2,1,0:T(8,128)(2,1)S(1)}, s16[2,208,128]{2,1,0:T(8,128)(2,1)S(1)}, u32[]{:S(2)}, u32[]{:S(2)}) collective-permute-start(s16[2,208,128]{2,1,0:T(8,128)(2,1)S(1)} %get-tuple-element.69), channel_id=1, source_target_pairs={{0,24},{8,0},{16,8},{24,16},{1,25},{9,1},{17,9},{25,17},{2,26},{10... | collective-permute-start | bytes 319496 | tf_op jit(solution)/shard_map/ppermute | solution.py:296
  114.5 2.9 %collective-permute-done.29.got2 = s16[2,208,128]{2,1,0:T(8,128)(2,1)S(1)} collective-permute-done((s16[2,208,128]{2,1,0:T(8,128)(2,1)S(1)}, s16[2,208,128]{2,1,0:T(8,128)(2,1)S(1)}, u32[]{:S(2)}, u32[]{:S(2)}) %collective-permute-start.29) | collective-permute-done | bytes 106528 | tf_op jit(solution)/shard_map/ppermute | solution.py:296
  117.3 3.6 %collective-permute-done.30.got3 = s16[2,208,128]{2,1,0:T(8,128)(2,1)S(1)} collective-permute-done((s16[2,208,128]{2,1,0:T(8,128)(2,1)S(1)}, s16[2,208,128]{2,1,0:T(8,128)(2,1)S(1)}, u32[]{:S(2)}, u32[]{:S(2)}) %collective-permute-start.30) | collective-permute-done | bytes 106528 | tf_op jit(solution)/shard_map/ppermute | solution.py:296
  122.0 4.8 %collective-permute-done.31.twin = s16[208,128]{1,0:T(8,128)(2,1)S(1)} collective-permute-done((s16[208,128]{1,0:T(8,128)(2,1)S(1)}, s16[208,128]{1,0:T(8,128)(2,1)S(1)}, u32[]{:S(2)}, u32[]{:S(2)}) %collective-permute-start.31) | collective-permute-done | bytes 53280 | tf_op jit(solution)/shard_map/ppermute | solution.py:300
  126.8 1.2 last.1
  (52 shorter events, 16.3 us)
Async XLA Ops:
  0.6 5.9 %collective-permute-start = (bf16[192,128]{1,0:T(8,128)(2,1)}, bf16[192,128]{1,0:T(8,128)(2,1)S(1)}, u32[]{:S(2)}, u32[]{:S(2)}) collective-permute-start(bf16[192,128]{1,0:T(8,128)(2,1)} %image.1), channel_id=1, source_target_pairs={{0,32},{32,0},{1,33},{33,1},{2,34},{34,2},{3,35},{35,3},{4,36},{36... | collective-permute-start | bytes 147464 | tf_op jit(solution)/shard_map/ppermute | solution.py:300
  7.3 13.6 %collective-permute-start.3 = (bf16[2,192,128]{2,1,0:T(8,128)(2,1)S(1)}, bf16[2,192,128]{2,1,0:T(8,128)(2,1)S(1)}, u32[]{:S(2)}, u32[]{:S(2)}) collective-permute-start(bf16[2,192,128]{2,1,0:T(8,128)(2,1)S(1)} %pair.1.both), channel_id=1, source_target_pairs={{0,24},{8,0},{16,8},{24,16},{1,25},{9,1},{17,9},{25,17},{2,26},{10... | collective-permute-start | bytes 294920 | tf_op jit(solution)/shard_map/ppermute | solution.py:296
  13.7 10.5 %collective-permute-start.2 = (bf16[2,192,128]{2,1,0:T(8,128)(2,1)S(1)}, bf16[2,192,128]{2,1,0:T(8,128)(2,1)S(1)}, u32[]{:S(2)}, u32[]{:S(2)}) collective-permute-start(bf16[2,192,128]{2,1,0:T(8,128)(2,1)S(1)} %pair.1.both), channel_id=1, source_target_pairs={{0,16},{8,24},{16,0},{24,8},{1,17},{9,25},{17,1},{25,9},{2,18},{10... | collective-permute-start | bytes 294920 | tf_op jit(solution)/shard_map/ppermute | solution.py:296
  14.7 9.5 %collective-permute-start.1 = (bf16[2,192,128]{2,1,0:T(8,128)(2,1)S(1)}, bf16[2,192,128]{2,1,0:T(8,128)(2,1)S(1)}, u32[]{:S(2)}, u32[]{:S(2)}) collective-permute-start(bf16[2,192,128]{2,1,0:T(8,128)(2,1)S(1)} %pair.1.both), channel_id=1, source_target_pairs={{0,8},{8,16},{16,24},{24,0},{1,9},{9,17},{17,25},{25,1},{2,10},{10... | collective-permute-start | bytes 294920 | tf_op jit(solution)/shard_map/ppermute | solution.py:296
  24.3 9.4 %collective-permute-start.5 = (bf16[192,1024]{1,0:T(8,128)(2,1)S(1)}, bf16[192,1024]{1,0:T(8,128)(2,1)S(1)}, u32[]{:S(2)}, u32[]{:S(2)}) collective-permute-start(bf16[192,1024]{1,0:T(8,128)(2,1)S(1)} %get-tuple-element.41.own), channel_id=1, source_target_pairs={{0,4},{4,0},{1,5},{5,1},{2,6},{6,2},{3,7},{7,3},{8,12},{12,8},{9,1... | collective-permute-start | bytes 1179656 | tf_op jit(solution)/shard_map/ppermute | solution.py:300
  25.3 9.9 %collective-permute-start.4 = (bf16[192,1024]{1,0:T(8,128)(2,1)S(1)}, bf16[192,1024]{1,0:T(8,128)(2,1)S(1)}, u32[]{:S(2)}, u32[]{:S(2)}) collective-permute-start(bf16[192,1024]{1,0:T(8,128)(2,1)S(1)} %get-tuple-element.41.own), channel_id=1, source_target_pairs={{0,2},{2,0},{1,3},{3,1},{4,6},{6,4},{5,7},{7,5},{8,10},{10,8},{9,1... | collective-permute-start | bytes 1179656 | tf_op jit(solution)/shard_map/ppermute | solution.py:300
  26.5 10.4 %collective-permute-start.9 = (bf16[8,192,128]{2,1,0:T(8,128)(2,1)S(1)}, bf16[8,192,128]{2,1,0:T(8,128)(2,1)S(1)}, u32[]{:S(2)}, u32[]{:S(2)}) collective-permute-start(bf16[8,192,128]{2,1,0:T(8,128)(2,1)S(1)} %get-tuple-element.42.after.refs_2_), channel_id=1, source_target_pairs={{0,192},{64,0},{128,64},{192,128},{1,193},{65,1},{129,65},{193,129... | collective-permute-start | bytes 1179656 | tf_op jit(solution)/shard_map/ppermute | solution.py:296
  29.5 10.6 %collective-permute-start.8 = (bf16[8,192,128]{2,1,0:T(8,128)(2,1)S(1)}, bf16[8,192,128]{2,1,0:T(8,128)(2,1)S(1)}, u32[]{:S(2)}, u32[]{:S(2)}) collective-permute-start(bf16[8,192,128]{2,1,0:T(8,128)(2,1)S(1)} %get-tuple-element.42.after.refs_2_), channel_id=1, source_target_pairs={{0,64},{64,128},{128,192},{192,0},{1,65},{65,129},{129,193},{193,1... | collective-permute-start | bytes 1179656 | tf_op jit(solution)/shard_map/ppermute | solution.py:296
  35.2 8.2 %collective-permute-start.6 = (bf16[96,1024]{1,0:T(8,128)(2,1)S(1)}, bf16[96,1024]{1,0:T(8,128)(2,1)S(1)}, u32[]{:S(2)}, u32[]{:S(2)}) collective-permute-start(bf16[96,1024]{1,0:T(8,128)(2,1)S(1)} %get-tuple-element.43), channel_id=1, source_target_pairs={{0,2},{2,0},{1,3},{3,1},{4,6},{6,4},{5,7},{7,5},{8,10},{10,8},{9,1... | collective-permute-start | bytes 589832 | tf_op jit(solution)/shard_map/ppermute | solution.py:300
  36.5 6.9 %collective-permute-start.7 = (bf16[96,1024]{1,0:T(8,128)(2,1)S(1)}, bf16[96,1024]{1,0:T(8,128)(2,1)S(1)}, u32[]{:S(2)}, u32[]{:S(2)}) collective-permute-start(bf16[96,1024]{1,0:T(8,128)(2,1)S(1)} %get-tuple-element.44), channel_id=1, source_target_pairs={{0,4},{4,0},{1,5},{5,1},{2,6},{6,2},{3,7},{7,3},{8,12},{12,8},{9,1... | collective-permute-start | bytes 589832 | tf_op jit(solution)/shard_map/ppermute | solution.py:300
  40.1 7.0 %collective-permute-start.10 = (bf16[4,192,128]{2,1,0:T(8,128)(2,1)S(1)}, bf16[4,192,128]{2,1,0:T(8,128)(2,1)S(1)}, u32[]{:S(2)}, u32[]{:S(2)}) collective-permute-start(bf16[4,192,128]{2,1,0:T(8,128)(2,1)S(1)} %get-tuple-element.45), channel_id=1, source_target_pairs={{0,64},{64,128},{128,192},{192,0},{1,65},{65,129},{129,193},{193,1... | collective-permute-start | bytes 589832 | tf_op jit(solution)/shard_map/ppermute | solution.py:296
  40.2 6.9 %collective-permute-start.11 = (bf16[4,192,128]{2,1,0:T(8,128)(2,1)S(1)}, bf16[4,192,128]{2,1,0:T(8,128)(2,1)S(1)}, u32[]{:S(2)}, u32[]{:S(2)}) collective-permute-start(bf16[4,192,128]{2,1,0:T(8,128)(2,1)S(1)} %get-tuple-element.46), channel_id=1, source_target_pairs={{0,192},{64,0},{128,64},{192,128},{1,193},{65,1},{129,65},{193,129... | collective-permute-start | bytes 589832 | tf_op jit(solution)/shard_map/ppermute | solution.py:296
  47.2 3.7 %collective-permute-start.12 = (bf16[768,1024]{1,0:T(8,128)(2,1)S(1)}, bf16[768,1024]{1,0:T(8,128)(2,1)S(1)}, u32[]{:S(2)}, u32[]{:S(2)}) collective-permute-start(bf16[768,1024]{1,0:T(8,128)(2,1)S(1)} %join.1.refs_0_.refs_11_), channel_id=1, source_target_pairs={{0,1},{1,0},{2,3},{3,2},{4,5},{5,4},{6,7},{7,6},{8,9},{9,8},{10,11... | collective-permute-start | bytes 4718600 | tf_op jit(solution)/shard_map/ppermute | solution.py:300
  55.6 4.1 %collective-permute-start.16 = (f32[2,1536]{1,0:T(2,128)S(1)}, f32[2,1536]{1,0:T(2,128)S(1)}, u32[]{:S(2)}, u32[]{:S(2)}) collective-permute-start(f32[2,1536]{1,0:T(2,128)S(1)} %get-tuple-element.50.c), channel_id=1, source_target_pairs={{0,1},{1,0},{2,3},{3,2},{4,5},{5,4},{6,7},{7,6},{8,9},{9,8},{10,11... | collective-permute-start | bytes 36872 | tf_op jit(solution)/shard_map/ppermute | solution.py:300
  55.8 9.3 %collective-permute-start.15 = (f32[2,768]{1,0:T(2,128)S(1)}, f32[2,768]{1,0:T(2,128)S(1)}, u32[]{:S(2)}, u32[]{:S(2)}) collective-permute-start(f32[2,768]{1,0:T(2,128)S(1)} %get-tuple-element.49.refs_0_), channel_id=1, source_target_pairs={{0,24},{8,0},{16,8},{24,16},{1,25},{9,1},{17,9},{25,17},{2,26},{10... | collective-permute-start | bytes 18440 | tf_op jit(solution)/shard_map/ppermute | solution.py:296
  59.7 11.1 %collective-permute-start.19 = (f32[2,1536]{1,0:T(2,128)S(1)}, f32[2,1536]{1,0:T(2,128)S(1)}, u32[]{:S(2)}, u32[]{:S(2)}) collective-permute-start(f32[2,1536]{1,0:T(2,128)S(1)} %meet.1.refs_4_), channel_id=1, source_target_pairs={{0,6},{2,4},{4,2},{6,0},{1,7},{3,5},{5,3},{7,1},{8,14},{10,12},{12... | collective-permute-start | bytes 36872 | tf_op jit(solution)/shard_map/ppermute | solution.py:344
  60.5 10.4 %collective-permute-start.18 = (f32[2,1536]{1,0:T(2,128)S(1)}, f32[2,1536]{1,0:T(2,128)S(1)}, u32[]{:S(2)}, u32[]{:S(2)}) collective-permute-start(f32[2,1536]{1,0:T(2,128)S(1)} %meet.1.refs_4_), channel_id=1, source_target_pairs={{0,4},{2,6},{4,0},{6,2},{1,5},{3,7},{5,1},{7,3},{8,12},{10,14},{12... | collective-permute-start | bytes 36872 | tf_op jit(solution)/shard_map/ppermute | solution.py:344
  62.1 8.8 %collective-permute-start.17 = (f32[2,1536]{1,0:T(2,128)S(1)}, f32[2,1536]{1,0:T(2,128)S(1)}, u32[]{:S(2)}, u32[]{:S(2)}) collective-permute-start(f32[2,1536]{1,0:T(2,128)S(1)} %meet.1.refs_4_), channel_id=1, source_target_pairs={{0,2},{2,0},{4,6},{6,4},{1,3},{3,1},{5,7},{7,5},{8,10},{10,8},{12,... | collective-permute-start | bytes 36872 | tf_op jit(solution)/shard_map/ppermute | solution.py:344
  63.3 7.5 %collective-permute-start.14 = (f32[2,768]{1,0:T(2,128)S(1)}, f32[2,768]{1,0:T(2,128)S(1)}, u32[]{:S(2)}, u32[]{:S(2)}) collective-permute-start(f32[2,768]{1,0:T(2,128)S(1)} %get-tuple-element.49.refs_0_), channel_id=1, source_target_pairs={{0,16},{8,24},{16,0},{24,8},{1,17},{9,25},{17,1},{25,9},{2,18},{10... | collective-permute-start | bytes 18440 | tf_op jit(solution)/shard_map/ppermute | solution.py:296
  65.0 5.8 %collective-permute-start.13 = (f32[2,768]{1,0:T(2,128)S(1)}, f32[2,768]{1,0:T(2,128)S(1)}, u32[]{:S(2)}, u32[]{:S(2)}) collective-permute-start(f32[2,768]{1,0:T(2,128)S(1)} %get-tuple-element.49.refs_0_), channel_id=1, source_target_pairs={{0,8},{8,16},{16,24},{24,0},{1,9},{9,17},{17,25},{25,1},{2,10},{10... | collective-permute-start | bytes 18440 | tf_op jit(solution)/shard_map/ppermute | solution.py:296
  78.7 3.6 %collective-permute-start.20 = (s16[4,208,1024]{2,1,0:T(8,128)(2,1)S(1)}, s16[4,208,1024]{2,1,0:T(8,128)(2,1)S(1)}, u32[]{:S(2)}, u32[]{:S(2)}) collective-permute-start(s16[4,208,1024]{2,1,0:T(8,128)(2,1)S(1)} %get-tuple-element.54), channel_id=1, source_target_pairs={{0,1},{1,0},{2,3},{3,2},{4,5},{5,4},{6,7},{7,6},{8,9},{9,8},{10,11... | collective-permute-start | bytes 5111816 | tf_op jit(solution)/shard_map/ppermute | solution.py:300
  78.7 9.0 %collective-permute-start.24 = (s16[400,256]{1,0:T(8,128)(2,1)S(1)}, s16[400,256]{1,0:T(8,128)(2,1)S(1)}, u32[]{:S(2)}, u32[]{:S(2)}) collective-permute-start(s16[400,256]{1,0:T(8,128)(2,1)S(1)} %get-tuple-element.62), channel_id=1, source_target_pairs={{0,64},{64,128},{128,192},{192,0},{1,65},{65,129},{129,193},{193,1... | collective-permute-start | bytes 614408 | tf_op jit(solution)/shard_map/ppermute | solution.py:296
  78.7 9.0 %collective-permute-start.25 = (s16[400,256]{1,0:T(8,128)(2,1)S(1)}, s16[400,256]{1,0:T(8,128)(2,1)S(1)}, u32[]{:S(2)}, u32[]{:S(2)}) collective-permute-start(s16[400,256]{1,0:T(8,128)(2,1)S(1)} %get-tuple-element.63), channel_id=1, source_target_pairs={{0,192},{64,0},{128,64},{192,128},{1,193},{65,1},{129,65},{193,129... | collective-permute-start | bytes 614408 | tf_op jit(solution)/shard_map/ppermute | solution.py:296
  83.3 17.2 %collective-permute-start.21 = (s16[208,1024]{1,0:T(8,128)(2,1)S(1)}, s16[208,1024]{1,0:T(8,128)(2,1)S(1)}, u32[]{:S(2)}, u32[]{:S(2)}) collective-permute-start(s16[208,1024]{1,0:T(8,128)(2,1)S(1)} %get-tuple-element.56), channel_id=1, source_target_pairs={{0,2},{2,0},{1,3},{3,1},{4,6},{6,4},{5,7},{7,5},{8,10},{10,8},{9,1... | collective-permute-start | bytes 1277960 | tf_op jit(solution)/shard_map/ppermute | solution.py:300
  84.2 16.3 %collective-permute-start.22 = (s16[208,1024]{1,0:T(8,128)(2,1)S(1)}, s16[208,1024]{1,0:T(8,128)(2,1)S(1)}, u32[]{:S(2)}, u32[]{:S(2)}) collective-permute-start(s16[208,1024]{1,0:T(8,128)(2,1)S(1)} %get-tuple-element.57), channel_id=1, source_target_pairs={{0,4},{4,0},{1,5},{5,1},{2,6},{6,2},{3,7},{7,3},{8,12},{12,8},{9,1... | collective-permute-start | bytes 1277960 | tf_op jit(solution)/shard_map/ppermute | solution.py:300
  84.6 21.0 %collective-permute-start.23 = (s16[208,1024]{1,0:T(8,128)(2,1)S(1)}, s16[208,1024]{1,0:T(8,128)(2,1)S(1)}, u32[]{:S(2)}, u32[]{:S(2)}) collective-permute-start(s16[208,1024]{1,0:T(8,128)(2,1)S(1)} %get-tuple-element.58), channel_id=1, source_target_pairs={{0,6},{2,4},{4,2},{6,0},{1,7},{3,5},{5,3},{7,1},{8,14},{10,12},{12... | collective-permute-start | bytes 1277960 | tf_op jit(solution)/shard_map/ppermute | solution.py:366
  88.1 12.4 %collective-permute-start.26 = (s16[784,256]{1,0:T(8,128)(2,1)S(1)}, s16[784,256]{1,0:T(8,128)(2,1)S(1)}, u32[]{:S(2)}, u32[]{:S(2)}) collective-permute-start(s16[784,256]{1,0:T(8,128)(2,1)S(1)} %get-tuple-element.64), channel_id=1, source_target_pairs={{0,64},{64,128},{128,192},{192,0},{1,65},{65,129},{129,193},{193,1... | collective-permute-start | bytes 1204232 | tf_op jit(solution)/shard_map/ppermute | solution.py:296
  89.3 11.2 %collective-permute-start.27 = (s16[784,256]{1,0:T(8,128)(2,1)S(1)}, s16[784,256]{1,0:T(8,128)(2,1)S(1)}, u32[]{:S(2)}, u32[]{:S(2)}) collective-permute-start(s16[784,256]{1,0:T(8,128)(2,1)S(1)} %get-tuple-element.65), channel_id=1, source_target_pairs={{0,192},{64,0},{128,64},{192,128},{1,193},{65,1},{129,65},{193,129... | collective-permute-start | bytes 1204232 | tf_op jit(solution)/shard_map/ppermute | solution.py:296
  106.1 8.3 %collective-permute-start.28 = (s16[2,208,128]{2,1,0:T(8,128)(2,1)S(1)}, s16[2,208,128]{2,1,0:T(8,128)(2,1)S(1)}, u32[]{:S(2)}, u32[]{:S(2)}) collective-permute-start(s16[2,208,128]{2,1,0:T(8,128)(2,1)S(1)} %get-tuple-element.67), channel_id=1, source_target_pairs={{0,8},{8,16},{16,24},{24,0},{1,9},{9,17},{17,25},{25,1},{2,10},{10... | collective-permute-start | bytes 319496 | tf_op jit(solution)/shard_map/ppermute | solution.py:296
  106.8 10.5 %collective-permute-start.29 = (s16[2,208,128]{2,1,0:T(8,128)(2,1)S(1)}, s16[2,208,128]{2,1,0:T(8,128)(2,1)S(1)}, u32[]{:S(2)}, u32[]{:S(2)}) collective-permute-start(s16[2,208,128]{2,1,0:T(8,128)(2,1)S(1)} %get-tuple-element.68), channel_id=1, source_target_pairs={{0,16},{8,24},{16,0},{24,8},{1,17},{9,25},{17,1},{25,9},{2,18},{10... | collective-permute-start | bytes 319496 | tf_op jit(solution)/shard_map/ppermute | solution.py:296
  110.4 10.5 %collective-permute-start.30 = (s16[2,208,128]{2,1,0:T(8,128)(2,1)S(1)}, s16[2,208,128]{2,1,0:T(8,128)(2,1)S(1)}, u32[]{:S(2)}, u32[]{:S(2)}) collective-permute-start(s16[2,208,128]{2,1,0:T(8,128)(2,1)S(1)} %get-tuple-element.69), channel_id=1, source_target_pairs={{0,24},{8,0},{16,8},{24,16},{1,25},{9,1},{17,9},{25,17},{2,26},{10... | collective-permute-start | bytes 319496 | tf_op jit(solution)/shard_map/ppermute | solution.py:296
  121.1 5.7 %collective-permute-start.31 = (s16[208,128]{1,0:T(8,128)(2,1)S(1)}, s16[208,128]{1,0:T(8,128)(2,1)S(1)}, u32[]{:S(2)}, u32[]{:S(2)}) collective-permute-start(s16[208,128]{1,0:T(8,128)(2,1)S(1)} %get-tuple-element.71), channel_id=1, source_target_pairs={{0,32},{32,0},{1,33},{33,1},{2,34},{34,2},{3,35},{35,3},{4,36},{36... | collective-permute-start | bytes 159752 | tf_op jit(solution)/shard_map/ppermute | solution.py:300
  (3 other events, 2.5 us)

commit v3 on v2

--- a/solution.py
+++ b/solution.py
@@ -180,8 +180,10 @@
             stats(c - chunk)
     stats(2 * part - chunk)
     top, total, pick = row[0]
-    rs[0:1, :] = to_lanes(top + jnp.log(total))
-    rs[1:2, :] = to_lanes(pick)
+    lse, pick = to_lanes(top + jnp.log(total)), to_lanes(pick)
+    for k in range(rs.shape[0]):
+        rs[k, 0:1, :] = lse
+        rs[k, 1:2, :] = pick
 
 
 def merge(parts):
@@ -202,8 +204,8 @@
 
 
 def weights_kernel(scale, tile, *refs):
-    rparts, cparts = refs[:4], refs[4:8]
-    pairs, cols, s_ref, k0, k1, im, own, p1, p3, o2a, o2b, mine, sent, rl, cl, w_ref, total = refs[8:]
+    rparts, cparts = refs[0], refs[1:5]
+    pairs, cols, s_ref, k0, k1, im, own, p1, p3, o2a, o2b, mine, sent, rl, cl, w_ref, total = refs[5:]
     n_im, n_ks = s_ref.shape
     keys = (k0, k1)
     half, part = n_ks // 2, n_ks // 4
@@ -212,7 +214,7 @@
     lse_col = cstat[0:1]
     rows = cl.shape[1]
     cl[...] = turn_left(lse_col - cstat[1:2], lax.axis_index("xl") * rows)[:, :rows]
-    rstat = meet([r[...] for r in rparts])
+    rstat = meet([rparts[k] for k in range(rparts.shape[0])])
     lse_row = rstat[0:1]
     rl[...] = turn_left(lse_row - rstat[1:2], lax.axis_index("zh") * rows)[:, :rows]
 
@@ -272,8 +274,7 @@
     image_out[...] = own[...] + decode(twin[...])
 
 
-def image_sum_kernel(after_x, after_z, after_both, own, got1, got3, keep, to1, to2, to3, total):
-    del after_x, after_z, after_both
+def image_sum_kernel(own, got1, got3, keep, to1, to2, to3, total):
     zh, xh = lax.axis_index("zh"), lax.axis_index("xh")
     rows, width = keep.shape[1:]
     total[...] = own[...] + decode(got1[...]) + decode(got3[...])
@@ -287,7 +288,8 @@
                 out[o] = x
 
 
-def image_twin_kernel(keep, got1, got2, got3, own, to_twin):
+def image_twin_kernel(after_x, after_z, after_both, keep, got1, got2, got3, own, to_twin):
+    del after_x, after_z, after_both
     own[...] = keep[0] + decode(got1[0]) + decode(got2[0]) + decode(got3[0])
     encode(keep[1] + decode(got1[1]) + decode(got2[1]) + decode(got3[1]), to_twin)
 
@@ -334,12 +336,12 @@
     tile = min(384, n_im)
     scores, im, rs, cs = call(
         functools.partial(scores_kernel, scale),
-        [shape((n_im, n_ks), F32), shape((n_im, d), BF16), shape((2, n_im), F32), shape((2, n_ks), F32)],
+        [shape((n_im, n_ks), F32), shape((n_im, d), BF16), shape((nzh, 2, n_im), F32), shape((2, n_ks), F32)],
         "scores",
         28,
         in_specs=[vmem] * 9,
     )(*ks, i0, i1, i3, ia, ib, pairs, cols)
-    rstats = [rs] + [shift(rs, "zh", 4, k) for k in (1, 2, 3)]
+    rs = lax.all_to_all(rs, "zh", 0, 0)
     cs = call(meet_kernel, shape((2, n_ks), F32), "meet", 4, in_specs=[vmem] * 2)(cs, flip(cs, "core", 2, 1))
     cstats = [cs] + [lax.ppermute(cs, ("zl", "xl"), [(i, i ^ k) for i in range(4)]) for k in (1, 2, 3)]
     outs = [shape((n_im, 2 * width), F32)] * 3 + [shape((n_im // 2 + PAD, 2 * width), I16)] * 2
@@ -349,9 +351,9 @@
         outs,
         "weights",
         36,
-        in_specs=[vmem] * 14,
+        in_specs=[vmem] * 11,
         scratch_shapes=[pltpu.VMEM((n_im, n_ks), BF16), pltpu.VMEM((n_im, d), F32)],
-    )(*rstats, *cstats, pairs, cols, scores, *ks, im)
+    )(rs, *cstats, pairs, cols, scores, *ks, im)
     q1, q3 = call(
         relay_kernel, [shape((n_im + PAD, 2 * width), I16)] * 2, "relay", 12, in_specs=[vmem] * 4
     )(p1, p3, shift(q2a, "y", 4, 1), shift(q2b, "y", 4, 3))
@@ -371,17 +373,17 @@
         [shape((2, rows, width), F32), coded, coded, coded],
         "image_sum",
         12,
-        in_specs=[vmem] * 6,
+        in_specs=[vmem] * 3,
         scratch_shapes=[pltpu.VMEM((n_im, 2 * width), F32)],
-    )(*pieces, own, q1, q3)
+    )(own, q1, q3)
     to2, to1, to3 = shift(to2, "zh", 4, 2), shift(to1, "zh", 4, 1), shift(to3, "zh", 4, 3)
     own, to_twin = call(
         image_twin_kernel,
         [shape((rows, width), F32), shape((rows + PAD, width), I16)],
         "image_twin",
         8,
-        in_specs=[vmem] * 4,
-    )(keep, to1, to2, to3)
+        in_specs=[vmem] * 7,
+    )(*pieces, keep, to1, to2, to3)
     modality_grad, image_grad = call(
         last_kernel, [shape((rows, d), F32), shape((rows, width), F32)], "last", 8, in_specs=[vmem] * 6
     )(own_key, *pieces, own, flip(to_twin, "xh", 2, 1))

time: 129 us -> 141 us (1.093)
  local copies, waits for them, and re-layouts: 2.53 us -> 9.59 us
  waiting for transfers between devices: 54.7 us -> 61.4 us
  starting transfers between devices: 53.7 us -> 52.1 us
    ppermute x17 -> x14, waiting for transfers between devices: 31.8 us -> 39.7 us  [shift(): return lax.ppermute(x, axis, [(i, (i + k) % n) for i in range(n)])]
    ppermute x17 -> x14, starting transfers between devices: 39.1 us -> 31.8 us  [shift(): return lax.ppermute(x, axis, [(i, (i + k) % n) for i in range(n)])]
    unnamed x6 -> x14, local copies, waits for them, and re-layouts: 2.53 us -> 9.59 us
    all_to_all x0 -> x1, starting transfers between devices: none -> 5.87 us  [on_device(): rs = lax.all_to_all(rs, 'zh', 0, 0)]
    ppermute x1, waiting for transfers between devices: 5.07 us -> 0.01 us  [on_device(): lax.ppermute(to_both, ('zl', 'xl'), [(i, 3 - i) for i in range(4)])]
    ppermute x3, waiting for transfers between devices: 0.01 us -> 2.5 us  [on_device(): lax.ppermute(cs, ('zl', 'xl'), [(i, i ^ k) for i in range(4)])]
  transfers between devices with their start and end apart: 32 -> 30, of which waited for: 16 -> 18; matrix products, arithmetic and copies ran while one was open for 0% -> 0% of each run, Pallas kernels for 1% -> 2%
where the time goes in v3:
time: 141 us
  waiting for transfers between devices  61.4 us (44%)
  starting transfers between devices  52.1 us (37%)
  Pallas kernels  17.1 us (12%)
  local copies, waits for them, and re-layouts  9.59 us (7%)
    ppermute x14, waiting for transfers between devices, shift(): return lax.ppermute(x, axis, [(i, (i + k) % n) for i in range(n)])  39.7 us
    ppermute x14, starting transfers between devices, shift(): return lax.ppermute(x, axis, [(i, (i + k) % n) for i in range(n)])  31.8 us
    ppermute x11, waiting for transfers between devices, flip(): return lax.ppermute(x, axis, [(i, i ^ d) for i in range(n)])  18.7 us
    unnamed x14, local copies, waits for them, and re-layouts  9.59 us
    ppermute x11, starting transfers between devices, flip(): return lax.ppermute(x, axis, [(i, i ^ d) for i in range(n)])  8.59 us
    pallas_call x1, Pallas kernels, on_device(): call(functools.partial(weights_kernel, scale, tile), outs, 'weights', 36,...  7.87 us
    all_to_all x1, starting transfers between devices, on_device(): rs = lax.all_to_all(rs, 'zh', 0, 0)  5.87 us
    pallas_call x1, Pallas kernels, on_device(): call(functools.partial(scores_kernel, scale), [shape((n_im, n_ks), F32),...  5.54 us
  transfers between devices with their start and end apart: 30, of which 18 were waited for; matrix products, arithmetic and copies ran while one was open for 0% of the time, Pallas kernels for 2%

profile of v3, /device:TPU:4, one launch (start us, length us, event | category | flops | bytes accessed | tf_op | source)
XLA Modules:
  0.0 141.0 jit_solution(18198632871982635494)
XLA Ops:
  0.6 2.3 %collective-permute-start = (bf16[192,128]{1,0:T(8,128)(2,1)}, bf16[192,128]{1,0:T(8,128)(2,1)S(1)}, u32[]{:S(2)}, u32[]{:S(2)}) collective-permute-start(bf16[192,128]{1,0:T(8,128)(2,1)} %image.1), channel_id=1, source_target_pairs={{0,32},{32,0},{1,33},{33,1},{2,34},{34,2},{3,35},{35,3},{4,36},{36... | collective-permute-start | bytes 147464 | tf_op jit(solution)/shard_map/ppermute | solution.py:302
  3.0 3.6 %collective-permute-done.twin = bf16[192,128]{1,0:T(8,128)(2,1)S(1)} collective-permute-done((bf16[192,128]{1,0:T(8,128)(2,1)}, bf16[192,128]{1,0:T(8,128)(2,1)S(1)}, u32[]{:S(2)}, u32[]{:S(2)}) %collective-permute-start) | collective-permute-done | bytes 49184 | tf_op jit(solution)/shard_map/ppermute | solution.py:302
  7.3 6.4 %collective-permute-start.3 = (bf16[2,192,128]{2,1,0:T(8,128)(2,1)S(1)}, bf16[2,192,128]{2,1,0:T(8,128)(2,1)S(1)}, u32[]{:S(2)}, u32[]{:S(2)}) collective-permute-start(bf16[2,192,128]{2,1,0:T(8,128)(2,1)S(1)} %pair.1.both), channel_id=1, source_target_pairs={{0,24},{8,0},{16,8},{24,16},{1,25},{9,1},{17,9},{25,17},{2,26},{10... | collective-permute-start | bytes 294920 | tf_op jit(solution)/shard_map/ppermute | solution.py:298
  14.7 2.8 %collective-permute-start.1 = (bf16[2,192,128]{2,1,0:T(8,128)(2,1)S(1)}, bf16[2,192,128]{2,1,0:T(8,128)(2,1)S(1)}, u32[]{:S(2)}, u32[]{:S(2)}) collective-permute-start(bf16[2,192,128]{2,1,0:T(8,128)(2,1)S(1)} %pair.1.both), channel_id=1, source_target_pairs={{0,8},{8,16},{16,24},{24,0},{1,9},{9,17},{17,25},{25,1},{2,10},{10... | collective-permute-start | bytes 294920 | tf_op jit(solution)/shard_map/ppermute | solution.py:298
  19.5 1.5 %collective-permute-done.3.b3 = bf16[2,192,128]{2,1,0:T(8,128)(2,1)S(1)} collective-permute-done((bf16[2,192,128]{2,1,0:T(8,128)(2,1)S(1)}, bf16[2,192,128]{2,1,0:T(8,128)(2,1)S(1)}, u32[]{:S(2)}, u32[]{:S(2)}) %collective-permute-start.3) | collective-permute-done | bytes 98336 | tf_op jit(solution)/shard_map/ppermute | solution.py:298
  21.0 3.3 %collective-permute-done.2.b2 = bf16[2,192,128]{2,1,0:T(8,128)(2,1)S(1)} collective-permute-done((bf16[2,192,128]{2,1,0:T(8,128)(2,1)S(1)}, bf16[2,192,128]{2,1,0:T(8,128)(2,1)S(1)}, u32[]{:S(2)}, u32[]{:S(2)}) %collective-permute-start.2) | collective-permute-done | bytes 98336 | tf_op jit(solution)/shard_map/ppermute | solution.py:298
  26.5 3.0 %collective-permute-start.9 = (bf16[8,192,128]{2,1,0:T(8,128)(2,1)S(1)}, bf16[8,192,128]{2,1,0:T(8,128)(2,1)S(1)}, u32[]{:S(2)}, u32[]{:S(2)}) collective-permute-start(bf16[8,192,128]{2,1,0:T(8,128)(2,1)S(1)} %get-tuple-element.42.after.refs_2_), channel_id=1, source_target_pairs={{0,192},{64,0},{128,64},{192,128},{1,193},{65,1},{129,65},{193,129... | collective-permute-start | bytes 1179656 | tf_op jit(solution)/shard_map/ppermute | solution.py:298
  29.5 4.2 %collective-permute-done.5.z = bf16[192,1024]{1,0:T(8,128)(2,1)S(1)} collective-permute-done((bf16[192,1024]{1,0:T(8,128)(2,1)S(1)}, bf16[192,1024]{1,0:T(8,128)(2,1)S(1)}, u32[]{:S(2)}, u32[]{:S(2)}) %collective-permute-start.5) | collective-permute-done | bytes 393248 | tf_op jit(solution)/shard_map/ppermute | solution.py:302
  33.7 1.5 %collective-permute-done.4.x = bf16[192,1024]{1,0:T(8,128)(2,1)S(1)} collective-permute-done((bf16[192,1024]{1,0:T(8,128)(2,1)S(1)}, bf16[192,1024]{1,0:T(8,128)(2,1)S(1)}, u32[]{:S(2)}, u32[]{:S(2)}) %collective-permute-start.4) | collective-permute-done | bytes 393248 | tf_op jit(solution)/shard_map/ppermute | solution.py:302
  36.9 3.2 %collective-permute-done.8.behind.refs_3_ = bf16[8,192,128]{2,1,0:T(8,128)(2,1)S(1)} collective-permute-done((bf16[8,192,128]{2,1,0:T(8,128)(2,1)S(1)}, bf16[8,192,128]{2,1,0:T(8,128)(2,1)S(1)}, u32[]{:S(2)}, u32[]{:S(2)}) %collective-permute-start.8) | collective-permute-done | bytes 393248 | tf_op jit(solution)/shard_map/ppermute | solution.py:298
  40.2 3.2 %collective-permute-start.11 = (bf16[4,192,128]{2,1,0:T(8,128)(2,1)S(1)}, bf16[4,192,128]{2,1,0:T(8,128)(2,1)S(1)}, u32[]{:S(2)}, u32[]{:S(2)}) collective-permute-start(bf16[4,192,128]{2,1,0:T(8,128)(2,1)S(1)} %get-tuple-element.46), channel_id=1, source_target_pairs={{0,192},{64,0},{128,64},{192,128},{1,193},{65,1},{129,65},{193,129... | collective-permute-start | bytes 589832 | tf_op jit(solution)/shard_map/ppermute | solution.py:298
  43.4 3.6 %collective-permute-done.10.after_a.refs_5_ = bf16[4,192,128]{2,1,0:T(8,128)(2,1)S(1)} collective-permute-done((bf16[4,192,128]{2,1,0:T(8,128)(2,1)S(1)}, bf16[4,192,128]{2,1,0:T(8,128)(2,1)S(1)}, u32[]{:S(2)}, u32[]{:S(2)}) %collective-permute-start.10) | collective-permute-done | bytes 196640 | tf_op jit(solution)/shard_map/ppermute | solution.py:298
  47.4 3.4 %collective-permute-done.12.refs_1_.refs_9_ = bf16[768,1024]{1,0:T(8,128)(2,1)S(1)} collective-permute-done((bf16[768,1024]{1,0:T(8,128)(2,1)S(1)}, bf16[768,1024]{1,0:T(8,128)(2,1)S(1)}, u32[]{:S(2)}, u32[]{:S(2)}) %collective-permute-start.12) | collective-permute-done | bytes 1572896 | tf_op jit(solution)/shard_map/ppermute | solution.py:302
  50.8 5.5 %scores.1 = (f32[768,1536]{1,0:T(8,128)S(1)}, bf16[768,1024]{1,0:T(8,128)(2,1)S(1)}, f32[4,2,768]{2,1,0:T(2,128)}, f32[2,1536]{1,0:T(2,128)S(1)}) custom-call(bf16[768,1024]{1,0:T(8,128)(2,1)S(1)} %join.1.refs_0_.refs_8_, bf16[768,1024]{1,0:T(8,128)(2,1)S(1)} %collective-permute-done.12.refs_1_.refs_9_, ...), custom_call_target="tpu_custom_call" | custom-call | flops 1000 | bytes 1000 | tf_op jit(solution)/shard_map/scores/pallas_call | solution.py:337
  56.4 2.1 %copy-done = f32[768,1536]{1,0:T(8,128)} copy-done((f32[768,1536]{1,0:T(8,128)}, f32[768,1536]{1,0:T(8,128)S(1)}, u32[]{:S(2)}) %copy-start) | copy-done | bytes 4718616
  59.7 5.9 %all-to-all-start = ((f32[4,2,768]{2,1,0:T(2,128)}), f32[4,2,768]{2,1,0:T(2,128)S(1)}, u32[]{:S(2)}, u32[]{:S(2)}) async-start(f32[4,2,768]{2,1,0:T(2,128)} %get-tuple-element.49), calls=%async_computation | async-start | bytes 49152 | tf_op jit(solution)/shard_map/all_to_all | solution.py:344
  67.5 1.7 %collective-permute-start.15 = (f32[2,1536]{1,0:T(2,128)S(1)}, f32[2,1536]{1,0:T(2,128)S(1)}, u32[]{:S(2)}, u32[]{:S(2)}) collective-permute-start(f32[2,1536]{1,0:T(2,128)S(1)} %meet.1.refs_1_), channel_id=1, source_target_pairs={{0,4},{2,6},{4,0},{6,2},{1,5},{3,7},{5,1},{7,3},{8,12},{10,14},{12... | collective-permute-start | bytes 36872 | tf_op jit(solution)/shard_map/ppermute | solution.py:346
  71.5 1.4 collective-permute-done.14.refs_2_
  73.4 2.3 %copy-done.1 = f32[768,1536]{1,0:T(8,128)S(1)} copy-done((f32[768,1536]{1,0:T(8,128)S(1)}, f32[768,1536]{1,0:T(8,128)}, u32[]{:S(2)}) %copy-start.1) | copy-done | bytes 4718616
  75.7 1.4 copy-done.3
  77.1 7.9 %weights.1 = (f32[768,256]{1,0:T(8,128)S(1)}, f32[768,256]{1,0:T(8,128)S(1)}, f32[768,256]{1,0:T(8,128)S(1)}, s16[400,256]{1,0:T(8,128)(2,1)S(1)}, s16[400,256]{...) custom-call(f32[4,2,768]{2,1,0:T(2,128)S(1)} %all-to-all-done.refs_0, ...), custom_call_target="tpu_custom_call" | custom-call | flops 1000 | bytes 1000 | tf_op jit(solution)/shard_map/weights/pallas_call | solution.py:349
  85.0 3.3 %collective-permute-start.22 = (s16[400,256]{1,0:T(8,128)(2,1)S(1)}, s16[400,256]{1,0:T(8,128)(2,1)S(1)}, u32[]{:S(2)}, u32[]{:S(2)}) collective-permute-start(s16[400,256]{1,0:T(8,128)(2,1)S(1)} %get-tuple-element.63), channel_id=1, source_target_pairs={{0,192},{64,0},{128,64},{192,128},{1,193},{65,1},{129,65},{193,129... | collective-permute-start | bytes 614408 | tf_op jit(solution)/shard_map/ppermute | solution.py:298
  88.3 5.7 %collective-permute-done.21.got_a = s16[400,256]{1,0:T(8,128)(2,1)S(1)} collective-permute-done((s16[400,256]{1,0:T(8,128)(2,1)S(1)}, s16[400,256]{1,0:T(8,128)(2,1)S(1)}, u32[]{:S(2)}, u32[]{:S(2)}) %collective-permute-start.21) | collective-permute-done | bytes 204832 | tf_op jit(solution)/shard_map/ppermute | solution.py:298
  95.6 2.1 %collective-permute-start.24 = (s16[784,256]{1,0:T(8,128)(2,1)S(1)}, s16[784,256]{1,0:T(8,128)(2,1)S(1)}, u32[]{:S(2)}, u32[]{:S(2)}) collective-permute-start(s16[784,256]{1,0:T(8,128)(2,1)S(1)} %get-tuple-element.65), channel_id=1, source_target_pairs={{0,192},{64,0},{128,64},{192,128},{1,193},{65,1},{129,65},{193,129... | collective-permute-start | bytes 1204232 | tf_op jit(solution)/shard_map/ppermute | solution.py:298
  99.9 2.3 %collective-permute-start.20 = (s16[208,1024]{1,0:T(8,128)(2,1)S(1)}, s16[208,1024]{1,0:T(8,128)(2,1)S(1)}, u32[]{:S(2)}, u32[]{:S(2)}) collective-permute-start(s16[208,1024]{1,0:T(8,128)(2,1)S(1)} %get-tuple-element.58), channel_id=1, source_target_pairs={{0,6},{2,4},{4,2},{6,0},{1,7},{3,5},{5,3},{7,1},{8,14},{10,12},{12... | collective-permute-start | bytes 1277960 | tf_op jit(solution)/shard_map/ppermute | solution.py:368
  102.2 4.6 %collective-permute-done.23.got1 = s16[784,256]{1,0:T(8,128)(2,1)S(1)} collective-permute-done((s16[784,256]{1,0:T(8,128)(2,1)S(1)}, s16[784,256]{1,0:T(8,128)(2,1)S(1)}, u32[]{:S(2)}, u32[]{:S(2)}) %collective-permute-start.23) | collective-permute-done | bytes 401440 | tf_op jit(solution)/shard_map/ppermute | solution.py:298
  107.4 2.5 %collective-permute-start.25 = (s16[2,208,128]{2,1,0:T(8,128)(2,1)S(1)}, s16[2,208,128]{2,1,0:T(8,128)(2,1)S(1)}, u32[]{:S(2)}, u32[]{:S(2)}) collective-permute-start(s16[2,208,128]{2,1,0:T(8,128)(2,1)S(1)} %get-tuple-element.67), channel_id=1, source_target_pairs={{0,8},{8,16},{16,24},{24,0},{1,9},{9,17},{17,25},{25,1},{2,10},{10... | collective-permute-start | bytes 319496 | tf_op jit(solution)/shard_map/ppermute | solution.py:298
  109.8 3.6 %collective-permute-start.26 = (s16[2,208,128]{2,1,0:T(8,128)(2,1)S(1)}, s16[2,208,128]{2,1,0:T(8,128)(2,1)S(1)}, u32[]{:S(2)}, u32[]{:S(2)}) collective-permute-start(s16[2,208,128]{2,1,0:T(8,128)(2,1)S(1)} %get-tuple-element.68), channel_id=1, source_target_pairs={{0,16},{8,24},{16,0},{24,8},{1,17},{9,25},{17,1},{25,9},{2,18},{10... | collective-permute-start | bytes 319496 | tf_op jit(solution)/shard_map/ppermute | solution.py:298
  113.4 14.9 %collective-permute-done.25.got1 = s16[2,208,128]{2,1,0:T(8,128)(2,1)S(1)} collective-permute-done((s16[2,208,128]{2,1,0:T(8,128)(2,1)S(1)}, s16[2,208,128]{2,1,0:T(8,128)(2,1)S(1)}, u32[]{:S(2)}, u32[]{:S(2)}) %collective-permute-start.25) | collective-permute-done | bytes 106528 | tf_op jit(solution)/shard_map/ppermute | solution.py:298
  128.3 2.6 %collective-permute-start.27 = (s16[2,208,128]{2,1,0:T(8,128)(2,1)S(1)}, s16[2,208,128]{2,1,0:T(8,128)(2,1)S(1)}, u32[]{:S(2)}, u32[]{:S(2)}) collective-permute-start(s16[2,208,128]{2,1,0:T(8,128)(2,1)S(1)} %get-tuple-element.69), channel_id=1, source_target_pairs={{0,24},{8,0},{16,8},{24,16},{1,25},{9,1},{17,9},{25,17},{2,26},{10... | collective-permute-start | bytes 319496 | tf_op jit(solution)/shard_map/ppermute | solution.py:298
  131.6 2.3 %collective-permute-done.27.got3 = s16[2,208,128]{2,1,0:T(8,128)(2,1)S(1)} collective-permute-done((s16[2,208,128]{2,1,0:T(8,128)(2,1)S(1)}, s16[2,208,128]{2,1,0:T(8,128)(2,1)S(1)}, u32[]{:S(2)}, u32[]{:S(2)}) %collective-permute-start.27) | collective-permute-done | bytes 106528 | tf_op jit(solution)/shard_map/ppermute | solution.py:298
  135.0 4.8 %collective-permute-done.28.twin = s16[208,128]{1,0:T(8,128)(2,1)S(1)} collective-permute-done((s16[208,128]{1,0:T(8,128)(2,1)S(1)}, s16[208,128]{1,0:T(8,128)(2,1)S(1)}, u32[]{:S(2)}, u32[]{:S(2)}) %collective-permute-start.28) | collective-permute-done | bytes 53280 | tf_op jit(solution)/shard_map/ppermute | solution.py:302
  (56 shorter events, 21.4 us)
Async XLA Ops:
  0.6 5.9 %collective-permute-start = (bf16[192,128]{1,0:T(8,128)(2,1)}, bf16[192,128]{1,0:T(8,128)(2,1)S(1)}, u32[]{:S(2)}, u32[]{:S(2)}) collective-permute-start(bf16[192,128]{1,0:T(8,128)(2,1)} %image.1), channel_id=1, source_target_pairs={{0,32},{32,0},{1,33},{33,1},{2,34},{34,2},{3,35},{35,3},{4,36},{36... | collective-permute-start | bytes 147464 | tf_op jit(solution)/shard_map/ppermute | solution.py:302
  7.3 13.6 %collective-permute-start.3 = (bf16[2,192,128]{2,1,0:T(8,128)(2,1)S(1)}, bf16[2,192,128]{2,1,0:T(8,128)(2,1)S(1)}, u32[]{:S(2)}, u32[]{:S(2)}) collective-permute-start(bf16[2,192,128]{2,1,0:T(8,128)(2,1)S(1)} %pair.1.both), channel_id=1, source_target_pairs={{0,24},{8,0},{16,8},{24,16},{1,25},{9,1},{17,9},{25,17},{2,26},{10... | collective-permute-start | bytes 294920 | tf_op jit(solution)/shard_map/ppermute | solution.py:298
  13.7 10.5 %collective-permute-start.2 = (bf16[2,192,128]{2,1,0:T(8,128)(2,1)S(1)}, bf16[2,192,128]{2,1,0:T(8,128)(2,1)S(1)}, u32[]{:S(2)}, u32[]{:S(2)}) collective-permute-start(bf16[2,192,128]{2,1,0:T(8,128)(2,1)S(1)} %pair.1.both), channel_id=1, source_target_pairs={{0,16},{8,24},{16,0},{24,8},{1,17},{9,25},{17,1},{25,9},{2,18},{10... | collective-permute-start | bytes 294920 | tf_op jit(solution)/shard_map/ppermute | solution.py:298
  14.7 9.5 %collective-permute-start.1 = (bf16[2,192,128]{2,1,0:T(8,128)(2,1)S(1)}, bf16[2,192,128]{2,1,0:T(8,128)(2,1)S(1)}, u32[]{:S(2)}, u32[]{:S(2)}) collective-permute-start(bf16[2,192,128]{2,1,0:T(8,128)(2,1)S(1)} %pair.1.both), channel_id=1, source_target_pairs={{0,8},{8,16},{16,24},{24,0},{1,9},{9,17},{17,25},{25,1},{2,10},{10... | collective-permute-start | bytes 294920 | tf_op jit(solution)/shard_map/ppermute | solution.py:298
  24.3 9.4 %collective-permute-start.5 = (bf16[192,1024]{1,0:T(8,128)(2,1)S(1)}, bf16[192,1024]{1,0:T(8,128)(2,1)S(1)}, u32[]{:S(2)}, u32[]{:S(2)}) collective-permute-start(bf16[192,1024]{1,0:T(8,128)(2,1)S(1)} %get-tuple-element.41.own), channel_id=1, source_target_pairs={{0,4},{4,0},{1,5},{5,1},{2,6},{6,2},{3,7},{7,3},{8,12},{12,8},{9,1... | collective-permute-start | bytes 1179656 | tf_op jit(solution)/shard_map/ppermute | solution.py:302
  25.3 9.9 %collective-permute-start.4 = (bf16[192,1024]{1,0:T(8,128)(2,1)S(1)}, bf16[192,1024]{1,0:T(8,128)(2,1)S(1)}, u32[]{:S(2)}, u32[]{:S(2)}) collective-permute-start(bf16[192,1024]{1,0:T(8,128)(2,1)S(1)} %get-tuple-element.41.own), channel_id=1, source_target_pairs={{0,2},{2,0},{1,3},{3,1},{4,6},{6,4},{5,7},{7,5},{8,10},{10,8},{9,1... | collective-permute-start | bytes 1179656 | tf_op jit(solution)/shard_map/ppermute | solution.py:302
  26.5 10.4 %collective-permute-start.9 = (bf16[8,192,128]{2,1,0:T(8,128)(2,1)S(1)}, bf16[8,192,128]{2,1,0:T(8,128)(2,1)S(1)}, u32[]{:S(2)}, u32[]{:S(2)}) collective-permute-start(bf16[8,192,128]{2,1,0:T(8,128)(2,1)S(1)} %get-tuple-element.42.after.refs_2_), channel_id=1, source_target_pairs={{0,192},{64,0},{128,64},{192,128},{1,193},{65,1},{129,65},{193,129... | collective-permute-start | bytes 1179656 | tf_op jit(solution)/shard_map/ppermute | solution.py:298
  29.5 10.6 %collective-permute-start.8 = (bf16[8,192,128]{2,1,0:T(8,128)(2,1)S(1)}, bf16[8,192,128]{2,1,0:T(8,128)(2,1)S(1)}, u32[]{:S(2)}, u32[]{:S(2)}) collective-permute-start(bf16[8,192,128]{2,1,0:T(8,128)(2,1)S(1)} %get-tuple-element.42.after.refs_2_), channel_id=1, source_target_pairs={{0,64},{64,128},{128,192},{192,0},{1,65},{65,129},{129,193},{193,1... | collective-permute-start | bytes 1179656 | tf_op jit(solution)/shard_map/ppermute | solution.py:298
  35.2 8.2 %collective-permute-start.6 = (bf16[96,1024]{1,0:T(8,128)(2,1)S(1)}, bf16[96,1024]{1,0:T(8,128)(2,1)S(1)}, u32[]{:S(2)}, u32[]{:S(2)}) collective-permute-start(bf16[96,1024]{1,0:T(8,128)(2,1)S(1)} %get-tuple-element.43), channel_id=1, source_target_pairs={{0,2},{2,0},{1,3},{3,1},{4,6},{6,4},{5,7},{7,5},{8,10},{10,8},{9,1... | collective-permute-start | bytes 589832 | tf_op jit(solution)/shard_map/ppermute | solution.py:302
  36.5 6.9 %collective-permute-start.7 = (bf16[96,1024]{1,0:T(8,128)(2,1)S(1)}, bf16[96,1024]{1,0:T(8,128)(2,1)S(1)}, u32[]{:S(2)}, u32[]{:S(2)}) collective-permute-start(bf16[96,1024]{1,0:T(8,128)(2,1)S(1)} %get-tuple-element.44), channel_id=1, source_target_pairs={{0,4},{4,0},{1,5},{5,1},{2,6},{6,2},{3,7},{7,3},{8,12},{12,8},{9,1... | collective-permute-start | bytes 589832 | tf_op jit(solution)/shard_map/ppermute | solution.py:302
  40.1 7.0 %collective-permute-start.10 = (bf16[4,192,128]{2,1,0:T(8,128)(2,1)S(1)}, bf16[4,192,128]{2,1,0:T(8,128)(2,1)S(1)}, u32[]{:S(2)}, u32[]{:S(2)}) collective-permute-start(bf16[4,192,128]{2,1,0:T(8,128)(2,1)S(1)} %get-tuple-element.45), channel_id=1, source_target_pairs={{0,64},{64,128},{128,192},{192,0},{1,65},{65,129},{129,193},{193,1... | collective-permute-start | bytes 589832 | tf_op jit(solution)/shard_map/ppermute | solution.py:298
  40.2 6.9 %collective-permute-start.11 = (bf16[4,192,128]{2,1,0:T(8,128)(2,1)S(1)}, bf16[4,192,128]{2,1,0:T(8,128)(2,1)S(1)}, u32[]{:S(2)}, u32[]{:S(2)}) collective-permute-start(bf16[4,192,128]{2,1,0:T(8,128)(2,1)S(1)} %get-tuple-element.46), channel_id=1, source_target_pairs={{0,192},{64,0},{128,64},{192,128},{1,193},{65,1},{129,65},{193,129... | collective-permute-start | bytes 589832 | tf_op jit(solution)/shard_map/ppermute | solution.py:298
  47.2 3.7 %collective-permute-start.12 = (bf16[768,1024]{1,0:T(8,128)(2,1)S(1)}, bf16[768,1024]{1,0:T(8,128)(2,1)S(1)}, u32[]{:S(2)}, u32[]{:S(2)}) collective-permute-start(bf16[768,1024]{1,0:T(8,128)(2,1)S(1)} %join.1.refs_0_.refs_8_), channel_id=1, source_target_pairs={{0,1},{1,0},{2,3},{3,2},{4,5},{5,4},{6,7},{7,6},{8,9},{9,8},{10,11... | collective-permute-start | bytes 4718600 | tf_op jit(solution)/shard_map/ppermute | solution.py:302
  56.4 2.1 %copy-start = (f32[768,1536]{1,0:T(8,128)}, f32[768,1536]{1,0:T(8,128)S(1)}, u32[]{:S(2)}) copy-start(f32[768,1536]{1,0:T(8,128)S(1)} %get-tuple-element.51.refs_7_) | copy-start | bytes 14155780
  59.7 13.7 %all-to-all-start = ((f32[4,2,768]{2,1,0:T(2,128)}), f32[4,2,768]{2,1,0:T(2,128)S(1)}, u32[]{:S(2)}, u32[]{:S(2)}) async-start(f32[4,2,768]{2,1,0:T(2,128)} %get-tuple-element.49), calls=%async_computation | async-start | bytes 49152 | tf_op jit(solution)/shard_map/all_to_all | solution.py:344
  65.6 1.2 collective-permute-start.13
  66.8 4.7 %collective-permute-start.16 = (f32[2,1536]{1,0:T(2,128)S(1)}, f32[2,1536]{1,0:T(2,128)S(1)}, u32[]{:S(2)}, u32[]{:S(2)}) collective-permute-start(f32[2,1536]{1,0:T(2,128)S(1)} %meet.1.refs_1_), channel_id=1, source_target_pairs={{0,6},{2,4},{4,2},{6,0},{1,7},{3,5},{5,3},{7,1},{8,14},{10,12},{12... | collective-permute-start | bytes 36872 | tf_op jit(solution)/shard_map/ppermute | solution.py:346
  67.5 4.0 %collective-permute-start.15 = (f32[2,1536]{1,0:T(2,128)S(1)}, f32[2,1536]{1,0:T(2,128)S(1)}, u32[]{:S(2)}, u32[]{:S(2)}) collective-permute-start(f32[2,1536]{1,0:T(2,128)S(1)} %meet.1.refs_1_), channel_id=1, source_target_pairs={{0,4},{2,6},{4,0},{6,2},{1,5},{3,7},{5,1},{7,3},{8,12},{10,14},{12... | collective-permute-start | bytes 36872 | tf_op jit(solution)/shard_map/ppermute | solution.py:346
  69.2 3.7 %collective-permute-start.14 = (f32[2,1536]{1,0:T(2,128)S(1)}, f32[2,1536]{1,0:T(2,128)S(1)}, u32[]{:S(2)}, u32[]{:S(2)}) collective-permute-start(f32[2,1536]{1,0:T(2,128)S(1)} %meet.1.refs_1_), channel_id=1, source_target_pairs={{0,2},{2,0},{4,6},{6,4},{1,3},{3,1},{5,7},{7,5},{8,10},{10,8},{12,... | collective-permute-start | bytes 36872 | tf_op jit(solution)/shard_map/ppermute | solution.py:346
  73.4 2.3 %copy-start.1 = (f32[768,1536]{1,0:T(8,128)S(1)}, f32[768,1536]{1,0:T(8,128)}, u32[]{:S(2)}) copy-start(f32[768,1536]{1,0:T(8,128)} %copy-done) | copy-start | bytes 14155780
  85.0 12.7 %collective-permute-start.17 = (s16[4,208,1024]{2,1,0:T(8,128)(2,1)S(1)}, s16[4,208,1024]{2,1,0:T(8,128)(2,1)S(1)}, u32[]{:S(2)}, u32[]{:S(2)}) collective-permute-start(s16[4,208,1024]{2,1,0:T(8,128)(2,1)S(1)} %get-tuple-element.54), channel_id=1, source_target_pairs={{0,1},{1,0},{2,3},{3,2},{4,5},{5,4},{6,7},{7,6},{8,9},{9,8},{10,11... | collective-permute-start | bytes 5111816 | tf_op jit(solution)/shard_map/ppermute | solution.py:302
  85.0 9.0 %collective-permute-start.21 = (s16[400,256]{1,0:T(8,128)(2,1)S(1)}, s16[400,256]{1,0:T(8,128)(2,1)S(1)}, u32[]{:S(2)}, u32[]{:S(2)}) collective-permute-start(s16[400,256]{1,0:T(8,128)(2,1)S(1)} %get-tuple-element.62), channel_id=1, source_target_pairs={{0,64},{64,128},{128,192},{192,0},{1,65},{65,129},{129,193},{193,1... | collective-permute-start | bytes 614408 | tf_op jit(solution)/shard_map/ppermute | solution.py:298
  85.0 9.0 %collective-permute-start.22 = (s16[400,256]{1,0:T(8,128)(2,1)S(1)}, s16[400,256]{1,0:T(8,128)(2,1)S(1)}, u32[]{:S(2)}, u32[]{:S(2)}) collective-permute-start(s16[400,256]{1,0:T(8,128)(2,1)S(1)} %get-tuple-element.63), channel_id=1, source_target_pairs={{0,192},{64,0},{128,64},{192,128},{1,193},{65,1},{129,65},{193,129... | collective-permute-start | bytes 614408 | tf_op jit(solution)/shard_map/ppermute | solution.py:298
  94.4 12.4 %collective-permute-start.23 = (s16[784,256]{1,0:T(8,128)(2,1)S(1)}, s16[784,256]{1,0:T(8,128)(2,1)S(1)}, u32[]{:S(2)}, u32[]{:S(2)}) collective-permute-start(s16[784,256]{1,0:T(8,128)(2,1)S(1)} %get-tuple-element.64), channel_id=1, source_target_pairs={{0,64},{64,128},{128,192},{192,0},{1,65},{65,129},{129,193},{193,1... | collective-permute-start | bytes 1204232 | tf_op jit(solution)/shard_map/ppermute | solution.py:298
  95.6 11.2 %collective-permute-start.24 = (s16[784,256]{1,0:T(8,128)(2,1)S(1)}, s16[784,256]{1,0:T(8,128)(2,1)S(1)}, u32[]{:S(2)}, u32[]{:S(2)}) collective-permute-start(s16[784,256]{1,0:T(8,128)(2,1)S(1)} %get-tuple-element.65), channel_id=1, source_target_pairs={{0,192},{64,0},{128,64},{192,128},{1,193},{65,1},{129,65},{193,129... | collective-permute-start | bytes 1204232 | tf_op jit(solution)/shard_map/ppermute | solution.py:298
  98.6 35.3 %collective-permute-start.18 = (s16[208,1024]{1,0:T(8,128)(2,1)S(1)}, s16[208,1024]{1,0:T(8,128)(2,1)S(1)}, u32[]{:S(2)}, u32[]{:S(2)}) collective-permute-start(s16[208,1024]{1,0:T(8,128)(2,1)S(1)} %get-tuple-element.56), channel_id=1, source_target_pairs={{0,2},{2,0},{1,3},{3,1},{4,6},{6,4},{5,7},{7,5},{8,10},{10,8},{9,1... | collective-permute-start | bytes 1277960 | tf_op jit(solution)/shard_map/ppermute | solution.py:302
  99.5 34.4 %collective-permute-start.19 = (s16[208,1024]{1,0:T(8,128)(2,1)S(1)}, s16[208,1024]{1,0:T(8,128)(2,1)S(1)}, u32[]{:S(2)}, u32[]{:S(2)}) collective-permute-start(s16[208,1024]{1,0:T(8,128)(2,1)S(1)} %get-tuple-element.57), channel_id=1, source_target_pairs={{0,4},{4,0},{1,5},{5,1},{2,6},{6,2},{3,7},{7,3},{8,12},{12,8},{9,1... | collective-permute-start | bytes 1277960 | tf_op jit(solution)/shard_map/ppermute | solution.py:302
  99.9 34.0 %collective-permute-start.20 = (s16[208,1024]{1,0:T(8,128)(2,1)S(1)}, s16[208,1024]{1,0:T(8,128)(2,1)S(1)}, u32[]{:S(2)}, u32[]{:S(2)}) collective-permute-start(s16[208,1024]{1,0:T(8,128)(2,1)S(1)} %get-tuple-element.58), channel_id=1, source_target_pairs={{0,6},{2,4},{4,2},{6,0},{1,7},{3,5},{5,3},{7,1},{8,14},{10,12},{12... | collective-permute-start | bytes 1277960 | tf_op jit(solution)/shard_map/ppermute | solution.py:368
  107.4 21.0 %collective-permute-start.25 = (s16[2,208,128]{2,1,0:T(8,128)(2,1)S(1)}, s16[2,208,128]{2,1,0:T(8,128)(2,1)S(1)}, u32[]{:S(2)}, u32[]{:S(2)}) collective-permute-start(s16[2,208,128]{2,1,0:T(8,128)(2,1)S(1)} %get-tuple-element.67), channel_id=1, source_target_pairs={{0,8},{8,16},{16,24},{24,0},{1,9},{9,17},{17,25},{25,1},{2,10},{10... | collective-permute-start | bytes 319496 | tf_op jit(solution)/shard_map/ppermute | solution.py:298
  109.8 21.8 %collective-permute-start.26 = (s16[2,208,128]{2,1,0:T(8,128)(2,1)S(1)}, s16[2,208,128]{2,1,0:T(8,128)(2,1)S(1)}, u32[]{:S(2)}, u32[]{:S(2)}) collective-permute-start(s16[2,208,128]{2,1,0:T(8,128)(2,1)S(1)} %get-tuple-element.68), channel_id=1, source_target_pairs={{0,16},{8,24},{16,0},{24,8},{1,17},{9,25},{17,1},{25,9},{2,18},{10... | collective-permute-start | bytes 319496 | tf_op jit(solution)/shard_map/ppermute | solution.py:298
  128.3 5.6 %collective-permute-start.27 = (s16[2,208,128]{2,1,0:T(8,128)(2,1)S(1)}, s16[2,208,128]{2,1,0:T(8,128)(2,1)S(1)}, u32[]{:S(2)}, u32[]{:S(2)}) collective-permute-start(s16[2,208,128]{2,1,0:T(8,128)(2,1)S(1)} %get-tuple-element.69), channel_id=1, source_target_pairs={{0,24},{8,0},{16,8},{24,16},{1,25},{9,1},{17,9},{25,17},{2,26},{10... | collective-permute-start | bytes 319496 | tf_op jit(solution)/shard_map/ppermute | solution.py:298
  134.1 5.7 %collective-permute-start.28 = (s16[208,128]{1,0:T(8,128)(2,1)S(1)}, s16[208,128]{1,0:T(8,128)(2,1)S(1)}, u32[]{:S(2)}, u32[]{:S(2)}) collective-permute-start(s16[208,128]{1,0:T(8,128)(2,1)S(1)} %get-tuple-element.71), channel_id=1, source_target_pairs={{0,32},{32,0},{1,33},{33,1},{2,34},{34,2},{3,35},{35,3},{4,36},{36... | collective-permute-start | bytes 159752 | tf_op jit(solution)/shard_map/ppermute | solution.py:302
  (5 other events, 5.1 us)

commit v4 on v2

--- a/solution.py
+++ b/solution.py
@@ -113,12 +113,16 @@
             at += n
 
 
-def stack_kernel(both, b1, b2, b3, keys, out, held):
+def copy_kernel(keys, after, out):
+    del after
+    out[...] = keys[...]
+
+
+def stack_kernel(both, b1, b2, b3, out):
     zh = lax.axis_index("zh")
     for k, ref in enumerate((both, b1, b2, b3)):
         for xh in range(2):
             out[pl.ds(4 * xh + lax.rem(zh + 4 - k, 4), 1)] = ref[xh : xh + 1]
-    held[...] = keys[...]
 
 
 def hold_kernel(x, z, after, z_top, x_low):
@@ -204,7 +208,7 @@
 def weights_kernel(scale, tile, *refs):
     rparts, cparts = refs[:4], refs[4:8]
     pairs, cols, s_ref, k0, k1, im, own, p1, p3, o2a, o2b, mine, sent, rl, cl, w_ref, total = refs[8:]
-    n_im, n_ks = s_ref.shape
+    n_ks = s_ref.shape[1]
     keys = (k0, k1)
     half, part = n_ks // 2, n_ks // 4
     width = own.shape[1]
@@ -216,37 +220,53 @@
     lse_row = rstat[0:1]
     rl[...] = turn_left(lse_row - rstat[1:2], lax.axis_index("zh") * rows)[:, :rows]
 
-    def weigh(a):
-        rows = slice(a, a + tile)
-        s = s_ref[rows, :]
-        two = jnp.where(to_rows(pairs[:, rows]) == cols[...], F32(2), F32(0))
-        w = jnp.exp(s - to_rows(lse_row[:, rows])) + jnp.exp(s - lse_col) - two
-        w_ref[rows, :] = w.astype(BF16)
-
-    def term(a):
-        rows = slice(a, a + tile)
+    lse_rows, targets = to_rows(lse_row), to_rows(pairs[...])
+
+    def weigh(a, n):
+        x = s_ref[a : a + n, :]
+        two = jnp.where(targets[a : a + n] == cols[...], F32(2), F32(0))
+        w = jnp.exp(x - lse_rows[a : a + n]) + jnp.exp(x - lse_col) - two
+        w_ref[a : a + n, :] = w.astype(BF16)
+
+    def term(a, f):
+        lanes = slice(f * width, (f + 1) * width)
         x = sum(
-            jnp.dot(w_ref[rows, k * half : (k + 1) * half], keys[k][...], preferred_element_type=F32) for k in range(2)
+            jnp.dot(
+                w_ref[a : a + tile, k * half : (k + 1) * half], keys[k][:, lanes], preferred_element_type=F32
+            )
+            for k in range(2)
         )
-        total[rows, :] = x * scale
-
-    tiles = range(0, n_im, tile)
-    weigh(0)
-    for a in tiles:
-        if a + tile < n_im:
-            weigh(a + tile)
-        term(a)
-    for k, out in ((2, None), (1, p1), (3, p3), (0, own)):
-        lanes = pl.ds(pl.multiple_of(lax.rem(lax.axis_index("y") + k, 4) * width, 128), width)
-        if k == 2:
-            encode(total[: n_im // 2, lanes], o2a)
-            encode(total[n_im // 2 :, lanes], o2b)
+        total[a : a + tile, lanes] = x * scale
+
+    def quarter(k):
+        return pl.ds(pl.multiple_of(lax.rem(lax.axis_index("y") + k, 4) * width, 128), width)
+
+    def key_part(a):
+        return lax.dot_general(w_ref[:, a : a + tile], im[...], FIRST, preferred_element_type=F32) * scale
+
+    def send(x, first):
+        for p in range(tile // rows):
+            encode(x[p * rows : (p + 1) * rows, :], sent.at[first + p])
+
+    weigh(0, tile)
+    for f in range(4):
+        term(0, f)
+        weigh(tile + f * (tile // 4), tile // 4)
+    for f in range(4):
+        term(tile, f)
+        if f == 0:
+            encode(total[:tile, quarter(2)], o2a)
         else:
-            out[...] = total[:, lanes]
-    other = lax.dot_general(w_ref[:, half:], im[...], FIRST, preferred_element_type=F32) * scale
-    for p in range(4):
-        encode(other[p * rows : (p + 1) * rows, :], sent.at[p])
-    mine[...] = lax.dot_general(w_ref[:, :half], im[...], FIRST, preferred_element_type=F32) * scale
+            ((own, 0), (p1, 1), (p3, 3))[f - 1][0][:tile, :] = total[:tile, quarter((0, 1, 3)[f - 1])]
+    first = key_part(half)
+    encode(total[tile:, quarter(2)], o2b)
+    second = key_part(half + tile)
+    send(first, 0)
+    mine[:tile, :] = key_part(0)
+    send(second, tile // rows)
+    mine[tile:, :] = key_part(tile)
+    for out, k in ((own, 0), (p1, 1), (p3, 3)):
+        out[tile:, :] = total[tile:, quarter(k)]
 
 
 def relay_kernel(p1, p3, got_a, got_b, o1, o3):
@@ -272,24 +292,33 @@
     image_out[...] = own[...] + decode(twin[...])
 
 
-def image_sum_kernel(after_x, after_z, after_both, own, got1, got3, keep, to1, to2, to3, total):
-    del after_x, after_z, after_both
+def image_sum_kernel(own, got1, got3, keep, to_a, to_b, total):
     zh, xh = lax.axis_index("zh"), lax.axis_index("xh")
     rows, width = keep.shape[1:]
     total[...] = own[...] + decode(got1[...]) + decode(got3[...])
-    for k, out in ((2, to2), (1, to1), (3, to3), (0, keep)):
-        row = pl.multiple_of(lax.rem(zh + k, 4) * rows, 16)
-        for o in range(2):
-            x = total[pl.ds(row, rows), pl.ds(pl.multiple_of((xh ^ o) * width, 128), width)]
-            if k:
-                encode(x, out.at[o])
-            else:
-                out[o] = x
-
-
-def image_twin_kernel(keep, got1, got2, got3, own, to_twin):
-    own[...] = keep[0] + decode(got1[0]) + decode(got2[0]) + decode(got3[0])
-    encode(keep[1] + decode(got1[1]) + decode(got2[1]) + decode(got3[1]), to_twin)
+
+    def piece(o, j):
+        row = pl.multiple_of(lax.rem(zh + j, 4) * rows, 16)
+        return total[pl.ds(row, rows), pl.ds(pl.multiple_of((xh ^ o) * width, 128), width)]
+
+    encode(piece(0, 2), to_a)
+    encode(piece(1, 2), to_b)
+    for o in range(2):
+        for at, j in enumerate((0, 1, 3)):
+            keep[3 * o + at] = piece(o, j)
+
+
+def image_relay_kernel(keep, got_a, got_b, up, down):
+    encode(keep[1] + decode(got_a[...]), up.at[0])
+    encode(keep[4], up.at[1])
+    encode(keep[2], down.at[0])
+    encode(keep[5] + decode(got_b[...]), down.at[1])
+
+
+def image_twin_kernel(after_x, after_z, after_both, keep, up, down, own, to_twin):
+    del after_x, after_z, after_both
+    own[...] = keep[0] + decode(up[0]) + decode(down[0])
+    encode(keep[3] + decode(up[1]) + decode(down[1]), to_twin)
 
 
 def shift(x, axis, n, k):
@@ -314,10 +343,11 @@
     pairs, cols, held = call(
         prep_kernel, [shape((1, n_im), F32), shape((1, n_ks), F32), key_block], "prep", 8, in_specs=[vmem] * 2
     )(pair_index, keys)
-    i0, held = call(stack_kernel, [shape((8, rows, width), BF16), key_block], "stack", 8, in_specs=[vmem] * 5)(
-        both, *[shift(both, "zh", 4, k) for k in (1, 2, 3)], held
+    i0 = call(stack_kernel, shape((8, rows, width), BF16), "stack", 8, in_specs=[vmem] * 4)(
+        both, *[shift(both, "zh", 4, k) for k in (1, 2, 3)]
     )
     i1, i3 = shift(i0, "y", 4, 1), shift(i0, "y", 4, 3)
+    held = call(copy_kernel, key_block, "copy", 8, in_specs=[vmem] * 2)(held, i0)
     key_x = flip(held, "xl", 2, 1)
     key_z = flip(held, "zl", 2, 1)
     quarter = shape((rows // 2, d), BF16)
@@ -331,7 +361,7 @@
     )
     ks = [k0, flip(k0, "core", 2, 1)]
 
-    tile = min(384, n_im)
+    tile = n_im // 2
     scores, im, rs, cs = call(
         functools.partial(scores_kernel, scale),
         [shape((n_im, n_ks), F32), shape((n_im, d), BF16), shape((2, n_im), F32), shape((2, n_ks), F32)],
@@ -365,23 +395,21 @@
     )(mine, flip(sent, "core", 2, 1))
     to_both = lax.ppermute(to_both, ("zl", "xl"), [(i, 3 - i) for i in range(4)])
     pieces = [flip(to_x, "xl", 2, 1), flip(to_z, "zl", 2, 1), to_both]
-    coded = shape((2, rows + PAD, width), I16)
-    keep, to1, to2, to3 = call(
+    coded, coded2 = shape((rows + PAD, width), I16), shape((2, rows + PAD, width), I16)
+    keep, to_a, to_b = call(
         image_sum_kernel,
-        [shape((2, rows, width), F32), coded, coded, coded],
+        [shape((6, rows, width), F32), coded, coded],
         "image_sum",
         12,
-        in_specs=[vmem] * 6,
+        in_specs=[vmem] * 3,
         scratch_shapes=[pltpu.VMEM((n_im, 2 * width), F32)],
-    )(*pieces, own, q1, q3)
-    to2, to1, to3 = shift(to2, "zh", 4, 2), shift(to1, "zh", 4, 1), shift(to3, "zh", 4, 3)
-    own, to_twin = call(
-        image_twin_kernel,
-        [shape((rows, width), F32), shape((rows + PAD, width), I16)],
-        "image_twin",
-        8,
-        in_specs=[vmem] * 4,
-    )(keep, to1, to2, to3)
+    )(own, q1, q3)
+    up, down = call(image_relay_kernel, [coded2] * 2, "image_relay", 8, in_specs=[vmem] * 3)(
+        keep, shift(to_a, "zh", 4, 1), shift(to_b, "zh", 4, 3)
+    )
+    own, to_twin = call(image_twin_kernel, [shape((rows, width), F32), coded], "image_twin", 8, in_specs=[vmem] * 6)(
+        *pieces, keep, shift(up, "zh", 4, 1), shift(down, "zh", 4, 3)
+    )
     modality_grad, image_grad = call(
         last_kernel, [shape((rows, d), F32), shape((rows, width), F32)], "last", 8, in_specs=[vmem] * 6
     )(own_key, *pieces, own, flip(to_twin, "xh", 2, 1))

time: 129 us -> 133 us (1.031)
  waiting for transfers between devices: 54.7 us -> 57.4 us
  starting transfers between devices: 53.7 us -> 55.1 us
    ppermute x17 -> x18, waiting for transfers between devices: 31.8 us -> 42.1 us  [shift(): return lax.ppermute(x, axis, [(i, (i + k) % n) for i in range(n)])]
    ppermute x1, waiting for transfers between devices: 5.07 us -> 0.01 us  [on_device(): lax.ppermute(to_both, ('zl', 'xl'), [(i, 3 - i) for i in range(4)])]
    ppermute x11, starting transfers between devices: 8.8 us -> 11.8 us  [flip(): return lax.ppermute(x, axis, [(i, i ^ d) for i in range(n)])]
    ppermute x11, waiting for transfers between devices: 17.8 us -> 15.4 us  [flip(): return lax.ppermute(x, axis, [(i, i ^ d) for i in range(n)])]
    ppermute x1, starting transfers between devices: 2.29 us -> 0.64 us  [on_device(): lax.ppermute(to_both, ('zl', 'xl'), [(i, 3 - i) for i in range(4)])]
    ppermute x17 -> x18, starting transfers between devices: 39.1 us -> 39 us  [shift(): return lax.ppermute(x, axis, [(i, (i + k) % n) for i in range(n)])]
  transfers between devices with their start and end apart: 32 -> 33, of which waited for: 16 -> 15; matrix products, arithmetic and copies ran while one was open for 0% -> 0% of each run, Pallas kernels for 1% -> 2%
where the time goes in v4:
time: 133 us
  waiting for transfers between devices  57.4 us (43%)
  starting transfers between devices  55.1 us (41%)
  Pallas kernels  16.7 us (13%)
  local copies, waits for them, and re-layouts  2.53 us (2%)
    ppermute x18, waiting for transfers between devices, shift(): return lax.ppermute(x, axis, [(i, (i + k) % n) for i in range(n)])  42.1 us
    ppermute x18, starting transfers between devices, shift(): return lax.ppermute(x, axis, [(i, (i + k) % n) for i in range(n)])  39 us
    ppermute x11, waiting for transfers between devices, flip(): return lax.ppermute(x, axis, [(i, i ^ d) for i in range(n)])  15.4 us
    ppermute x11, starting transfers between devices, flip(): return lax.ppermute(x, axis, [(i, i ^ d) for i in range(n)])  11.8 us
    pallas_call x1, Pallas kernels, on_device(): call(functools.partial(weights_kernel, scale, tile), outs, 'weights', 36,...  8.28 us
    pallas_call x1, Pallas kernels, on_device(): call(functools.partial(scores_kernel, scale), [shape((n_im, n_ks), F32),...  4.7 us
    ppermute x3, starting transfers between devices, on_device(): lax.ppermute(cs, ('zl', 'xl'), [(i, i ^ k) for i in range(4)])  3.58 us
  transfers between devices with their start and end apart: 33, of which 15 were waited for; matrix products, arithmetic and copies ran while one was open for 0% of the time, Pallas kernels for 2%

profile of v4, /device:TPU:4, one launch (start us, length us, event | category | flops | bytes accessed | tf_op | source)
XLA Modules:
  0.0 132.5 jit_solution(13248302011032637383)
XLA Ops:
  0.6 2.3 %collective-permute-start = (bf16[192,128]{1,0:T(8,128)(2,1)}, bf16[192,128]{1,0:T(8,128)(2,1)S(1)}, u32[]{:S(2)}, u32[]{:S(2)}) collective-permute-start(bf16[192,128]{1,0:T(8,128)(2,1)} %image.1), channel_id=1, source_target_pairs={{0,32},{32,0},{1,33},{33,1},{2,34},{34,2},{3,35},{35,3},{4,36},{36... | collective-permute-start | bytes 147464 | tf_op jit(solution)/shard_map/ppermute | solution.py:329
  3.0 3.6 %collective-permute-done.twin = bf16[192,128]{1,0:T(8,128)(2,1)S(1)} collective-permute-done((bf16[192,128]{1,0:T(8,128)(2,1)}, bf16[192,128]{1,0:T(8,128)(2,1)S(1)}, u32[]{:S(2)}, u32[]{:S(2)}) %collective-permute-start) | collective-permute-done | bytes 49184 | tf_op jit(solution)/shard_map/ppermute | solution.py:329
  7.3 6.4 %collective-permute-start.3 = (bf16[2,192,128]{2,1,0:T(8,128)(2,1)S(1)}, bf16[2,192,128]{2,1,0:T(8,128)(2,1)S(1)}, u32[]{:S(2)}, u32[]{:S(2)}) collective-permute-start(bf16[2,192,128]{2,1,0:T(8,128)(2,1)S(1)} %pair.1.both), channel_id=1, source_target_pairs={{0,24},{8,0},{16,8},{24,16},{1,25},{9,1},{17,9},{25,17},{2,26},{10... | collective-permute-start | bytes 294920 | tf_op jit(solution)/shard_map/ppermute | solution.py:325
  14.7 2.8 %collective-permute-start.1 = (bf16[2,192,128]{2,1,0:T(8,128)(2,1)S(1)}, bf16[2,192,128]{2,1,0:T(8,128)(2,1)S(1)}, u32[]{:S(2)}, u32[]{:S(2)}) collective-permute-start(bf16[2,192,128]{2,1,0:T(8,128)(2,1)S(1)} %pair.1.both), channel_id=1, source_target_pairs={{0,8},{8,16},{16,24},{24,0},{1,9},{9,17},{17,25},{25,1},{2,10},{10... | collective-permute-start | bytes 294920 | tf_op jit(solution)/shard_map/ppermute | solution.py:325
  17.5 3.4 %collective-permute-done.3.b3 = bf16[2,192,128]{2,1,0:T(8,128)(2,1)S(1)} collective-permute-done((bf16[2,192,128]{2,1,0:T(8,128)(2,1)S(1)}, bf16[2,192,128]{2,1,0:T(8,128)(2,1)S(1)}, u32[]{:S(2)}, u32[]{:S(2)}) %collective-permute-start.3) | collective-permute-done | bytes 98336 | tf_op jit(solution)/shard_map/ppermute | solution.py:325
  21.0 3.3 %collective-permute-done.2.b2 = bf16[2,192,128]{2,1,0:T(8,128)(2,1)S(1)} collective-permute-done((bf16[2,192,128]{2,1,0:T(8,128)(2,1)S(1)}, bf16[2,192,128]{2,1,0:T(8,128)(2,1)S(1)}, u32[]{:S(2)}, u32[]{:S(2)}) %collective-permute-start.2) | collective-permute-done | bytes 98336 | tf_op jit(solution)/shard_map/ppermute | solution.py:325
  24.3 3.1 %collective-permute-start.9 = (bf16[8,192,128]{2,1,0:T(8,128)(2,1)S(1)}, bf16[8,192,128]{2,1,0:T(8,128)(2,1)S(1)}, u32[]{:S(2)}, u32[]{:S(2)}) collective-permute-start(bf16[8,192,128]{2,1,0:T(8,128)(2,1)S(1)} %stack.1.after.refs_2_), channel_id=1, source_target_pairs={{0,192},{64,0},{128,64},{192,128},{1,193},{65,1},{129,65},{193,129... | collective-permute-start | bytes 1179656 | tf_op jit(solution)/shard_map/ppermute | solution.py:325
  32.7 4.7 %collective-permute-done.8.behind.refs_3_ = bf16[8,192,128]{2,1,0:T(8,128)(2,1)S(1)} collective-permute-done((bf16[8,192,128]{2,1,0:T(8,128)(2,1)S(1)}, bf16[8,192,128]{2,1,0:T(8,128)(2,1)S(1)}, u32[]{:S(2)}, u32[]{:S(2)}) %collective-permute-start.8) | collective-permute-done | bytes 393248 | tf_op jit(solution)/shard_map/ppermute | solution.py:325
  37.5 3.2 %collective-permute-start.11 = (bf16[4,192,128]{2,1,0:T(8,128)(2,1)S(1)}, bf16[4,192,128]{2,1,0:T(8,128)(2,1)S(1)}, u32[]{:S(2)}, u32[]{:S(2)}) collective-permute-start(bf16[4,192,128]{2,1,0:T(8,128)(2,1)S(1)} %get-tuple-element.43), channel_id=1, source_target_pairs={{0,192},{64,0},{128,64},{192,128},{1,193},{65,1},{129,65},{193,129... | collective-permute-start | bytes 589832 | tf_op jit(solution)/shard_map/ppermute | solution.py:325
  40.8 1.3 collective-permute-start.6
  42.1 2.0 %collective-permute-start.7 = (bf16[96,1024]{1,0:T(8,128)(2,1)S(1)}, bf16[96,1024]{1,0:T(8,128)(2,1)S(1)}, u32[]{:S(2)}, u32[]{:S(2)}) collective-permute-start(bf16[96,1024]{1,0:T(8,128)(2,1)S(1)} %get-tuple-element.41), channel_id=1, source_target_pairs={{0,4},{4,0},{1,5},{5,1},{2,6},{6,2},{3,7},{7,3},{8,12},{12,8},{9,1... | collective-permute-start | bytes 589832 | tf_op jit(solution)/shard_map/ppermute | solution.py:329
  44.4 2.1 %collective-permute-done.6.d_top = bf16[96,1024]{1,0:T(8,128)(2,1)S(1)} collective-permute-done((bf16[96,1024]{1,0:T(8,128)(2,1)S(1)}, bf16[96,1024]{1,0:T(8,128)(2,1)S(1)}, u32[]{:S(2)}, u32[]{:S(2)}) %collective-permute-start.6) | collective-permute-done | bytes 196640 | tf_op jit(solution)/shard_map/ppermute | solution.py:329
  48.2 3.4 %collective-permute-done.12.refs_1_.refs_12_ = bf16[768,1024]{1,0:T(8,128)(2,1)S(1)} collective-permute-done((bf16[768,1024]{1,0:T(8,128)(2,1)S(1)}, bf16[768,1024]{1,0:T(8,128)(2,1)S(1)}, u32[]{:S(2)}, u32[]{:S(2)}) %collective-permute-start.12) | collective-permute-done | bytes 1572896 | tf_op jit(solution)/shard_map/ppermute | solution.py:329
  51.6 4.7 %scores.1 = (f32[768,1536]{1,0:T(8,128)S(1)}, bf16[768,1024]{1,0:T(8,128)(2,1)S(1)}, f32[2,768]{1,0:T(2,128)S(1)}, f32[2,1536]{1,0:T(2,128)S(1)}) custom-call(bf16[768,1024]{1,0:T(8,128)(2,1)S(1)} %join.1.refs_0_.refs_11_, bf16[768,1024]{1,0:T(8,128)(2,1)S(1)} %collective-permute-done.12.refs_1_.refs_12_, bf16[8,192,128]{2,1,0:T(8,128)(2,1)S(1)} %stack.1.after.refs_2_, ...), custom_call_target="tpu_custom_call" | custom-call | flops 1000 | bytes 1000 | tf_op jit(solution)/shard_map/scores/pallas_call | solution.py:365
  56.5 3.8 %collective-permute-start.15 = (f32[2,768]{1,0:T(2,128)S(1)}, f32[2,768]{1,0:T(2,128)S(1)}, u32[]{:S(2)}, u32[]{:S(2)}) collective-permute-start(f32[2,768]{1,0:T(2,128)S(1)} %get-tuple-element.46.refs_0_), channel_id=1, source_target_pairs={{0,24},{8,0},{16,8},{24,16},{1,25},{9,1},{17,9},{25,17},{2,26},{10... | collective-permute-start | bytes 18440 | tf_op jit(solution)/shard_map/ppermute | solution.py:325
  60.4 2.4 %collective-permute-start.19 = (f32[2,1536]{1,0:T(2,128)S(1)}, f32[2,1536]{1,0:T(2,128)S(1)}, u32[]{:S(2)}, u32[]{:S(2)}) collective-permute-start(f32[2,1536]{1,0:T(2,128)S(1)} %meet.1.refs_4_), channel_id=1, source_target_pairs={{0,6},{2,4},{4,2},{6,0},{1,7},{3,5},{5,3},{7,1},{8,14},{10,12},{12... | collective-permute-start | bytes 36872 | tf_op jit(solution)/shard_map/ppermute | solution.py:374
  63.9 1.7 %collective-permute-start.14 = (f32[2,768]{1,0:T(2,128)S(1)}, f32[2,768]{1,0:T(2,128)S(1)}, u32[]{:S(2)}, u32[]{:S(2)}) collective-permute-start(f32[2,768]{1,0:T(2,128)S(1)} %get-tuple-element.46.refs_0_), channel_id=1, source_target_pairs={{0,16},{8,24},{16,0},{24,8},{1,17},{9,25},{17,1},{25,9},{2,18},{10... | collective-permute-start | bytes 18440 | tf_op jit(solution)/shard_map/ppermute | solution.py:325
  65.7 1.9 %collective-permute-start.13 = (f32[2,768]{1,0:T(2,128)S(1)}, f32[2,768]{1,0:T(2,128)S(1)}, u32[]{:S(2)}, u32[]{:S(2)}) collective-permute-start(f32[2,768]{1,0:T(2,128)S(1)} %get-tuple-element.46.refs_0_), channel_id=1, source_target_pairs={{0,8},{8,16},{16,24},{24,0},{1,9},{9,17},{17,25},{25,1},{2,10},{10... | collective-permute-start | bytes 18440 | tf_op jit(solution)/shard_map/ppermute | solution.py:325
  67.6 3.9 %collective-permute-done.14.refs_2_ = f32[2,768]{1,0:T(2,128)S(1)} collective-permute-done((f32[2,768]{1,0:T(2,128)S(1)}, f32[2,768]{1,0:T(2,128)S(1)}, u32[]{:S(2)}, u32[]{:S(2)}) %collective-permute-start.14) | collective-permute-done | bytes 6176 | tf_op jit(solution)/shard_map/ppermute | solution.py:325
  71.5 8.3 %weights.1 = (f32[768,256]{1,0:T(8,128)S(1)}, f32[768,256]{1,0:T(8,128)S(1)}, f32[768,256]{1,0:T(8,128)S(1)}, s16[400,256]{1,0:T(8,128)(2,1)S(1)}, s16[400,256]{...) custom-call(f32[2,768]{1,0:T(2,128)S(1)} %get-tuple-element.46.refs_, ...), custom_call_target="tpu_custom_call" | custom-call | flops 1000 | bytes 1000 | tf_op jit(solution)/shard_map/weights/pallas_call | solution.py:377
  79.8 3.2 %collective-permute-start.25 = (s16[400,256]{1,0:T(8,128)(2,1)S(1)}, s16[400,256]{1,0:T(8,128)(2,1)S(1)}, u32[]{:S(2)}, u32[]{:S(2)}) collective-permute-start(s16[400,256]{1,0:T(8,128)(2,1)S(1)} %get-tuple-element.60), channel_id=1, source_target_pairs={{0,192},{64,0},{128,64},{192,128},{1,193},{65,1},{129,65},{193,129... | collective-permute-start | bytes 614408 | tf_op jit(solution)/shard_map/ppermute | solution.py:325
  83.0 5.5 %collective-permute-done.24.got_a = s16[400,256]{1,0:T(8,128)(2,1)S(1)} collective-permute-done((s16[400,256]{1,0:T(8,128)(2,1)S(1)}, s16[400,256]{1,0:T(8,128)(2,1)S(1)}, u32[]{:S(2)}, u32[]{:S(2)}) %collective-permute-start.24) | collective-permute-done | bytes 204832 | tf_op jit(solution)/shard_map/ppermute | solution.py:325
  89.3 2.8 %collective-permute-start.27 = (s16[784,256]{1,0:T(8,128)(2,1)S(1)}, s16[784,256]{1,0:T(8,128)(2,1)S(1)}, u32[]{:S(2)}, u32[]{:S(2)}) collective-permute-start(s16[784,256]{1,0:T(8,128)(2,1)S(1)} %get-tuple-element.62), channel_id=1, source_target_pairs={{0,192},{64,0},{128,64},{192,128},{1,193},{65,1},{129,65},{193,129... | collective-permute-start | bytes 1204232 | tf_op jit(solution)/shard_map/ppermute | solution.py:325
  94.0 2.0 %collective-permute-start.22 = (s16[208,1024]{1,0:T(8,128)(2,1)S(1)}, s16[208,1024]{1,0:T(8,128)(2,1)S(1)}, u32[]{:S(2)}, u32[]{:S(2)}) collective-permute-start(s16[208,1024]{1,0:T(8,128)(2,1)S(1)} %get-tuple-element.54), channel_id=1, source_target_pairs={{0,4},{4,0},{1,5},{5,1},{2,6},{6,2},{3,7},{7,3},{8,12},{12,8},{9,1... | collective-permute-start | bytes 1277960 | tf_op jit(solution)/shard_map/ppermute | solution.py:329
  96.7 4.4 %collective-permute-done.26.got1 = s16[784,256]{1,0:T(8,128)(2,1)S(1)} collective-permute-done((s16[784,256]{1,0:T(8,128)(2,1)S(1)}, s16[784,256]{1,0:T(8,128)(2,1)S(1)}, u32[]{:S(2)}, u32[]{:S(2)}) %collective-permute-start.26) | collective-permute-done | bytes 401440 | tf_op jit(solution)/shard_map/ppermute | solution.py:325
  102.3 3.5 %collective-permute-start.29 = (s16[208,128]{1,0:T(8,128)(2,1)S(1)}, s16[208,128]{1,0:T(8,128)(2,1)S(1)}, u32[]{:S(2)}, u32[]{:S(2)}) collective-permute-start(s16[208,128]{1,0:T(8,128)(2,1)S(1)} %get-tuple-element.65), channel_id=1, source_target_pairs={{0,24},{8,0},{16,8},{24,16},{1,25},{9,1},{17,9},{25,17},{2,26},{10... | collective-permute-start | bytes 159752 | tf_op jit(solution)/shard_map/ppermute | solution.py:325
  105.8 11.5 %collective-permute-done.28.got_a = s16[208,128]{1,0:T(8,128)(2,1)S(1)} collective-permute-done((s16[208,128]{1,0:T(8,128)(2,1)S(1)}, s16[208,128]{1,0:T(8,128)(2,1)S(1)}, u32[]{:S(2)}, u32[]{:S(2)}) %collective-permute-start.28) | collective-permute-done | bytes 53280 | tf_op jit(solution)/shard_map/ppermute | solution.py:325
  117.4 1.7 %collective-permute-start.30 = (s16[2,208,128]{2,1,0:T(8,128)(2,1)S(1)}, s16[2,208,128]{2,1,0:T(8,128)(2,1)S(1)}, u32[]{:S(2)}, u32[]{:S(2)}) collective-permute-start(s16[2,208,128]{2,1,0:T(8,128)(2,1)S(1)} %get-tuple-element.66), channel_id=1, source_target_pairs={{0,8},{8,16},{16,24},{24,0},{1,9},{9,17},{17,25},{25,1},{2,10},{10... | collective-permute-start | bytes 319496 | tf_op jit(solution)/shard_map/ppermute | solution.py:325
  119.2 2.5 %collective-permute-start.31 = (s16[2,208,128]{2,1,0:T(8,128)(2,1)S(1)}, s16[2,208,128]{2,1,0:T(8,128)(2,1)S(1)}, u32[]{:S(2)}, u32[]{:S(2)}) collective-permute-start(s16[2,208,128]{2,1,0:T(8,128)(2,1)S(1)} %get-tuple-element.67), channel_id=1, source_target_pairs={{0,24},{8,0},{16,8},{24,16},{1,25},{9,1},{17,9},{25,17},{2,26},{10... | collective-permute-start | bytes 319496 | tf_op jit(solution)/shard_map/ppermute | solution.py:325
  121.7 3.8 %collective-permute-done.30.up = s16[2,208,128]{2,1,0:T(8,128)(2,1)S(1)} collective-permute-done((s16[2,208,128]{2,1,0:T(8,128)(2,1)S(1)}, s16[2,208,128]{2,1,0:T(8,128)(2,1)S(1)}, u32[]{:S(2)}, u32[]{:S(2)}) %collective-permute-start.30) | collective-permute-done | bytes 106528 | tf_op jit(solution)/shard_map/ppermute | solution.py:325
  126.3 5.0 %collective-permute-done.32.twin = s16[208,128]{1,0:T(8,128)(2,1)S(1)} collective-permute-done((s16[208,128]{1,0:T(8,128)(2,1)S(1)}, s16[208,128]{1,0:T(8,128)(2,1)S(1)}, u32[]{:S(2)}, u32[]{:S(2)}) %collective-permute-start.32) | collective-permute-done | bytes 53280 | tf_op jit(solution)/shard_map/ppermute | solution.py:329
  131.3 1.2 last.1
  (56 shorter events, 16.2 us)
Async XLA Ops:
  0.6 5.9 %collective-permute-start = (bf16[192,128]{1,0:T(8,128)(2,1)}, bf16[192,128]{1,0:T(8,128)(2,1)S(1)}, u32[]{:S(2)}, u32[]{:S(2)}) collective-permute-start(bf16[192,128]{1,0:T(8,128)(2,1)} %image.1), channel_id=1, source_target_pairs={{0,32},{32,0},{1,33},{33,1},{2,34},{34,2},{3,35},{35,3},{4,36},{36... | collective-permute-start | bytes 147464 | tf_op jit(solution)/shard_map/ppermute | solution.py:329
  7.3 13.6 %collective-permute-start.3 = (bf16[2,192,128]{2,1,0:T(8,128)(2,1)S(1)}, bf16[2,192,128]{2,1,0:T(8,128)(2,1)S(1)}, u32[]{:S(2)}, u32[]{:S(2)}) collective-permute-start(bf16[2,192,128]{2,1,0:T(8,128)(2,1)S(1)} %pair.1.both), channel_id=1, source_target_pairs={{0,24},{8,0},{16,8},{24,16},{1,25},{9,1},{17,9},{25,17},{2,26},{10... | collective-permute-start | bytes 294920 | tf_op jit(solution)/shard_map/ppermute | solution.py:325
  13.7 10.5 %collective-permute-start.2 = (bf16[2,192,128]{2,1,0:T(8,128)(2,1)S(1)}, bf16[2,192,128]{2,1,0:T(8,128)(2,1)S(1)}, u32[]{:S(2)}, u32[]{:S(2)}) collective-permute-start(bf16[2,192,128]{2,1,0:T(8,128)(2,1)S(1)} %pair.1.both), channel_id=1, source_target_pairs={{0,16},{8,24},{16,0},{24,8},{1,17},{9,25},{17,1},{25,9},{2,18},{10... | collective-permute-start | bytes 294920 | tf_op jit(solution)/shard_map/ppermute | solution.py:325
  14.7 9.5 %collective-permute-start.1 = (bf16[2,192,128]{2,1,0:T(8,128)(2,1)S(1)}, bf16[2,192,128]{2,1,0:T(8,128)(2,1)S(1)}, u32[]{:S(2)}, u32[]{:S(2)}) collective-permute-start(bf16[2,192,128]{2,1,0:T(8,128)(2,1)S(1)} %pair.1.both), channel_id=1, source_target_pairs={{0,8},{8,16},{16,24},{24,0},{1,9},{9,17},{17,25},{25,1},{2,10},{10... | collective-permute-start | bytes 294920 | tf_op jit(solution)/shard_map/ppermute | solution.py:325
  24.3 8.4 %collective-permute-start.9 = (bf16[8,192,128]{2,1,0:T(8,128)(2,1)S(1)}, bf16[8,192,128]{2,1,0:T(8,128)(2,1)S(1)}, u32[]{:S(2)}, u32[]{:S(2)}) collective-permute-start(bf16[8,192,128]{2,1,0:T(8,128)(2,1)S(1)} %stack.1.after.refs_2_), channel_id=1, source_target_pairs={{0,192},{64,0},{128,64},{192,128},{1,193},{65,1},{129,65},{193,129... | collective-permute-start | bytes 1179656 | tf_op jit(solution)/shard_map/ppermute | solution.py:325
  27.4 10.0 %collective-permute-start.8 = (bf16[8,192,128]{2,1,0:T(8,128)(2,1)S(1)}, bf16[8,192,128]{2,1,0:T(8,128)(2,1)S(1)}, u32[]{:S(2)}, u32[]{:S(2)}) collective-permute-start(bf16[8,192,128]{2,1,0:T(8,128)(2,1)S(1)} %stack.1.after.refs_2_), channel_id=1, source_target_pairs={{0,64},{64,128},{128,192},{192,0},{1,65},{65,129},{129,193},{193,1... | collective-permute-start | bytes 1179656 | tf_op jit(solution)/shard_map/ppermute | solution.py:325
  29.4 11.4 %collective-permute-start.5 = (bf16[192,1024]{1,0:T(8,128)(2,1)S(1)}, bf16[192,1024]{1,0:T(8,128)(2,1)S(1)}, u32[]{:S(2)}, u32[]{:S(2)}) collective-permute-start(bf16[192,1024]{1,0:T(8,128)(2,1)S(1)} %copy.8.own), channel_id=1, source_target_pairs={{0,4},{4,0},{1,5},{5,1},{2,6},{6,2},{3,7},{7,3},{8,12},{12,8},{9,1... | collective-permute-start | bytes 1179656 | tf_op jit(solution)/shard_map/ppermute | solution.py:329
  30.3 10.5 %collective-permute-start.4 = (bf16[192,1024]{1,0:T(8,128)(2,1)S(1)}, bf16[192,1024]{1,0:T(8,128)(2,1)S(1)}, u32[]{:S(2)}, u32[]{:S(2)}) collective-permute-start(bf16[192,1024]{1,0:T(8,128)(2,1)S(1)} %copy.8.own), channel_id=1, source_target_pairs={{0,2},{2,0},{1,3},{3,1},{4,6},{6,4},{5,7},{7,5},{8,10},{10,8},{9,1... | collective-permute-start | bytes 1179656 | tf_op jit(solution)/shard_map/ppermute | solution.py:329
  37.4 7.0 %collective-permute-start.10 = (bf16[4,192,128]{2,1,0:T(8,128)(2,1)S(1)}, bf16[4,192,128]{2,1,0:T(8,128)(2,1)S(1)}, u32[]{:S(2)}, u32[]{:S(2)}) collective-permute-start(bf16[4,192,128]{2,1,0:T(8,128)(2,1)S(1)} %get-tuple-element.42), channel_id=1, source_target_pairs={{0,64},{64,128},{128,192},{192,0},{1,65},{65,129},{129,193},{193,1... | collective-permute-start | bytes 589832 | tf_op jit(solution)/shard_map/ppermute | solution.py:325
  37.5 6.9 %collective-permute-start.11 = (bf16[4,192,128]{2,1,0:T(8,128)(2,1)S(1)}, bf16[4,192,128]{2,1,0:T(8,128)(2,1)S(1)}, u32[]{:S(2)}, u32[]{:S(2)}) collective-permute-start(bf16[4,192,128]{2,1,0:T(8,128)(2,1)S(1)} %get-tuple-element.43), channel_id=1, source_target_pairs={{0,192},{64,0},{128,64},{192,128},{1,193},{65,1},{129,65},{193,129... | collective-permute-start | bytes 589832 | tf_op jit(solution)/shard_map/ppermute | solution.py:325
  40.8 5.8 %collective-permute-start.6 = (bf16[96,1024]{1,0:T(8,128)(2,1)S(1)}, bf16[96,1024]{1,0:T(8,128)(2,1)S(1)}, u32[]{:S(2)}, u32[]{:S(2)}) collective-permute-start(bf16[96,1024]{1,0:T(8,128)(2,1)S(1)} %get-tuple-element.40), channel_id=1, source_target_pairs={{0,2},{2,0},{1,3},{3,1},{4,6},{6,4},{5,7},{7,5},{8,10},{10,8},{9,1... | collective-permute-start | bytes 589832 | tf_op jit(solution)/shard_map/ppermute | solution.py:329
  42.1 5.7 %collective-permute-start.7 = (bf16[96,1024]{1,0:T(8,128)(2,1)S(1)}, bf16[96,1024]{1,0:T(8,128)(2,1)S(1)}, u32[]{:S(2)}, u32[]{:S(2)}) collective-permute-start(bf16[96,1024]{1,0:T(8,128)(2,1)S(1)} %get-tuple-element.41), channel_id=1, source_target_pairs={{0,4},{4,0},{1,5},{5,1},{2,6},{6,2},{3,7},{7,3},{8,12},{12,8},{9,1... | collective-permute-start | bytes 589832 | tf_op jit(solution)/shard_map/ppermute | solution.py:329
  56.3 4.1 %collective-permute-start.16 = (f32[2,1536]{1,0:T(2,128)S(1)}, f32[2,1536]{1,0:T(2,128)S(1)}, u32[]{:S(2)}, u32[]{:S(2)}) collective-permute-start(f32[2,1536]{1,0:T(2,128)S(1)} %get-tuple-element.47.c), channel_id=1, source_target_pairs={{0,1},{1,0},{2,3},{3,2},{4,5},{5,4},{6,7},{7,6},{8,9},{9,8},{10,11... | collective-permute-start | bytes 36872 | tf_op jit(solution)/shard_map/ppermute | solution.py:329
  56.5 9.2 %collective-permute-start.15 = (f32[2,768]{1,0:T(2,128)S(1)}, f32[2,768]{1,0:T(2,128)S(1)}, u32[]{:S(2)}, u32[]{:S(2)}) collective-permute-start(f32[2,768]{1,0:T(2,128)S(1)} %get-tuple-element.46.refs_0_), channel_id=1, source_target_pairs={{0,24},{8,0},{16,8},{24,16},{1,25},{9,1},{17,9},{25,17},{2,26},{10... | collective-permute-start | bytes 18440 | tf_op jit(solution)/shard_map/ppermute | solution.py:325
  60.4 11.1 %collective-permute-start.19 = (f32[2,1536]{1,0:T(2,128)S(1)}, f32[2,1536]{1,0:T(2,128)S(1)}, u32[]{:S(2)}, u32[]{:S(2)}) collective-permute-start(f32[2,1536]{1,0:T(2,128)S(1)} %meet.1.refs_4_), channel_id=1, source_target_pairs={{0,6},{2,4},{4,2},{6,0},{1,7},{3,5},{5,3},{7,1},{8,14},{10,12},{12... | collective-permute-start | bytes 36872 | tf_op jit(solution)/shard_map/ppermute | solution.py:374
  62.7 8.7 %collective-permute-start.18 = (f32[2,1536]{1,0:T(2,128)S(1)}, f32[2,1536]{1,0:T(2,128)S(1)}, u32[]{:S(2)}, u32[]{:S(2)}) collective-permute-start(f32[2,1536]{1,0:T(2,128)S(1)} %meet.1.refs_4_), channel_id=1, source_target_pairs={{0,4},{2,6},{4,0},{6,2},{1,5},{3,7},{5,1},{7,3},{8,12},{10,14},{12... | collective-permute-start | bytes 36872 | tf_op jit(solution)/shard_map/ppermute | solution.py:374
  62.8 8.7 %collective-permute-start.17 = (f32[2,1536]{1,0:T(2,128)S(1)}, f32[2,1536]{1,0:T(2,128)S(1)}, u32[]{:S(2)}, u32[]{:S(2)}) collective-permute-start(f32[2,1536]{1,0:T(2,128)S(1)} %meet.1.refs_4_), channel_id=1, source_target_pairs={{0,2},{2,0},{4,6},{6,4},{1,3},{3,1},{5,7},{7,5},{8,10},{10,8},{12,... | collective-permute-start | bytes 36872 | tf_op jit(solution)/shard_map/ppermute | solution.py:374
  63.9 7.5 %collective-permute-start.14 = (f32[2,768]{1,0:T(2,128)S(1)}, f32[2,768]{1,0:T(2,128)S(1)}, u32[]{:S(2)}, u32[]{:S(2)}) collective-permute-start(f32[2,768]{1,0:T(2,128)S(1)} %get-tuple-element.46.refs_0_), channel_id=1, source_target_pairs={{0,16},{8,24},{16,0},{24,8},{1,17},{9,25},{17,1},{25,9},{2,18},{10... | collective-permute-start | bytes 18440 | tf_op jit(solution)/shard_map/ppermute | solution.py:325
  65.7 5.8 %collective-permute-start.13 = (f32[2,768]{1,0:T(2,128)S(1)}, f32[2,768]{1,0:T(2,128)S(1)}, u32[]{:S(2)}, u32[]{:S(2)}) collective-permute-start(f32[2,768]{1,0:T(2,128)S(1)} %get-tuple-element.46.refs_0_), channel_id=1, source_target_pairs={{0,8},{8,16},{16,24},{24,0},{1,9},{9,17},{17,25},{25,1},{2,10},{10... | collective-permute-start | bytes 18440 | tf_op jit(solution)/shard_map/ppermute | solution.py:325
  79.8 12.4 %collective-permute-start.20 = (s16[4,208,1024]{2,1,0:T(8,128)(2,1)S(1)}, s16[4,208,1024]{2,1,0:T(8,128)(2,1)S(1)}, u32[]{:S(2)}, u32[]{:S(2)}) collective-permute-start(s16[4,208,1024]{2,1,0:T(8,128)(2,1)S(1)} %get-tuple-element.51), channel_id=1, source_target_pairs={{0,1},{1,0},{2,3},{3,2},{4,5},{5,4},{6,7},{7,6},{8,9},{9,8},{10,11... | collective-permute-start | bytes 5111816 | tf_op jit(solution)/shard_map/ppermute | solution.py:329
  79.8 8.7 %collective-permute-start.24 = (s16[400,256]{1,0:T(8,128)(2,1)S(1)}, s16[400,256]{1,0:T(8,128)(2,1)S(1)}, u32[]{:S(2)}, u32[]{:S(2)}) collective-permute-start(s16[400,256]{1,0:T(8,128)(2,1)S(1)} %get-tuple-element.59), channel_id=1, source_target_pairs={{0,64},{64,128},{128,192},{192,0},{1,65},{65,129},{129,193},{193,1... | collective-permute-start | bytes 614408 | tf_op jit(solution)/shard_map/ppermute | solution.py:325
  79.8 8.7 %collective-permute-start.25 = (s16[400,256]{1,0:T(8,128)(2,1)S(1)}, s16[400,256]{1,0:T(8,128)(2,1)S(1)}, u32[]{:S(2)}, u32[]{:S(2)}) collective-permute-start(s16[400,256]{1,0:T(8,128)(2,1)S(1)} %get-tuple-element.60), channel_id=1, source_target_pairs={{0,192},{64,0},{128,64},{192,128},{1,193},{65,1},{129,65},{193,129... | collective-permute-start | bytes 614408 | tf_op jit(solution)/shard_map/ppermute | solution.py:325
  88.9 12.2 %collective-permute-start.26 = (s16[784,256]{1,0:T(8,128)(2,1)S(1)}, s16[784,256]{1,0:T(8,128)(2,1)S(1)}, u32[]{:S(2)}, u32[]{:S(2)}) collective-permute-start(s16[784,256]{1,0:T(8,128)(2,1)S(1)} %get-tuple-element.61), channel_id=1, source_target_pairs={{0,64},{64,128},{128,192},{192,0},{1,65},{65,129},{129,193},{193,1... | collective-permute-start | bytes 1204232 | tf_op jit(solution)/shard_map/ppermute | solution.py:325
  89.3 11.7 %collective-permute-start.27 = (s16[784,256]{1,0:T(8,128)(2,1)S(1)}, s16[784,256]{1,0:T(8,128)(2,1)S(1)}, u32[]{:S(2)}, u32[]{:S(2)}) collective-permute-start(s16[784,256]{1,0:T(8,128)(2,1)S(1)} %get-tuple-element.62), channel_id=1, source_target_pairs={{0,192},{64,0},{128,64},{192,128},{1,193},{65,1},{129,65},{193,129... | collective-permute-start | bytes 1204232 | tf_op jit(solution)/shard_map/ppermute | solution.py:325
  93.1 32.3 %collective-permute-start.21 = (s16[208,1024]{1,0:T(8,128)(2,1)S(1)}, s16[208,1024]{1,0:T(8,128)(2,1)S(1)}, u32[]{:S(2)}, u32[]{:S(2)}) collective-permute-start(s16[208,1024]{1,0:T(8,128)(2,1)S(1)} %get-tuple-element.53), channel_id=1, source_target_pairs={{0,2},{2,0},{1,3},{3,1},{4,6},{6,4},{5,7},{7,5},{8,10},{10,8},{9,1... | collective-permute-start | bytes 1277960 | tf_op jit(solution)/shard_map/ppermute | solution.py:329
  94.0 31.4 %collective-permute-start.22 = (s16[208,1024]{1,0:T(8,128)(2,1)S(1)}, s16[208,1024]{1,0:T(8,128)(2,1)S(1)}, u32[]{:S(2)}, u32[]{:S(2)}) collective-permute-start(s16[208,1024]{1,0:T(8,128)(2,1)S(1)} %get-tuple-element.54), channel_id=1, source_target_pairs={{0,4},{4,0},{1,5},{5,1},{2,6},{6,2},{3,7},{7,3},{8,12},{12,8},{9,1... | collective-permute-start | bytes 1277960 | tf_op jit(solution)/shard_map/ppermute | solution.py:329
  96.1 29.4 %collective-permute-start.23 = (s16[208,1024]{1,0:T(8,128)(2,1)S(1)}, s16[208,1024]{1,0:T(8,128)(2,1)S(1)}, u32[]{:S(2)}, u32[]{:S(2)}) collective-permute-start(s16[208,1024]{1,0:T(8,128)(2,1)S(1)} %get-tuple-element.55), channel_id=1, source_target_pairs={{0,6},{2,4},{4,2},{6,0},{1,7},{3,5},{5,3},{7,1},{8,14},{10,12},{12... | collective-permute-start | bytes 1277960 | tf_op jit(solution)/shard_map/ppermute | solution.py:396
  101.6 15.7 %collective-permute-start.28 = (s16[208,128]{1,0:T(8,128)(2,1)S(1)}, s16[208,128]{1,0:T(8,128)(2,1)S(1)}, u32[]{:S(2)}, u32[]{:S(2)}) collective-permute-start(s16[208,128]{1,0:T(8,128)(2,1)S(1)} %get-tuple-element.64), channel_id=1, source_target_pairs={{0,8},{8,16},{16,24},{24,0},{1,9},{9,17},{17,25},{25,1},{2,10},{10... | collective-permute-start | bytes 159752 | tf_op jit(solution)/shard_map/ppermute | solution.py:325
  102.3 15.1 %collective-permute-start.29 = (s16[208,128]{1,0:T(8,128)(2,1)S(1)}, s16[208,128]{1,0:T(8,128)(2,1)S(1)}, u32[]{:S(2)}, u32[]{:S(2)}) collective-permute-start(s16[208,128]{1,0:T(8,128)(2,1)S(1)} %get-tuple-element.65), channel_id=1, source_target_pairs={{0,24},{8,0},{16,8},{24,16},{1,25},{9,1},{17,9},{25,17},{2,26},{10... | collective-permute-start | bytes 159752 | tf_op jit(solution)/shard_map/ppermute | solution.py:325
  117.4 8.0 %collective-permute-start.30 = (s16[2,208,128]{2,1,0:T(8,128)(2,1)S(1)}, s16[2,208,128]{2,1,0:T(8,128)(2,1)S(1)}, u32[]{:S(2)}, u32[]{:S(2)}) collective-permute-start(s16[2,208,128]{2,1,0:T(8,128)(2,1)S(1)} %get-tuple-element.66), channel_id=1, source_target_pairs={{0,8},{8,16},{16,24},{24,0},{1,9},{9,17},{17,25},{25,1},{2,10},{10... | collective-permute-start | bytes 319496 | tf_op jit(solution)/shard_map/ppermute | solution.py:325
  119.2 6.3 %collective-permute-start.31 = (s16[2,208,128]{2,1,0:T(8,128)(2,1)S(1)}, s16[2,208,128]{2,1,0:T(8,128)(2,1)S(1)}, u32[]{:S(2)}, u32[]{:S(2)}) collective-permute-start(s16[2,208,128]{2,1,0:T(8,128)(2,1)S(1)} %get-tuple-element.67), channel_id=1, source_target_pairs={{0,24},{8,0},{16,8},{24,16},{1,25},{9,1},{17,9},{25,17},{2,26},{10... | collective-permute-start | bytes 319496 | tf_op jit(solution)/shard_map/ppermute | solution.py:325
  125.6 5.7 %collective-permute-start.32 = (s16[208,128]{1,0:T(8,128)(2,1)S(1)}, s16[208,128]{1,0:T(8,128)(2,1)S(1)}, u32[]{:S(2)}, u32[]{:S(2)}) collective-permute-start(s16[208,128]{1,0:T(8,128)(2,1)S(1)} %get-tuple-element.69), channel_id=1, source_target_pairs={{0,32},{32,0},{1,33},{33,1},{2,34},{34,2},{3,35},{35,3},{4,36},{36... | collective-permute-start | bytes 159752 | tf_op jit(solution)/shard_map/ppermute | solution.py:329
  (4 other events, 6.2 us)

commit v5 on v2

--- a/solution.py
+++ b/solution.py
@@ -113,12 +113,17 @@
             at += n
 
 
-def stack_kernel(both, b1, b2, b3, keys, out, held):
+def copy_kernel(keys, after, out):
+    del after
+    out[...] = keys[...]
+
+
+def stack_kernel(both, b1, b2, b3, after, out):
+    del after
     zh = lax.axis_index("zh")
     for k, ref in enumerate((both, b1, b2, b3)):
         for xh in range(2):
             out[pl.ds(4 * xh + lax.rem(zh + 4 - k, 4), 1)] = ref[xh : xh + 1]
-    held[...] = keys[...]
 
 
 def hold_kernel(x, z, after, z_top, x_low):
@@ -249,7 +254,8 @@
     mine[...] = lax.dot_general(w_ref[:, :half], im[...], FIRST, preferred_element_type=F32) * scale
 
 
-def relay_kernel(p1, p3, got_a, got_b, o1, o3):
+def relay_kernel(after, p1, p3, got_a, got_b, o1, o3):
+    del after
     n = p1.shape[0] // 2
     encode(jnp.concatenate([p1[:n, :] + decode(got_a[...]), p1[n:, :]], axis=0), o1)
     encode(jnp.concatenate([p3[:n, :], p3[n:, :] + decode(got_b[...])], axis=0), o3)
@@ -272,24 +278,34 @@
     image_out[...] = own[...] + decode(twin[...])
 
 
-def image_sum_kernel(after_x, after_z, after_both, own, got1, got3, keep, to1, to2, to3, total):
-    del after_x, after_z, after_both
+def image_sum_kernel(after_x, after_z, own, got1, got3, keep, to_a, to_b, total):
+    del after_x, after_z
     zh, xh = lax.axis_index("zh"), lax.axis_index("xh")
     rows, width = keep.shape[1:]
     total[...] = own[...] + decode(got1[...]) + decode(got3[...])
-    for k, out in ((2, to2), (1, to1), (3, to3), (0, keep)):
-        row = pl.multiple_of(lax.rem(zh + k, 4) * rows, 16)
-        for o in range(2):
-            x = total[pl.ds(row, rows), pl.ds(pl.multiple_of((xh ^ o) * width, 128), width)]
-            if k:
-                encode(x, out.at[o])
-            else:
-                out[o] = x
-
-
-def image_twin_kernel(keep, got1, got2, got3, own, to_twin):
-    own[...] = keep[0] + decode(got1[0]) + decode(got2[0]) + decode(got3[0])
-    encode(keep[1] + decode(got1[1]) + decode(got2[1]) + decode(got3[1]), to_twin)
+
+    def piece(o, j):
+        row = pl.multiple_of(lax.rem(zh + j, 4) * rows, 16)
+        return total[pl.ds(row, rows), pl.ds(pl.multiple_of((xh ^ o) * width, 128), width)]
+
+    encode(piece(0, 2), to_a)
+    encode(piece(1, 2), to_b)
+    for o in range(2):
+        for at, j in enumerate((0, 1, 3)):
+            keep[3 * o + at] = piece(o, j)
+
+
+def image_relay_kernel(keep, got_a, got_b, up, down):
+    encode(keep[1] + decode(got_a[...]), up.at[0])
+    encode(keep[4], up.at[1])
+    encode(keep[2], down.at[0])
+    encode(keep[5] + decode(got_b[...]), down.at[1])
+
+
+def image_twin_kernel(after, keep, up, down, own, to_twin):
+    del after
+    own[...] = keep[0] + decode(up[0]) + decode(down[0])
+    encode(keep[3] + decode(up[1]) + decode(down[1]), to_twin)
 
 
 def shift(x, axis, n, k):
@@ -314,10 +330,11 @@
     pairs, cols, held = call(
         prep_kernel, [shape((1, n_im), F32), shape((1, n_ks), F32), key_block], "prep", 8, in_specs=[vmem] * 2
     )(pair_index, keys)
-    i0, held = call(stack_kernel, [shape((8, rows, width), BF16), key_block], "stack", 8, in_specs=[vmem] * 5)(
-        both, *[shift(both, "zh", 4, k) for k in (1, 2, 3)], held
+    i0 = call(stack_kernel, shape((8, rows, width), BF16), "stack", 8, in_specs=[vmem] * 5)(
+        both, *[shift(both, "zh", 4, k) for k in (1, 2, 3)], pairs
     )
     i1, i3 = shift(i0, "y", 4, 1), shift(i0, "y", 4, 3)
+    held = call(copy_kernel, key_block, "copy", 8, in_specs=[vmem] * 2)(held, i0)
     key_x = flip(held, "xl", 2, 1)
     key_z = flip(held, "zl", 2, 1)
     quarter = shape((rows // 2, d), BF16)
@@ -352,10 +369,6 @@
         in_specs=[vmem] * 14,
         scratch_shapes=[pltpu.VMEM((n_im, n_ks), BF16), pltpu.VMEM((n_im, d), F32)],
     )(*rstats, *cstats, pairs, cols, scores, *ks, im)
-    q1, q3 = call(
-        relay_kernel, [shape((n_im + PAD, 2 * width), I16)] * 2, "relay", 12, in_specs=[vmem] * 4
-    )(p1, p3, shift(q2a, "y", 4, 1), shift(q2b, "y", 4, 3))
-    q1, q3 = shift(q1, "y", 4, 1), shift(q3, "y", 4, 3)
     own_key, to_x, to_z, to_both = call(
         key_sum_kernel,
         [shape((rows, d), F32)] + [shape((rows + PAD, d), I16)] * 3,
@@ -365,23 +378,25 @@
     )(mine, flip(sent, "core", 2, 1))
     to_both = lax.ppermute(to_both, ("zl", "xl"), [(i, 3 - i) for i in range(4)])
     pieces = [flip(to_x, "xl", 2, 1), flip(to_z, "zl", 2, 1), to_both]
-    coded = shape((2, rows + PAD, width), I16)
-    keep, to1, to2, to3 = call(
+    q1, q3 = call(
+        relay_kernel, [shape((n_im + PAD, 2 * width), I16)] * 2, "relay", 12, in_specs=[vmem] * 5
+    )(own_key, p1, p3, shift(q2a, "y", 4, 1), shift(q2b, "y", 4, 3))
+    q1, q3 = shift(q1, "y", 4, 1), shift(q3, "y", 4, 3)
+    coded, coded2 = shape((rows + PAD, width), I16), shape((2, rows + PAD, width), I16)
+    keep, to_a, to_b = call(
         image_sum_kernel,
-        [shape((2, rows, width), F32), coded, coded, coded],
+        [shape((6, rows, width), F32), coded, coded],
         "image_sum",
         12,
-        in_specs=[vmem] * 6,
+        in_specs=[vmem] * 5,
         scratch_shapes=[pltpu.VMEM((n_im, 2 * width), F32)],
-    )(*pieces, own, q1, q3)
-    to2, to1, to3 = shift(to2, "zh", 4, 2), shift(to1, "zh", 4, 1), shift(to3, "zh", 4, 3)
-    own, to_twin = call(
-        image_twin_kernel,
-        [shape((rows, width), F32), shape((rows + PAD, width), I16)],
-        "image_twin",
-        8,
-        in_specs=[vmem] * 4,
-    )(keep, to1, to2, to3)
+    )(*pieces[:2], own, q1, q3)
+    up, down = call(image_relay_kernel, [coded2] * 2, "image_relay", 8, in_specs=[vmem] * 3)(
+        keep, shift(to_a, "zh", 4, 1), shift(to_b, "zh", 4, 3)
+    )
+    own, to_twin = call(image_twin_kernel, [shape((rows, width), F32), coded], "image_twin", 8, in_specs=[vmem] * 4)(
+        pieces[2], keep, shift(up, "zh", 4, 1), shift(down, "zh", 4, 3)
+    )
     modality_grad, image_grad = call(
         last_kernel, [shape((rows, d), F32), shape((rows, width), F32)], "last", 8, in_specs=[vmem] * 6
     )(own_key, *pieces, own, flip(to_twin, "xh", 2, 1))

time: 129 us -> 126 us (0.977)
  starting transfers between devices: 53.7 us -> 52.2 us
    ppermute x1, waiting for transfers between devices: 5.07 us -> 0.01 us  [on_device(): lax.ppermute(to_both, ('zl', 'xl'), [(i, 3 - i) for i in range(4)])]
    ppermute x17 -> x18, waiting for transfers between devices: 31.8 us -> 36.3 us  [shift(): return lax.ppermute(x, axis, [(i, (i + k) % n) for i in range(n)])]
    ppermute x1, starting transfers between devices: 2.29 us -> 0.63 us  [on_device(): lax.ppermute(to_both, ('zl', 'xl'), [(i, 3 - i) for i in range(4)])]
    ppermute x17 -> x18, starting transfers between devices: 39.1 us -> 39.1 us  [shift(): return lax.ppermute(x, axis, [(i, (i + k) % n) for i in range(n)])]
  transfers between devices with their start and end apart: 32 -> 33, of which waited for: 16 -> 17; matrix products, arithmetic and copies ran while one was open for 0% -> 0% of each run, Pallas kernels for 1% -> 2%
where the time goes in v5:
time: 126 us
  waiting for transfers between devices  54.1 us (43%)
  starting transfers between devices  52.2 us (41%)
  Pallas kernels  16.3 us (13%)
  local copies, waits for them, and re-layouts  2.53 us (2%)
    ppermute x18, starting transfers between devices, shift(): return lax.ppermute(x, axis, [(i, (i + k) % n) for i in range(n)])  39.1 us
    ppermute x18, waiting for transfers between devices, shift(): return lax.ppermute(x, axis, [(i, (i + k) % n) for i in range(n)])  36.3 us
    ppermute x11, waiting for transfers between devices, flip(): return lax.ppermute(x, axis, [(i, i ^ d) for i in range(n)])  17.7 us
    ppermute x11, starting transfers between devices, flip(): return lax.ppermute(x, axis, [(i, i ^ d) for i in range(n)])  8.86 us
    pallas_call x1, Pallas kernels, on_device(): call(functools.partial(weights_kernel, scale, tile), outs, 'weights', 36,...  7.84 us
    pallas_call x1, Pallas kernels, on_device(): call(functools.partial(scores_kernel, scale), [shape((n_im, n_ks), F32),...  4.69 us
    ppermute x3, starting transfers between devices, on_device(): lax.ppermute(cs, ('zl', 'xl'), [(i, i ^ k) for i in range(4)])  3.58 us
    unnamed x6, local copies, waits for them, and re-layouts  2.53 us
  transfers between devices with their start and end apart: 33, of which 17 were waited for; matrix products, arithmetic and copies ran while one was open for 0% of the time, Pallas kernels for 2%

profile of v5, /device:TPU:4, one launch (start us, length us, event | category | flops | bytes accessed | tf_op | source)
XLA Modules:
  0.0 125.8 jit_solution(4943004509758608133)
XLA Ops:
  0.6 2.3 %collective-permute-start = (bf16[192,128]{1,0:T(8,128)(2,1)}, bf16[192,128]{1,0:T(8,128)(2,1)S(1)}, u32[]{:S(2)}, u32[]{:S(2)}) collective-permute-start(bf16[192,128]{1,0:T(8,128)(2,1)} %image.1), channel_id=1, source_target_pairs={{0,32},{32,0},{1,33},{33,1},{2,34},{34,2},{3,35},{35,3},{4,36},{36... | collective-permute-start | bytes 147464 | tf_op jit(solution)/shard_map/ppermute | solution.py:316
  3.0 3.6 %collective-permute-done.twin = bf16[192,128]{1,0:T(8,128)(2,1)S(1)} collective-permute-done((bf16[192,128]{1,0:T(8,128)(2,1)}, bf16[192,128]{1,0:T(8,128)(2,1)S(1)}, u32[]{:S(2)}, u32[]{:S(2)}) %collective-permute-start) | collective-permute-done | bytes 49184 | tf_op jit(solution)/shard_map/ppermute | solution.py:316
  7.3 6.4 %collective-permute-start.3 = (bf16[2,192,128]{2,1,0:T(8,128)(2,1)S(1)}, bf16[2,192,128]{2,1,0:T(8,128)(2,1)S(1)}, u32[]{:S(2)}, u32[]{:S(2)}) collective-permute-start(bf16[2,192,128]{2,1,0:T(8,128)(2,1)S(1)} %pair.1.both), channel_id=1, source_target_pairs={{0,24},{8,0},{16,8},{24,16},{1,25},{9,1},{17,9},{25,17},{2,26},{10... | collective-permute-start | bytes 294920 | tf_op jit(solution)/shard_map/ppermute | solution.py:312
  14.7 2.8 %collective-permute-start.1 = (bf16[2,192,128]{2,1,0:T(8,128)(2,1)S(1)}, bf16[2,192,128]{2,1,0:T(8,128)(2,1)S(1)}, u32[]{:S(2)}, u32[]{:S(2)}) collective-permute-start(bf16[2,192,128]{2,1,0:T(8,128)(2,1)S(1)} %pair.1.both), channel_id=1, source_target_pairs={{0,8},{8,16},{16,24},{24,0},{1,9},{9,17},{17,25},{25,1},{2,10},{10... | collective-permute-start | bytes 294920 | tf_op jit(solution)/shard_map/ppermute | solution.py:312
  19.5 1.5 %collective-permute-done.3.b3 = bf16[2,192,128]{2,1,0:T(8,128)(2,1)S(1)} collective-permute-done((bf16[2,192,128]{2,1,0:T(8,128)(2,1)S(1)}, bf16[2,192,128]{2,1,0:T(8,128)(2,1)S(1)}, u32[]{:S(2)}, u32[]{:S(2)}) %collective-permute-start.3) | collective-permute-done | bytes 98336 | tf_op jit(solution)/shard_map/ppermute | solution.py:312
  21.0 3.3 %collective-permute-done.2.b2 = bf16[2,192,128]{2,1,0:T(8,128)(2,1)S(1)} collective-permute-done((bf16[2,192,128]{2,1,0:T(8,128)(2,1)S(1)}, bf16[2,192,128]{2,1,0:T(8,128)(2,1)S(1)}, u32[]{:S(2)}, u32[]{:S(2)}) %collective-permute-start.2) | collective-permute-done | bytes 98336 | tf_op jit(solution)/shard_map/ppermute | solution.py:312
  26.5 3.0 %collective-permute-start.9 = (bf16[8,192,128]{2,1,0:T(8,128)(2,1)S(1)}, bf16[8,192,128]{2,1,0:T(8,128)(2,1)S(1)}, u32[]{:S(2)}, u32[]{:S(2)}) collective-permute-start(bf16[8,192,128]{2,1,0:T(8,128)(2,1)S(1)} %stack.1.after.refs_2_), channel_id=1, source_target_pairs={{0,192},{64,0},{128,64},{192,128},{1,193},{65,1},{129,65},{193,129... | collective-permute-start | bytes 1179656 | tf_op jit(solution)/shard_map/ppermute | solution.py:312
  29.5 4.2 %collective-permute-done.5.z = bf16[192,1024]{1,0:T(8,128)(2,1)S(1)} collective-permute-done((bf16[192,1024]{1,0:T(8,128)(2,1)S(1)}, bf16[192,1024]{1,0:T(8,128)(2,1)S(1)}, u32[]{:S(2)}, u32[]{:S(2)}) %collective-permute-start.5) | collective-permute-done | bytes 393248 | tf_op jit(solution)/shard_map/ppermute | solution.py:316
  33.7 1.5 %collective-permute-done.4.x = bf16[192,1024]{1,0:T(8,128)(2,1)S(1)} collective-permute-done((bf16[192,1024]{1,0:T(8,128)(2,1)S(1)}, bf16[192,1024]{1,0:T(8,128)(2,1)S(1)}, u32[]{:S(2)}, u32[]{:S(2)}) %collective-permute-start.4) | collective-permute-done | bytes 393248 | tf_op jit(solution)/shard_map/ppermute | solution.py:316
  35.2 1.3 %collective-permute-start.6 = (bf16[96,1024]{1,0:T(8,128)(2,1)S(1)}, bf16[96,1024]{1,0:T(8,128)(2,1)S(1)}, u32[]{:S(2)}, u32[]{:S(2)}) collective-permute-start(bf16[96,1024]{1,0:T(8,128)(2,1)S(1)} %get-tuple-element.41), channel_id=1, source_target_pairs={{0,2},{2,0},{1,3},{3,1},{4,6},{6,4},{5,7},{7,5},{8,10},{10,8},{9,1... | collective-permute-start | bytes 589832 | tf_op jit(solution)/shard_map/ppermute | solution.py:316
  36.9 3.2 %collective-permute-done.8.behind.refs_3_ = bf16[8,192,128]{2,1,0:T(8,128)(2,1)S(1)} collective-permute-done((bf16[8,192,128]{2,1,0:T(8,128)(2,1)S(1)}, bf16[8,192,128]{2,1,0:T(8,128)(2,1)S(1)}, u32[]{:S(2)}, u32[]{:S(2)}) %collective-permute-start.8) | collective-permute-done | bytes 393248 | tf_op jit(solution)/shard_map/ppermute | solution.py:312
  40.2 3.2 %collective-permute-start.11 = (bf16[4,192,128]{2,1,0:T(8,128)(2,1)S(1)}, bf16[4,192,128]{2,1,0:T(8,128)(2,1)S(1)}, u32[]{:S(2)}, u32[]{:S(2)}) collective-permute-start(bf16[4,192,128]{2,1,0:T(8,128)(2,1)S(1)} %get-tuple-element.44), channel_id=1, source_target_pairs={{0,192},{64,0},{128,64},{192,128},{1,193},{65,1},{129,65},{193,129... | collective-permute-start | bytes 589832 | tf_op jit(solution)/shard_map/ppermute | solution.py:312
  43.4 3.6 %collective-permute-done.10.after_a.refs_5_ = bf16[4,192,128]{2,1,0:T(8,128)(2,1)S(1)} collective-permute-done((bf16[4,192,128]{2,1,0:T(8,128)(2,1)S(1)}, bf16[4,192,128]{2,1,0:T(8,128)(2,1)S(1)}, u32[]{:S(2)}, u32[]{:S(2)}) %collective-permute-start.10) | collective-permute-done | bytes 196640 | tf_op jit(solution)/shard_map/ppermute | solution.py:312
  47.4 3.4 %collective-permute-done.12.refs_1_.refs_12_ = bf16[768,1024]{1,0:T(8,128)(2,1)S(1)} collective-permute-done((bf16[768,1024]{1,0:T(8,128)(2,1)S(1)}, bf16[768,1024]{1,0:T(8,128)(2,1)S(1)}, u32[]{:S(2)}, u32[]{:S(2)}) %collective-permute-start.12) | collective-permute-done | bytes 1572896 | tf_op jit(solution)/shard_map/ppermute | solution.py:316
  50.8 4.7 %scores.1 = (f32[768,1536]{1,0:T(8,128)S(1)}, bf16[768,1024]{1,0:T(8,128)(2,1)S(1)}, f32[2,768]{1,0:T(2,128)S(1)}, f32[2,1536]{1,0:T(2,128)S(1)}) custom-call(bf16[768,1024]{1,0:T(8,128)(2,1)S(1)} %join.1.refs_0_.refs_11_, bf16[768,1024]{1,0:T(8,128)(2,1)S(1)} %collective-permute-done.12.refs_1_.refs_12_, bf16[8,192,128]{2,1,0:T(8,128)(2,1)S(1)} %stack.1.after.refs_2_, ...), custom_call_target="tpu_custom_call" | custom-call | flops 1000 | bytes 1000 | tf_op jit(solution)/shard_map/scores/pallas_call | solution.py:352
  55.8 3.9 %collective-permute-start.15 = (f32[2,768]{1,0:T(2,128)S(1)}, f32[2,768]{1,0:T(2,128)S(1)}, u32[]{:S(2)}, u32[]{:S(2)}) collective-permute-start(f32[2,768]{1,0:T(2,128)S(1)} %get-tuple-element.46.refs_0_), channel_id=1, source_target_pairs={{0,24},{8,0},{16,8},{24,16},{1,25},{9,1},{17,9},{25,17},{2,26},{10... | collective-permute-start | bytes 18440 | tf_op jit(solution)/shard_map/ppermute | solution.py:312
  60.5 1.7 %collective-permute-start.18 = (f32[2,1536]{1,0:T(2,128)S(1)}, f32[2,1536]{1,0:T(2,128)S(1)}, u32[]{:S(2)}, u32[]{:S(2)}) collective-permute-start(f32[2,1536]{1,0:T(2,128)S(1)} %meet.1.refs_4_), channel_id=1, source_target_pairs={{0,4},{2,6},{4,0},{6,2},{1,5},{3,7},{5,1},{7,3},{8,12},{10,14},{12... | collective-permute-start | bytes 36872 | tf_op jit(solution)/shard_map/ppermute | solution.py:361
  63.3 1.7 %collective-permute-start.14 = (f32[2,768]{1,0:T(2,128)S(1)}, f32[2,768]{1,0:T(2,128)S(1)}, u32[]{:S(2)}, u32[]{:S(2)}) collective-permute-start(f32[2,768]{1,0:T(2,128)S(1)} %get-tuple-element.46.refs_0_), channel_id=1, source_target_pairs={{0,16},{8,24},{16,0},{24,8},{1,17},{9,25},{17,1},{25,9},{2,18},{10... | collective-permute-start | bytes 18440 | tf_op jit(solution)/shard_map/ppermute | solution.py:312
  65.0 1.9 %collective-permute-start.13 = (f32[2,768]{1,0:T(2,128)S(1)}, f32[2,768]{1,0:T(2,128)S(1)}, u32[]{:S(2)}, u32[]{:S(2)}) collective-permute-start(f32[2,768]{1,0:T(2,128)S(1)} %get-tuple-element.46.refs_0_), channel_id=1, source_target_pairs={{0,8},{8,16},{16,24},{24,0},{1,9},{9,17},{17,25},{25,1},{2,10},{10... | collective-permute-start | bytes 18440 | tf_op jit(solution)/shard_map/ppermute | solution.py:312
  66.9 3.9 %collective-permute-done.14.refs_2_ = f32[2,768]{1,0:T(2,128)S(1)} collective-permute-done((f32[2,768]{1,0:T(2,128)S(1)}, f32[2,768]{1,0:T(2,128)S(1)}, u32[]{:S(2)}, u32[]{:S(2)}) %collective-permute-start.14) | collective-permute-done | bytes 6176 | tf_op jit(solution)/shard_map/ppermute | solution.py:312
  70.9 7.8 %weights.1 = (f32[768,256]{1,0:T(8,128)S(1)}, f32[768,256]{1,0:T(8,128)S(1)}, f32[768,256]{1,0:T(8,128)S(1)}, s16[400,256]{1,0:T(8,128)(2,1)S(1)}, s16[400,256]{...) custom-call(f32[2,768]{1,0:T(2,128)S(1)} %get-tuple-element.46.refs_, ...), custom_call_target="tpu_custom_call" | custom-call | flops 1000 | bytes 1000 | tf_op jit(solution)/shard_map/weights/pallas_call | solution.py:364
  78.7 3.3 %collective-permute-start.25 = (s16[400,256]{1,0:T(8,128)(2,1)S(1)}, s16[400,256]{1,0:T(8,128)(2,1)S(1)}, u32[]{:S(2)}, u32[]{:S(2)}) collective-permute-start(s16[400,256]{1,0:T(8,128)(2,1)S(1)} %get-tuple-element.60), channel_id=1, source_target_pairs={{0,192},{64,0},{128,64},{192,128},{1,193},{65,1},{129,65},{193,129... | collective-permute-start | bytes 614408 | tf_op jit(solution)/shard_map/ppermute | solution.py:312
  84.5 3.2 %collective-permute-done.24.got_a = s16[400,256]{1,0:T(8,128)(2,1)S(1)} collective-permute-done((s16[400,256]{1,0:T(8,128)(2,1)S(1)}, s16[400,256]{1,0:T(8,128)(2,1)S(1)}, u32[]{:S(2)}, u32[]{:S(2)}) %collective-permute-start.24) | collective-permute-done | bytes 204832 | tf_op jit(solution)/shard_map/ppermute | solution.py:312
  89.3 2.1 %collective-permute-start.27 = (s16[784,256]{1,0:T(8,128)(2,1)S(1)}, s16[784,256]{1,0:T(8,128)(2,1)S(1)}, u32[]{:S(2)}, u32[]{:S(2)}) collective-permute-start(s16[784,256]{1,0:T(8,128)(2,1)S(1)} %get-tuple-element.62), channel_id=1, source_target_pairs={{0,192},{64,0},{128,64},{192,128},{1,193},{65,1},{129,65},{193,129... | collective-permute-start | bytes 1204232 | tf_op jit(solution)/shard_map/ppermute | solution.py:312
  92.0 8.5 %collective-permute-done.26.got1 = s16[784,256]{1,0:T(8,128)(2,1)S(1)} collective-permute-done((s16[784,256]{1,0:T(8,128)(2,1)S(1)}, s16[784,256]{1,0:T(8,128)(2,1)S(1)}, u32[]{:S(2)}, u32[]{:S(2)}) %collective-permute-start.26) | collective-permute-done | bytes 401440 | tf_op jit(solution)/shard_map/ppermute | solution.py:312
  101.7 3.5 %collective-permute-start.29 = (s16[208,128]{1,0:T(8,128)(2,1)S(1)}, s16[208,128]{1,0:T(8,128)(2,1)S(1)}, u32[]{:S(2)}, u32[]{:S(2)}) collective-permute-start(s16[208,128]{1,0:T(8,128)(2,1)S(1)} %get-tuple-element.65), channel_id=1, source_target_pairs={{0,24},{8,0},{16,8},{24,16},{1,25},{9,1},{17,9},{25,17},{2,26},{10... | collective-permute-start | bytes 159752 | tf_op jit(solution)/shard_map/ppermute | solution.py:312
  105.2 2.1 %collective-permute-done.28.got_a = s16[208,128]{1,0:T(8,128)(2,1)S(1)} collective-permute-done((s16[208,128]{1,0:T(8,128)(2,1)S(1)}, s16[208,128]{1,0:T(8,128)(2,1)S(1)}, u32[]{:S(2)}, u32[]{:S(2)}) %collective-permute-start.28) | collective-permute-done | bytes 53280 | tf_op jit(solution)/shard_map/ppermute | solution.py:312
  108.4 4.2 %collective-permute-start.30 = (s16[2,208,128]{2,1,0:T(8,128)(2,1)S(1)}, s16[2,208,128]{2,1,0:T(8,128)(2,1)S(1)}, u32[]{:S(2)}, u32[]{:S(2)}) collective-permute-start(s16[2,208,128]{2,1,0:T(8,128)(2,1)S(1)} %get-tuple-element.66), channel_id=1, source_target_pairs={{0,8},{8,16},{16,24},{24,0},{1,9},{9,17},{17,25},{25,1},{2,10},{10... | collective-permute-start | bytes 319496 | tf_op jit(solution)/shard_map/ppermute | solution.py:312
  112.6 3.8 %collective-permute-done.30.up = s16[2,208,128]{2,1,0:T(8,128)(2,1)S(1)} collective-permute-done((s16[2,208,128]{2,1,0:T(8,128)(2,1)S(1)}, s16[2,208,128]{2,1,0:T(8,128)(2,1)S(1)}, u32[]{:S(2)}, u32[]{:S(2)}) %collective-permute-start.30) | collective-permute-done | bytes 106528 | tf_op jit(solution)/shard_map/ppermute | solution.py:312
  116.4 2.4 %collective-permute-done.31.down = s16[2,208,128]{2,1,0:T(8,128)(2,1)S(1)} collective-permute-done((s16[2,208,128]{2,1,0:T(8,128)(2,1)S(1)}, s16[2,208,128]{2,1,0:T(8,128)(2,1)S(1)}, u32[]{:S(2)}, u32[]{:S(2)}) %collective-permute-start.31) | collective-permute-done | bytes 106528 | tf_op jit(solution)/shard_map/ppermute | solution.py:312
  119.8 4.8 %collective-permute-done.32.twin = s16[208,128]{1,0:T(8,128)(2,1)S(1)} collective-permute-done((s16[208,128]{1,0:T(8,128)(2,1)S(1)}, s16[208,128]{1,0:T(8,128)(2,1)S(1)}, u32[]{:S(2)}, u32[]{:S(2)}) %collective-permute-start.32) | collective-permute-done | bytes 53280 | tf_op jit(solution)/shard_map/ppermute | solution.py:316
  124.6 1.2 last.1
  (56 shorter events, 17.1 us)
Async XLA Ops:
  0.6 5.9 %collective-permute-start = (bf16[192,128]{1,0:T(8,128)(2,1)}, bf16[192,128]{1,0:T(8,128)(2,1)S(1)}, u32[]{:S(2)}, u32[]{:S(2)}) collective-permute-start(bf16[192,128]{1,0:T(8,128)(2,1)} %image.1), channel_id=1, source_target_pairs={{0,32},{32,0},{1,33},{33,1},{2,34},{34,2},{3,35},{35,3},{4,36},{36... | collective-permute-start | bytes 147464 | tf_op jit(solution)/shard_map/ppermute | solution.py:316
  7.3 13.6 %collective-permute-start.3 = (bf16[2,192,128]{2,1,0:T(8,128)(2,1)S(1)}, bf16[2,192,128]{2,1,0:T(8,128)(2,1)S(1)}, u32[]{:S(2)}, u32[]{:S(2)}) collective-permute-start(bf16[2,192,128]{2,1,0:T(8,128)(2,1)S(1)} %pair.1.both), channel_id=1, source_target_pairs={{0,24},{8,0},{16,8},{24,16},{1,25},{9,1},{17,9},{25,17},{2,26},{10... | collective-permute-start | bytes 294920 | tf_op jit(solution)/shard_map/ppermute | solution.py:312
  13.7 10.5 %collective-permute-start.2 = (bf16[2,192,128]{2,1,0:T(8,128)(2,1)S(1)}, bf16[2,192,128]{2,1,0:T(8,128)(2,1)S(1)}, u32[]{:S(2)}, u32[]{:S(2)}) collective-permute-start(bf16[2,192,128]{2,1,0:T(8,128)(2,1)S(1)} %pair.1.both), channel_id=1, source_target_pairs={{0,16},{8,24},{16,0},{24,8},{1,17},{9,25},{17,1},{25,9},{2,18},{10... | collective-permute-start | bytes 294920 | tf_op jit(solution)/shard_map/ppermute | solution.py:312
  14.7 9.5 %collective-permute-start.1 = (bf16[2,192,128]{2,1,0:T(8,128)(2,1)S(1)}, bf16[2,192,128]{2,1,0:T(8,128)(2,1)S(1)}, u32[]{:S(2)}, u32[]{:S(2)}) collective-permute-start(bf16[2,192,128]{2,1,0:T(8,128)(2,1)S(1)} %pair.1.both), channel_id=1, source_target_pairs={{0,8},{8,16},{16,24},{24,0},{1,9},{9,17},{17,25},{25,1},{2,10},{10... | collective-permute-start | bytes 294920 | tf_op jit(solution)/shard_map/ppermute | solution.py:312
  24.3 9.4 %collective-permute-start.5 = (bf16[192,1024]{1,0:T(8,128)(2,1)S(1)}, bf16[192,1024]{1,0:T(8,128)(2,1)S(1)}, u32[]{:S(2)}, u32[]{:S(2)}) collective-permute-start(bf16[192,1024]{1,0:T(8,128)(2,1)S(1)} %copy.8.own), channel_id=1, source_target_pairs={{0,4},{4,0},{1,5},{5,1},{2,6},{6,2},{3,7},{7,3},{8,12},{12,8},{9,1... | collective-permute-start | bytes 1179656 | tf_op jit(solution)/shard_map/ppermute | solution.py:316
  25.3 9.9 %collective-permute-start.4 = (bf16[192,1024]{1,0:T(8,128)(2,1)S(1)}, bf16[192,1024]{1,0:T(8,128)(2,1)S(1)}, u32[]{:S(2)}, u32[]{:S(2)}) collective-permute-start(bf16[192,1024]{1,0:T(8,128)(2,1)S(1)} %copy.8.own), channel_id=1, source_target_pairs={{0,2},{2,0},{1,3},{3,1},{4,6},{6,4},{5,7},{7,5},{8,10},{10,8},{9,1... | collective-permute-start | bytes 1179656 | tf_op jit(solution)/shard_map/ppermute | solution.py:316
  26.5 10.4 %collective-permute-start.9 = (bf16[8,192,128]{2,1,0:T(8,128)(2,1)S(1)}, bf16[8,192,128]{2,1,0:T(8,128)(2,1)S(1)}, u32[]{:S(2)}, u32[]{:S(2)}) collective-permute-start(bf16[8,192,128]{2,1,0:T(8,128)(2,1)S(1)} %stack.1.after.refs_2_), channel_id=1, source_target_pairs={{0,192},{64,0},{128,64},{192,128},{1,193},{65,1},{129,65},{193,129... | collective-permute-start | bytes 1179656 | tf_op jit(solution)/shard_map/ppermute | solution.py:312
  29.5 10.6 %collective-permute-start.8 = (bf16[8,192,128]{2,1,0:T(8,128)(2,1)S(1)}, bf16[8,192,128]{2,1,0:T(8,128)(2,1)S(1)}, u32[]{:S(2)}, u32[]{:S(2)}) collective-permute-start(bf16[8,192,128]{2,1,0:T(8,128)(2,1)S(1)} %stack.1.after.refs_2_), channel_id=1, source_target_pairs={{0,64},{64,128},{128,192},{192,0},{1,65},{65,129},{129,193},{193,1... | collective-permute-start | bytes 1179656 | tf_op jit(solution)/shard_map/ppermute | solution.py:312
  35.2 8.2 %collective-permute-start.6 = (bf16[96,1024]{1,0:T(8,128)(2,1)S(1)}, bf16[96,1024]{1,0:T(8,128)(2,1)S(1)}, u32[]{:S(2)}, u32[]{:S(2)}) collective-permute-start(bf16[96,1024]{1,0:T(8,128)(2,1)S(1)} %get-tuple-element.41), channel_id=1, source_target_pairs={{0,2},{2,0},{1,3},{3,1},{4,6},{6,4},{5,7},{7,5},{8,10},{10,8},{9,1... | collective-permute-start | bytes 589832 | tf_op jit(solution)/shard_map/ppermute | solution.py:316
  36.5 6.9 %collective-permute-start.7 = (bf16[96,1024]{1,0:T(8,128)(2,1)S(1)}, bf16[96,1024]{1,0:T(8,128)(2,1)S(1)}, u32[]{:S(2)}, u32[]{:S(2)}) collective-permute-start(bf16[96,1024]{1,0:T(8,128)(2,1)S(1)} %get-tuple-element.42), channel_id=1, source_target_pairs={{0,4},{4,0},{1,5},{5,1},{2,6},{6,2},{3,7},{7,3},{8,12},{12,8},{9,1... | collective-permute-start | bytes 589832 | tf_op jit(solution)/shard_map/ppermute | solution.py:316
  40.1 7.0 %collective-permute-start.10 = (bf16[4,192,128]{2,1,0:T(8,128)(2,1)S(1)}, bf16[4,192,128]{2,1,0:T(8,128)(2,1)S(1)}, u32[]{:S(2)}, u32[]{:S(2)}) collective-permute-start(bf16[4,192,128]{2,1,0:T(8,128)(2,1)S(1)} %get-tuple-element.43), channel_id=1, source_target_pairs={{0,64},{64,128},{128,192},{192,0},{1,65},{65,129},{129,193},{193,1... | collective-permute-start | bytes 589832 | tf_op jit(solution)/shard_map/ppermute | solution.py:312
  40.2 6.9 %collective-permute-start.11 = (bf16[4,192,128]{2,1,0:T(8,128)(2,1)S(1)}, bf16[4,192,128]{2,1,0:T(8,128)(2,1)S(1)}, u32[]{:S(2)}, u32[]{:S(2)}) collective-permute-start(bf16[4,192,128]{2,1,0:T(8,128)(2,1)S(1)} %get-tuple-element.44), channel_id=1, source_target_pairs={{0,192},{64,0},{128,64},{192,128},{1,193},{65,1},{129,65},{193,129... | collective-permute-start | bytes 589832 | tf_op jit(solution)/shard_map/ppermute | solution.py:312
  47.2 3.7 %collective-permute-start.12 = (bf16[768,1024]{1,0:T(8,128)(2,1)S(1)}, bf16[768,1024]{1,0:T(8,128)(2,1)S(1)}, u32[]{:S(2)}, u32[]{:S(2)}) collective-permute-start(bf16[768,1024]{1,0:T(8,128)(2,1)S(1)} %join.1.refs_0_.refs_11_), channel_id=1, source_target_pairs={{0,1},{1,0},{2,3},{3,2},{4,5},{5,4},{6,7},{7,6},{8,9},{9,8},{10,11... | collective-permute-start | bytes 4718600 | tf_op jit(solution)/shard_map/ppermute | solution.py:316
  55.5 4.1 %collective-permute-start.16 = (f32[2,1536]{1,0:T(2,128)S(1)}, f32[2,1536]{1,0:T(2,128)S(1)}, u32[]{:S(2)}, u32[]{:S(2)}) collective-permute-start(f32[2,1536]{1,0:T(2,128)S(1)} %get-tuple-element.47.c), channel_id=1, source_target_pairs={{0,1},{1,0},{2,3},{3,2},{4,5},{5,4},{6,7},{7,6},{8,9},{9,8},{10,11... | collective-permute-start | bytes 36872 | tf_op jit(solution)/shard_map/ppermute | solution.py:316
  55.8 9.3 %collective-permute-start.15 = (f32[2,768]{1,0:T(2,128)S(1)}, f32[2,768]{1,0:T(2,128)S(1)}, u32[]{:S(2)}, u32[]{:S(2)}) collective-permute-start(f32[2,768]{1,0:T(2,128)S(1)} %get-tuple-element.46.refs_0_), channel_id=1, source_target_pairs={{0,24},{8,0},{16,8},{24,16},{1,25},{9,1},{17,9},{25,17},{2,26},{10... | collective-permute-start | bytes 18440 | tf_op jit(solution)/shard_map/ppermute | solution.py:312
  59.7 11.1 %collective-permute-start.19 = (f32[2,1536]{1,0:T(2,128)S(1)}, f32[2,1536]{1,0:T(2,128)S(1)}, u32[]{:S(2)}, u32[]{:S(2)}) collective-permute-start(f32[2,1536]{1,0:T(2,128)S(1)} %meet.1.refs_4_), channel_id=1, source_target_pairs={{0,6},{2,4},{4,2},{6,0},{1,7},{3,5},{5,3},{7,1},{8,14},{10,12},{12... | collective-permute-start | bytes 36872 | tf_op jit(solution)/shard_map/ppermute | solution.py:361
  60.5 10.4 %collective-permute-start.18 = (f32[2,1536]{1,0:T(2,128)S(1)}, f32[2,1536]{1,0:T(2,128)S(1)}, u32[]{:S(2)}, u32[]{:S(2)}) collective-permute-start(f32[2,1536]{1,0:T(2,128)S(1)} %meet.1.refs_4_), channel_id=1, source_target_pairs={{0,4},{2,6},{4,0},{6,2},{1,5},{3,7},{5,1},{7,3},{8,12},{10,14},{12... | collective-permute-start | bytes 36872 | tf_op jit(solution)/shard_map/ppermute | solution.py:361
  62.1 8.7 %collective-permute-start.17 = (f32[2,1536]{1,0:T(2,128)S(1)}, f32[2,1536]{1,0:T(2,128)S(1)}, u32[]{:S(2)}, u32[]{:S(2)}) collective-permute-start(f32[2,1536]{1,0:T(2,128)S(1)} %meet.1.refs_4_), channel_id=1, source_target_pairs={{0,2},{2,0},{4,6},{6,4},{1,3},{3,1},{5,7},{7,5},{8,10},{10,8},{12,... | collective-permute-start | bytes 36872 | tf_op jit(solution)/shard_map/ppermute | solution.py:361
  63.3 7.5 %collective-permute-start.14 = (f32[2,768]{1,0:T(2,128)S(1)}, f32[2,768]{1,0:T(2,128)S(1)}, u32[]{:S(2)}, u32[]{:S(2)}) collective-permute-start(f32[2,768]{1,0:T(2,128)S(1)} %get-tuple-element.46.refs_0_), channel_id=1, source_target_pairs={{0,16},{8,24},{16,0},{24,8},{1,17},{9,25},{17,1},{25,9},{2,18},{10... | collective-permute-start | bytes 18440 | tf_op jit(solution)/shard_map/ppermute | solution.py:312
  65.0 5.8 %collective-permute-start.13 = (f32[2,768]{1,0:T(2,128)S(1)}, f32[2,768]{1,0:T(2,128)S(1)}, u32[]{:S(2)}, u32[]{:S(2)}) collective-permute-start(f32[2,768]{1,0:T(2,128)S(1)} %get-tuple-element.46.refs_0_), channel_id=1, source_target_pairs={{0,8},{8,16},{16,24},{24,0},{1,9},{9,17},{17,25},{25,1},{2,10},{10... | collective-permute-start | bytes 18440 | tf_op jit(solution)/shard_map/ppermute | solution.py:312
  78.7 9.0 %collective-permute-start.24 = (s16[400,256]{1,0:T(8,128)(2,1)S(1)}, s16[400,256]{1,0:T(8,128)(2,1)S(1)}, u32[]{:S(2)}, u32[]{:S(2)}) collective-permute-start(s16[400,256]{1,0:T(8,128)(2,1)S(1)} %get-tuple-element.59), channel_id=1, source_target_pairs={{0,64},{64,128},{128,192},{192,0},{1,65},{65,129},{129,193},{193,1... | collective-permute-start | bytes 614408 | tf_op jit(solution)/shard_map/ppermute | solution.py:312
  78.7 9.0 %collective-permute-start.25 = (s16[400,256]{1,0:T(8,128)(2,1)S(1)}, s16[400,256]{1,0:T(8,128)(2,1)S(1)}, u32[]{:S(2)}, u32[]{:S(2)}) collective-permute-start(s16[400,256]{1,0:T(8,128)(2,1)S(1)} %get-tuple-element.60), channel_id=1, source_target_pairs={{0,192},{64,0},{128,64},{192,128},{1,193},{65,1},{129,65},{193,129... | collective-permute-start | bytes 614408 | tf_op jit(solution)/shard_map/ppermute | solution.py:312
  83.2 17.2 %collective-permute-start.21 = (s16[208,1024]{1,0:T(8,128)(2,1)S(1)}, s16[208,1024]{1,0:T(8,128)(2,1)S(1)}, u32[]{:S(2)}, u32[]{:S(2)}) collective-permute-start(s16[208,1024]{1,0:T(8,128)(2,1)S(1)} %get-tuple-element.53), channel_id=1, source_target_pairs={{0,2},{2,0},{1,3},{3,1},{4,6},{6,4},{5,7},{7,5},{8,10},{10,8},{9,1... | collective-permute-start | bytes 1277960 | tf_op jit(solution)/shard_map/ppermute | solution.py:316
  84.2 16.3 %collective-permute-start.22 = (s16[208,1024]{1,0:T(8,128)(2,1)S(1)}, s16[208,1024]{1,0:T(8,128)(2,1)S(1)}, u32[]{:S(2)}, u32[]{:S(2)}) collective-permute-start(s16[208,1024]{1,0:T(8,128)(2,1)S(1)} %get-tuple-element.54), channel_id=1, source_target_pairs={{0,4},{4,0},{1,5},{5,1},{2,6},{6,2},{3,7},{7,3},{8,12},{12,8},{9,1... | collective-permute-start | bytes 1277960 | tf_op jit(solution)/shard_map/ppermute | solution.py:316
  88.1 12.4 %collective-permute-start.26 = (s16[784,256]{1,0:T(8,128)(2,1)S(1)}, s16[784,256]{1,0:T(8,128)(2,1)S(1)}, u32[]{:S(2)}, u32[]{:S(2)}) collective-permute-start(s16[784,256]{1,0:T(8,128)(2,1)S(1)} %get-tuple-element.61), channel_id=1, source_target_pairs={{0,64},{64,128},{128,192},{192,0},{1,65},{65,129},{129,193},{193,1... | collective-permute-start | bytes 1204232 | tf_op jit(solution)/shard_map/ppermute | solution.py:312
  89.3 11.2 %collective-permute-start.27 = (s16[784,256]{1,0:T(8,128)(2,1)S(1)}, s16[784,256]{1,0:T(8,128)(2,1)S(1)}, u32[]{:S(2)}, u32[]{:S(2)}) collective-permute-start(s16[784,256]{1,0:T(8,128)(2,1)S(1)} %get-tuple-element.62), channel_id=1, source_target_pairs={{0,192},{64,0},{128,64},{192,128},{1,193},{65,1},{129,65},{193,129... | collective-permute-start | bytes 1204232 | tf_op jit(solution)/shard_map/ppermute | solution.py:312
  91.4 21.2 %collective-permute-start.23 = (s16[208,1024]{1,0:T(8,128)(2,1)S(1)}, s16[208,1024]{1,0:T(8,128)(2,1)S(1)}, u32[]{:S(2)}, u32[]{:S(2)}) collective-permute-start(s16[208,1024]{1,0:T(8,128)(2,1)S(1)} %get-tuple-element.55), channel_id=1, source_target_pairs={{0,6},{2,4},{4,2},{6,0},{1,7},{3,5},{5,3},{7,1},{8,14},{10,12},{12... | collective-permute-start | bytes 1277960 | tf_op jit(solution)/shard_map/ppermute | solution.py:379
  101.0 6.3 %collective-permute-start.28 = (s16[208,128]{1,0:T(8,128)(2,1)S(1)}, s16[208,128]{1,0:T(8,128)(2,1)S(1)}, u32[]{:S(2)}, u32[]{:S(2)}) collective-permute-start(s16[208,128]{1,0:T(8,128)(2,1)S(1)} %get-tuple-element.64), channel_id=1, source_target_pairs={{0,8},{8,16},{16,24},{24,0},{1,9},{9,17},{17,25},{25,1},{2,10},{10... | collective-permute-start | bytes 159752 | tf_op jit(solution)/shard_map/ppermute | solution.py:312
  101.7 6.6 %collective-permute-start.29 = (s16[208,128]{1,0:T(8,128)(2,1)S(1)}, s16[208,128]{1,0:T(8,128)(2,1)S(1)}, u32[]{:S(2)}, u32[]{:S(2)}) collective-permute-start(s16[208,128]{1,0:T(8,128)(2,1)S(1)} %get-tuple-element.65), channel_id=1, source_target_pairs={{0,24},{8,0},{16,8},{24,16},{1,25},{9,1},{17,9},{25,17},{2,26},{10... | collective-permute-start | bytes 159752 | tf_op jit(solution)/shard_map/ppermute | solution.py:312
  108.4 8.0 %collective-permute-start.30 = (s16[2,208,128]{2,1,0:T(8,128)(2,1)S(1)}, s16[2,208,128]{2,1,0:T(8,128)(2,1)S(1)}, u32[]{:S(2)}, u32[]{:S(2)}) collective-permute-start(s16[2,208,128]{2,1,0:T(8,128)(2,1)S(1)} %get-tuple-element.66), channel_id=1, source_target_pairs={{0,8},{8,16},{16,24},{24,0},{1,9},{9,17},{17,25},{25,1},{2,10},{10... | collective-permute-start | bytes 319496 | tf_op jit(solution)/shard_map/ppermute | solution.py:312
  112.6 6.2 %collective-permute-start.31 = (s16[2,208,128]{2,1,0:T(8,128)(2,1)S(1)}, s16[2,208,128]{2,1,0:T(8,128)(2,1)S(1)}, u32[]{:S(2)}, u32[]{:S(2)}) collective-permute-start(s16[2,208,128]{2,1,0:T(8,128)(2,1)S(1)} %get-tuple-element.67), channel_id=1, source_target_pairs={{0,24},{8,0},{16,8},{24,16},{1,25},{9,1},{17,9},{25,17},{2,26},{10... | collective-permute-start | bytes 319496 | tf_op jit(solution)/shard_map/ppermute | solution.py:312
  118.9 5.7 %collective-permute-start.32 = (s16[208,128]{1,0:T(8,128)(2,1)S(1)}, s16[208,128]{1,0:T(8,128)(2,1)S(1)}, u32[]{:S(2)}, u32[]{:S(2)}) collective-permute-start(s16[208,128]{1,0:T(8,128)(2,1)S(1)} %get-tuple-element.69), channel_id=1, source_target_pairs={{0,32},{32,0},{1,33},{33,1},{2,34},{34,2},{3,35},{35,3},{4,36},{36... | collective-permute-start | bytes 159752 | tf_op jit(solution)/shard_map/ppermute | solution.py:316
  (4 other events, 6.1 us)

commit v6 on v1

--- a/solution.py
+++ b/solution.py
@@ -82,7 +82,14 @@
     return pltpu.roll(jnp.broadcast_to(v, (8, lanes)), lax.rem(lanes - n, lanes), 1)[0:1]
 
 
-def prep_kernel(pair_index, keys, pairs, cols, keys_out):
+def pair_kernel(image, twin, both):
+    xh = lax.axis_index("xh")
+    both[pl.ds(xh, 1)] = image[...][None]
+    both[pl.ds(1 - xh, 1)] = twin[...][None]
+
+
+def prep_kernel(pair_index, keys, after, pairs, cols, keys_out):
+    del after
     keys_out[...] = keys[...]
     n_im, n_ks = pairs.shape[1], cols.shape[1]
     rows = n_ks // 8
@@ -107,11 +114,26 @@
             at += n
 
 
-def hold_kernel(x, z, after, z_top, x_low):
-    del after
-    n = z_top.shape[0]
-    z_top[...] = z[:n, :]
-    x_low[...] = x[n:, :]
+def stack_kernel(both, b1, b2, b3, after, out):
+    del after
+    zh = lax.axis_index("zh")
+    for k, ref in enumerate((both, b1, b2, b3)):
+        for xh in range(2):
+            out[pl.ds(4 * xh + lax.rem(zh + 4 - k, 4), 1)] = ref[xh : xh + 1]
+
+
+def hold_kernel(keys, after, out):
+    del after
+    out[...] = keys[...]
+
+
+def low_kernel(x, after, out):
+    del after
+    out[...] = x[out.shape[0] :, :]
+
+
+def top_kernel(z, out):
+    out[...] = z[: out.shape[0], :]
 
 
 def turn_kernel(behind, ahead, half_a, half_b):
@@ -183,13 +205,17 @@
     return jnp.concatenate([c[:, (k ^ 1) * n : ((k ^ 1) + 1) * n] for k in range(c.shape[1] // n)], axis=1)
 
 
+def meet_rows_kernel(r, r_other, out):
+    out[...] = meet([r[...], r_other[...]])
+
+
 def meet_kernel(c, c_other, out):
     out[...] = meet([c[...], turned(c_other[...], c.shape[1] // 2)])
 
 
 def weights_kernel(scale, tile, *refs):
-    rparts, cparts = refs[:4], refs[4:8]
-    pairs, cols, s_ref, k0, k1, im, own, p1, p3, o2a, o2b, mine, sent, rl, cl, w_ref, total = refs[8:]
+    rparts, cparts = refs[:2], refs[2:6]
+    pairs, cols, s_ref, k0, k1, im, own, p1, p3, o2a, o2b, mine, sent, rl, cl, w_ref, total = refs[6:]
     n_im, n_ks = s_ref.shape
     keys = (k0, k1)
     half, part = n_ks // 2, n_ks // 4
@@ -235,7 +261,8 @@
     mine[...] = lax.dot_general(w_ref[:, :half], im[...], FIRST, preferred_element_type=F32) * scale
 
 
-def relay_kernel(p1, p3, got_a, got_b, o1, o3):
+def relay_kernel(after, p1, p3, got_a, got_b, o1, o3):
+    del after
     n = p1.shape[0] // 2
     encode(jnp.concatenate([p1[:n, :] + decode(got_a[...]), p1[n:, :]], axis=0), o1)
     encode(jnp.concatenate([p3[:n, :], p3[n:, :] + decode(got_b[...])], axis=0), o3)
@@ -260,8 +287,7 @@
     own[...] = piece(0)
 
 
-def key_relay_kernel(after, own, keep_x, keep_z, from_x, from_z, total, to_x, to_z):
-    del after
+def key_relay_kernel(own, keep_x, keep_z, from_x, from_z, total, to_x, to_z):
     n = keep_x.shape[1]
     total[:, :n] = own[:, :n] + decode(from_x[0])
     total[:, n:] = own[:, n:] + decode(from_z[0])
@@ -280,22 +306,21 @@
     del after
     zh, xh = lax.axis_index("zh"), lax.axis_index("xh")
     rows, width = keep.shape[1:]
-    n = own.shape[0] // rows
     total[...] = own[...] + decode(got1[...]) + decode(got3[...])
 
     def piece(o, j):
-        row = pl.multiple_of(lax.rem(zh + j, n) * rows, 16)
+        row = pl.multiple_of(lax.rem(zh + j, 4) * rows, 16)
         return total[pl.ds(row, rows), pl.ds(pl.multiple_of((xh ^ o) * width, 128), width)]
 
     encode(piece(0, 2), to_a)
     encode(piece(1, 2), to_b)
     for o in range(2):
-        for at, j in enumerate((0, 1, n - 1)):
+        for at, j in enumerate((0, 1, 3)):
             keep[3 * o + at] = piece(o, j)
 
 
-def image_relay_kernel(after, keep, got_a, got_b, up, down):
-    del after
+def image_relay_kernel(after_x, after_z, keep, got_a, got_b, up, down):
+    del after_x, after_z
     encode(keep[1] + decode(got_a[...]), up.at[0])
     encode(keep[4], up.at[1])
     encode(keep[2], down.at[0])
@@ -324,20 +349,21 @@
     n_im, n_ks = nzh * rows, 8 * rows
     half = n_ks // 2
     vmem = pl.BlockSpec(memory_space=pltpu.VMEM)
+    key_block = shape((rows, d), BF16)
+    both = call(pair_kernel, shape((2, rows, width), BF16), "pair", 4, in_specs=[vmem] * 2)(image, flip(image, "xh", 2, 1))
     pairs, cols, held = call(
-        prep_kernel,
-        [shape((1, n_im), F32), shape((1, n_ks), F32), shape((rows, d), BF16)],
-        "prep",
-        8,
-        in_specs=[vmem] * 2,
-    )(pair_index, keys)
-    i0 = lax.all_to_all(jnp.broadcast_to(image, (2 * nzh, rows, width)), ("xh", "zh"), 0, 0)
+        prep_kernel, [shape((1, n_im), F32), shape((1, n_ks), F32), key_block], "prep", 8, in_specs=[vmem] * 3
+    )(pair_index, keys, both)
+    key_x = flip(held, "xl", 2, 1)
+    i0 = call(stack_kernel, shape((8, rows, width), BF16), "stack", 8, in_specs=[vmem] * 5)(
+        both, *[shift(both, "zh", 4, k) for k in (1, 2, 3)], pairs
+    )
     i1, i3 = shift(i0, "y", 4, 1), shift(i0, "y", 4, 3)
-    key_x = flip(keys, "xl", 2, 1)
-    key_z = flip(keys, "zl", 2, 1)
     quarter = shape((rows // 2, d), BF16)
-    d_top, d_low = call(hold_kernel, [quarter] * 2, "hold", 8, in_specs=[vmem] * 3)(key_x, key_z, i0)
-    d_top, d_low = flip(d_top, "xl", 2, 1), flip(d_low, "zl", 2, 1)
+    held = call(hold_kernel, key_block, "hold", 8, in_specs=[vmem] * 2)(held, i0)
+    key_z = flip(held, "zl", 2, 1)
+    d_low = flip(call(low_kernel, quarter, "low", 8, in_specs=[vmem] * 2)(key_x, i0), "zl", 2, 1)
+    d_top = flip(call(top_kernel, quarter, "top", 8, in_specs=[vmem])(key_z), "xl", 2, 1)
     half_block = shape((nzh, rows, width), BF16)
     ia, ib = call(turn_kernel, [half_block] * 2, "turn", 12, in_specs=[vmem] * 2)(i1, i3)
     ia, ib = shift(ia, "y", 4, 1), shift(ib, "y", 4, 3)
@@ -354,7 +380,8 @@
         28,
         in_specs=[vmem] * 9,
     )(*ks, i0, i1, i3, ia, ib, pairs, cols)
-    rstats = [rs] + [shift(rs, "zh", 4, k) for k in (1, 2, 3)]
+    rs = call(meet_rows_kernel, shape((2, n_im), F32), "meet_rows", 4, in_specs=[vmem] * 2)(rs, flip(rs, "zh", 4, 1))
+    rstats = [rs, flip(rs, "zh", 4, 3)]
     cs = call(meet_kernel, shape((2, n_ks), F32), "meet", 4, in_specs=[vmem] * 2)(cs, flip(cs, "core", 2, 1))
     cstats = [cs] + [lax.ppermute(cs, ("zl", "xl"), [(i, i ^ k) for i in range(4)]) for k in (1, 2, 3)]
     outs = [shape((n_im, 2 * width), F32)] * 3 + [shape((n_im // 2 + PAD, 2 * width), I16)] * 2
@@ -364,13 +391,9 @@
         outs,
         "weights",
         36,
-        in_specs=[vmem] * 14,
+        in_specs=[vmem] * 12,
         scratch_shapes=[pltpu.VMEM((n_im, n_ks), BF16), pltpu.VMEM((n_im, d), F32)],
     )(*rstats, *cstats, pairs, cols, scores, *ks, im)
-    q1, q3 = call(
-        relay_kernel, [shape((n_im + PAD, 2 * width), I16)] * 2, "relay", 12, in_specs=[vmem] * 4
-    )(p1, p3, shift(q2a, "y", 4, 1), shift(q2b, "y", 4, 3))
-    q1, q3 = shift(q1, "y", 4, 1), shift(q3, "y", 4, 3)
     own_key, keep_x, keep_z, to_x, to_z = call(
         key_sum_kernel,
         [shape((rows, d), F32)] + [shape((rows, d // 2), F32)] * 2 + [shape((2, rows + PAD, d // 2), I16)] * 2,
@@ -378,9 +401,19 @@
         16,
         in_specs=[vmem] * 2,
     )(mine, flip(sent, "core", 2, 1))
+    q1, q3 = call(
+        relay_kernel, [shape((n_im + PAD, 2 * width), I16)] * 2, "relay", 12, in_specs=[vmem] * 5
+    )(own_key, p1, p3, shift(q2a, "y", 4, 1), shift(q2b, "y", 4, 3))
+    q1, q3 = shift(q1, "y", 4, 1), shift(q3, "y", 4, 3)
+    own_key, to_x, to_z = call(
+        key_relay_kernel,
+        [shape((rows, d), F32)] + [shape((rows + PAD, d // 2), I16)] * 2,
+        "key_relay",
+        12,
+        in_specs=[vmem] * 5,
+    )(own_key, keep_x, keep_z, flip(to_x, "xl", 2, 1), flip(to_z, "zl", 2, 1))
     from_x, from_z = flip(to_x, "xl", 2, 1), flip(to_z, "zl", 2, 1)
-    coded = shape((rows + PAD, width), I16)
-    coded2 = shape((2, rows + PAD, width), I16)
+    coded, coded2 = shape((rows + PAD, width), I16), shape((2, rows + PAD, width), I16)
     keep, to_a, to_b = call(
         image_sum_kernel,
         [shape((6, rows, width), F32), coded, coded],
@@ -388,23 +421,16 @@
         12,
         in_specs=[vmem] * 4,
         scratch_shapes=[pltpu.VMEM((n_im, 2 * width), F32)],
-    )(keep_z, own, q1, q3)
-    own_key, to_x, to_z = call(
-        key_relay_kernel,
-        [shape((rows, d), F32)] + [shape((rows + PAD, d // 2), I16)] * 2,
-        "key_relay",
-        12,
-        in_specs=[vmem] * 6,
-    )(to_a, own_key, keep_x, keep_z, from_x, from_z)
-    up, down = call(image_relay_kernel, [coded2] * 2, "image_relay", 8, in_specs=[vmem] * 4)(
-        to_x, keep, shift(to_a, "zh", 4, 1), shift(to_b, "zh", 4, 3)
+    )(own_key, own, q1, q3)
+    up, down = call(image_relay_kernel, [coded2] * 2, "image_relay", 8, in_specs=[vmem] * 5)(
+        from_x, from_z, keep, shift(to_a, "zh", 4, 1), shift(to_b, "zh", 4, 3)
     )
     own, to_twin = call(image_twin_kernel, [shape((rows, width), F32), coded], "image_twin", 8, in_specs=[vmem] * 3)(
         keep, shift(up, "zh", 4, 1), shift(down, "zh", 4, 3)
     )
     modality_grad, image_grad = call(
         last_kernel, [shape((rows, d), F32), shape((rows, width), F32)], "last", 8, in_specs=[vmem] * 5
-    )(own_key, flip(to_x, "xl", 2, 1), flip(to_z, "zl", 2, 1), own, flip(to_twin, "xh", 2, 1))
+    )(own_key, from_x, from_z, own, flip(to_twin, "xh", 2, 1))
     return (image_grad, modality_grad[None], row_loss, col_loss)
 
 

time: 127 us -> 122 us (0.961)
  waiting for transfers between devices: 53.7 us -> 49.7 us
    ppermute x12 -> x15, waiting for transfers between devices: 9.28 us -> 25.4 us  [flip(): return lax.ppermute(x, axis, [(i, i ^ d) for i in range(n)])]
    all_to_all x1 -> x0, waiting for transfers between devices: 11.6 us -> none  [on_device(): lax.all_to_all(jnp.broadcast_to(image, (2 * nzh, rows, width)), ('xh', 'z...]
    all_to_all x1 -> x0, starting transfers between devices: 11.4 us -> none  [on_device(): lax.all_to_all(jnp.broadcast_to(image, (2 * nzh, rows, width)), ('xh', 'z...]
    ppermute x15, waiting for transfers between devices: 32.9 us -> 24.3 us  [shift(): return lax.ppermute(x, axis, [(i, (i + k) % n) for i in range(n)])]
    ppermute x15, starting transfers between devices: 23.4 us -> 31.6 us  [shift(): return lax.ppermute(x, axis, [(i, (i + k) % n) for i in range(n)])]
    ppermute x12 -> x15, starting transfers between devices: 14 us -> 16.8 us  [flip(): return lax.ppermute(x, axis, [(i, i ^ d) for i in range(n)])]
    unnamed x4 -> x6, local copies, waits for them, and re-layouts: 0.01 us -> 2.53 us
    broadcast_in_dim x1 -> x0, local copies, waits for them, and re-layouts: 1.64 us -> none  [on_device(): jnp.broadcast_to(image, (2 * nzh, rows, width))]
  transfers between devices with their start and end apart: 31 -> 33, of which waited for: 14 -> 19; matrix products, arithmetic and copies ran while one was open for 0% -> 0% of each run, Pallas kernels for 2% -> 2%
where the time goes in v6:
time: 122 us; the launch traced here: 121 us
  starting transfers between devices  52 us (43%)
  waiting for transfers between devices  49.7 us (41%)
  Pallas kernels  16.5 us (14%)
  local copies, waits for them, and re-layouts  2.53 us (2%)
    ppermute x15, starting transfers between devices, shift(): return lax.ppermute(x, axis, [(i, (i + k) % n) for i in range(n)])  31.6 us
    ppermute x15, waiting for transfers between devices, flip(): return lax.ppermute(x, axis, [(i, i ^ d) for i in range(n)])  25.4 us
    ppermute x15, waiting for transfers between devices, shift(): return lax.ppermute(x, axis, [(i, (i + k) % n) for i in range(n)])  24.3 us
    ppermute x15, starting transfers between devices, flip(): return lax.ppermute(x, axis, [(i, i ^ d) for i in range(n)])  16.8 us
    pallas_call x1, Pallas kernels, on_device(): call(functools.partial(weights_kernel, scale, tile), outs, 'weights', 36,...  7.84 us
    pallas_call x1, Pallas kernels, on_device(): call(functools.partial(scores_kernel, scale), [shape((n_im, n_ks), F32),...  4.69 us
    ppermute x3, starting transfers between devices, on_device(): lax.ppermute(cs, ('zl', 'xl'), [(i, i ^ k) for i in range(4)])  3.58 us
    unnamed x6, local copies, waits for them, and re-layouts  2.53 us
  transfers between devices with their start and end apart: 33, of which 19 were waited for; matrix products, arithmetic and copies ran while one was open for 0% of the time, Pallas kernels for 2%

profile of v6, /device:TPU:4, one launch (start us, length us, event | category | flops | bytes accessed | tf_op | source)
XLA Modules:
  0.0 121.4 jit_solution(7369715236894972290)
XLA Ops:
  0.6 2.3 %collective-permute-start = (bf16[192,128]{1,0:T(8,128)(2,1)}, bf16[192,128]{1,0:T(8,128)(2,1)S(1)}, u32[]{:S(2)}, u32[]{:S(2)}) collective-permute-start(bf16[192,128]{1,0:T(8,128)(2,1)} %image.1), channel_id=1, source_target_pairs={{0,32},{32,0},{1,33},{33,1},{2,34},{34,2},{3,35},{35,3},{4,36},{36... | collective-permute-start | bytes 147464 | tf_op jit(solution)/shard_map/ppermute | solution.py:340
  3.0 3.6 %collective-permute-done.twin = bf16[192,128]{1,0:T(8,128)(2,1)S(1)} collective-permute-done((bf16[192,128]{1,0:T(8,128)(2,1)}, bf16[192,128]{1,0:T(8,128)(2,1)S(1)}, u32[]{:S(2)}, u32[]{:S(2)}) %collective-permute-start) | collective-permute-done | bytes 49184 | tf_op jit(solution)/shard_map/ppermute | solution.py:340
  7.3 6.4 %collective-permute-start.3 = (bf16[2,192,128]{2,1,0:T(8,128)(2,1)S(1)}, bf16[2,192,128]{2,1,0:T(8,128)(2,1)S(1)}, u32[]{:S(2)}, u32[]{:S(2)}) collective-permute-start(bf16[2,192,128]{2,1,0:T(8,128)(2,1)S(1)} %pair.1.after.both), channel_id=1, source_target_pairs={{0,24},{8,0},{16,8},{24,16},{1,25},{9,1},{17,9},{25,17},{2,26},{10... | collective-permute-start | bytes 294920 | tf_op jit(solution)/shard_map/ppermute | solution.py:336
  14.7 2.8 %collective-permute-start.1 = (bf16[2,192,128]{2,1,0:T(8,128)(2,1)S(1)}, bf16[2,192,128]{2,1,0:T(8,128)(2,1)S(1)}, u32[]{:S(2)}, u32[]{:S(2)}) collective-permute-start(bf16[2,192,128]{2,1,0:T(8,128)(2,1)S(1)} %pair.1.after.both), channel_id=1, source_target_pairs={{0,8},{8,16},{16,24},{24,0},{1,9},{9,17},{17,25},{25,1},{2,10},{10... | collective-permute-start | bytes 294920 | tf_op jit(solution)/shard_map/ppermute | solution.py:336
  19.5 1.3 %collective-permute-start.4 = (bf16[192,1024]{1,0:T(8,128)(2,1)S(1)}, bf16[192,1024]{1,0:T(8,128)(2,1)S(1)}, u32[]{:S(2)}, u32[]{:S(2)}) collective-permute-start(bf16[192,1024]{1,0:T(8,128)(2,1)S(1)} %get-tuple-element.41.keys), channel_id=1, source_target_pairs={{0,2},{2,0},{1,3},{3,1},{4,6},{6,4},{5,7},{7,5},{8,10},{10,8},{9,1... | collective-permute-start | bytes 1179656 | tf_op jit(solution)/shard_map/ppermute | solution.py:340
  21.0 3.3 %collective-permute-done.2.b2 = bf16[2,192,128]{2,1,0:T(8,128)(2,1)S(1)} collective-permute-done((bf16[2,192,128]{2,1,0:T(8,128)(2,1)S(1)}, bf16[2,192,128]{2,1,0:T(8,128)(2,1)S(1)}, u32[]{:S(2)}, u32[]{:S(2)}) %collective-permute-start.2) | collective-permute-done | bytes 98336 | tf_op jit(solution)/shard_map/ppermute | solution.py:336
  25.3 3.0 %collective-permute-start.9 = (bf16[8,192,128]{2,1,0:T(8,128)(2,1)S(1)}, bf16[8,192,128]{2,1,0:T(8,128)(2,1)S(1)}, u32[]{:S(2)}, u32[]{:S(2)}) collective-permute-start(bf16[8,192,128]{2,1,0:T(8,128)(2,1)S(1)} %stack.1.after.refs_2_), channel_id=1, source_target_pairs={{0,192},{64,0},{128,64},{192,128},{1,193},{65,1},{129,65},{193,129... | collective-permute-start | bytes 1179656 | tf_op jit(solution)/shard_map/ppermute | solution.py:336
  29.6 6.3 %collective-permute-done.5.z = bf16[192,1024]{1,0:T(8,128)(2,1)S(1)} collective-permute-done((bf16[192,1024]{1,0:T(8,128)(2,1)S(1)}, bf16[192,1024]{1,0:T(8,128)(2,1)S(1)}, u32[]{:S(2)}, u32[]{:S(2)}) %collective-permute-start.5) | collective-permute-done | bytes 393248 | tf_op jit(solution)/shard_map/ppermute | solution.py:340
  35.9 1.3 %collective-permute-start.6 = (bf16[96,1024]{1,0:T(8,128)(2,1)S(1)}, bf16[96,1024]{1,0:T(8,128)(2,1)S(1)}, u32[]{:S(2)}, u32[]{:S(2)}) collective-permute-start(bf16[96,1024]{1,0:T(8,128)(2,1)S(1)} %top.1), channel_id=1, source_target_pairs={{0,2},{2,0},{1,3},{3,1},{4,6},{6,4},{5,7},{7,5},{8,10},{10,8},{9,1... | collective-permute-start | bytes 589832 | tf_op jit(solution)/shard_map/ppermute | solution.py:340
  37.1 2.0 %collective-permute-done.8.behind.refs_3_ = bf16[8,192,128]{2,1,0:T(8,128)(2,1)S(1)} collective-permute-done((bf16[8,192,128]{2,1,0:T(8,128)(2,1)S(1)}, bf16[8,192,128]{2,1,0:T(8,128)(2,1)S(1)}, u32[]{:S(2)}, u32[]{:S(2)}) %collective-permute-start.8) | collective-permute-done | bytes 393248 | tf_op jit(solution)/shard_map/ppermute | solution.py:336
  39.3 3.2 %collective-permute-start.11 = (bf16[4,192,128]{2,1,0:T(8,128)(2,1)S(1)}, bf16[4,192,128]{2,1,0:T(8,128)(2,1)S(1)}, u32[]{:S(2)}, u32[]{:S(2)}) collective-permute-start(bf16[4,192,128]{2,1,0:T(8,128)(2,1)S(1)} %get-tuple-element.44), channel_id=1, source_target_pairs={{0,192},{64,0},{128,64},{192,128},{1,193},{65,1},{129,65},{193,129... | collective-permute-start | bytes 589832 | tf_op jit(solution)/shard_map/ppermute | solution.py:336
  42.5 3.6 %collective-permute-done.10.after_a.refs_5_ = bf16[4,192,128]{2,1,0:T(8,128)(2,1)S(1)} collective-permute-done((bf16[4,192,128]{2,1,0:T(8,128)(2,1)S(1)}, bf16[4,192,128]{2,1,0:T(8,128)(2,1)S(1)}, u32[]{:S(2)}, u32[]{:S(2)}) %collective-permute-start.10) | collective-permute-done | bytes 196640 | tf_op jit(solution)/shard_map/ppermute | solution.py:336
  46.5 3.4 %collective-permute-done.12.refs_1_.refs_10_ = bf16[768,1024]{1,0:T(8,128)(2,1)S(1)} collective-permute-done((bf16[768,1024]{1,0:T(8,128)(2,1)S(1)}, bf16[768,1024]{1,0:T(8,128)(2,1)S(1)}, u32[]{:S(2)}, u32[]{:S(2)}) %collective-permute-start.12) | collective-permute-done | bytes 1572896 | tf_op jit(solution)/shard_map/ppermute | solution.py:340
  49.9 4.7 %scores.1 = (f32[768,1536]{1,0:T(8,128)S(1)}, bf16[768,1024]{1,0:T(8,128)(2,1)S(1)}, f32[2,768]{1,0:T(2,128)S(1)}, f32[2,1536]{1,0:T(2,128)S(1)}) custom-call(bf16[768,1024]{1,0:T(8,128)(2,1)S(1)} %join.1.refs_0_.refs_9_, bf16[768,1024]{1,0:T(8,128)(2,1)S(1)} %collective-permute-done.12.refs_1_.refs_10_, bf16[8,192,128]{2,1,0:T(8,128)(2,1)S(1)} %stack.1.after.refs_2_, ...), custom_call_target="tpu_custom_call" | custom-call | flops 1000 | bytes 1000 | tf_op jit(solution)/shard_map/scores/pallas_call | solution.py:376
  54.8 1.8 %collective-permute-start.13 = (f32[2,768]{1,0:T(2,128)S(1)}, f32[2,768]{1,0:T(2,128)S(1)}, u32[]{:S(2)}, u32[]{:S(2)}) collective-permute-start(f32[2,768]{1,0:T(2,128)S(1)} %get-tuple-element.46.r), channel_id=1, source_target_pairs={{0,8},{8,0},{16,24},{24,16},{1,9},{9,1},{17,25},{25,17},{2,10},{10... | collective-permute-start | bytes 18440 | tf_op jit(solution)/shard_map/ppermute | solution.py:340
  57.7 1.6 %collective-permute-start.17 = (f32[2,1536]{1,0:T(2,128)S(1)}, f32[2,1536]{1,0:T(2,128)S(1)}, u32[]{:S(2)}, u32[]{:S(2)}) collective-permute-start(f32[2,1536]{1,0:T(2,128)S(1)} %meet.1.refs_2_), channel_id=1, source_target_pairs={{0,4},{2,6},{4,0},{6,2},{1,5},{3,7},{5,1},{7,3},{8,12},{10,14},{12... | collective-permute-start | bytes 36872 | tf_op jit(solution)/shard_map/ppermute | solution.py:386
  60.3 3.7 %collective-permute-start.14 = (f32[2,768]{1,0:T(2,128)S(1)}, f32[2,768]{1,0:T(2,128)S(1)}, u32[]{:S(2)}, u32[]{:S(2)}) collective-permute-start(f32[2,768]{1,0:T(2,128)S(1)} %meet_rows.1.refs_0_), channel_id=1, source_target_pairs={{0,24},{8,16},{16,8},{24,0},{1,25},{9,17},{17,9},{25,1},{2,26},{10... | collective-permute-start | bytes 18440 | tf_op jit(solution)/shard_map/ppermute | solution.py:340
  64.0 2.3 %collective-permute-done.14.refs_1_ = f32[2,768]{1,0:T(2,128)S(1)} collective-permute-done((f32[2,768]{1,0:T(2,128)S(1)}, f32[2,768]{1,0:T(2,128)S(1)}, u32[]{:S(2)}, u32[]{:S(2)}) %collective-permute-start.14) | collective-permute-done | bytes 6176 | tf_op jit(solution)/shard_map/ppermute | solution.py:340
  66.3 7.8 %weights.1 = (f32[768,256]{1,0:T(8,128)S(1)}, f32[768,256]{1,0:T(8,128)S(1)}, f32[768,256]{1,0:T(8,128)S(1)}, s16[400,256]{1,0:T(8,128)(2,1)S(1)}, s16[400,256]{...) custom-call(f32[2,768]{1,0:T(2,128)S(1)} %meet_rows.1.refs_0_, ...), custom_call_target="tpu_custom_call" | custom-call | flops 1000 | bytes 1000 | tf_op jit(solution)/shard_map/weights/pallas_call | solution.py:389
  74.2 3.3 %collective-permute-start.25 = (s16[400,256]{1,0:T(8,128)(2,1)S(1)}, s16[400,256]{1,0:T(8,128)(2,1)S(1)}, u32[]{:S(2)}, u32[]{:S(2)}) collective-permute-start(s16[400,256]{1,0:T(8,128)(2,1)S(1)} %get-tuple-element.64), channel_id=1, source_target_pairs={{0,192},{64,0},{128,64},{192,128},{1,193},{65,1},{129,65},{193,129... | collective-permute-start | bytes 614408 | tf_op jit(solution)/shard_map/ppermute | solution.py:336
  78.7 1.3 %collective-permute-start.20 = (s16[2,208,512]{2,1,0:T(8,128)(2,1)S(1)}, s16[2,208,512]{2,1,0:T(8,128)(2,1)S(1)}, u32[]{:S(2)}, u32[]{:S(2)}) collective-permute-start(s16[2,208,512]{2,1,0:T(8,128)(2,1)S(1)} %get-tuple-element.55), channel_id=1, source_target_pairs={{0,2},{2,0},{1,3},{3,1},{4,6},{6,4},{5,7},{7,5},{8,10},{10,8},{9,1... | collective-permute-start | bytes 1277960 | tf_op jit(solution)/shard_map/ppermute | solution.py:340
  80.3 2.8 %collective-permute-done.24.got_a = s16[400,256]{1,0:T(8,128)(2,1)S(1)} collective-permute-done((s16[400,256]{1,0:T(8,128)(2,1)S(1)}, s16[400,256]{1,0:T(8,128)(2,1)S(1)}, u32[]{:S(2)}, u32[]{:S(2)}) %collective-permute-start.24) | collective-permute-done | bytes 204832 | tf_op jit(solution)/shard_map/ppermute | solution.py:336
  84.7 2.2 %collective-permute-start.27 = (s16[784,256]{1,0:T(8,128)(2,1)S(1)}, s16[784,256]{1,0:T(8,128)(2,1)S(1)}, u32[]{:S(2)}, u32[]{:S(2)}) collective-permute-start(s16[784,256]{1,0:T(8,128)(2,1)S(1)} %get-tuple-element.66), channel_id=1, source_target_pairs={{0,192},{64,0},{128,64},{192,128},{1,193},{65,1},{129,65},{193,129... | collective-permute-start | bytes 1204232 | tf_op jit(solution)/shard_map/ppermute | solution.py:336
  86.9 3.7 %collective-permute-done.20.from_x = s16[2,208,512]{2,1,0:T(8,128)(2,1)S(1)} collective-permute-done((s16[2,208,512]{2,1,0:T(8,128)(2,1)S(1)}, s16[2,208,512]{2,1,0:T(8,128)(2,1)S(1)}, u32[]{:S(2)}, u32[]{:S(2)}) %collective-permute-start.20) | collective-permute-done | bytes 426016 | tf_op jit(solution)/shard_map/ppermute | solution.py:340
  93.2 2.7 %collective-permute-done.26.got1 = s16[784,256]{1,0:T(8,128)(2,1)S(1)} collective-permute-done((s16[784,256]{1,0:T(8,128)(2,1)S(1)}, s16[784,256]{1,0:T(8,128)(2,1)S(1)}, u32[]{:S(2)}, u32[]{:S(2)}) %collective-permute-start.26) | collective-permute-done | bytes 401440 | tf_op jit(solution)/shard_map/ppermute | solution.py:336
  97.7 3.0 %collective-permute-start.29 = (s16[208,128]{1,0:T(8,128)(2,1)S(1)}, s16[208,128]{1,0:T(8,128)(2,1)S(1)}, u32[]{:S(2)}, u32[]{:S(2)}) collective-permute-start(s16[208,128]{1,0:T(8,128)(2,1)S(1)} %get-tuple-element.69), channel_id=1, source_target_pairs={{0,24},{8,0},{16,8},{24,16},{1,25},{9,1},{17,9},{25,17},{2,26},{10... | collective-permute-start | bytes 159752 | tf_op jit(solution)/shard_map/ppermute | solution.py:336
  100.7 2.1 %collective-permute-done.28.got_a = s16[208,128]{1,0:T(8,128)(2,1)S(1)} collective-permute-done((s16[208,128]{1,0:T(8,128)(2,1)S(1)}, s16[208,128]{1,0:T(8,128)(2,1)S(1)}, u32[]{:S(2)}, u32[]{:S(2)}) %collective-permute-start.28) | collective-permute-done | bytes 53280 | tf_op jit(solution)/shard_map/ppermute | solution.py:336
  102.8 1.3 %collective-permute-done.29.got_b = s16[208,128]{1,0:T(8,128)(2,1)S(1)} collective-permute-done((s16[208,128]{1,0:T(8,128)(2,1)S(1)}, s16[208,128]{1,0:T(8,128)(2,1)S(1)}, u32[]{:S(2)}, u32[]{:S(2)}) %collective-permute-start.29) | collective-permute-done | bytes 53280 | tf_op jit(solution)/shard_map/ppermute | solution.py:336
  104.2 4.2 %collective-permute-start.30 = (s16[2,208,128]{2,1,0:T(8,128)(2,1)S(1)}, s16[2,208,128]{2,1,0:T(8,128)(2,1)S(1)}, u32[]{:S(2)}, u32[]{:S(2)}) collective-permute-start(s16[2,208,128]{2,1,0:T(8,128)(2,1)S(1)} %get-tuple-element.70), channel_id=1, source_target_pairs={{0,8},{8,16},{16,24},{24,0},{1,9},{9,17},{17,25},{25,1},{2,10},{10... | collective-permute-start | bytes 319496 | tf_op jit(solution)/shard_map/ppermute | solution.py:336
  108.4 3.8 %collective-permute-done.30.up = s16[2,208,128]{2,1,0:T(8,128)(2,1)S(1)} collective-permute-done((s16[2,208,128]{2,1,0:T(8,128)(2,1)S(1)}, s16[2,208,128]{2,1,0:T(8,128)(2,1)S(1)}, u32[]{:S(2)}, u32[]{:S(2)}) %collective-permute-start.30) | collective-permute-done | bytes 106528 | tf_op jit(solution)/shard_map/ppermute | solution.py:336
  112.2 2.4 %collective-permute-done.31.down = s16[2,208,128]{2,1,0:T(8,128)(2,1)S(1)} collective-permute-done((s16[2,208,128]{2,1,0:T(8,128)(2,1)S(1)}, s16[2,208,128]{2,1,0:T(8,128)(2,1)S(1)}, u32[]{:S(2)}, u32[]{:S(2)}) %collective-permute-start.31) | collective-permute-done | bytes 106528 | tf_op jit(solution)/shard_map/ppermute | solution.py:336
  115.6 4.8 %collective-permute-done.32.twin = s16[208,128]{1,0:T(8,128)(2,1)S(1)} collective-permute-done((s16[208,128]{1,0:T(8,128)(2,1)S(1)}, s16[208,128]{1,0:T(8,128)(2,1)S(1)}, u32[]{:S(2)}, u32[]{:S(2)}) %collective-permute-start.32) | collective-permute-done | bytes 53280 | tf_op jit(solution)/shard_map/ppermute | solution.py:340
  (59 shorter events, 18.7 us)
Async XLA Ops:
  0.6 5.9 %collective-permute-start = (bf16[192,128]{1,0:T(8,128)(2,1)}, bf16[192,128]{1,0:T(8,128)(2,1)S(1)}, u32[]{:S(2)}, u32[]{:S(2)}) collective-permute-start(bf16[192,128]{1,0:T(8,128)(2,1)} %image.1), channel_id=1, source_target_pairs={{0,32},{32,0},{1,33},{33,1},{2,34},{34,2},{3,35},{35,3},{4,36},{36... | collective-permute-start | bytes 147464 | tf_op jit(solution)/shard_map/ppermute | solution.py:340
  7.3 13.6 %collective-permute-start.3 = (bf16[2,192,128]{2,1,0:T(8,128)(2,1)S(1)}, bf16[2,192,128]{2,1,0:T(8,128)(2,1)S(1)}, u32[]{:S(2)}, u32[]{:S(2)}) collective-permute-start(bf16[2,192,128]{2,1,0:T(8,128)(2,1)S(1)} %pair.1.after.both), channel_id=1, source_target_pairs={{0,24},{8,0},{16,8},{24,16},{1,25},{9,1},{17,9},{25,17},{2,26},{10... | collective-permute-start | bytes 294920 | tf_op jit(solution)/shard_map/ppermute | solution.py:336
  13.7 10.5 %collective-permute-start.2 = (bf16[2,192,128]{2,1,0:T(8,128)(2,1)S(1)}, bf16[2,192,128]{2,1,0:T(8,128)(2,1)S(1)}, u32[]{:S(2)}, u32[]{:S(2)}) collective-permute-start(bf16[2,192,128]{2,1,0:T(8,128)(2,1)S(1)} %pair.1.after.both), channel_id=1, source_target_pairs={{0,16},{8,24},{16,0},{24,8},{1,17},{9,25},{17,1},{25,9},{2,18},{10... | collective-permute-start | bytes 294920 | tf_op jit(solution)/shard_map/ppermute | solution.py:336
  14.7 9.5 %collective-permute-start.1 = (bf16[2,192,128]{2,1,0:T(8,128)(2,1)S(1)}, bf16[2,192,128]{2,1,0:T(8,128)(2,1)S(1)}, u32[]{:S(2)}, u32[]{:S(2)}) collective-permute-start(bf16[2,192,128]{2,1,0:T(8,128)(2,1)S(1)} %pair.1.after.both), channel_id=1, source_target_pairs={{0,8},{8,16},{16,24},{24,0},{1,9},{9,17},{17,25},{25,1},{2,10},{10... | collective-permute-start | bytes 294920 | tf_op jit(solution)/shard_map/ppermute | solution.py:336
  19.5 8.9 %collective-permute-start.4 = (bf16[192,1024]{1,0:T(8,128)(2,1)S(1)}, bf16[192,1024]{1,0:T(8,128)(2,1)S(1)}, u32[]{:S(2)}, u32[]{:S(2)}) collective-permute-start(bf16[192,1024]{1,0:T(8,128)(2,1)S(1)} %get-tuple-element.41.keys), channel_id=1, source_target_pairs={{0,2},{2,0},{1,3},{3,1},{4,6},{6,4},{5,7},{7,5},{8,10},{10,8},{9,1... | collective-permute-start | bytes 1179656 | tf_op jit(solution)/shard_map/ppermute | solution.py:340
  24.3 11.5 %collective-permute-start.5 = (bf16[192,1024]{1,0:T(8,128)(2,1)S(1)}, bf16[192,1024]{1,0:T(8,128)(2,1)S(1)}, u32[]{:S(2)}, u32[]{:S(2)}) collective-permute-start(bf16[192,1024]{1,0:T(8,128)(2,1)S(1)} %hold.1.own), channel_id=1, source_target_pairs={{0,4},{4,0},{1,5},{5,1},{2,6},{6,2},{3,7},{7,3},{8,12},{12,8},{9,1... | collective-permute-start | bytes 1179656 | tf_op jit(solution)/shard_map/ppermute | solution.py:340
  25.3 11.9 %collective-permute-start.9 = (bf16[8,192,128]{2,1,0:T(8,128)(2,1)S(1)}, bf16[8,192,128]{2,1,0:T(8,128)(2,1)S(1)}, u32[]{:S(2)}, u32[]{:S(2)}) collective-permute-start(bf16[8,192,128]{2,1,0:T(8,128)(2,1)S(1)} %stack.1.after.refs_2_), channel_id=1, source_target_pairs={{0,192},{64,0},{128,64},{192,128},{1,193},{65,1},{129,65},{193,129... | collective-permute-start | bytes 1179656 | tf_op jit(solution)/shard_map/ppermute | solution.py:336
  28.3 10.9 %collective-permute-start.8 = (bf16[8,192,128]{2,1,0:T(8,128)(2,1)S(1)}, bf16[8,192,128]{2,1,0:T(8,128)(2,1)S(1)}, u32[]{:S(2)}, u32[]{:S(2)}) collective-permute-start(bf16[8,192,128]{2,1,0:T(8,128)(2,1)S(1)} %stack.1.after.refs_2_), channel_id=1, source_target_pairs={{0,64},{64,128},{128,192},{192,0},{1,65},{65,129},{129,193},{193,1... | collective-permute-start | bytes 1179656 | tf_op jit(solution)/shard_map/ppermute | solution.py:336
  28.4 14.1 %collective-permute-start.7 = (bf16[96,1024]{1,0:T(8,128)(2,1)S(1)}, bf16[96,1024]{1,0:T(8,128)(2,1)S(1)}, u32[]{:S(2)}, u32[]{:S(2)}) collective-permute-start(bf16[96,1024]{1,0:T(8,128)(2,1)S(1)} %low.1), channel_id=1, source_target_pairs={{0,4},{4,0},{1,5},{5,1},{2,6},{6,2},{3,7},{7,3},{8,12},{12,8},{9,1... | collective-permute-start | bytes 589832 | tf_op jit(solution)/shard_map/ppermute | solution.py:340
  35.9 6.6 %collective-permute-start.6 = (bf16[96,1024]{1,0:T(8,128)(2,1)S(1)}, bf16[96,1024]{1,0:T(8,128)(2,1)S(1)}, u32[]{:S(2)}, u32[]{:S(2)}) collective-permute-start(bf16[96,1024]{1,0:T(8,128)(2,1)S(1)} %top.1), channel_id=1, source_target_pairs={{0,2},{2,0},{1,3},{3,1},{4,6},{6,4},{5,7},{7,5},{8,10},{10,8},{9,1... | collective-permute-start | bytes 589832 | tf_op jit(solution)/shard_map/ppermute | solution.py:340
  39.2 7.0 %collective-permute-start.10 = (bf16[4,192,128]{2,1,0:T(8,128)(2,1)S(1)}, bf16[4,192,128]{2,1,0:T(8,128)(2,1)S(1)}, u32[]{:S(2)}, u32[]{:S(2)}) collective-permute-start(bf16[4,192,128]{2,1,0:T(8,128)(2,1)S(1)} %get-tuple-element.43), channel_id=1, source_target_pairs={{0,64},{64,128},{128,192},{192,0},{1,65},{65,129},{129,193},{193,1... | collective-permute-start | bytes 589832 | tf_op jit(solution)/shard_map/ppermute | solution.py:336
  39.3 6.9 %collective-permute-start.11 = (bf16[4,192,128]{2,1,0:T(8,128)(2,1)S(1)}, bf16[4,192,128]{2,1,0:T(8,128)(2,1)S(1)}, u32[]{:S(2)}, u32[]{:S(2)}) collective-permute-start(bf16[4,192,128]{2,1,0:T(8,128)(2,1)S(1)} %get-tuple-element.44), channel_id=1, source_target_pairs={{0,192},{64,0},{128,64},{192,128},{1,193},{65,1},{129,65},{193,129... | collective-permute-start | bytes 589832 | tf_op jit(solution)/shard_map/ppermute | solution.py:336
  46.2 3.7 %collective-permute-start.12 = (bf16[768,1024]{1,0:T(8,128)(2,1)S(1)}, bf16[768,1024]{1,0:T(8,128)(2,1)S(1)}, u32[]{:S(2)}, u32[]{:S(2)}) collective-permute-start(bf16[768,1024]{1,0:T(8,128)(2,1)S(1)} %join.1.refs_0_.refs_9_), channel_id=1, source_target_pairs={{0,1},{1,0},{2,3},{3,2},{4,5},{5,4},{6,7},{7,6},{8,9},{9,8},{10,11... | collective-permute-start | bytes 4718600 | tf_op jit(solution)/shard_map/ppermute | solution.py:340
  54.8 5.4 %collective-permute-start.13 = (f32[2,768]{1,0:T(2,128)S(1)}, f32[2,768]{1,0:T(2,128)S(1)}, u32[]{:S(2)}, u32[]{:S(2)}) collective-permute-start(f32[2,768]{1,0:T(2,128)S(1)} %get-tuple-element.46.r), channel_id=1, source_target_pairs={{0,8},{8,0},{16,24},{24,16},{1,9},{9,1},{17,25},{25,17},{2,10},{10... | collective-permute-start | bytes 18440 | tf_op jit(solution)/shard_map/ppermute | solution.py:340
  56.7 9.7 %collective-permute-start.18 = (f32[2,1536]{1,0:T(2,128)S(1)}, f32[2,1536]{1,0:T(2,128)S(1)}, u32[]{:S(2)}, u32[]{:S(2)}) collective-permute-start(f32[2,1536]{1,0:T(2,128)S(1)} %meet.1.refs_2_), channel_id=1, source_target_pairs={{0,6},{2,4},{4,2},{6,0},{1,7},{3,5},{5,3},{7,1},{8,14},{10,12},{12... | collective-permute-start | bytes 36872 | tf_op jit(solution)/shard_map/ppermute | solution.py:386
  57.7 8.6 %collective-permute-start.17 = (f32[2,1536]{1,0:T(2,128)S(1)}, f32[2,1536]{1,0:T(2,128)S(1)}, u32[]{:S(2)}, u32[]{:S(2)}) collective-permute-start(f32[2,1536]{1,0:T(2,128)S(1)} %meet.1.refs_2_), channel_id=1, source_target_pairs={{0,4},{2,6},{4,0},{6,2},{1,5},{3,7},{5,1},{7,3},{8,12},{10,14},{12... | collective-permute-start | bytes 36872 | tf_op jit(solution)/shard_map/ppermute | solution.py:386
  59.4 6.9 %collective-permute-start.16 = (f32[2,1536]{1,0:T(2,128)S(1)}, f32[2,1536]{1,0:T(2,128)S(1)}, u32[]{:S(2)}, u32[]{:S(2)}) collective-permute-start(f32[2,1536]{1,0:T(2,128)S(1)} %meet.1.refs_2_), channel_id=1, source_target_pairs={{0,2},{2,0},{4,6},{6,4},{1,3},{3,1},{5,7},{7,5},{8,10},{10,8},{12,... | collective-permute-start | bytes 36872 | tf_op jit(solution)/shard_map/ppermute | solution.py:386
  60.3 6.0 %collective-permute-start.14 = (f32[2,768]{1,0:T(2,128)S(1)}, f32[2,768]{1,0:T(2,128)S(1)}, u32[]{:S(2)}, u32[]{:S(2)}) collective-permute-start(f32[2,768]{1,0:T(2,128)S(1)} %meet_rows.1.refs_0_), channel_id=1, source_target_pairs={{0,24},{8,16},{16,8},{24,0},{1,25},{9,17},{17,9},{25,1},{2,26},{10... | collective-permute-start | bytes 18440 | tf_op jit(solution)/shard_map/ppermute | solution.py:340
  74.2 3.6 %collective-permute-start.19 = (s16[4,208,1024]{2,1,0:T(8,128)(2,1)S(1)}, s16[4,208,1024]{2,1,0:T(8,128)(2,1)S(1)}, u32[]{:S(2)}, u32[]{:S(2)}) collective-permute-start(s16[4,208,1024]{2,1,0:T(8,128)(2,1)S(1)} %get-tuple-element.51), channel_id=1, source_target_pairs={{0,1},{1,0},{2,3},{3,2},{4,5},{5,4},{6,7},{7,6},{8,9},{9,8},{10,11... | collective-permute-start | bytes 5111816 | tf_op jit(solution)/shard_map/ppermute | solution.py:340
  74.2 9.0 %collective-permute-start.24 = (s16[400,256]{1,0:T(8,128)(2,1)S(1)}, s16[400,256]{1,0:T(8,128)(2,1)S(1)}, u32[]{:S(2)}, u32[]{:S(2)}) collective-permute-start(s16[400,256]{1,0:T(8,128)(2,1)S(1)} %get-tuple-element.63), channel_id=1, source_target_pairs={{0,64},{64,128},{128,192},{192,0},{1,65},{65,129},{129,193},{193,1... | collective-permute-start | bytes 614408 | tf_op jit(solution)/shard_map/ppermute | solution.py:336
  74.2 9.0 %collective-permute-start.25 = (s16[400,256]{1,0:T(8,128)(2,1)S(1)}, s16[400,256]{1,0:T(8,128)(2,1)S(1)}, u32[]{:S(2)}, u32[]{:S(2)}) collective-permute-start(s16[400,256]{1,0:T(8,128)(2,1)S(1)} %get-tuple-element.64), channel_id=1, source_target_pairs={{0,192},{64,0},{128,64},{192,128},{1,193},{65,1},{129,65},{193,129... | collective-permute-start | bytes 614408 | tf_op jit(solution)/shard_map/ppermute | solution.py:336
  78.7 11.9 %collective-permute-start.20 = (s16[2,208,512]{2,1,0:T(8,128)(2,1)S(1)}, s16[2,208,512]{2,1,0:T(8,128)(2,1)S(1)}, u32[]{:S(2)}, u32[]{:S(2)}) collective-permute-start(s16[2,208,512]{2,1,0:T(8,128)(2,1)S(1)} %get-tuple-element.55), channel_id=1, source_target_pairs={{0,2},{2,0},{1,3},{3,1},{4,6},{6,4},{5,7},{7,5},{8,10},{10,8},{9,1... | collective-permute-start | bytes 1277960 | tf_op jit(solution)/shard_map/ppermute | solution.py:340
  79.9 11.6 %collective-permute-start.21 = (s16[2,208,512]{2,1,0:T(8,128)(2,1)S(1)}, s16[2,208,512]{2,1,0:T(8,128)(2,1)S(1)}, u32[]{:S(2)}, u32[]{:S(2)}) collective-permute-start(s16[2,208,512]{2,1,0:T(8,128)(2,1)S(1)} %get-tuple-element.56), channel_id=1, source_target_pairs={{0,4},{4,0},{1,5},{5,1},{2,6},{6,2},{3,7},{7,3},{8,12},{12,8},{9,1... | collective-permute-start | bytes 1277960 | tf_op jit(solution)/shard_map/ppermute | solution.py:340
  83.5 12.4 %collective-permute-start.26 = (s16[784,256]{1,0:T(8,128)(2,1)S(1)}, s16[784,256]{1,0:T(8,128)(2,1)S(1)}, u32[]{:S(2)}, u32[]{:S(2)}) collective-permute-start(s16[784,256]{1,0:T(8,128)(2,1)S(1)} %get-tuple-element.65), channel_id=1, source_target_pairs={{0,64},{64,128},{128,192},{192,0},{1,65},{65,129},{129,193},{193,1... | collective-permute-start | bytes 1204232 | tf_op jit(solution)/shard_map/ppermute | solution.py:336
  84.7 11.2 %collective-permute-start.27 = (s16[784,256]{1,0:T(8,128)(2,1)S(1)}, s16[784,256]{1,0:T(8,128)(2,1)S(1)}, u32[]{:S(2)}, u32[]{:S(2)}) collective-permute-start(s16[784,256]{1,0:T(8,128)(2,1)S(1)} %get-tuple-element.66), channel_id=1, source_target_pairs={{0,192},{64,0},{128,64},{192,128},{1,193},{65,1},{129,65},{193,129... | collective-permute-start | bytes 1204232 | tf_op jit(solution)/shard_map/ppermute | solution.py:336
  91.9 12.1 %collective-permute-start.22 = (s16[208,512]{1,0:T(8,128)(2,1)S(1)}, s16[208,512]{1,0:T(8,128)(2,1)S(1)}, u32[]{:S(2)}, u32[]{:S(2)}) collective-permute-start(s16[208,512]{1,0:T(8,128)(2,1)S(1)} %get-tuple-element.58), channel_id=1, source_target_pairs={{0,2},{2,0},{1,3},{3,1},{4,6},{6,4},{5,7},{7,5},{8,10},{10,8},{9,1... | collective-permute-start | bytes 638984 | tf_op jit(solution)/shard_map/ppermute | solution.py:340
  92.9 11.2 %collective-permute-start.23 = (s16[208,512]{1,0:T(8,128)(2,1)S(1)}, s16[208,512]{1,0:T(8,128)(2,1)S(1)}, u32[]{:S(2)}, u32[]{:S(2)}) collective-permute-start(s16[208,512]{1,0:T(8,128)(2,1)S(1)} %get-tuple-element.59), channel_id=1, source_target_pairs={{0,4},{4,0},{1,5},{5,1},{2,6},{6,2},{3,7},{7,3},{8,12},{12,8},{9,1... | collective-permute-start | bytes 638984 | tf_op jit(solution)/shard_map/ppermute | solution.py:340
  96.5 6.3 %collective-permute-start.28 = (s16[208,128]{1,0:T(8,128)(2,1)S(1)}, s16[208,128]{1,0:T(8,128)(2,1)S(1)}, u32[]{:S(2)}, u32[]{:S(2)}) collective-permute-start(s16[208,128]{1,0:T(8,128)(2,1)S(1)} %get-tuple-element.68), channel_id=1, source_target_pairs={{0,8},{8,16},{16,24},{24,0},{1,9},{9,17},{17,25},{25,1},{2,10},{10... | collective-permute-start | bytes 159752 | tf_op jit(solution)/shard_map/ppermute | solution.py:336
  97.7 6.4 %collective-permute-start.29 = (s16[208,128]{1,0:T(8,128)(2,1)S(1)}, s16[208,128]{1,0:T(8,128)(2,1)S(1)}, u32[]{:S(2)}, u32[]{:S(2)}) collective-permute-start(s16[208,128]{1,0:T(8,128)(2,1)S(1)} %get-tuple-element.69), channel_id=1, source_target_pairs={{0,24},{8,0},{16,8},{24,16},{1,25},{9,1},{17,9},{25,17},{2,26},{10... | collective-permute-start | bytes 159752 | tf_op jit(solution)/shard_map/ppermute | solution.py:336
  104.2 8.0 %collective-permute-start.30 = (s16[2,208,128]{2,1,0:T(8,128)(2,1)S(1)}, s16[2,208,128]{2,1,0:T(8,128)(2,1)S(1)}, u32[]{:S(2)}, u32[]{:S(2)}) collective-permute-start(s16[2,208,128]{2,1,0:T(8,128)(2,1)S(1)} %get-tuple-element.70), channel_id=1, source_target_pairs={{0,8},{8,16},{16,24},{24,0},{1,9},{9,17},{17,25},{25,1},{2,10},{10... | collective-permute-start | bytes 319496 | tf_op jit(solution)/shard_map/ppermute | solution.py:336
  108.4 6.2 %collective-permute-start.31 = (s16[2,208,128]{2,1,0:T(8,128)(2,1)S(1)}, s16[2,208,128]{2,1,0:T(8,128)(2,1)S(1)}, u32[]{:S(2)}, u32[]{:S(2)}) collective-permute-start(s16[2,208,128]{2,1,0:T(8,128)(2,1)S(1)} %get-tuple-element.71), channel_id=1, source_target_pairs={{0,24},{8,0},{16,8},{24,16},{1,25},{9,1},{17,9},{25,17},{2,26},{10... | collective-permute-start | bytes 319496 | tf_op jit(solution)/shard_map/ppermute | solution.py:336
  114.7 5.7 %collective-permute-start.32 = (s16[208,128]{1,0:T(8,128)(2,1)S(1)}, s16[208,128]{1,0:T(8,128)(2,1)S(1)}, u32[]{:S(2)}, u32[]{:S(2)}) collective-permute-start(s16[208,128]{1,0:T(8,128)(2,1)S(1)} %get-tuple-element.73), channel_id=1, source_target_pairs={{0,32},{32,0},{1,33},{33,1},{2,34},{34,2},{3,35},{35,3},{4,36},{36... | collective-permute-start | bytes 159752 | tf_op jit(solution)/shard_map/ppermute | solution.py:340
  (4 other events, 4.5 us)

commit v7 on v6

--- a/solution.py
+++ b/solution.py
@@ -102,8 +102,8 @@
     cols[...] = (lax.axis_index("zh") * n_ks + (block - k) * rows + p).astype(F32)
 
 
-def join_kernel(own, x, z, d_top, d_low, after_a, after_b, out):
-    del after_a, after_b
+def join_kernel(own, x, z, d_top, d_low, after, out):
+    del after
     rows = own.shape[0]
     xl = lax.axis_index("xl")
     for k, parts in enumerate(((own,), (x,), (z,), (d_top, d_low))):
@@ -295,41 +295,20 @@
     encode(keep_x[...] + decode(from_z[1]), to_x)
 
 
-def last_kernel(own_key, from_x, from_z, own, twin, key_out, image_out):
+def last_kernel(own_key, from_x, from_z, pieces, key_out, image_out):
     n = own_key.shape[1] // 2
     key_out[:, :n] = own_key[:, :n] + decode(from_z[...])
     key_out[:, n:] = own_key[:, n:] + decode(from_x[...])
-    image_out[...] = own[...] + decode(twin[...])
-
-
-def image_sum_kernel(after, own, got1, got3, keep, to_a, to_b, total):
-    del after
-    zh, xh = lax.axis_index("zh"), lax.axis_index("xh")
-    rows, width = keep.shape[1:]
-    total[...] = own[...] + decode(got1[...]) + decode(got3[...])
-
-    def piece(o, j):
-        row = pl.multiple_of(lax.rem(zh + j, 4) * rows, 16)
-        return total[pl.ds(row, rows), pl.ds(pl.multiple_of((xh ^ o) * width, 128), width)]
-
-    encode(piece(0, 2), to_a)
-    encode(piece(1, 2), to_b)
-    for o in range(2):
-        for at, j in enumerate((0, 1, 3)):
-            keep[3 * o + at] = piece(o, j)
-
-
-def image_relay_kernel(after_x, after_z, keep, got_a, got_b, up, down):
+    image_out[...] = sum(decode(pieces[k]) for k in range(pieces.shape[0]))
+
+
+def image_sum_kernel(after_x, after_z, own, got1, got3, out):
     del after_x, after_z
-    encode(keep[1] + decode(got_a[...]), up.at[0])
-    encode(keep[4], up.at[1])
-    encode(keep[2], down.at[0])
-    encode(keep[5] + decode(got_b[...]), down.at[1])
-
-
-def image_twin_kernel(keep, up, down, own, to_twin):
-    own[...] = keep[0] + decode(up[0]) + decode(down[0])
-    encode(keep[3] + decode(up[1]) + decode(down[1]), to_twin)
+    rows, width = out.shape[1] - PAD, out.shape[2]
+    total = own[...] + decode(got1[...]) + decode(got3[...])
+    for xh in range(2):
+        for zh in range(4):
+            encode(total[zh * rows : (zh + 1) * rows, xh * width : (xh + 1) * width], out.at[4 * xh + zh])
 
 
 def shift(x, axis, n, k):
@@ -366,10 +345,10 @@
     d_top = flip(call(top_kernel, quarter, "top", 8, in_specs=[vmem])(key_z), "xl", 2, 1)
     half_block = shape((nzh, rows, width), BF16)
     ia, ib = call(turn_kernel, [half_block] * 2, "turn", 12, in_specs=[vmem] * 2)(i1, i3)
+    k0 = call(join_kernel, shape((half, d), BF16), "join", 12, in_specs=[vmem] * 6)(
+        held, key_x, key_z, d_top, d_low, ia
+    )
     ia, ib = shift(ia, "y", 4, 1), shift(ib, "y", 4, 3)
-    k0 = call(join_kernel, shape((half, d), BF16), "join", 12, in_specs=[vmem] * 7)(
-        held, key_x, key_z, d_top, d_low, ia, ib
-    )
     ks = [k0, flip(k0, "core", 2, 1)]
 
     tile = min(384, n_im)
@@ -413,24 +392,13 @@
         in_specs=[vmem] * 5,
     )(own_key, keep_x, keep_z, flip(to_x, "xl", 2, 1), flip(to_z, "zl", 2, 1))
     from_x, from_z = flip(to_x, "xl", 2, 1), flip(to_z, "zl", 2, 1)
-    coded, coded2 = shape((rows + PAD, width), I16), shape((2, rows + PAD, width), I16)
-    keep, to_a, to_b = call(
-        image_sum_kernel,
-        [shape((6, rows, width), F32), coded, coded],
-        "image_sum",
-        12,
-        in_specs=[vmem] * 4,
-        scratch_shapes=[pltpu.VMEM((n_im, 2 * width), F32)],
-    )(own_key, own, q1, q3)
-    up, down = call(image_relay_kernel, [coded2] * 2, "image_relay", 8, in_specs=[vmem] * 5)(
-        from_x, from_z, keep, shift(to_a, "zh", 4, 1), shift(to_b, "zh", 4, 3)
-    )
-    own, to_twin = call(image_twin_kernel, [shape((rows, width), F32), coded], "image_twin", 8, in_specs=[vmem] * 3)(
-        keep, shift(up, "zh", 4, 1), shift(down, "zh", 4, 3)
-    )
+    pieces = call(
+        image_sum_kernel, shape((8, rows + PAD, width), I16), "image_sum", 12, in_specs=[vmem] * 5
+    )(from_x, from_z, own, q1, q3)
+    pieces = lax.all_to_all(pieces, ("xh", "zh"), 0, 0)
     modality_grad, image_grad = call(
-        last_kernel, [shape((rows, d), F32), shape((rows, width), F32)], "last", 8, in_specs=[vmem] * 5
-    )(own_key, from_x, from_z, own, flip(to_twin, "xh", 2, 1))
+        last_kernel, [shape((rows, d), F32), shape((rows, width), F32)], "last", 8, in_specs=[vmem] * 4
+    )(own_key, from_x, from_z, pieces)
     return (image_grad, modality_grad[None], row_loss, col_loss)
 
 

time: 122 us -> 127 us (1.041)
  the two profiles are of different devices: /device:TPU:4 before, /device:TPU:56 now
where the time goes in v7:
time: 127 us
  starting transfers between devices  42.6 us (34%)
  waiting for transfers between devices  42.1 us (33%)
  blocking collectives  22.4 us (18%)
  Pallas kernels  16.1 us (13%)
  local copies, waits for them, and re-layouts  2.53 us (2%)
    ppermute x11, waiting for transfers between devices, shift(): return lax.ppermute(x, axis, [(i, (i + k) % n) for i in range(n)])  22.6 us
    all_to_all x1, blocking collectives, on_device(): pieces = lax.all_to_all(pieces, ('xh', 'zh'), 0, 0)  22.4 us
    ppermute x11, starting transfers between devices, shift(): return lax.ppermute(x, axis, [(i, (i + k) % n) for i in range(n)])  20.9 us
    ppermute x14, waiting for transfers between devices, flip(): return lax.ppermute(x, axis, [(i, i ^ d) for i in range(n)])  19.5 us
    ppermute x14, starting transfers between devices, flip(): return lax.ppermute(x, axis, [(i, i ^ d) for i in range(n)])  18.2 us
    pallas_call x1, Pallas kernels, on_device(): call(functools.partial(weights_kernel, scale, tile), outs, 'weights', 36,...  7.84 us
    pallas_call x1, Pallas kernels, on_device(): call(functools.partial(scores_kernel, scale), [shape((n_im, n_ks), F32),...  4.68 us
    ppermute x3, starting transfers between devices, on_device(): lax.ppermute(cs, ('zl', 'xl'), [(i, i ^ k) for i in range(4)])  3.58 us
  transfers between devices with their start and end apart: 28, of which 13 were waited for; matrix products, arithmetic and copies ran while one was open for 0% of the time, Pallas kernels for 1%

profile of v7, /device:TPU:56, one launch (start us, length us, event | category | flops | bytes accessed | tf_op | source)
XLA Modules:
  0.0 126.5 jit_solution(11282262784944006497)
XLA Ops:
  0.6 3.1 %collective-permute-start = (bf16[192,128]{1,0:T(8,128)(2,1)}, bf16[192,128]{1,0:T(8,128)(2,1)S(1)}, u32[]{:S(2)}, u32[]{:S(2)}) collective-permute-start(bf16[192,128]{1,0:T(8,128)(2,1)} %image.1), channel_id=1, source_target_pairs={{0,32},{32,0},{1,33},{33,1},{2,34},{34,2},{3,35},{35,3},{4,36},{36... | collective-permute-start | bytes 147464 | tf_op jit(solution)/shard_map/ppermute | solution.py:319
  3.7 2.8 %collective-permute-done.twin = bf16[192,128]{1,0:T(8,128)(2,1)S(1)} collective-permute-done((bf16[192,128]{1,0:T(8,128)(2,1)}, bf16[192,128]{1,0:T(8,128)(2,1)S(1)}, u32[]{:S(2)}, u32[]{:S(2)}) %collective-permute-start) | collective-permute-done | bytes 49184 | tf_op jit(solution)/shard_map/ppermute | solution.py:319
  7.3 5.5 %collective-permute-start.3 = (bf16[2,192,128]{2,1,0:T(8,128)(2,1)S(1)}, bf16[2,192,128]{2,1,0:T(8,128)(2,1)S(1)}, u32[]{:S(2)}, u32[]{:S(2)}) collective-permute-start(bf16[2,192,128]{2,1,0:T(8,128)(2,1)S(1)} %pair.1.after.both), channel_id=1, source_target_pairs={{0,24},{8,0},{16,8},{24,16},{1,25},{9,1},{17,9},{25,17},{2,26},{10... | collective-permute-start | bytes 294920 | tf_op jit(solution)/shard_map/ppermute | solution.py:315
  12.8 1.4 %collective-permute-start.2 = (bf16[2,192,128]{2,1,0:T(8,128)(2,1)S(1)}, bf16[2,192,128]{2,1,0:T(8,128)(2,1)S(1)}, u32[]{:S(2)}, u32[]{:S(2)}) collective-permute-start(bf16[2,192,128]{2,1,0:T(8,128)(2,1)S(1)} %pair.1.after.both), channel_id=1, source_target_pairs={{0,16},{8,24},{16,0},{24,8},{1,17},{9,25},{17,1},{25,9},{2,18},{10... | collective-permute-start | bytes 294920 | tf_op jit(solution)/shard_map/ppermute | solution.py:315
  14.3 2.4 %collective-permute-start.1 = (bf16[2,192,128]{2,1,0:T(8,128)(2,1)S(1)}, bf16[2,192,128]{2,1,0:T(8,128)(2,1)S(1)}, u32[]{:S(2)}, u32[]{:S(2)}) collective-permute-start(bf16[2,192,128]{2,1,0:T(8,128)(2,1)S(1)} %pair.1.after.both), channel_id=1, source_target_pairs={{0,8},{8,16},{16,24},{24,0},{1,9},{9,17},{17,25},{25,1},{2,10},{10... | collective-permute-start | bytes 294920 | tf_op jit(solution)/shard_map/ppermute | solution.py:315
  18.6 1.5 %collective-permute-start.4 = (bf16[192,1024]{1,0:T(8,128)(2,1)S(1)}, bf16[192,1024]{1,0:T(8,128)(2,1)S(1)}, u32[]{:S(2)}, u32[]{:S(2)}) collective-permute-start(bf16[192,1024]{1,0:T(8,128)(2,1)S(1)} %get-tuple-element.34.keys), channel_id=1, source_target_pairs={{0,2},{2,0},{1,3},{3,1},{4,6},{6,4},{5,7},{7,5},{8,10},{10,8},{9,1... | collective-permute-start | bytes 1179656 | tf_op jit(solution)/shard_map/ppermute | solution.py:319
  20.1 2.8 %collective-permute-done.2.b2 = bf16[2,192,128]{2,1,0:T(8,128)(2,1)S(1)} collective-permute-done((bf16[2,192,128]{2,1,0:T(8,128)(2,1)S(1)}, bf16[2,192,128]{2,1,0:T(8,128)(2,1)S(1)}, u32[]{:S(2)}, u32[]{:S(2)}) %collective-permute-start.2) | collective-permute-done | bytes 98336 | tf_op jit(solution)/shard_map/ppermute | solution.py:315
  23.3 1.2 collective-permute-start.5
  25.3 2.5 %collective-permute-start.8 = (bf16[8,192,128]{2,1,0:T(8,128)(2,1)S(1)}, bf16[8,192,128]{2,1,0:T(8,128)(2,1)S(1)}, u32[]{:S(2)}, u32[]{:S(2)}) collective-permute-start(bf16[8,192,128]{2,1,0:T(8,128)(2,1)S(1)} %stack.1.after.refs_2_), channel_id=1, source_target_pairs={{0,64},{64,128},{128,192},{192,0},{1,65},{65,129},{129,193},{193,1... | collective-permute-start | bytes 1179656 | tf_op jit(solution)/shard_map/ppermute | solution.py:315
  28.7 6.7 %collective-permute-done.5.z = bf16[192,1024]{1,0:T(8,128)(2,1)S(1)} collective-permute-done((bf16[192,1024]{1,0:T(8,128)(2,1)S(1)}, bf16[192,1024]{1,0:T(8,128)(2,1)S(1)}, u32[]{:S(2)}, u32[]{:S(2)}) %collective-permute-start.5) | collective-permute-done | bytes 393248 | tf_op jit(solution)/shard_map/ppermute | solution.py:319
  35.4 1.6 %collective-permute-start.6 = (bf16[96,1024]{1,0:T(8,128)(2,1)S(1)}, bf16[96,1024]{1,0:T(8,128)(2,1)S(1)}, u32[]{:S(2)}, u32[]{:S(2)}) collective-permute-start(bf16[96,1024]{1,0:T(8,128)(2,1)S(1)} %top.1), channel_id=1, source_target_pairs={{0,2},{2,0},{1,3},{3,1},{4,6},{6,4},{5,7},{7,5},{8,10},{10,8},{9,1... | collective-permute-start | bytes 589832 | tf_op jit(solution)/shard_map/ppermute | solution.py:319
  37.8 3.4 %collective-permute-done.6.d_top = bf16[96,1024]{1,0:T(8,128)(2,1)S(1)} collective-permute-done((bf16[96,1024]{1,0:T(8,128)(2,1)S(1)}, bf16[96,1024]{1,0:T(8,128)(2,1)S(1)}, u32[]{:S(2)}, u32[]{:S(2)}) %collective-permute-start.6) | collective-permute-done | bytes 196640 | tf_op jit(solution)/shard_map/ppermute | solution.py:319
  42.2 2.5 %collective-permute-start.11 = (bf16[4,192,128]{2,1,0:T(8,128)(2,1)S(1)}, bf16[4,192,128]{2,1,0:T(8,128)(2,1)S(1)}, u32[]{:S(2)}, u32[]{:S(2)}) collective-permute-start(bf16[4,192,128]{2,1,0:T(8,128)(2,1)S(1)} %get-tuple-element.36.after), channel_id=1, source_target_pairs={{0,64},{64,128},{128,192},{192,0},{1,65},{65,129},{129,193},{193,1... | collective-permute-start | bytes 589832 | tf_op jit(solution)/shard_map/ppermute | solution.py:315
  44.7 5.2 %collective-permute-done.12.refs_6_ = bf16[4,192,128]{2,1,0:T(8,128)(2,1)S(1)} collective-permute-done((bf16[4,192,128]{2,1,0:T(8,128)(2,1)S(1)}, bf16[4,192,128]{2,1,0:T(8,128)(2,1)S(1)}, u32[]{:S(2)}, u32[]{:S(2)}) %collective-permute-start.12) | collective-permute-done | bytes 196640 | tf_op jit(solution)/shard_map/ppermute | solution.py:315
  49.9 4.7 %scores.1 = (f32[768,1536]{1,0:T(8,128)S(1)}, bf16[768,1024]{1,0:T(8,128)(2,1)S(1)}, f32[2,768]{1,0:T(2,128)S(1)}, f32[2,1536]{1,0:T(2,128)S(1)}) custom-call(bf16[768,1024]{1,0:T(8,128)(2,1)S(1)} %join.1.refs_0_.refs_9_, bf16[768,1024]{1,0:T(8,128)(2,1)S(1)} %collective-permute-done.10.refs_1_.refs_10_, bf16[8,192,128]{2,1,0:T(8,128)(2,1)S(1)} %stack.1.after.refs_2_, ...), custom_call_target="tpu_custom_call" | custom-call | flops 1000 | bytes 1000 | tf_op jit(solution)/shard_map/scores/pallas_call | solution.py:355
  54.7 1.8 %collective-permute-start.13 = (f32[2,768]{1,0:T(2,128)S(1)}, f32[2,768]{1,0:T(2,128)S(1)}, u32[]{:S(2)}, u32[]{:S(2)}) collective-permute-start(f32[2,768]{1,0:T(2,128)S(1)} %get-tuple-element.39.r), channel_id=1, source_target_pairs={{0,8},{8,0},{16,24},{24,16},{1,9},{9,1},{17,25},{25,17},{2,10},{10... | collective-permute-start | bytes 18440 | tf_op jit(solution)/shard_map/ppermute | solution.py:319
  56.6 1.0 collective-permute-start.18
  57.6 2.0 %collective-permute-start.17 = (f32[2,1536]{1,0:T(2,128)S(1)}, f32[2,1536]{1,0:T(2,128)S(1)}, u32[]{:S(2)}, u32[]{:S(2)}) collective-permute-start(f32[2,1536]{1,0:T(2,128)S(1)} %meet.1.refs_2_), channel_id=1, source_target_pairs={{0,4},{2,6},{4,0},{6,2},{1,5},{3,7},{5,1},{7,3},{8,12},{10,14},{12... | collective-permute-start | bytes 36872 | tf_op jit(solution)/shard_map/ppermute | solution.py:365
  60.2 3.8 %collective-permute-start.14 = (f32[2,768]{1,0:T(2,128)S(1)}, f32[2,768]{1,0:T(2,128)S(1)}, u32[]{:S(2)}, u32[]{:S(2)}) collective-permute-start(f32[2,768]{1,0:T(2,128)S(1)} %meet_rows.1.refs_0_), channel_id=1, source_target_pairs={{0,24},{8,16},{16,8},{24,0},{1,25},{9,17},{17,9},{25,1},{2,26},{10... | collective-permute-start | bytes 18440 | tf_op jit(solution)/shard_map/ppermute | solution.py:319
  63.9 2.3 %collective-permute-done.14.refs_1_ = f32[2,768]{1,0:T(2,128)S(1)} collective-permute-done((f32[2,768]{1,0:T(2,128)S(1)}, f32[2,768]{1,0:T(2,128)S(1)}, u32[]{:S(2)}, u32[]{:S(2)}) %collective-permute-start.14) | collective-permute-done | bytes 6176 | tf_op jit(solution)/shard_map/ppermute | solution.py:319
  66.2 7.8 %weights.1 = (f32[768,256]{1,0:T(8,128)S(1)}, f32[768,256]{1,0:T(8,128)S(1)}, f32[768,256]{1,0:T(8,128)S(1)}, s16[400,256]{1,0:T(8,128)(2,1)S(1)}, s16[400,256]{...) custom-call(f32[2,768]{1,0:T(2,128)S(1)} %meet_rows.1.refs_0_, ...), custom_call_target="tpu_custom_call" | custom-call | flops 1000 | bytes 1000 | tf_op jit(solution)/shard_map/weights/pallas_call | solution.py:368
  74.1 3.6 %collective-permute-done.19.got = s16[4,208,1024]{2,1,0:T(8,128)(2,1)S(1)} collective-permute-done((s16[4,208,1024]{2,1,0:T(8,128)(2,1)S(1)}, s16[4,208,1024]{2,1,0:T(8,128)(2,1)S(1)}, u32[]{:S(2)}, u32[]{:S(2)}) %collective-permute-start.19) | collective-permute-done | bytes 1703968 | tf_op jit(solution)/shard_map/ppermute | solution.py:319
  78.6 1.6 %collective-permute-start.20 = (s16[2,208,512]{2,1,0:T(8,128)(2,1)S(1)}, s16[2,208,512]{2,1,0:T(8,128)(2,1)S(1)}, u32[]{:S(2)}, u32[]{:S(2)}) collective-permute-start(s16[2,208,512]{2,1,0:T(8,128)(2,1)S(1)} %get-tuple-element.48), channel_id=1, source_target_pairs={{0,2},{2,0},{1,3},{3,1},{4,6},{6,4},{5,7},{7,5},{8,10},{10,8},{9,1... | collective-permute-start | bytes 1277960 | tf_op jit(solution)/shard_map/ppermute | solution.py:319
  80.2 3.0 %collective-permute-start.24 = (s16[400,256]{1,0:T(8,128)(2,1)S(1)}, s16[400,256]{1,0:T(8,128)(2,1)S(1)}, u32[]{:S(2)}, u32[]{:S(2)}) collective-permute-start(s16[400,256]{1,0:T(8,128)(2,1)S(1)} %get-tuple-element.56), channel_id=1, source_target_pairs={{0,64},{64,128},{128,192},{192,0},{1,65},{65,129},{129,193},{193,1... | collective-permute-start | bytes 614408 | tf_op jit(solution)/shard_map/ppermute | solution.py:315
  83.1 4.3 %collective-permute-done.24.got_a = s16[400,256]{1,0:T(8,128)(2,1)S(1)} collective-permute-done((s16[400,256]{1,0:T(8,128)(2,1)S(1)}, s16[400,256]{1,0:T(8,128)(2,1)S(1)}, u32[]{:S(2)}, u32[]{:S(2)}) %collective-permute-start.24) | collective-permute-done | bytes 204832 | tf_op jit(solution)/shard_map/ppermute | solution.py:315
  87.5 3.4 %collective-permute-done.25.got_b = s16[400,256]{1,0:T(8,128)(2,1)S(1)} collective-permute-done((s16[400,256]{1,0:T(8,128)(2,1)S(1)}, s16[400,256]{1,0:T(8,128)(2,1)S(1)}, u32[]{:S(2)}, u32[]{:S(2)}) %collective-permute-start.25) | collective-permute-done | bytes 204832 | tf_op jit(solution)/shard_map/ppermute | solution.py:315
  91.6 1.7 %collective-permute-start.27 = (s16[784,256]{1,0:T(8,128)(2,1)S(1)}, s16[784,256]{1,0:T(8,128)(2,1)S(1)}, u32[]{:S(2)}, u32[]{:S(2)}) collective-permute-start(s16[784,256]{1,0:T(8,128)(2,1)S(1)} %get-tuple-element.59), channel_id=1, source_target_pairs={{0,192},{64,0},{128,64},{192,128},{1,193},{65,1},{129,65},{193,129... | collective-permute-start | bytes 1204232 | tf_op jit(solution)/shard_map/ppermute | solution.py:315
  94.4 1.7 %collective-permute-start.23 = (s16[208,512]{1,0:T(8,128)(2,1)S(1)}, s16[208,512]{1,0:T(8,128)(2,1)S(1)}, u32[]{:S(2)}, u32[]{:S(2)}) collective-permute-start(s16[208,512]{1,0:T(8,128)(2,1)S(1)} %get-tuple-element.52), channel_id=1, source_target_pairs={{0,4},{4,0},{1,5},{5,1},{2,6},{6,2},{3,7},{7,3},{8,12},{12,8},{9,1... | collective-permute-start | bytes 638984 | tf_op jit(solution)/shard_map/ppermute | solution.py:319
  96.2 5.0 %collective-permute-done.26.got1 = s16[784,256]{1,0:T(8,128)(2,1)S(1)} collective-permute-done((s16[784,256]{1,0:T(8,128)(2,1)S(1)}, s16[784,256]{1,0:T(8,128)(2,1)S(1)}, u32[]{:S(2)}, u32[]{:S(2)}) %collective-permute-start.26) | collective-permute-done | bytes 401440 | tf_op jit(solution)/shard_map/ppermute | solution.py:315
  101.2 1.5 %collective-permute-done.27.got3 = s16[784,256]{1,0:T(8,128)(2,1)S(1)} collective-permute-done((s16[784,256]{1,0:T(8,128)(2,1)S(1)}, s16[784,256]{1,0:T(8,128)(2,1)S(1)}, u32[]{:S(2)}, u32[]{:S(2)}) %collective-permute-start.27) | collective-permute-done | bytes 401440 | tf_op jit(solution)/shard_map/ppermute | solution.py:315
  103.1 22.4 %all_to_all.5.pieces = s16[8,208,128]{2,1,0:T(8,128)(2,1)S(1)} all-to-all(s16[8,208,128]{2,1,0:T(8,128)(2,1)S(1)} %image_sum.1), channel_id=1, replica_groups=mesh['y'=4,'xh'=2,'zh'=4,'zl'=2,'xl'=2,'core'=2] {'xh','zh'}, dimensions={0} | all-to-all | bytes 851968 | tf_op jit(solution)/shard_map/all_to_all | solution.py:398
  125.5 1.0 last.1
  (48 shorter events, 10.4 us)
Async XLA Ops:
  0.6 5.9 %collective-permute-start = (bf16[192,128]{1,0:T(8,128)(2,1)}, bf16[192,128]{1,0:T(8,128)(2,1)S(1)}, u32[]{:S(2)}, u32[]{:S(2)}) collective-permute-start(bf16[192,128]{1,0:T(8,128)(2,1)} %image.1), channel_id=1, source_target_pairs={{0,32},{32,0},{1,33},{33,1},{2,34},{34,2},{3,35},{35,3},{4,36},{36... | collective-permute-start | bytes 147464 | tf_op jit(solution)/shard_map/ppermute | solution.py:319
  6.5 0.8 copy-start.1
  7.3 12.8 %collective-permute-start.3 = (bf16[2,192,128]{2,1,0:T(8,128)(2,1)S(1)}, bf16[2,192,128]{2,1,0:T(8,128)(2,1)S(1)}, u32[]{:S(2)}, u32[]{:S(2)}) collective-permute-start(bf16[2,192,128]{2,1,0:T(8,128)(2,1)S(1)} %pair.1.after.both), channel_id=1, source_target_pairs={{0,24},{8,0},{16,8},{24,16},{1,25},{9,1},{17,9},{25,17},{2,26},{10... | collective-permute-start | bytes 294920 | tf_op jit(solution)/shard_map/ppermute | solution.py:315
  12.8 10.1 %collective-permute-start.2 = (bf16[2,192,128]{2,1,0:T(8,128)(2,1)S(1)}, bf16[2,192,128]{2,1,0:T(8,128)(2,1)S(1)}, u32[]{:S(2)}, u32[]{:S(2)}) collective-permute-start(bf16[2,192,128]{2,1,0:T(8,128)(2,1)S(1)} %pair.1.after.both), channel_id=1, source_target_pairs={{0,16},{8,24},{16,0},{24,8},{1,17},{9,25},{17,1},{25,9},{2,18},{10... | collective-permute-start | bytes 294920 | tf_op jit(solution)/shard_map/ppermute | solution.py:315
  14.3 8.9 %collective-permute-start.1 = (bf16[2,192,128]{2,1,0:T(8,128)(2,1)S(1)}, bf16[2,192,128]{2,1,0:T(8,128)(2,1)S(1)}, u32[]{:S(2)}, u32[]{:S(2)}) collective-permute-start(bf16[2,192,128]{2,1,0:T(8,128)(2,1)S(1)} %pair.1.after.both), channel_id=1, source_target_pairs={{0,8},{8,16},{16,24},{24,0},{1,9},{9,17},{17,25},{25,1},{2,10},{10... | collective-permute-start | bytes 294920 | tf_op jit(solution)/shard_map/ppermute | solution.py:315
  16.6 1.0 copy-start
  17.6 0.7 copy-start.2
  18.6 9.2 %collective-permute-start.4 = (bf16[192,1024]{1,0:T(8,128)(2,1)S(1)}, bf16[192,1024]{1,0:T(8,128)(2,1)S(1)}, u32[]{:S(2)}, u32[]{:S(2)}) collective-permute-start(bf16[192,1024]{1,0:T(8,128)(2,1)S(1)} %get-tuple-element.34.keys), channel_id=1, source_target_pairs={{0,2},{2,0},{1,3},{3,1},{4,6},{6,4},{5,7},{7,5},{8,10},{10,8},{9,1... | collective-permute-start | bytes 1179656 | tf_op jit(solution)/shard_map/ppermute | solution.py:319
  23.3 12.1 %collective-permute-start.5 = (bf16[192,1024]{1,0:T(8,128)(2,1)S(1)}, bf16[192,1024]{1,0:T(8,128)(2,1)S(1)}, u32[]{:S(2)}, u32[]{:S(2)}) collective-permute-start(bf16[192,1024]{1,0:T(8,128)(2,1)S(1)} %hold.1.own), channel_id=1, source_target_pairs={{0,4},{4,0},{1,5},{5,1},{2,6},{6,2},{3,7},{7,3},{8,12},{12,8},{9,1... | collective-permute-start | bytes 1179656 | tf_op jit(solution)/shard_map/ppermute | solution.py:319
  24.5 12.5 %collective-permute-start.9 = (bf16[8,192,128]{2,1,0:T(8,128)(2,1)S(1)}, bf16[8,192,128]{2,1,0:T(8,128)(2,1)S(1)}, u32[]{:S(2)}, u32[]{:S(2)}) collective-permute-start(bf16[8,192,128]{2,1,0:T(8,128)(2,1)S(1)} %stack.1.after.refs_2_), channel_id=1, source_target_pairs={{0,192},{64,0},{128,64},{192,128},{1,193},{65,1},{129,65},{193,129... | collective-permute-start | bytes 1179656 | tf_op jit(solution)/shard_map/ppermute | solution.py:315
  25.3 11.7 %collective-permute-start.8 = (bf16[8,192,128]{2,1,0:T(8,128)(2,1)S(1)}, bf16[8,192,128]{2,1,0:T(8,128)(2,1)S(1)}, u32[]{:S(2)}, u32[]{:S(2)}) collective-permute-start(bf16[8,192,128]{2,1,0:T(8,128)(2,1)S(1)} %stack.1.after.refs_2_), channel_id=1, source_target_pairs={{0,64},{64,128},{128,192},{192,0},{1,65},{65,129},{129,193},{193,1... | collective-permute-start | bytes 1179656 | tf_op jit(solution)/shard_map/ppermute | solution.py:315
  27.8 10.0 %collective-permute-start.7 = (bf16[96,1024]{1,0:T(8,128)(2,1)S(1)}, bf16[96,1024]{1,0:T(8,128)(2,1)S(1)}, u32[]{:S(2)}, u32[]{:S(2)}) collective-permute-start(bf16[96,1024]{1,0:T(8,128)(2,1)S(1)} %low.1), channel_id=1, source_target_pairs={{0,4},{4,0},{1,5},{5,1},{2,6},{6,2},{3,7},{7,3},{8,12},{12,8},{9,1... | collective-permute-start | bytes 589832 | tf_op jit(solution)/shard_map/ppermute | solution.py:319
  35.4 5.8 %collective-permute-start.6 = (bf16[96,1024]{1,0:T(8,128)(2,1)S(1)}, bf16[96,1024]{1,0:T(8,128)(2,1)S(1)}, u32[]{:S(2)}, u32[]{:S(2)}) collective-permute-start(bf16[96,1024]{1,0:T(8,128)(2,1)S(1)} %top.1), channel_id=1, source_target_pairs={{0,2},{2,0},{1,3},{3,1},{4,6},{6,4},{5,7},{7,5},{8,10},{10,8},{9,1... | collective-permute-start | bytes 589832 | tf_op jit(solution)/shard_map/ppermute | solution.py:319
  41.3 8.6 %collective-permute-start.10 = (bf16[768,1024]{1,0:T(8,128)(2,1)S(1)}, bf16[768,1024]{1,0:T(8,128)(2,1)S(1)}, u32[]{:S(2)}, u32[]{:S(2)}) collective-permute-start(bf16[768,1024]{1,0:T(8,128)(2,1)S(1)} %join.1.refs_0_.refs_9_), channel_id=1, source_target_pairs={{0,1},{1,0},{2,3},{3,2},{4,5},{5,4},{6,7},{7,6},{8,9},{9,8},{10,11... | collective-permute-start | bytes 4718600 | tf_op jit(solution)/shard_map/ppermute | solution.py:319
  41.4 8.5 %collective-permute-start.12 = (bf16[4,192,128]{2,1,0:T(8,128)(2,1)S(1)}, bf16[4,192,128]{2,1,0:T(8,128)(2,1)S(1)}, u32[]{:S(2)}, u32[]{:S(2)}) collective-permute-start(bf16[4,192,128]{2,1,0:T(8,128)(2,1)S(1)} %get-tuple-element.37), channel_id=1, source_target_pairs={{0,192},{64,0},{128,64},{192,128},{1,193},{65,1},{129,65},{193,129... | collective-permute-start | bytes 589832 | tf_op jit(solution)/shard_map/ppermute | solution.py:315
  42.2 7.7 %collective-permute-start.11 = (bf16[4,192,128]{2,1,0:T(8,128)(2,1)S(1)}, bf16[4,192,128]{2,1,0:T(8,128)(2,1)S(1)}, u32[]{:S(2)}, u32[]{:S(2)}) collective-permute-start(bf16[4,192,128]{2,1,0:T(8,128)(2,1)S(1)} %get-tuple-element.36.after), channel_id=1, source_target_pairs={{0,64},{64,128},{128,192},{192,0},{1,65},{65,129},{129,193},{193,1... | collective-permute-start | bytes 589832 | tf_op jit(solution)/shard_map/ppermute | solution.py:315
  54.6 1.9 %collective-permute-start.15 = (f32[2,1536]{1,0:T(2,128)S(1)}, f32[2,1536]{1,0:T(2,128)S(1)}, u32[]{:S(2)}, u32[]{:S(2)}) collective-permute-start(f32[2,1536]{1,0:T(2,128)S(1)} %get-tuple-element.40.c), channel_id=1, source_target_pairs={{0,1},{1,0},{2,3},{3,2},{4,5},{5,4},{6,7},{7,6},{8,9},{9,8},{10,11... | collective-permute-start | bytes 36872 | tf_op jit(solution)/shard_map/ppermute | solution.py:319
  54.7 5.4 %collective-permute-start.13 = (f32[2,768]{1,0:T(2,128)S(1)}, f32[2,768]{1,0:T(2,128)S(1)}, u32[]{:S(2)}, u32[]{:S(2)}) collective-permute-start(f32[2,768]{1,0:T(2,128)S(1)} %get-tuple-element.39.r), channel_id=1, source_target_pairs={{0,8},{8,0},{16,24},{24,16},{1,9},{9,1},{17,25},{25,17},{2,10},{10... | collective-permute-start | bytes 18440 | tf_op jit(solution)/shard_map/ppermute | solution.py:319
  56.6 9.7 %collective-permute-start.18 = (f32[2,1536]{1,0:T(2,128)S(1)}, f32[2,1536]{1,0:T(2,128)S(1)}, u32[]{:S(2)}, u32[]{:S(2)}) collective-permute-start(f32[2,1536]{1,0:T(2,128)S(1)} %meet.1.refs_2_), channel_id=1, source_target_pairs={{0,6},{2,4},{4,2},{6,0},{1,7},{3,5},{5,3},{7,1},{8,14},{10,12},{12... | collective-permute-start | bytes 36872 | tf_op jit(solution)/shard_map/ppermute | solution.py:365
  57.6 8.6 %collective-permute-start.17 = (f32[2,1536]{1,0:T(2,128)S(1)}, f32[2,1536]{1,0:T(2,128)S(1)}, u32[]{:S(2)}, u32[]{:S(2)}) collective-permute-start(f32[2,1536]{1,0:T(2,128)S(1)} %meet.1.refs_2_), channel_id=1, source_target_pairs={{0,4},{2,6},{4,0},{6,2},{1,5},{3,7},{5,1},{7,3},{8,12},{10,14},{12... | collective-permute-start | bytes 36872 | tf_op jit(solution)/shard_map/ppermute | solution.py:365
  59.6 6.6 %collective-permute-start.16 = (f32[2,1536]{1,0:T(2,128)S(1)}, f32[2,1536]{1,0:T(2,128)S(1)}, u32[]{:S(2)}, u32[]{:S(2)}) collective-permute-start(f32[2,1536]{1,0:T(2,128)S(1)} %meet.1.refs_2_), channel_id=1, source_target_pairs={{0,2},{2,0},{4,6},{6,4},{1,3},{3,1},{5,7},{7,5},{8,10},{10,8},{12,... | collective-permute-start | bytes 36872 | tf_op jit(solution)/shard_map/ppermute | solution.py:365
  60.2 6.0 %collective-permute-start.14 = (f32[2,768]{1,0:T(2,128)S(1)}, f32[2,768]{1,0:T(2,128)S(1)}, u32[]{:S(2)}, u32[]{:S(2)}) collective-permute-start(f32[2,768]{1,0:T(2,128)S(1)} %meet_rows.1.refs_0_), channel_id=1, source_target_pairs={{0,24},{8,16},{16,8},{24,0},{1,25},{9,17},{17,9},{25,1},{2,26},{10... | collective-permute-start | bytes 18440 | tf_op jit(solution)/shard_map/ppermute | solution.py:319
  74.1 3.6 %collective-permute-start.19 = (s16[4,208,1024]{2,1,0:T(8,128)(2,1)S(1)}, s16[4,208,1024]{2,1,0:T(8,128)(2,1)S(1)}, u32[]{:S(2)}, u32[]{:S(2)}) collective-permute-start(s16[4,208,1024]{2,1,0:T(8,128)(2,1)S(1)} %get-tuple-element.44), channel_id=1, source_target_pairs={{0,1},{1,0},{2,3},{3,2},{4,5},{5,4},{6,7},{7,6},{8,9},{9,8},{10,11... | collective-permute-start | bytes 5111816 | tf_op jit(solution)/shard_map/ppermute | solution.py:319
  78.6 14.8 %collective-permute-start.20 = (s16[2,208,512]{2,1,0:T(8,128)(2,1)S(1)}, s16[2,208,512]{2,1,0:T(8,128)(2,1)S(1)}, u32[]{:S(2)}, u32[]{:S(2)}) collective-permute-start(s16[2,208,512]{2,1,0:T(8,128)(2,1)S(1)} %get-tuple-element.48), channel_id=1, source_target_pairs={{0,2},{2,0},{1,3},{3,1},{4,6},{6,4},{5,7},{7,5},{8,10},{10,8},{9,1... | collective-permute-start | bytes 1277960 | tf_op jit(solution)/shard_map/ppermute | solution.py:319
  80.2 13.2 %collective-permute-start.21 = (s16[2,208,512]{2,1,0:T(8,128)(2,1)S(1)}, s16[2,208,512]{2,1,0:T(8,128)(2,1)S(1)}, u32[]{:S(2)}, u32[]{:S(2)}) collective-permute-start(s16[2,208,512]{2,1,0:T(8,128)(2,1)S(1)} %get-tuple-element.49), channel_id=1, source_target_pairs={{0,4},{4,0},{1,5},{5,1},{2,6},{6,2},{3,7},{7,3},{8,12},{12,8},{9,1... | collective-permute-start | bytes 1277960 | tf_op jit(solution)/shard_map/ppermute | solution.py:319
  80.2 7.3 %collective-permute-start.24 = (s16[400,256]{1,0:T(8,128)(2,1)S(1)}, s16[400,256]{1,0:T(8,128)(2,1)S(1)}, u32[]{:S(2)}, u32[]{:S(2)}) collective-permute-start(s16[400,256]{1,0:T(8,128)(2,1)S(1)} %get-tuple-element.56), channel_id=1, source_target_pairs={{0,64},{64,128},{128,192},{192,0},{1,65},{65,129},{129,193},{193,1... | collective-permute-start | bytes 614408 | tf_op jit(solution)/shard_map/ppermute | solution.py:315
  83.1 7.8 %collective-permute-start.25 = (s16[400,256]{1,0:T(8,128)(2,1)S(1)}, s16[400,256]{1,0:T(8,128)(2,1)S(1)}, u32[]{:S(2)}, u32[]{:S(2)}) collective-permute-start(s16[400,256]{1,0:T(8,128)(2,1)S(1)} %get-tuple-element.57), channel_id=1, source_target_pairs={{0,192},{64,0},{128,64},{192,128},{1,193},{65,1},{129,65},{193,129... | collective-permute-start | bytes 614408 | tf_op jit(solution)/shard_map/ppermute | solution.py:315
  91.2 9.9 %collective-permute-start.26 = (s16[784,256]{1,0:T(8,128)(2,1)S(1)}, s16[784,256]{1,0:T(8,128)(2,1)S(1)}, u32[]{:S(2)}, u32[]{:S(2)}) collective-permute-start(s16[784,256]{1,0:T(8,128)(2,1)S(1)} %get-tuple-element.58), channel_id=1, source_target_pairs={{0,64},{64,128},{128,192},{192,0},{1,65},{65,129},{129,193},{193,1... | collective-permute-start | bytes 1204232 | tf_op jit(solution)/shard_map/ppermute | solution.py:315
  91.6 11.1 %collective-permute-start.27 = (s16[784,256]{1,0:T(8,128)(2,1)S(1)}, s16[784,256]{1,0:T(8,128)(2,1)S(1)}, u32[]{:S(2)}, u32[]{:S(2)}) collective-permute-start(s16[784,256]{1,0:T(8,128)(2,1)S(1)} %get-tuple-element.59), channel_id=1, source_target_pairs={{0,192},{64,0},{128,64},{192,128},{1,193},{65,1},{129,65},{193,129... | collective-permute-start | bytes 1204232 | tf_op jit(solution)/shard_map/ppermute | solution.py:315
  93.8 8.9 %collective-permute-start.22 = (s16[208,512]{1,0:T(8,128)(2,1)S(1)}, s16[208,512]{1,0:T(8,128)(2,1)S(1)}, u32[]{:S(2)}, u32[]{:S(2)}) collective-permute-start(s16[208,512]{1,0:T(8,128)(2,1)S(1)} %get-tuple-element.51), channel_id=1, source_target_pairs={{0,2},{2,0},{1,3},{3,1},{4,6},{6,4},{5,7},{7,5},{8,10},{10,8},{9,1... | collective-permute-start | bytes 638984 | tf_op jit(solution)/shard_map/ppermute | solution.py:319
  94.4 8.3 %collective-permute-start.23 = (s16[208,512]{1,0:T(8,128)(2,1)S(1)}, s16[208,512]{1,0:T(8,128)(2,1)S(1)}, u32[]{:S(2)}, u32[]{:S(2)}) collective-permute-start(s16[208,512]{1,0:T(8,128)(2,1)S(1)} %get-tuple-element.52), channel_id=1, source_target_pairs={{0,4},{4,0},{1,5},{5,1},{2,6},{6,2},{3,7},{7,3},{8,12},{12,8},{9,1... | collective-permute-start | bytes 638984 | tf_op jit(solution)/shard_map/ppermute | solution.py:319

commit v8 on v7

--- a/solution.py
+++ b/solution.py
@@ -12,12 +12,12 @@
 PAD = 16
 
 
-def call(kernel, out, name, mib, **kw):
+def call(kernel, out, name, mib, flops=1000, **kw):
     return pl.pallas_call(
         kernel,
         out_shape=out,
         compiler_params=pltpu.CompilerParams(vmem_limit_bytes=mib * 2**20),
-        cost_estimate=pl.CostEstimate(flops=1000, bytes_accessed=1000, transcendentals=0),
+        cost_estimate=pl.CostEstimate(flops=flops, bytes_accessed=1000, transcendentals=0),
         name=name,
         **kw,
     )
@@ -140,6 +140,11 @@
     n = half_a.shape[0]
     half_a[...] = behind[:n]
     half_b[...] = ahead[n:]
+
+
+def beyond_kernel(a, b, out_a, out_b):
+    out_a[...] = a[...]
+    out_b[...] = b[...]
 
 
 def scores_kernel(scale, *refs):
@@ -302,8 +307,8 @@
     image_out[...] = sum(decode(pieces[k]) for k in range(pieces.shape[0]))
 
 
-def image_sum_kernel(after_x, after_z, own, got1, got3, out):
-    del after_x, after_z
+def image_sum_kernel(after, own, got1, got3, out):
+    del after
     rows, width = out.shape[1] - PAD, out.shape[2]
     total = own[...] + decode(got1[...]) + decode(got3[...])
     for xh in range(2):
@@ -348,7 +353,9 @@
     k0 = call(join_kernel, shape((half, d), BF16), "join", 12, in_specs=[vmem] * 6)(
         held, key_x, key_z, d_top, d_low, ia
     )
-    ia, ib = shift(ia, "y", 4, 1), shift(ib, "y", 4, 3)
+    ia, ib = call(beyond_kernel, [half_block] * 2, "beyond", 8, 20 * 10**9, in_specs=[vmem] * 2)(
+        shift(ia, "y", 4, 1), shift(ib, "y", 4, 3)
+    )
     ks = [k0, flip(k0, "core", 2, 1)]
 
     tile = min(384, n_im)
@@ -381,7 +388,7 @@
         in_specs=[vmem] * 2,
     )(mine, flip(sent, "core", 2, 1))
     q1, q3 = call(
-        relay_kernel, [shape((n_im + PAD, 2 * width), I16)] * 2, "relay", 12, in_specs=[vmem] * 5
+        relay_kernel, [shape((n_im + PAD, 2 * width), I16)] * 2, "relay", 12, 20 * 10**9, in_specs=[vmem] * 5
     )(own_key, p1, p3, shift(q2a, "y", 4, 1), shift(q2b, "y", 4, 3))
     q1, q3 = shift(q1, "y", 4, 1), shift(q3, "y", 4, 3)
     own_key, to_x, to_z = call(
@@ -393,8 +400,8 @@
     )(own_key, keep_x, keep_z, flip(to_x, "xl", 2, 1), flip(to_z, "zl", 2, 1))
     from_x, from_z = flip(to_x, "xl", 2, 1), flip(to_z, "zl", 2, 1)
     pieces = call(
-        image_sum_kernel, shape((8, rows + PAD, width), I16), "image_sum", 12, in_specs=[vmem] * 5
-    )(from_x, from_z, own, q1, q3)
+        image_sum_kernel, shape((8, rows + PAD, width), I16), "image_sum", 12, in_specs=[vmem] * 4
+    )(own_key, own, q1, q3)
     pieces = lax.all_to_all(pieces, ("xh", "zh"), 0, 0)
     modality_grad, image_grad = call(
         last_kernel, [shape((rows, d), F32), shape((rows, width), F32)], "last", 8, in_specs=[vmem] * 4

time: 127 us -> 119 us (0.937)
  the two profiles are of different devices: /device:TPU:56 before, /device:TPU:4 now
where the time goes in v8:
time: 119 us; the launch traced here: 118 us
  starting transfers between devices  52.5 us (44%)
  waiting for transfers between devices  45 us (38%)
  Pallas kernels  16.9 us (14%)
  local copies, waits for them, and re-layouts  2.53 us (2%)
    ppermute x14, waiting for transfers between devices, flip(): return lax.ppermute(x, axis, [(i, i ^ d) for i in range(n)])  29.5 us
    ppermute x11, starting transfers between devices, shift(): return lax.ppermute(x, axis, [(i, (i + k) % n) for i in range(n)])  21.9 us
    ppermute x14, starting transfers between devices, flip(): return lax.ppermute(x, axis, [(i, i ^ d) for i in range(n)])  18.4 us
    ppermute x11, waiting for transfers between devices, shift(): return lax.ppermute(x, axis, [(i, (i + k) % n) for i in range(n)])  15.5 us
    all_to_all x1, starting transfers between devices, on_device(): pieces = lax.all_to_all(pieces, ('xh', 'zh'), 0, 0)  8.73 us
    pallas_call x1, Pallas kernels, on_device(): call(functools.partial(weights_kernel, scale, tile), outs, 'weights', 36,...  7.84 us
    pallas_call x1, Pallas kernels, on_device(): call(functools.partial(scores_kernel, scale), [shape((n_im, n_ks), F32),...  4.69 us
    ppermute x3, starting transfers between devices, on_device(): lax.ppermute(cs, ('zl', 'xl'), [(i, i ^ k) for i in range(4)])  3.58 us
  transfers between devices with their start and end apart: 29, of which 17 were waited for; matrix products, arithmetic and copies ran while one was open for 0% of the time, Pallas kernels for 2%

profile of v8, /device:TPU:4, one launch (start us, length us, event | category | flops | bytes accessed | tf_op | source)
XLA Modules:
  0.0 117.7 jit_solution(17888470105746277634)
XLA Ops:
  0.6 2.3 %collective-permute-start = (bf16[192,128]{1,0:T(8,128)(2,1)}, bf16[192,128]{1,0:T(8,128)(2,1)S(1)}, u32[]{:S(2)}, u32[]{:S(2)}) collective-permute-start(bf16[192,128]{1,0:T(8,128)(2,1)} %image.1), channel_id=1, source_target_pairs={{0,32},{32,0},{1,33},{33,1},{2,34},{34,2},{3,35},{35,3},{4,36},{36... | collective-permute-start | bytes 147464 | tf_op jit(solution)/shard_map/ppermute | solution.py:324
  3.0 3.6 %collective-permute-done.twin = bf16[192,128]{1,0:T(8,128)(2,1)S(1)} collective-permute-done((bf16[192,128]{1,0:T(8,128)(2,1)}, bf16[192,128]{1,0:T(8,128)(2,1)S(1)}, u32[]{:S(2)}, u32[]{:S(2)}) %collective-permute-start) | collective-permute-done | bytes 49184 | tf_op jit(solution)/shard_map/ppermute | solution.py:324
  7.3 6.4 %collective-permute-start.3 = (bf16[2,192,128]{2,1,0:T(8,128)(2,1)S(1)}, bf16[2,192,128]{2,1,0:T(8,128)(2,1)S(1)}, u32[]{:S(2)}, u32[]{:S(2)}) collective-permute-start(bf16[2,192,128]{2,1,0:T(8,128)(2,1)S(1)} %pair.1.after.both), channel_id=1, source_target_pairs={{0,24},{8,0},{16,8},{24,16},{1,25},{9,1},{17,9},{25,17},{2,26},{10... | collective-permute-start | bytes 294920 | tf_op jit(solution)/shard_map/ppermute | solution.py:320
  14.7 2.8 %collective-permute-start.1 = (bf16[2,192,128]{2,1,0:T(8,128)(2,1)S(1)}, bf16[2,192,128]{2,1,0:T(8,128)(2,1)S(1)}, u32[]{:S(2)}, u32[]{:S(2)}) collective-permute-start(bf16[2,192,128]{2,1,0:T(8,128)(2,1)S(1)} %pair.1.after.both), channel_id=1, source_target_pairs={{0,8},{8,16},{16,24},{24,0},{1,9},{9,17},{17,25},{25,1},{2,10},{10... | collective-permute-start | bytes 294920 | tf_op jit(solution)/shard_map/ppermute | solution.py:320
  19.5 1.3 %collective-permute-start.4 = (bf16[192,1024]{1,0:T(8,128)(2,1)S(1)}, bf16[192,1024]{1,0:T(8,128)(2,1)S(1)}, u32[]{:S(2)}, u32[]{:S(2)}) collective-permute-start(bf16[192,1024]{1,0:T(8,128)(2,1)S(1)} %get-tuple-element.36.keys), channel_id=1, source_target_pairs={{0,2},{2,0},{1,3},{3,1},{4,6},{6,4},{5,7},{7,5},{8,10},{10,8},{9,1... | collective-permute-start | bytes 1179656 | tf_op jit(solution)/shard_map/ppermute | solution.py:324
  21.0 3.3 %collective-permute-done.2.b2 = bf16[2,192,128]{2,1,0:T(8,128)(2,1)S(1)} collective-permute-done((bf16[2,192,128]{2,1,0:T(8,128)(2,1)S(1)}, bf16[2,192,128]{2,1,0:T(8,128)(2,1)S(1)}, u32[]{:S(2)}, u32[]{:S(2)}) %collective-permute-start.2) | collective-permute-done | bytes 98336 | tf_op jit(solution)/shard_map/ppermute | solution.py:320
  25.3 3.0 %collective-permute-start.9 = (bf16[8,192,128]{2,1,0:T(8,128)(2,1)S(1)}, bf16[8,192,128]{2,1,0:T(8,128)(2,1)S(1)}, u32[]{:S(2)}, u32[]{:S(2)}) collective-permute-start(bf16[8,192,128]{2,1,0:T(8,128)(2,1)S(1)} %stack.1.after.refs_2_), channel_id=1, source_target_pairs={{0,192},{64,0},{128,64},{192,128},{1,193},{65,1},{129,65},{193,129... | collective-permute-start | bytes 1179656 | tf_op jit(solution)/shard_map/ppermute | solution.py:320
  28.4 1.1 collective-permute-start.7
  29.6 6.3 %collective-permute-done.5.z = bf16[192,1024]{1,0:T(8,128)(2,1)S(1)} collective-permute-done((bf16[192,1024]{1,0:T(8,128)(2,1)S(1)}, bf16[192,1024]{1,0:T(8,128)(2,1)S(1)}, u32[]{:S(2)}, u32[]{:S(2)}) %collective-permute-start.5) | collective-permute-done | bytes 393248 | tf_op jit(solution)/shard_map/ppermute | solution.py:324
  35.9 1.3 %collective-permute-start.6 = (bf16[96,1024]{1,0:T(8,128)(2,1)S(1)}, bf16[96,1024]{1,0:T(8,128)(2,1)S(1)}, u32[]{:S(2)}, u32[]{:S(2)}) collective-permute-start(bf16[96,1024]{1,0:T(8,128)(2,1)S(1)} %top.1), channel_id=1, source_target_pairs={{0,2},{2,0},{1,3},{3,1},{4,6},{6,4},{5,7},{7,5},{8,10},{10,8},{9,1... | collective-permute-start | bytes 589832 | tf_op jit(solution)/shard_map/ppermute | solution.py:324
  37.1 2.0 %collective-permute-done.8.behind.refs_3_ = bf16[8,192,128]{2,1,0:T(8,128)(2,1)S(1)} collective-permute-done((bf16[8,192,128]{2,1,0:T(8,128)(2,1)S(1)}, bf16[8,192,128]{2,1,0:T(8,128)(2,1)S(1)}, u32[]{:S(2)}, u32[]{:S(2)}) %collective-permute-start.8) | collective-permute-done | bytes 393248 | tf_op jit(solution)/shard_map/ppermute | solution.py:320
  39.2 1.1 collective-permute-start.12
  42.0 2.9 %collective-permute-done.12.b = bf16[4,192,128]{2,1,0:T(8,128)(2,1)S(1)} collective-permute-done((bf16[4,192,128]{2,1,0:T(8,128)(2,1)S(1)}, bf16[4,192,128]{2,1,0:T(8,128)(2,1)S(1)}, u32[]{:S(2)}, u32[]{:S(2)}) %collective-permute-start.12) | collective-permute-done | bytes 196640 | tf_op jit(solution)/shard_map/ppermute | solution.py:320
  44.9 2.2 %collective-permute-done.11.a = bf16[4,192,128]{2,1,0:T(8,128)(2,1)S(1)} collective-permute-done((bf16[4,192,128]{2,1,0:T(8,128)(2,1)S(1)}, bf16[4,192,128]{2,1,0:T(8,128)(2,1)S(1)}, u32[]{:S(2)}, u32[]{:S(2)}) %collective-permute-start.11) | collective-permute-done | bytes 196640 | tf_op jit(solution)/shard_map/ppermute | solution.py:320
  47.2 4.7 %scores.1 = (f32[768,1536]{1,0:T(8,128)S(1)}, bf16[768,1024]{1,0:T(8,128)(2,1)S(1)}, f32[2,768]{1,0:T(2,128)S(1)}, f32[2,1536]{1,0:T(2,128)S(1)}) custom-call(bf16[768,1024]{1,0:T(8,128)(2,1)S(1)} %join.1.refs_0_.refs_9_, bf16[768,1024]{1,0:T(8,128)(2,1)S(1)} %collective-permute-done.10.refs_1_.refs_10_, bf16[8,192,128]{2,1,0:T(8,128)(2,1)S(1)} %stack.1.after.refs_2_, ...), custom_call_target="tpu_custom_call" | custom-call | flops 1000 | bytes 1000 | tf_op jit(solution)/shard_map/scores/pallas_call | solution.py:362
  52.0 1.3 %collective-permute-start.13 = (f32[2,768]{1,0:T(2,128)S(1)}, f32[2,768]{1,0:T(2,128)S(1)}, u32[]{:S(2)}, u32[]{:S(2)}) collective-permute-start(f32[2,768]{1,0:T(2,128)S(1)} %get-tuple-element.43.r), channel_id=1, source_target_pairs={{0,8},{8,0},{16,24},{24,16},{1,9},{9,1},{17,25},{25,17},{2,10},{10... | collective-permute-start | bytes 18440 | tf_op jit(solution)/shard_map/ppermute | solution.py:324
  53.3 2.4 %collective-permute-start.18 = (f32[2,1536]{1,0:T(2,128)S(1)}, f32[2,1536]{1,0:T(2,128)S(1)}, u32[]{:S(2)}, u32[]{:S(2)}) collective-permute-start(f32[2,1536]{1,0:T(2,128)S(1)} %meet.1.refs_2_), channel_id=1, source_target_pairs={{0,6},{2,4},{4,2},{6,0},{1,7},{3,5},{5,3},{7,1},{8,14},{10,12},{12... | collective-permute-start | bytes 36872 | tf_op jit(solution)/shard_map/ppermute | solution.py:372
  56.9 4.3 %collective-permute-start.14 = (f32[2,768]{1,0:T(2,128)S(1)}, f32[2,768]{1,0:T(2,128)S(1)}, u32[]{:S(2)}, u32[]{:S(2)}) collective-permute-start(f32[2,768]{1,0:T(2,128)S(1)} %meet_rows.1.refs_0_), channel_id=1, source_target_pairs={{0,24},{8,16},{16,8},{24,0},{1,25},{9,17},{17,9},{25,1},{2,26},{10... | collective-permute-start | bytes 18440 | tf_op jit(solution)/shard_map/ppermute | solution.py:324
  61.2 1.8 %collective-permute-done.14.refs_1_ = f32[2,768]{1,0:T(2,128)S(1)} collective-permute-done((f32[2,768]{1,0:T(2,128)S(1)}, f32[2,768]{1,0:T(2,128)S(1)}, u32[]{:S(2)}, u32[]{:S(2)}) %collective-permute-start.14) | collective-permute-done | bytes 6176 | tf_op jit(solution)/shard_map/ppermute | solution.py:324
  63.0 7.8 %weights.1 = (f32[768,256]{1,0:T(8,128)S(1)}, f32[768,256]{1,0:T(8,128)S(1)}, f32[768,256]{1,0:T(8,128)S(1)}, s16[400,256]{1,0:T(8,128)(2,1)S(1)}, s16[400,256]{...) custom-call(f32[2,768]{1,0:T(2,128)S(1)} %meet_rows.1.refs_0_, ...), custom_call_target="tpu_custom_call" | custom-call | flops 1000 | bytes 1000 | tf_op jit(solution)/shard_map/weights/pallas_call | solution.py:375
  71.2 2.9 %collective-permute-start.25 = (s16[400,256]{1,0:T(8,128)(2,1)S(1)}, s16[400,256]{1,0:T(8,128)(2,1)S(1)}, u32[]{:S(2)}, u32[]{:S(2)}) collective-permute-start(s16[400,256]{1,0:T(8,128)(2,1)S(1)} %get-tuple-element.61), channel_id=1, source_target_pairs={{0,192},{64,0},{128,64},{192,128},{1,193},{65,1},{129,65},{193,129... | collective-permute-start | bytes 614408 | tf_op jit(solution)/shard_map/ppermute | solution.py:320
  75.3 1.1 collective-permute-start.20
  76.4 1.8 %collective-permute-start.21 = (s16[2,208,512]{2,1,0:T(8,128)(2,1)S(1)}, s16[2,208,512]{2,1,0:T(8,128)(2,1)S(1)}, u32[]{:S(2)}, u32[]{:S(2)}) collective-permute-start(s16[2,208,512]{2,1,0:T(8,128)(2,1)S(1)} %get-tuple-element.53), channel_id=1, source_target_pairs={{0,4},{4,0},{1,5},{5,1},{2,6},{6,2},{3,7},{7,3},{8,12},{12,8},{9,1... | collective-permute-start | bytes 1277960 | tf_op jit(solution)/shard_map/ppermute | solution.py:324
  78.2 1.3 %collective-permute-done.24.got_a = s16[400,256]{1,0:T(8,128)(2,1)S(1)} collective-permute-done((s16[400,256]{1,0:T(8,128)(2,1)S(1)}, s16[400,256]{1,0:T(8,128)(2,1)S(1)}, u32[]{:S(2)}, u32[]{:S(2)}) %collective-permute-start.24) | collective-permute-done | bytes 204832 | tf_op jit(solution)/shard_map/ppermute | solution.py:320
  80.0 3.2 %collective-permute-start.27 = (s16[784,256]{1,0:T(8,128)(2,1)S(1)}, s16[784,256]{1,0:T(8,128)(2,1)S(1)}, u32[]{:S(2)}, u32[]{:S(2)}) collective-permute-start(s16[784,256]{1,0:T(8,128)(2,1)S(1)} %get-tuple-element.63), channel_id=1, source_target_pairs={{0,192},{64,0},{128,64},{192,128},{1,193},{65,1},{129,65},{193,129... | collective-permute-start | bytes 1204232 | tf_op jit(solution)/shard_map/ppermute | solution.py:320
  83.2 4.1 %collective-permute-done.20.from_x = s16[2,208,512]{2,1,0:T(8,128)(2,1)S(1)} collective-permute-done((s16[2,208,512]{2,1,0:T(8,128)(2,1)S(1)}, s16[2,208,512]{2,1,0:T(8,128)(2,1)S(1)}, u32[]{:S(2)}, u32[]{:S(2)}) %collective-permute-start.20) | collective-permute-done | bytes 426016 | tf_op jit(solution)/shard_map/ppermute | solution.py:324
  88.5 3.6 %collective-permute-done.26.got1 = s16[784,256]{1,0:T(8,128)(2,1)S(1)} collective-permute-done((s16[784,256]{1,0:T(8,128)(2,1)S(1)}, s16[784,256]{1,0:T(8,128)(2,1)S(1)}, u32[]{:S(2)}, u32[]{:S(2)}) %collective-permute-start.26) | collective-permute-done | bytes 401440 | tf_op jit(solution)/shard_map/ppermute | solution.py:320
  92.1 1.1 image_sum.1
  93.2 8.7 %all-to-all-start = ((s16[8,208,128]{2,1,0:T(8,128)(2,1)}), s16[8,208,128]{2,1,0:T(8,128)(2,1)S(1)}, u32[]{:S(2)}, u32[]{:S(2)}) async-start(s16[8,208,128]{2,1,0:T(8,128)(2,1)} %image_sum.1), calls=%async_computation | async-start | bytes 851968 | tf_op jit(solution)/shard_map/all_to_all | solution.py:405
  103.0 1.5 %collective-permute-start.23 = (s16[208,512]{1,0:T(8,128)(2,1)S(1)}, s16[208,512]{1,0:T(8,128)(2,1)S(1)}, u32[]{:S(2)}, u32[]{:S(2)}) collective-permute-start(s16[208,512]{1,0:T(8,128)(2,1)S(1)} %get-tuple-element.56), channel_id=1, source_target_pairs={{0,4},{4,0},{1,5},{5,1},{2,6},{6,2},{3,7},{7,3},{8,12},{12,8},{9,1... | collective-permute-start | bytes 638984 | tf_op jit(solution)/shard_map/ppermute | solution.py:324
  104.5 5.8 %collective-permute-done.22.from_x = s16[208,512]{1,0:T(8,128)(2,1)S(1)} collective-permute-done((s16[208,512]{1,0:T(8,128)(2,1)S(1)}, s16[208,512]{1,0:T(8,128)(2,1)S(1)}, u32[]{:S(2)}, u32[]{:S(2)}) %collective-permute-start.22) | collective-permute-done | bytes 213024 | tf_op jit(solution)/shard_map/ppermute | solution.py:324
  110.3 6.4 %collective-permute-done.23.from_z = s16[208,512]{1,0:T(8,128)(2,1)S(1)} collective-permute-done((s16[208,512]{1,0:T(8,128)(2,1)S(1)}, s16[208,512]{1,0:T(8,128)(2,1)S(1)}, u32[]{:S(2)}, u32[]{:S(2)}) %collective-permute-start.23) | collective-permute-done | bytes 213024 | tf_op jit(solution)/shard_map/ppermute | solution.py:324
  (50 shorter events, 13.7 us)
Async XLA Ops:
  0.6 5.9 %collective-permute-start = (bf16[192,128]{1,0:T(8,128)(2,1)}, bf16[192,128]{1,0:T(8,128)(2,1)S(1)}, u32[]{:S(2)}, u32[]{:S(2)}) collective-permute-start(bf16[192,128]{1,0:T(8,128)(2,1)} %image.1), channel_id=1, source_target_pairs={{0,32},{32,0},{1,33},{33,1},{2,34},{34,2},{3,35},{35,3},{4,36},{36... | collective-permute-start | bytes 147464 | tf_op jit(solution)/shard_map/ppermute | solution.py:324
  6.5 0.8 copy-start.1
  7.3 13.6 %collective-permute-start.3 = (bf16[2,192,128]{2,1,0:T(8,128)(2,1)S(1)}, bf16[2,192,128]{2,1,0:T(8,128)(2,1)S(1)}, u32[]{:S(2)}, u32[]{:S(2)}) collective-permute-start(bf16[2,192,128]{2,1,0:T(8,128)(2,1)S(1)} %pair.1.after.both), channel_id=1, source_target_pairs={{0,24},{8,0},{16,8},{24,16},{1,25},{9,1},{17,9},{25,17},{2,26},{10... | collective-permute-start | bytes 294920 | tf_op jit(solution)/shard_map/ppermute | solution.py:320
  13.7 10.5 %collective-permute-start.2 = (bf16[2,192,128]{2,1,0:T(8,128)(2,1)S(1)}, bf16[2,192,128]{2,1,0:T(8,128)(2,1)S(1)}, u32[]{:S(2)}, u32[]{:S(2)}) collective-permute-start(bf16[2,192,128]{2,1,0:T(8,128)(2,1)S(1)} %pair.1.after.both), channel_id=1, source_target_pairs={{0,16},{8,24},{16,0},{24,8},{1,17},{9,25},{17,1},{25,9},{2,18},{10... | collective-permute-start | bytes 294920 | tf_op jit(solution)/shard_map/ppermute | solution.py:320
  14.7 9.5 %collective-permute-start.1 = (bf16[2,192,128]{2,1,0:T(8,128)(2,1)S(1)}, bf16[2,192,128]{2,1,0:T(8,128)(2,1)S(1)}, u32[]{:S(2)}, u32[]{:S(2)}) collective-permute-start(bf16[2,192,128]{2,1,0:T(8,128)(2,1)S(1)} %pair.1.after.both), channel_id=1, source_target_pairs={{0,8},{8,16},{16,24},{24,0},{1,9},{9,17},{17,25},{25,1},{2,10},{10... | collective-permute-start | bytes 294920 | tf_op jit(solution)/shard_map/ppermute | solution.py:320
  17.5 1.0 copy-start
  18.5 0.7 copy-start.2
  19.5 8.9 %collective-permute-start.4 = (bf16[192,1024]{1,0:T(8,128)(2,1)S(1)}, bf16[192,1024]{1,0:T(8,128)(2,1)S(1)}, u32[]{:S(2)}, u32[]{:S(2)}) collective-permute-start(bf16[192,1024]{1,0:T(8,128)(2,1)S(1)} %get-tuple-element.36.keys), channel_id=1, source_target_pairs={{0,2},{2,0},{1,3},{3,1},{4,6},{6,4},{5,7},{7,5},{8,10},{10,8},{9,1... | collective-permute-start | bytes 1179656 | tf_op jit(solution)/shard_map/ppermute | solution.py:324
  24.3 11.5 %collective-permute-start.5 = (bf16[192,1024]{1,0:T(8,128)(2,1)S(1)}, bf16[192,1024]{1,0:T(8,128)(2,1)S(1)}, u32[]{:S(2)}, u32[]{:S(2)}) collective-permute-start(bf16[192,1024]{1,0:T(8,128)(2,1)S(1)} %hold.1.own), channel_id=1, source_target_pairs={{0,4},{4,0},{1,5},{5,1},{2,6},{6,2},{3,7},{7,3},{8,12},{12,8},{9,1... | collective-permute-start | bytes 1179656 | tf_op jit(solution)/shard_map/ppermute | solution.py:324
  25.3 11.9 %collective-permute-start.9 = (bf16[8,192,128]{2,1,0:T(8,128)(2,1)S(1)}, bf16[8,192,128]{2,1,0:T(8,128)(2,1)S(1)}, u32[]{:S(2)}, u32[]{:S(2)}) collective-permute-start(bf16[8,192,128]{2,1,0:T(8,128)(2,1)S(1)} %stack.1.after.refs_2_), channel_id=1, source_target_pairs={{0,192},{64,0},{128,64},{192,128},{1,193},{65,1},{129,65},{193,129... | collective-permute-start | bytes 1179656 | tf_op jit(solution)/shard_map/ppermute | solution.py:320
  28.3 10.9 %collective-permute-start.8 = (bf16[8,192,128]{2,1,0:T(8,128)(2,1)S(1)}, bf16[8,192,128]{2,1,0:T(8,128)(2,1)S(1)}, u32[]{:S(2)}, u32[]{:S(2)}) collective-permute-start(bf16[8,192,128]{2,1,0:T(8,128)(2,1)S(1)} %stack.1.after.refs_2_), channel_id=1, source_target_pairs={{0,64},{64,128},{128,192},{192,0},{1,65},{65,129},{129,193},{193,1... | collective-permute-start | bytes 1179656 | tf_op jit(solution)/shard_map/ppermute | solution.py:320
  28.4 12.9 %collective-permute-start.7 = (bf16[96,1024]{1,0:T(8,128)(2,1)S(1)}, bf16[96,1024]{1,0:T(8,128)(2,1)S(1)}, u32[]{:S(2)}, u32[]{:S(2)}) collective-permute-start(bf16[96,1024]{1,0:T(8,128)(2,1)S(1)} %low.1), channel_id=1, source_target_pairs={{0,4},{4,0},{1,5},{5,1},{2,6},{6,2},{3,7},{7,3},{8,12},{12,8},{9,1... | collective-permute-start | bytes 589832 | tf_op jit(solution)/shard_map/ppermute | solution.py:324
  35.9 5.8 %collective-permute-start.6 = (bf16[96,1024]{1,0:T(8,128)(2,1)S(1)}, bf16[96,1024]{1,0:T(8,128)(2,1)S(1)}, u32[]{:S(2)}, u32[]{:S(2)}) collective-permute-start(bf16[96,1024]{1,0:T(8,128)(2,1)S(1)} %top.1), channel_id=1, source_target_pairs={{0,2},{2,0},{1,3},{3,1},{4,6},{6,4},{5,7},{7,5},{8,10},{10,8},{9,1... | collective-permute-start | bytes 589832 | tf_op jit(solution)/shard_map/ppermute | solution.py:324
  39.2 5.7 %collective-permute-start.12 = (bf16[4,192,128]{2,1,0:T(8,128)(2,1)S(1)}, bf16[4,192,128]{2,1,0:T(8,128)(2,1)S(1)}, u32[]{:S(2)}, u32[]{:S(2)}) collective-permute-start(bf16[4,192,128]{2,1,0:T(8,128)(2,1)S(1)} %get-tuple-element.39), channel_id=1, source_target_pairs={{0,192},{64,0},{128,64},{192,128},{1,193},{65,1},{129,65},{193,129... | collective-permute-start | bytes 589832 | tf_op jit(solution)/shard_map/ppermute | solution.py:320
  40.3 6.9 %collective-permute-start.11 = (bf16[4,192,128]{2,1,0:T(8,128)(2,1)S(1)}, bf16[4,192,128]{2,1,0:T(8,128)(2,1)S(1)}, u32[]{:S(2)}, u32[]{:S(2)}) collective-permute-start(bf16[4,192,128]{2,1,0:T(8,128)(2,1)S(1)} %get-tuple-element.38.after), channel_id=1, source_target_pairs={{0,64},{64,128},{128,192},{192,0},{1,65},{65,129},{129,193},{193,1... | collective-permute-start | bytes 589832 | tf_op jit(solution)/shard_map/ppermute | solution.py:320
  41.7 5.5 %collective-permute-start.10 = (bf16[768,1024]{1,0:T(8,128)(2,1)S(1)}, bf16[768,1024]{1,0:T(8,128)(2,1)S(1)}, u32[]{:S(2)}, u32[]{:S(2)}) collective-permute-start(bf16[768,1024]{1,0:T(8,128)(2,1)S(1)} %join.1.refs_0_.refs_9_), channel_id=1, source_target_pairs={{0,1},{1,0},{2,3},{3,2},{4,5},{5,4},{6,7},{7,6},{8,9},{9,8},{10,11... | collective-permute-start | bytes 4718600 | tf_op jit(solution)/shard_map/ppermute | solution.py:324
  51.9 1.4 %collective-permute-start.15 = (f32[2,1536]{1,0:T(2,128)S(1)}, f32[2,1536]{1,0:T(2,128)S(1)}, u32[]{:S(2)}, u32[]{:S(2)}) collective-permute-start(f32[2,1536]{1,0:T(2,128)S(1)} %get-tuple-element.44.c), channel_id=1, source_target_pairs={{0,1},{1,0},{2,3},{3,2},{4,5},{5,4},{6,7},{7,6},{8,9},{9,8},{10,11... | collective-permute-start | bytes 36872 | tf_op jit(solution)/shard_map/ppermute | solution.py:324
  52.0 4.9 %collective-permute-start.13 = (f32[2,768]{1,0:T(2,128)S(1)}, f32[2,768]{1,0:T(2,128)S(1)}, u32[]{:S(2)}, u32[]{:S(2)}) collective-permute-start(f32[2,768]{1,0:T(2,128)S(1)} %get-tuple-element.43.r), channel_id=1, source_target_pairs={{0,8},{8,0},{16,24},{24,16},{1,9},{9,1},{17,25},{25,17},{2,10},{10... | collective-permute-start | bytes 18440 | tf_op jit(solution)/shard_map/ppermute | solution.py:324
  53.3 9.7 %collective-permute-start.18 = (f32[2,1536]{1,0:T(2,128)S(1)}, f32[2,1536]{1,0:T(2,128)S(1)}, u32[]{:S(2)}, u32[]{:S(2)}) collective-permute-start(f32[2,1536]{1,0:T(2,128)S(1)} %meet.1.refs_2_), channel_id=1, source_target_pairs={{0,6},{2,4},{4,2},{6,0},{1,7},{3,5},{5,3},{7,1},{8,14},{10,12},{12... | collective-permute-start | bytes 36872 | tf_op jit(solution)/shard_map/ppermute | solution.py:372
  55.7 7.3 %collective-permute-start.17 = (f32[2,1536]{1,0:T(2,128)S(1)}, f32[2,1536]{1,0:T(2,128)S(1)}, u32[]{:S(2)}, u32[]{:S(2)}) collective-permute-start(f32[2,1536]{1,0:T(2,128)S(1)} %meet.1.refs_2_), channel_id=1, source_target_pairs={{0,4},{2,6},{4,0},{6,2},{1,5},{3,7},{5,1},{7,3},{8,12},{10,14},{12... | collective-permute-start | bytes 36872 | tf_op jit(solution)/shard_map/ppermute | solution.py:372
  55.9 7.1 %collective-permute-start.16 = (f32[2,1536]{1,0:T(2,128)S(1)}, f32[2,1536]{1,0:T(2,128)S(1)}, u32[]{:S(2)}, u32[]{:S(2)}) collective-permute-start(f32[2,1536]{1,0:T(2,128)S(1)} %meet.1.refs_2_), channel_id=1, source_target_pairs={{0,2},{2,0},{4,6},{6,4},{1,3},{3,1},{5,7},{7,5},{8,10},{10,8},{12,... | collective-permute-start | bytes 36872 | tf_op jit(solution)/shard_map/ppermute | solution.py:372
  56.9 6.0 %collective-permute-start.14 = (f32[2,768]{1,0:T(2,128)S(1)}, f32[2,768]{1,0:T(2,128)S(1)}, u32[]{:S(2)}, u32[]{:S(2)}) collective-permute-start(f32[2,768]{1,0:T(2,128)S(1)} %meet_rows.1.refs_0_), channel_id=1, source_target_pairs={{0,24},{8,16},{16,8},{24,0},{1,25},{9,17},{17,9},{25,1},{2,26},{10... | collective-permute-start | bytes 18440 | tf_op jit(solution)/shard_map/ppermute | solution.py:324
  70.8 3.6 %collective-permute-start.19 = (s16[4,208,1024]{2,1,0:T(8,128)(2,1)S(1)}, s16[4,208,1024]{2,1,0:T(8,128)(2,1)S(1)}, u32[]{:S(2)}, u32[]{:S(2)}) collective-permute-start(s16[4,208,1024]{2,1,0:T(8,128)(2,1)S(1)} %get-tuple-element.48), channel_id=1, source_target_pairs={{0,1},{1,0},{2,3},{3,2},{4,5},{5,4},{6,7},{7,6},{8,9},{9,8},{10,11... | collective-permute-start | bytes 5111816 | tf_op jit(solution)/shard_map/ppermute | solution.py:324
  70.8 8.7 %collective-permute-start.24 = (s16[400,256]{1,0:T(8,128)(2,1)S(1)}, s16[400,256]{1,0:T(8,128)(2,1)S(1)}, u32[]{:S(2)}, u32[]{:S(2)}) collective-permute-start(s16[400,256]{1,0:T(8,128)(2,1)S(1)} %get-tuple-element.60), channel_id=1, source_target_pairs={{0,64},{64,128},{128,192},{192,0},{1,65},{65,129},{129,193},{193,1... | collective-permute-start | bytes 614408 | tf_op jit(solution)/shard_map/ppermute | solution.py:320
  71.2 8.3 %collective-permute-start.25 = (s16[400,256]{1,0:T(8,128)(2,1)S(1)}, s16[400,256]{1,0:T(8,128)(2,1)S(1)}, u32[]{:S(2)}, u32[]{:S(2)}) collective-permute-start(s16[400,256]{1,0:T(8,128)(2,1)S(1)} %get-tuple-element.61), channel_id=1, source_target_pairs={{0,192},{64,0},{128,64},{192,128},{1,193},{65,1},{129,65},{193,129... | collective-permute-start | bytes 614408 | tf_op jit(solution)/shard_map/ppermute | solution.py:320
  75.3 11.9 %collective-permute-start.20 = (s16[2,208,512]{2,1,0:T(8,128)(2,1)S(1)}, s16[2,208,512]{2,1,0:T(8,128)(2,1)S(1)}, u32[]{:S(2)}, u32[]{:S(2)}) collective-permute-start(s16[2,208,512]{2,1,0:T(8,128)(2,1)S(1)} %get-tuple-element.52), channel_id=1, source_target_pairs={{0,2},{2,0},{1,3},{3,1},{4,6},{6,4},{5,7},{7,5},{8,10},{10,8},{9,1... | collective-permute-start | bytes 1277960 | tf_op jit(solution)/shard_map/ppermute | solution.py:324
  76.4 11.6 %collective-permute-start.21 = (s16[2,208,512]{2,1,0:T(8,128)(2,1)S(1)}, s16[2,208,512]{2,1,0:T(8,128)(2,1)S(1)}, u32[]{:S(2)}, u32[]{:S(2)}) collective-permute-start(s16[2,208,512]{2,1,0:T(8,128)(2,1)S(1)} %get-tuple-element.53), channel_id=1, source_target_pairs={{0,4},{4,0},{1,5},{5,1},{2,6},{6,2},{3,7},{7,3},{8,12},{12,8},{9,1... | collective-permute-start | bytes 1277960 | tf_op jit(solution)/shard_map/ppermute | solution.py:324
  79.9 12.2 %collective-permute-start.26 = (s16[784,256]{1,0:T(8,128)(2,1)S(1)}, s16[784,256]{1,0:T(8,128)(2,1)S(1)}, u32[]{:S(2)}, u32[]{:S(2)}) collective-permute-start(s16[784,256]{1,0:T(8,128)(2,1)S(1)} %get-tuple-element.62), channel_id=1, source_target_pairs={{0,64},{64,128},{128,192},{192,0},{1,65},{65,129},{129,193},{193,1... | collective-permute-start | bytes 1204232 | tf_op jit(solution)/shard_map/ppermute | solution.py:320
  80.0 12.1 %collective-permute-start.27 = (s16[784,256]{1,0:T(8,128)(2,1)S(1)}, s16[784,256]{1,0:T(8,128)(2,1)S(1)}, u32[]{:S(2)}, u32[]{:S(2)}) collective-permute-start(s16[784,256]{1,0:T(8,128)(2,1)S(1)} %get-tuple-element.63), channel_id=1, source_target_pairs={{0,192},{64,0},{128,64},{192,128},{1,193},{65,1},{129,65},{193,129... | collective-permute-start | bytes 1204232 | tf_op jit(solution)/shard_map/ppermute | solution.py:320
  93.2 23.5 %all-to-all-start = ((s16[8,208,128]{2,1,0:T(8,128)(2,1)}), s16[8,208,128]{2,1,0:T(8,128)(2,1)S(1)}, u32[]{:S(2)}, u32[]{:S(2)}) async-start(s16[8,208,128]{2,1,0:T(8,128)(2,1)} %image_sum.1), calls=%async_computation | async-start | bytes 851968 | tf_op jit(solution)/shard_map/all_to_all | solution.py:405
  101.9 8.4 %collective-permute-start.22 = (s16[208,512]{1,0:T(8,128)(2,1)S(1)}, s16[208,512]{1,0:T(8,128)(2,1)S(1)}, u32[]{:S(2)}, u32[]{:S(2)}) collective-permute-start(s16[208,512]{1,0:T(8,128)(2,1)S(1)} %get-tuple-element.55), channel_id=1, source_target_pairs={{0,2},{2,0},{1,3},{3,1},{4,6},{6,4},{5,7},{7,5},{8,10},{10,8},{9,1... | collective-permute-start | bytes 638984 | tf_op jit(solution)/shard_map/ppermute | solution.py:324
  103.0 13.8 %collective-permute-start.23 = (s16[208,512]{1,0:T(8,128)(2,1)S(1)}, s16[208,512]{1,0:T(8,128)(2,1)S(1)}, u32[]{:S(2)}, u32[]{:S(2)}) collective-permute-start(s16[208,512]{1,0:T(8,128)(2,1)S(1)} %get-tuple-element.56), channel_id=1, source_target_pairs={{0,4},{4,0},{1,5},{5,1},{2,6},{6,2},{3,7},{7,3},{8,12},{12,8},{9,1... | collective-permute-start | bytes 638984 | tf_op jit(solution)/shard_map/ppermute | solution.py:324

commit v9 on v8

--- a/solution.py
+++ b/solution.py
@@ -309,8 +309,12 @@
 
 def image_sum_kernel(after, own, got1, got3, out):
     del after
+    out[...] = own[...] + decode(got1[...]) + decode(got3[...])
+
+
+def image_code_kernel(after_x, after_z, total, out):
+    del after_x, after_z
     rows, width = out.shape[1] - PAD, out.shape[2]
-    total = own[...] + decode(got1[...]) + decode(got3[...])
     for xh in range(2):
         for zh in range(4):
             encode(total[zh * rows : (zh + 1) * rows, xh * width : (xh + 1) * width], out.at[4 * xh + zh])
@@ -399,9 +403,12 @@
         in_specs=[vmem] * 5,
     )(own_key, keep_x, keep_z, flip(to_x, "xl", 2, 1), flip(to_z, "zl", 2, 1))
     from_x, from_z = flip(to_x, "xl", 2, 1), flip(to_z, "zl", 2, 1)
-    pieces = call(
-        image_sum_kernel, shape((8, rows + PAD, width), I16), "image_sum", 12, in_specs=[vmem] * 4
-    )(own_key, own, q1, q3)
+    total = call(image_sum_kernel, shape((n_im, 2 * width), F32), "image_sum", 12, in_specs=[vmem] * 4)(
+        own_key, own, q1, q3
+    )
+    pieces = call(image_code_kernel, shape((8, rows + PAD, width), I16), "image_code", 12, in_specs=[vmem] * 3)(
+        from_x, from_z, total
+    )
     pieces = lax.all_to_all(pieces, ("xh", "zh"), 0, 0)
     modality_grad, image_grad = call(
         last_kernel, [shape((rows, d), F32), shape((rows, width), F32)], "last", 8, in_specs=[vmem] * 4

time: 119 us -> 119 us (level)
  blocking collectives: 0 us -> 20.3 us
  waiting for transfers between devices: 45 us -> 33.4 us
  starting transfers between devices: 52.5 us -> 44.3 us
    all_to_all x0 -> x1, blocking collectives: none -> 20.3 us  [on_device(): pieces = lax.all_to_all(pieces, ('xh', 'zh'), 0, 0)]
    all_to_all x1 -> x0, starting transfers between devices: 8.73 us -> none  [on_device(): pieces = lax.all_to_all(pieces, ('xh', 'zh'), 0, 0)]
    ppermute x14, waiting for transfers between devices: 29.5 us -> 21 us  [flip(): return lax.ppermute(x, axis, [(i, i ^ d) for i in range(n)])]
    ppermute x11, waiting for transfers between devices: 15.5 us -> 12.4 us  [shift(): return lax.ppermute(x, axis, [(i, (i + k) % n) for i in range(n)])]
  transfers between devices with their start and end apart: 29 -> 28, of which waited for: 17 -> 17; matrix products, arithmetic and copies ran while one was open for 0% -> 0% of each run, Pallas kernels for 2% -> 2%
where the time goes in v9:
time: 119 us; the launch traced here: 117 us
  starting transfers between devices  44.3 us (37%)
  waiting for transfers between devices  33.4 us (28%)
  blocking collectives  20.3 us (17%)
  Pallas kernels  16.2 us (14%)
  local copies, waits for them, and re-layouts  2.53 us (2%)
    ppermute x11, starting transfers between devices, shift(): return lax.ppermute(x, axis, [(i, (i + k) % n) for i in range(n)])  21.9 us
    ppermute x14, waiting for transfers between devices, flip(): return lax.ppermute(x, axis, [(i, i ^ d) for i in range(n)])  21 us
    all_to_all x1, blocking collectives, on_device(): pieces = lax.all_to_all(pieces, ('xh', 'zh'), 0, 0)  20.3 us
    ppermute x14, starting transfers between devices, flip(): return lax.ppermute(x, axis, [(i, i ^ d) for i in range(n)])  18.8 us
    ppermute x11, waiting for transfers between devices, shift(): return lax.ppermute(x, axis, [(i, (i + k) % n) for i in range(n)])  12.4 us
    pallas_call x1, Pallas kernels, on_device(): call(functools.partial(weights_kernel, scale, tile), outs, 'weights', 36,...  7.84 us
    pallas_call x1, Pallas kernels, on_device(): call(functools.partial(scores_kernel, scale), [shape((n_im, n_ks), F32),...  4.69 us
    ppermute x3, starting transfers between devices, on_device(): lax.ppermute(cs, ('zl', 'xl'), [(i, i ^ k) for i in range(4)])  3.58 us
  transfers between devices with their start and end apart: 28, of which 17 were waited for; matrix products, arithmetic and copies ran while one was open for 0% of the time, Pallas kernels for 2%

profile of v9, /device:TPU:4, one launch (start us, length us, event | category | flops | bytes accessed | tf_op | source)
XLA Modules:
  0.0 117.5 jit_solution(11814213986732606889)
XLA Ops:
  0.6 2.3 %collective-permute-start = (bf16[192,128]{1,0:T(8,128)(2,1)}, bf16[192,128]{1,0:T(8,128)(2,1)S(1)}, u32[]{:S(2)}, u32[]{:S(2)}) collective-permute-start(bf16[192,128]{1,0:T(8,128)(2,1)} %image.1), channel_id=1, source_target_pairs={{0,32},{32,0},{1,33},{33,1},{2,34},{34,2},{3,35},{35,3},{4,36},{36... | collective-permute-start | bytes 147464 | tf_op jit(solution)/shard_map/ppermute | solution.py:328
  3.0 3.6 %collective-permute-done.twin = bf16[192,128]{1,0:T(8,128)(2,1)S(1)} collective-permute-done((bf16[192,128]{1,0:T(8,128)(2,1)}, bf16[192,128]{1,0:T(8,128)(2,1)S(1)}, u32[]{:S(2)}, u32[]{:S(2)}) %collective-permute-start) | collective-permute-done | bytes 49184 | tf_op jit(solution)/shard_map/ppermute | solution.py:328
  7.3 6.4 %collective-permute-start.3 = (bf16[2,192,128]{2,1,0:T(8,128)(2,1)S(1)}, bf16[2,192,128]{2,1,0:T(8,128)(2,1)S(1)}, u32[]{:S(2)}, u32[]{:S(2)}) collective-permute-start(bf16[2,192,128]{2,1,0:T(8,128)(2,1)S(1)} %pair.1.after.both), channel_id=1, source_target_pairs={{0,24},{8,0},{16,8},{24,16},{1,25},{9,1},{17,9},{25,17},{2,26},{10... | collective-permute-start | bytes 294920 | tf_op jit(solution)/shard_map/ppermute | solution.py:324
  14.7 2.8 %collective-permute-start.1 = (bf16[2,192,128]{2,1,0:T(8,128)(2,1)S(1)}, bf16[2,192,128]{2,1,0:T(8,128)(2,1)S(1)}, u32[]{:S(2)}, u32[]{:S(2)}) collective-permute-start(bf16[2,192,128]{2,1,0:T(8,128)(2,1)S(1)} %pair.1.after.both), channel_id=1, source_target_pairs={{0,8},{8,16},{16,24},{24,0},{1,9},{9,17},{17,25},{25,1},{2,10},{10... | collective-permute-start | bytes 294920 | tf_op jit(solution)/shard_map/ppermute | solution.py:324
  19.5 1.3 %collective-permute-start.4 = (bf16[192,1024]{1,0:T(8,128)(2,1)S(1)}, bf16[192,1024]{1,0:T(8,128)(2,1)S(1)}, u32[]{:S(2)}, u32[]{:S(2)}) collective-permute-start(bf16[192,1024]{1,0:T(8,128)(2,1)S(1)} %get-tuple-element.36.keys), channel_id=1, source_target_pairs={{0,2},{2,0},{1,3},{3,1},{4,6},{6,4},{5,7},{7,5},{8,10},{10,8},{9,1... | collective-permute-start | bytes 1179656 | tf_op jit(solution)/shard_map/ppermute | solution.py:328
  21.0 3.3 %collective-permute-done.2.b2 = bf16[2,192,128]{2,1,0:T(8,128)(2,1)S(1)} collective-permute-done((bf16[2,192,128]{2,1,0:T(8,128)(2,1)S(1)}, bf16[2,192,128]{2,1,0:T(8,128)(2,1)S(1)}, u32[]{:S(2)}, u32[]{:S(2)}) %collective-permute-start.2) | collective-permute-done | bytes 98336 | tf_op jit(solution)/shard_map/ppermute | solution.py:324
  25.3 3.0 %collective-permute-start.9 = (bf16[8,192,128]{2,1,0:T(8,128)(2,1)S(1)}, bf16[8,192,128]{2,1,0:T(8,128)(2,1)S(1)}, u32[]{:S(2)}, u32[]{:S(2)}) collective-permute-start(bf16[8,192,128]{2,1,0:T(8,128)(2,1)S(1)} %stack.1.after.refs_2_), channel_id=1, source_target_pairs={{0,192},{64,0},{128,64},{192,128},{1,193},{65,1},{129,65},{193,129... | collective-permute-start | bytes 1179656 | tf_op jit(solution)/shard_map/ppermute | solution.py:324
  28.4 1.1 collective-permute-start.7
  29.6 6.3 %collective-permute-done.5.z = bf16[192,1024]{1,0:T(8,128)(2,1)S(1)} collective-permute-done((bf16[192,1024]{1,0:T(8,128)(2,1)S(1)}, bf16[192,1024]{1,0:T(8,128)(2,1)S(1)}, u32[]{:S(2)}, u32[]{:S(2)}) %collective-permute-start.5) | collective-permute-done | bytes 393248 | tf_op jit(solution)/shard_map/ppermute | solution.py:328
  35.9 1.3 %collective-permute-start.6 = (bf16[96,1024]{1,0:T(8,128)(2,1)S(1)}, bf16[96,1024]{1,0:T(8,128)(2,1)S(1)}, u32[]{:S(2)}, u32[]{:S(2)}) collective-permute-start(bf16[96,1024]{1,0:T(8,128)(2,1)S(1)} %top.1), channel_id=1, source_target_pairs={{0,2},{2,0},{1,3},{3,1},{4,6},{6,4},{5,7},{7,5},{8,10},{10,8},{9,1... | collective-permute-start | bytes 589832 | tf_op jit(solution)/shard_map/ppermute | solution.py:328
  37.1 2.0 %collective-permute-done.8.behind.refs_3_ = bf16[8,192,128]{2,1,0:T(8,128)(2,1)S(1)} collective-permute-done((bf16[8,192,128]{2,1,0:T(8,128)(2,1)S(1)}, bf16[8,192,128]{2,1,0:T(8,128)(2,1)S(1)}, u32[]{:S(2)}, u32[]{:S(2)}) %collective-permute-start.8) | collective-permute-done | bytes 393248 | tf_op jit(solution)/shard_map/ppermute | solution.py:324
  39.2 1.1 collective-permute-start.12
  42.0 2.9 %collective-permute-done.12.b = bf16[4,192,128]{2,1,0:T(8,128)(2,1)S(1)} collective-permute-done((bf16[4,192,128]{2,1,0:T(8,128)(2,1)S(1)}, bf16[4,192,128]{2,1,0:T(8,128)(2,1)S(1)}, u32[]{:S(2)}, u32[]{:S(2)}) %collective-permute-start.12) | collective-permute-done | bytes 196640 | tf_op jit(solution)/shard_map/ppermute | solution.py:324
  44.9 2.2 %collective-permute-done.11.a = bf16[4,192,128]{2,1,0:T(8,128)(2,1)S(1)} collective-permute-done((bf16[4,192,128]{2,1,0:T(8,128)(2,1)S(1)}, bf16[4,192,128]{2,1,0:T(8,128)(2,1)S(1)}, u32[]{:S(2)}, u32[]{:S(2)}) %collective-permute-start.11) | collective-permute-done | bytes 196640 | tf_op jit(solution)/shard_map/ppermute | solution.py:324
  47.2 4.7 %scores.1 = (f32[768,1536]{1,0:T(8,128)S(1)}, bf16[768,1024]{1,0:T(8,128)(2,1)S(1)}, f32[2,768]{1,0:T(2,128)S(1)}, f32[2,1536]{1,0:T(2,128)S(1)}) custom-call(bf16[768,1024]{1,0:T(8,128)(2,1)S(1)} %join.1.refs_0_.refs_9_, bf16[768,1024]{1,0:T(8,128)(2,1)S(1)} %collective-permute-done.10.refs_1_.refs_10_, bf16[8,192,128]{2,1,0:T(8,128)(2,1)S(1)} %stack.1.after.refs_2_, ...), custom_call_target="tpu_custom_call" | custom-call | flops 1000 | bytes 1000 | tf_op jit(solution)/shard_map/scores/pallas_call | solution.py:366
  52.0 1.3 %collective-permute-start.13 = (f32[2,768]{1,0:T(2,128)S(1)}, f32[2,768]{1,0:T(2,128)S(1)}, u32[]{:S(2)}, u32[]{:S(2)}) collective-permute-start(f32[2,768]{1,0:T(2,128)S(1)} %get-tuple-element.43.r), channel_id=1, source_target_pairs={{0,8},{8,0},{16,24},{24,16},{1,9},{9,1},{17,25},{25,17},{2,10},{10... | collective-permute-start | bytes 18440 | tf_op jit(solution)/shard_map/ppermute | solution.py:328
  53.3 2.4 %collective-permute-start.18 = (f32[2,1536]{1,0:T(2,128)S(1)}, f32[2,1536]{1,0:T(2,128)S(1)}, u32[]{:S(2)}, u32[]{:S(2)}) collective-permute-start(f32[2,1536]{1,0:T(2,128)S(1)} %meet.1.refs_2_), channel_id=1, source_target_pairs={{0,6},{2,4},{4,2},{6,0},{1,7},{3,5},{5,3},{7,1},{8,14},{10,12},{12... | collective-permute-start | bytes 36872 | tf_op jit(solution)/shard_map/ppermute | solution.py:376
  56.9 4.3 %collective-permute-start.14 = (f32[2,768]{1,0:T(2,128)S(1)}, f32[2,768]{1,0:T(2,128)S(1)}, u32[]{:S(2)}, u32[]{:S(2)}) collective-permute-start(f32[2,768]{1,0:T(2,128)S(1)} %meet_rows.1.refs_0_), channel_id=1, source_target_pairs={{0,24},{8,16},{16,8},{24,0},{1,25},{9,17},{17,9},{25,1},{2,26},{10... | collective-permute-start | bytes 18440 | tf_op jit(solution)/shard_map/ppermute | solution.py:328
  61.2 1.8 %collective-permute-done.14.refs_1_ = f32[2,768]{1,0:T(2,128)S(1)} collective-permute-done((f32[2,768]{1,0:T(2,128)S(1)}, f32[2,768]{1,0:T(2,128)S(1)}, u32[]{:S(2)}, u32[]{:S(2)}) %collective-permute-start.14) | collective-permute-done | bytes 6176 | tf_op jit(solution)/shard_map/ppermute | solution.py:328
  63.0 7.8 %weights.1 = (f32[768,256]{1,0:T(8,128)S(1)}, f32[768,256]{1,0:T(8,128)S(1)}, f32[768,256]{1,0:T(8,128)S(1)}, s16[400,256]{1,0:T(8,128)(2,1)S(1)}, s16[400,256]{...) custom-call(f32[2,768]{1,0:T(2,128)S(1)} %meet_rows.1.refs_0_, ...), custom_call_target="tpu_custom_call" | custom-call | flops 1000 | bytes 1000 | tf_op jit(solution)/shard_map/weights/pallas_call | solution.py:379
  71.2 2.9 %collective-permute-start.25 = (s16[400,256]{1,0:T(8,128)(2,1)S(1)}, s16[400,256]{1,0:T(8,128)(2,1)S(1)}, u32[]{:S(2)}, u32[]{:S(2)}) collective-permute-start(s16[400,256]{1,0:T(8,128)(2,1)S(1)} %get-tuple-element.61), channel_id=1, source_target_pairs={{0,192},{64,0},{128,64},{192,128},{1,193},{65,1},{129,65},{193,129... | collective-permute-start | bytes 614408 | tf_op jit(solution)/shard_map/ppermute | solution.py:324
  75.3 1.1 collective-permute-start.20
  76.4 1.8 %collective-permute-start.21 = (s16[2,208,512]{2,1,0:T(8,128)(2,1)S(1)}, s16[2,208,512]{2,1,0:T(8,128)(2,1)S(1)}, u32[]{:S(2)}, u32[]{:S(2)}) collective-permute-start(s16[2,208,512]{2,1,0:T(8,128)(2,1)S(1)} %get-tuple-element.53), channel_id=1, source_target_pairs={{0,4},{4,0},{1,5},{5,1},{2,6},{6,2},{3,7},{7,3},{8,12},{12,8},{9,1... | collective-permute-start | bytes 1277960 | tf_op jit(solution)/shard_map/ppermute | solution.py:328
  78.2 1.3 %collective-permute-done.24.got_a = s16[400,256]{1,0:T(8,128)(2,1)S(1)} collective-permute-done((s16[400,256]{1,0:T(8,128)(2,1)S(1)}, s16[400,256]{1,0:T(8,128)(2,1)S(1)}, u32[]{:S(2)}, u32[]{:S(2)}) %collective-permute-start.24) | collective-permute-done | bytes 204832 | tf_op jit(solution)/shard_map/ppermute | solution.py:324
  80.0 3.2 %collective-permute-start.27 = (s16[784,256]{1,0:T(8,128)(2,1)S(1)}, s16[784,256]{1,0:T(8,128)(2,1)S(1)}, u32[]{:S(2)}, u32[]{:S(2)}) collective-permute-start(s16[784,256]{1,0:T(8,128)(2,1)S(1)} %get-tuple-element.63), channel_id=1, source_target_pairs={{0,192},{64,0},{128,64},{192,128},{1,193},{65,1},{129,65},{193,129... | collective-permute-start | bytes 1204232 | tf_op jit(solution)/shard_map/ppermute | solution.py:324
  83.2 4.1 %collective-permute-done.20.from_x = s16[2,208,512]{2,1,0:T(8,128)(2,1)S(1)} collective-permute-done((s16[2,208,512]{2,1,0:T(8,128)(2,1)S(1)}, s16[2,208,512]{2,1,0:T(8,128)(2,1)S(1)}, u32[]{:S(2)}, u32[]{:S(2)}) %collective-permute-start.20) | collective-permute-done | bytes 426016 | tf_op jit(solution)/shard_map/ppermute | solution.py:328
  88.5 1.3 %collective-permute-start.22 = (s16[208,512]{1,0:T(8,128)(2,1)S(1)}, s16[208,512]{1,0:T(8,128)(2,1)S(1)}, u32[]{:S(2)}, u32[]{:S(2)}) collective-permute-start(s16[208,512]{1,0:T(8,128)(2,1)S(1)} %get-tuple-element.55), channel_id=1, source_target_pairs={{0,2},{2,0},{1,3},{3,1},{4,6},{6,4},{5,7},{7,5},{8,10},{10,8},{9,1... | collective-permute-start | bytes 638984 | tf_op jit(solution)/shard_map/ppermute | solution.py:328
  89.8 1.7 %collective-permute-start.23 = (s16[208,512]{1,0:T(8,128)(2,1)S(1)}, s16[208,512]{1,0:T(8,128)(2,1)S(1)}, u32[]{:S(2)}, u32[]{:S(2)}) collective-permute-start(s16[208,512]{1,0:T(8,128)(2,1)S(1)} %get-tuple-element.56), channel_id=1, source_target_pairs={{0,4},{4,0},{1,5},{5,1},{2,6},{6,2},{3,7},{7,3},{8,12},{12,8},{9,1... | collective-permute-start | bytes 638984 | tf_op jit(solution)/shard_map/ppermute | solution.py:328
  92.3 2.5 %collective-permute-done.22.after_x.from_x = s16[208,512]{1,0:T(8,128)(2,1)S(1)} collective-permute-done((s16[208,512]{1,0:T(8,128)(2,1)S(1)}, s16[208,512]{1,0:T(8,128)(2,1)S(1)}, u32[]{:S(2)}, u32[]{:S(2)}) %collective-permute-start.22) | collective-permute-done | bytes 213024 | tf_op jit(solution)/shard_map/ppermute | solution.py:328
  94.8 1.2 %collective-permute-done.23.after_z.from_z = s16[208,512]{1,0:T(8,128)(2,1)S(1)} collective-permute-done((s16[208,512]{1,0:T(8,128)(2,1)S(1)}, s16[208,512]{1,0:T(8,128)(2,1)S(1)}, u32[]{:S(2)}, u32[]{:S(2)}) %collective-permute-start.23) | collective-permute-done | bytes 213024 | tf_op jit(solution)/shard_map/ppermute | solution.py:328
  96.2 20.3 %all_to_all.5.pieces = s16[8,208,128]{2,1,0:T(8,128)(2,1)S(1)} all-to-all(s16[8,208,128]{2,1,0:T(8,128)(2,1)S(1)} %image_code.1), channel_id=1, replica_groups=mesh['y'=4,'xh'=2,'zh'=4,'zl'=2,'xl'=2,'core'=2] {'xh','zh'}, dimensions={0} | all-to-all | bytes 851968 | tf_op jit(solution)/shard_map/all_to_all | solution.py:412
  116.5 1.0 last.1
  (50 shorter events, 12.5 us)
Async XLA Ops:
  0.6 5.9 %collective-permute-start = (bf16[192,128]{1,0:T(8,128)(2,1)}, bf16[192,128]{1,0:T(8,128)(2,1)S(1)}, u32[]{:S(2)}, u32[]{:S(2)}) collective-permute-start(bf16[192,128]{1,0:T(8,128)(2,1)} %image.1), channel_id=1, source_target_pairs={{0,32},{32,0},{1,33},{33,1},{2,34},{34,2},{3,35},{35,3},{4,36},{36... | collective-permute-start | bytes 147464 | tf_op jit(solution)/shard_map/ppermute | solution.py:328
  6.5 0.8 copy-start.1
  7.3 13.6 %collective-permute-start.3 = (bf16[2,192,128]{2,1,0:T(8,128)(2,1)S(1)}, bf16[2,192,128]{2,1,0:T(8,128)(2,1)S(1)}, u32[]{:S(2)}, u32[]{:S(2)}) collective-permute-start(bf16[2,192,128]{2,1,0:T(8,128)(2,1)S(1)} %pair.1.after.both), channel_id=1, source_target_pairs={{0,24},{8,0},{16,8},{24,16},{1,25},{9,1},{17,9},{25,17},{2,26},{10... | collective-permute-start | bytes 294920 | tf_op jit(solution)/shard_map/ppermute | solution.py:324
  13.7 10.5 %collective-permute-start.2 = (bf16[2,192,128]{2,1,0:T(8,128)(2,1)S(1)}, bf16[2,192,128]{2,1,0:T(8,128)(2,1)S(1)}, u32[]{:S(2)}, u32[]{:S(2)}) collective-permute-start(bf16[2,192,128]{2,1,0:T(8,128)(2,1)S(1)} %pair.1.after.both), channel_id=1, source_target_pairs={{0,16},{8,24},{16,0},{24,8},{1,17},{9,25},{17,1},{25,9},{2,18},{10... | collective-permute-start | bytes 294920 | tf_op jit(solution)/shard_map/ppermute | solution.py:324
  14.7 9.5 %collective-permute-start.1 = (bf16[2,192,128]{2,1,0:T(8,128)(2,1)S(1)}, bf16[2,192,128]{2,1,0:T(8,128)(2,1)S(1)}, u32[]{:S(2)}, u32[]{:S(2)}) collective-permute-start(bf16[2,192,128]{2,1,0:T(8,128)(2,1)S(1)} %pair.1.after.both), channel_id=1, source_target_pairs={{0,8},{8,16},{16,24},{24,0},{1,9},{9,17},{17,25},{25,1},{2,10},{10... | collective-permute-start | bytes 294920 | tf_op jit(solution)/shard_map/ppermute | solution.py:324
  17.5 1.0 copy-start
  18.5 0.7 copy-start.2
  19.5 8.9 %collective-permute-start.4 = (bf16[192,1024]{1,0:T(8,128)(2,1)S(1)}, bf16[192,1024]{1,0:T(8,128)(2,1)S(1)}, u32[]{:S(2)}, u32[]{:S(2)}) collective-permute-start(bf16[192,1024]{1,0:T(8,128)(2,1)S(1)} %get-tuple-element.36.keys), channel_id=1, source_target_pairs={{0,2},{2,0},{1,3},{3,1},{4,6},{6,4},{5,7},{7,5},{8,10},{10,8},{9,1... | collective-permute-start | bytes 1179656 | tf_op jit(solution)/shard_map/ppermute | solution.py:328
  24.3 11.5 %collective-permute-start.5 = (bf16[192,1024]{1,0:T(8,128)(2,1)S(1)}, bf16[192,1024]{1,0:T(8,128)(2,1)S(1)}, u32[]{:S(2)}, u32[]{:S(2)}) collective-permute-start(bf16[192,1024]{1,0:T(8,128)(2,1)S(1)} %hold.1.own), channel_id=1, source_target_pairs={{0,4},{4,0},{1,5},{5,1},{2,6},{6,2},{3,7},{7,3},{8,12},{12,8},{9,1... | collective-permute-start | bytes 1179656 | tf_op jit(solution)/shard_map/ppermute | solution.py:328
  25.3 11.9 %collective-permute-start.9 = (bf16[8,192,128]{2,1,0:T(8,128)(2,1)S(1)}, bf16[8,192,128]{2,1,0:T(8,128)(2,1)S(1)}, u32[]{:S(2)}, u32[]{:S(2)}) collective-permute-start(bf16[8,192,128]{2,1,0:T(8,128)(2,1)S(1)} %stack.1.after.refs_2_), channel_id=1, source_target_pairs={{0,192},{64,0},{128,64},{192,128},{1,193},{65,1},{129,65},{193,129... | collective-permute-start | bytes 1179656 | tf_op jit(solution)/shard_map/ppermute | solution.py:324
  28.3 10.9 %collective-permute-start.8 = (bf16[8,192,128]{2,1,0:T(8,128)(2,1)S(1)}, bf16[8,192,128]{2,1,0:T(8,128)(2,1)S(1)}, u32[]{:S(2)}, u32[]{:S(2)}) collective-permute-start(bf16[8,192,128]{2,1,0:T(8,128)(2,1)S(1)} %stack.1.after.refs_2_), channel_id=1, source_target_pairs={{0,64},{64,128},{128,192},{192,0},{1,65},{65,129},{129,193},{193,1... | collective-permute-start | bytes 1179656 | tf_op jit(solution)/shard_map/ppermute | solution.py:324
  28.4 12.9 %collective-permute-start.7 = (bf16[96,1024]{1,0:T(8,128)(2,1)S(1)}, bf16[96,1024]{1,0:T(8,128)(2,1)S(1)}, u32[]{:S(2)}, u32[]{:S(2)}) collective-permute-start(bf16[96,1024]{1,0:T(8,128)(2,1)S(1)} %low.1), channel_id=1, source_target_pairs={{0,4},{4,0},{1,5},{5,1},{2,6},{6,2},{3,7},{7,3},{8,12},{12,8},{9,1... | collective-permute-start | bytes 589832 | tf_op jit(solution)/shard_map/ppermute | solution.py:328
  35.9 5.8 %collective-permute-start.6 = (bf16[96,1024]{1,0:T(8,128)(2,1)S(1)}, bf16[96,1024]{1,0:T(8,128)(2,1)S(1)}, u32[]{:S(2)}, u32[]{:S(2)}) collective-permute-start(bf16[96,1024]{1,0:T(8,128)(2,1)S(1)} %top.1), channel_id=1, source_target_pairs={{0,2},{2,0},{1,3},{3,1},{4,6},{6,4},{5,7},{7,5},{8,10},{10,8},{9,1... | collective-permute-start | bytes 589832 | tf_op jit(solution)/shard_map/ppermute | solution.py:328
  39.2 5.7 %collective-permute-start.12 = (bf16[4,192,128]{2,1,0:T(8,128)(2,1)S(1)}, bf16[4,192,128]{2,1,0:T(8,128)(2,1)S(1)}, u32[]{:S(2)}, u32[]{:S(2)}) collective-permute-start(bf16[4,192,128]{2,1,0:T(8,128)(2,1)S(1)} %get-tuple-element.39), channel_id=1, source_target_pairs={{0,192},{64,0},{128,64},{192,128},{1,193},{65,1},{129,65},{193,129... | collective-permute-start | bytes 589832 | tf_op jit(solution)/shard_map/ppermute | solution.py:324
  40.3 6.9 %collective-permute-start.11 = (bf16[4,192,128]{2,1,0:T(8,128)(2,1)S(1)}, bf16[4,192,128]{2,1,0:T(8,128)(2,1)S(1)}, u32[]{:S(2)}, u32[]{:S(2)}) collective-permute-start(bf16[4,192,128]{2,1,0:T(8,128)(2,1)S(1)} %get-tuple-element.38.after), channel_id=1, source_target_pairs={{0,64},{64,128},{128,192},{192,0},{1,65},{65,129},{129,193},{193,1... | collective-permute-start | bytes 589832 | tf_op jit(solution)/shard_map/ppermute | solution.py:324
  41.7 5.5 %collective-permute-start.10 = (bf16[768,1024]{1,0:T(8,128)(2,1)S(1)}, bf16[768,1024]{1,0:T(8,128)(2,1)S(1)}, u32[]{:S(2)}, u32[]{:S(2)}) collective-permute-start(bf16[768,1024]{1,0:T(8,128)(2,1)S(1)} %join.1.refs_0_.refs_9_), channel_id=1, source_target_pairs={{0,1},{1,0},{2,3},{3,2},{4,5},{5,4},{6,7},{7,6},{8,9},{9,8},{10,11... | collective-permute-start | bytes 4718600 | tf_op jit(solution)/shard_map/ppermute | solution.py:328
  51.9 1.4 %collective-permute-start.15 = (f32[2,1536]{1,0:T(2,128)S(1)}, f32[2,1536]{1,0:T(2,128)S(1)}, u32[]{:S(2)}, u32[]{:S(2)}) collective-permute-start(f32[2,1536]{1,0:T(2,128)S(1)} %get-tuple-element.44.c), channel_id=1, source_target_pairs={{0,1},{1,0},{2,3},{3,2},{4,5},{5,4},{6,7},{7,6},{8,9},{9,8},{10,11... | collective-permute-start | bytes 36872 | tf_op jit(solution)/shard_map/ppermute | solution.py:328
  52.0 4.9 %collective-permute-start.13 = (f32[2,768]{1,0:T(2,128)S(1)}, f32[2,768]{1,0:T(2,128)S(1)}, u32[]{:S(2)}, u32[]{:S(2)}) collective-permute-start(f32[2,768]{1,0:T(2,128)S(1)} %get-tuple-element.43.r), channel_id=1, source_target_pairs={{0,8},{8,0},{16,24},{24,16},{1,9},{9,1},{17,25},{25,17},{2,10},{10... | collective-permute-start | bytes 18440 | tf_op jit(solution)/shard_map/ppermute | solution.py:328
  53.3 9.7 %collective-permute-start.18 = (f32[2,1536]{1,0:T(2,128)S(1)}, f32[2,1536]{1,0:T(2,128)S(1)}, u32[]{:S(2)}, u32[]{:S(2)}) collective-permute-start(f32[2,1536]{1,0:T(2,128)S(1)} %meet.1.refs_2_), channel_id=1, source_target_pairs={{0,6},{2,4},{4,2},{6,0},{1,7},{3,5},{5,3},{7,1},{8,14},{10,12},{12... | collective-permute-start | bytes 36872 | tf_op jit(solution)/shard_map/ppermute | solution.py:376
  55.7 7.3 %collective-permute-start.17 = (f32[2,1536]{1,0:T(2,128)S(1)}, f32[2,1536]{1,0:T(2,128)S(1)}, u32[]{:S(2)}, u32[]{:S(2)}) collective-permute-start(f32[2,1536]{1,0:T(2,128)S(1)} %meet.1.refs_2_), channel_id=1, source_target_pairs={{0,4},{2,6},{4,0},{6,2},{1,5},{3,7},{5,1},{7,3},{8,12},{10,14},{12... | collective-permute-start | bytes 36872 | tf_op jit(solution)/shard_map/ppermute | solution.py:376
  55.9 7.1 %collective-permute-start.16 = (f32[2,1536]{1,0:T(2,128)S(1)}, f32[2,1536]{1,0:T(2,128)S(1)}, u32[]{:S(2)}, u32[]{:S(2)}) collective-permute-start(f32[2,1536]{1,0:T(2,128)S(1)} %meet.1.refs_2_), channel_id=1, source_target_pairs={{0,2},{2,0},{4,6},{6,4},{1,3},{3,1},{5,7},{7,5},{8,10},{10,8},{12,... | collective-permute-start | bytes 36872 | tf_op jit(solution)/shard_map/ppermute | solution.py:376
  56.9 6.0 %collective-permute-start.14 = (f32[2,768]{1,0:T(2,128)S(1)}, f32[2,768]{1,0:T(2,128)S(1)}, u32[]{:S(2)}, u32[]{:S(2)}) collective-permute-start(f32[2,768]{1,0:T(2,128)S(1)} %meet_rows.1.refs_0_), channel_id=1, source_target_pairs={{0,24},{8,16},{16,8},{24,0},{1,25},{9,17},{17,9},{25,1},{2,26},{10... | collective-permute-start | bytes 18440 | tf_op jit(solution)/shard_map/ppermute | solution.py:328
  70.8 3.6 %collective-permute-start.19 = (s16[4,208,1024]{2,1,0:T(8,128)(2,1)S(1)}, s16[4,208,1024]{2,1,0:T(8,128)(2,1)S(1)}, u32[]{:S(2)}, u32[]{:S(2)}) collective-permute-start(s16[4,208,1024]{2,1,0:T(8,128)(2,1)S(1)} %get-tuple-element.48), channel_id=1, source_target_pairs={{0,1},{1,0},{2,3},{3,2},{4,5},{5,4},{6,7},{7,6},{8,9},{9,8},{10,11... | collective-permute-start | bytes 5111816 | tf_op jit(solution)/shard_map/ppermute | solution.py:328
  70.8 8.7 %collective-permute-start.24 = (s16[400,256]{1,0:T(8,128)(2,1)S(1)}, s16[400,256]{1,0:T(8,128)(2,1)S(1)}, u32[]{:S(2)}, u32[]{:S(2)}) collective-permute-start(s16[400,256]{1,0:T(8,128)(2,1)S(1)} %get-tuple-element.60), channel_id=1, source_target_pairs={{0,64},{64,128},{128,192},{192,0},{1,65},{65,129},{129,193},{193,1... | collective-permute-start | bytes 614408 | tf_op jit(solution)/shard_map/ppermute | solution.py:324
  71.2 8.3 %collective-permute-start.25 = (s16[400,256]{1,0:T(8,128)(2,1)S(1)}, s16[400,256]{1,0:T(8,128)(2,1)S(1)}, u32[]{:S(2)}, u32[]{:S(2)}) collective-permute-start(s16[400,256]{1,0:T(8,128)(2,1)S(1)} %get-tuple-element.61), channel_id=1, source_target_pairs={{0,192},{64,0},{128,64},{192,128},{1,193},{65,1},{129,65},{193,129... | collective-permute-start | bytes 614408 | tf_op jit(solution)/shard_map/ppermute | solution.py:324
  75.3 11.9 %collective-permute-start.20 = (s16[2,208,512]{2,1,0:T(8,128)(2,1)S(1)}, s16[2,208,512]{2,1,0:T(8,128)(2,1)S(1)}, u32[]{:S(2)}, u32[]{:S(2)}) collective-permute-start(s16[2,208,512]{2,1,0:T(8,128)(2,1)S(1)} %get-tuple-element.52), channel_id=1, source_target_pairs={{0,2},{2,0},{1,3},{3,1},{4,6},{6,4},{5,7},{7,5},{8,10},{10,8},{9,1... | collective-permute-start | bytes 1277960 | tf_op jit(solution)/shard_map/ppermute | solution.py:328
  76.4 11.6 %collective-permute-start.21 = (s16[2,208,512]{2,1,0:T(8,128)(2,1)S(1)}, s16[2,208,512]{2,1,0:T(8,128)(2,1)S(1)}, u32[]{:S(2)}, u32[]{:S(2)}) collective-permute-start(s16[2,208,512]{2,1,0:T(8,128)(2,1)S(1)} %get-tuple-element.53), channel_id=1, source_target_pairs={{0,4},{4,0},{1,5},{5,1},{2,6},{6,2},{3,7},{7,3},{8,12},{12,8},{9,1... | collective-permute-start | bytes 1277960 | tf_op jit(solution)/shard_map/ppermute | solution.py:328
  79.9 12.2 %collective-permute-start.26 = (s16[784,256]{1,0:T(8,128)(2,1)S(1)}, s16[784,256]{1,0:T(8,128)(2,1)S(1)}, u32[]{:S(2)}, u32[]{:S(2)}) collective-permute-start(s16[784,256]{1,0:T(8,128)(2,1)S(1)} %get-tuple-element.62), channel_id=1, source_target_pairs={{0,64},{64,128},{128,192},{192,0},{1,65},{65,129},{129,193},{193,1... | collective-permute-start | bytes 1204232 | tf_op jit(solution)/shard_map/ppermute | solution.py:324
  80.0 12.1 %collective-permute-start.27 = (s16[784,256]{1,0:T(8,128)(2,1)S(1)}, s16[784,256]{1,0:T(8,128)(2,1)S(1)}, u32[]{:S(2)}, u32[]{:S(2)}) collective-permute-start(s16[784,256]{1,0:T(8,128)(2,1)S(1)} %get-tuple-element.63), channel_id=1, source_target_pairs={{0,192},{64,0},{128,64},{192,128},{1,193},{65,1},{129,65},{193,129... | collective-permute-start | bytes 1204232 | tf_op jit(solution)/shard_map/ppermute | solution.py:324
  88.5 6.3 %collective-permute-start.22 = (s16[208,512]{1,0:T(8,128)(2,1)S(1)}, s16[208,512]{1,0:T(8,128)(2,1)S(1)}, u32[]{:S(2)}, u32[]{:S(2)}) collective-permute-start(s16[208,512]{1,0:T(8,128)(2,1)S(1)} %get-tuple-element.55), channel_id=1, source_target_pairs={{0,2},{2,0},{1,3},{3,1},{4,6},{6,4},{5,7},{7,5},{8,10},{10,8},{9,1... | collective-permute-start | bytes 638984 | tf_op jit(solution)/shard_map/ppermute | solution.py:328
  89.8 6.2 %collective-permute-start.23 = (s16[208,512]{1,0:T(8,128)(2,1)S(1)}, s16[208,512]{1,0:T(8,128)(2,1)S(1)}, u32[]{:S(2)}, u32[]{:S(2)}) collective-permute-start(s16[208,512]{1,0:T(8,128)(2,1)S(1)} %get-tuple-element.56), channel_id=1, source_target_pairs={{0,4},{4,0},{1,5},{5,1},{2,6},{6,2},{3,7},{7,3},{8,12},{12,8},{9,1... | collective-permute-start | bytes 638984 | tf_op jit(solution)/shard_map/ppermute | solution.py:328

commit v10 on v9

--- a/solution.py
+++ b/solution.py
@@ -362,7 +362,7 @@
     )
     ks = [k0, flip(k0, "core", 2, 1)]
 
-    tile = min(384, n_im)
+    tile = n_im
     scores, im, rs, cs = call(
         functools.partial(scores_kernel, scale),
         [shape((n_im, n_ks), F32), shape((n_im, d), BF16), shape((2, n_im), F32), shape((2, n_ks), F32)],

time: 119 us -> 119 us (level)
  no operation moved by 1% of the time
where the time goes in v10:
time: 119 us; the launch traced here: 118 us
  starting transfers between devices  44.3 us (37%)
  waiting for transfers between devices  33.4 us (28%)
  blocking collectives  20.3 us (17%)
  Pallas kernels  16.2 us (14%)
  local copies, waits for them, and re-layouts  2.53 us (2%)
    ppermute x11, starting transfers between devices, shift(): return lax.ppermute(x, axis, [(i, (i + k) % n) for i in range(n)])  21.9 us
    ppermute x14, waiting for transfers between devices, flip(): return lax.ppermute(x, axis, [(i, i ^ d) for i in range(n)])  21 us
    all_to_all x1, blocking collectives, on_device(): pieces = lax.all_to_all(pieces, ('xh', 'zh'), 0, 0)  20.3 us
    ppermute x14, starting transfers between devices, flip(): return lax.ppermute(x, axis, [(i, i ^ d) for i in range(n)])  18.8 us
    ppermute x11, waiting for transfers between devices, shift(): return lax.ppermute(x, axis, [(i, (i + k) % n) for i in range(n)])  12.4 us
    pallas_call x1, Pallas kernels, on_device(): call(functools.partial(weights_kernel, scale, tile), outs, 'weights', 36,...  7.88 us
    pallas_call x1, Pallas kernels, on_device(): call(functools.partial(scores_kernel, scale), [shape((n_im, n_ks), F32),...  4.69 us
    ppermute x3, starting transfers between devices, on_device(): lax.ppermute(cs, ('zl', 'xl'), [(i, i ^ k) for i in range(4)])  3.58 us
  transfers between devices with their start and end apart: 28, of which 17 were waited for; matrix products, arithmetic and copies ran while one was open for 0% of the time, Pallas kernels for 2%

profile of v10, /device:TPU:4, one launch (start us, length us, event | category | flops | bytes accessed | tf_op | source)
XLA Modules:
  0.0 117.5 jit_solution(7119067646612235295)
XLA Ops:
  0.6 2.3 %collective-permute-start = (bf16[192,128]{1,0:T(8,128)(2,1)}, bf16[192,128]{1,0:T(8,128)(2,1)S(1)}, u32[]{:S(2)}, u32[]{:S(2)}) collective-permute-start(bf16[192,128]{1,0:T(8,128)(2,1)} %image.1), channel_id=1, source_target_pairs={{0,32},{32,0},{1,33},{33,1},{2,34},{34,2},{3,35},{35,3},{4,36},{36... | collective-permute-start | bytes 147464 | tf_op jit(solution)/shard_map/ppermute | solution.py:328
  3.0 3.6 %collective-permute-done.twin = bf16[192,128]{1,0:T(8,128)(2,1)S(1)} collective-permute-done((bf16[192,128]{1,0:T(8,128)(2,1)}, bf16[192,128]{1,0:T(8,128)(2,1)S(1)}, u32[]{:S(2)}, u32[]{:S(2)}) %collective-permute-start) | collective-permute-done | bytes 49184 | tf_op jit(solution)/shard_map/ppermute | solution.py:328
  7.3 6.4 %collective-permute-start.3 = (bf16[2,192,128]{2,1,0:T(8,128)(2,1)S(1)}, bf16[2,192,128]{2,1,0:T(8,128)(2,1)S(1)}, u32[]{:S(2)}, u32[]{:S(2)}) collective-permute-start(bf16[2,192,128]{2,1,0:T(8,128)(2,1)S(1)} %pair.1.after.both), channel_id=1, source_target_pairs={{0,24},{8,0},{16,8},{24,16},{1,25},{9,1},{17,9},{25,17},{2,26},{10... | collective-permute-start | bytes 294920 | tf_op jit(solution)/shard_map/ppermute | solution.py:324
  14.7 2.8 %collective-permute-start.1 = (bf16[2,192,128]{2,1,0:T(8,128)(2,1)S(1)}, bf16[2,192,128]{2,1,0:T(8,128)(2,1)S(1)}, u32[]{:S(2)}, u32[]{:S(2)}) collective-permute-start(bf16[2,192,128]{2,1,0:T(8,128)(2,1)S(1)} %pair.1.after.both), channel_id=1, source_target_pairs={{0,8},{8,16},{16,24},{24,0},{1,9},{9,17},{17,25},{25,1},{2,10},{10... | collective-permute-start | bytes 294920 | tf_op jit(solution)/shard_map/ppermute | solution.py:324
  19.5 1.3 %collective-permute-start.4 = (bf16[192,1024]{1,0:T(8,128)(2,1)S(1)}, bf16[192,1024]{1,0:T(8,128)(2,1)S(1)}, u32[]{:S(2)}, u32[]{:S(2)}) collective-permute-start(bf16[192,1024]{1,0:T(8,128)(2,1)S(1)} %get-tuple-element.36.keys), channel_id=1, source_target_pairs={{0,2},{2,0},{1,3},{3,1},{4,6},{6,4},{5,7},{7,5},{8,10},{10,8},{9,1... | collective-permute-start | bytes 1179656 | tf_op jit(solution)/shard_map/ppermute | solution.py:328
  21.0 3.3 %collective-permute-done.2.b2 = bf16[2,192,128]{2,1,0:T(8,128)(2,1)S(1)} collective-permute-done((bf16[2,192,128]{2,1,0:T(8,128)(2,1)S(1)}, bf16[2,192,128]{2,1,0:T(8,128)(2,1)S(1)}, u32[]{:S(2)}, u32[]{:S(2)}) %collective-permute-start.2) | collective-permute-done | bytes 98336 | tf_op jit(solution)/shard_map/ppermute | solution.py:324
  25.3 3.0 %collective-permute-start.9 = (bf16[8,192,128]{2,1,0:T(8,128)(2,1)S(1)}, bf16[8,192,128]{2,1,0:T(8,128)(2,1)S(1)}, u32[]{:S(2)}, u32[]{:S(2)}) collective-permute-start(bf16[8,192,128]{2,1,0:T(8,128)(2,1)S(1)} %stack.1.after.refs_2_), channel_id=1, source_target_pairs={{0,192},{64,0},{128,64},{192,128},{1,193},{65,1},{129,65},{193,129... | collective-permute-start | bytes 1179656 | tf_op jit(solution)/shard_map/ppermute | solution.py:324
  28.4 1.1 collective-permute-start.7
  29.6 6.3 %collective-permute-done.5.z = bf16[192,1024]{1,0:T(8,128)(2,1)S(1)} collective-permute-done((bf16[192,1024]{1,0:T(8,128)(2,1)S(1)}, bf16[192,1024]{1,0:T(8,128)(2,1)S(1)}, u32[]{:S(2)}, u32[]{:S(2)}) %collective-permute-start.5) | collective-permute-done | bytes 393248 | tf_op jit(solution)/shard_map/ppermute | solution.py:328
  35.9 1.3 %collective-permute-start.6 = (bf16[96,1024]{1,0:T(8,128)(2,1)S(1)}, bf16[96,1024]{1,0:T(8,128)(2,1)S(1)}, u32[]{:S(2)}, u32[]{:S(2)}) collective-permute-start(bf16[96,1024]{1,0:T(8,128)(2,1)S(1)} %top.1), channel_id=1, source_target_pairs={{0,2},{2,0},{1,3},{3,1},{4,6},{6,4},{5,7},{7,5},{8,10},{10,8},{9,1... | collective-permute-start | bytes 589832 | tf_op jit(solution)/shard_map/ppermute | solution.py:328
  37.1 2.0 %collective-permute-done.8.behind.refs_3_ = bf16[8,192,128]{2,1,0:T(8,128)(2,1)S(1)} collective-permute-done((bf16[8,192,128]{2,1,0:T(8,128)(2,1)S(1)}, bf16[8,192,128]{2,1,0:T(8,128)(2,1)S(1)}, u32[]{:S(2)}, u32[]{:S(2)}) %collective-permute-start.8) | collective-permute-done | bytes 393248 | tf_op jit(solution)/shard_map/ppermute | solution.py:324
  39.2 1.1 collective-permute-start.12
  42.0 2.9 %collective-permute-done.12.b = bf16[4,192,128]{2,1,0:T(8,128)(2,1)S(1)} collective-permute-done((bf16[4,192,128]{2,1,0:T(8,128)(2,1)S(1)}, bf16[4,192,128]{2,1,0:T(8,128)(2,1)S(1)}, u32[]{:S(2)}, u32[]{:S(2)}) %collective-permute-start.12) | collective-permute-done | bytes 196640 | tf_op jit(solution)/shard_map/ppermute | solution.py:324
  44.9 2.2 %collective-permute-done.11.a = bf16[4,192,128]{2,1,0:T(8,128)(2,1)S(1)} collective-permute-done((bf16[4,192,128]{2,1,0:T(8,128)(2,1)S(1)}, bf16[4,192,128]{2,1,0:T(8,128)(2,1)S(1)}, u32[]{:S(2)}, u32[]{:S(2)}) %collective-permute-start.11) | collective-permute-done | bytes 196640 | tf_op jit(solution)/shard_map/ppermute | solution.py:324
  47.2 4.7 %scores.1 = (f32[768,1536]{1,0:T(8,128)S(1)}, bf16[768,1024]{1,0:T(8,128)(2,1)S(1)}, f32[2,768]{1,0:T(2,128)S(1)}, f32[2,1536]{1,0:T(2,128)S(1)}) custom-call(bf16[768,1024]{1,0:T(8,128)(2,1)S(1)} %join.1.refs_0_.refs_9_, bf16[768,1024]{1,0:T(8,128)(2,1)S(1)} %collective-permute-done.10.refs_1_.refs_10_, bf16[8,192,128]{2,1,0:T(8,128)(2,1)S(1)} %stack.1.after.refs_2_, ...), custom_call_target="tpu_custom_call" | custom-call | flops 1000 | bytes 1000 | tf_op jit(solution)/shard_map/scores/pallas_call | solution.py:366
  52.0 1.3 %collective-permute-start.13 = (f32[2,768]{1,0:T(2,128)S(1)}, f32[2,768]{1,0:T(2,128)S(1)}, u32[]{:S(2)}, u32[]{:S(2)}) collective-permute-start(f32[2,768]{1,0:T(2,128)S(1)} %get-tuple-element.43.r), channel_id=1, source_target_pairs={{0,8},{8,0},{16,24},{24,16},{1,9},{9,1},{17,25},{25,17},{2,10},{10... | collective-permute-start | bytes 18440 | tf_op jit(solution)/shard_map/ppermute | solution.py:328
  53.3 2.4 %collective-permute-start.18 = (f32[2,1536]{1,0:T(2,128)S(1)}, f32[2,1536]{1,0:T(2,128)S(1)}, u32[]{:S(2)}, u32[]{:S(2)}) collective-permute-start(f32[2,1536]{1,0:T(2,128)S(1)} %meet.1.refs_2_), channel_id=1, source_target_pairs={{0,6},{2,4},{4,2},{6,0},{1,7},{3,5},{5,3},{7,1},{8,14},{10,12},{12... | collective-permute-start | bytes 36872 | tf_op jit(solution)/shard_map/ppermute | solution.py:376
  56.9 4.3 %collective-permute-start.14 = (f32[2,768]{1,0:T(2,128)S(1)}, f32[2,768]{1,0:T(2,128)S(1)}, u32[]{:S(2)}, u32[]{:S(2)}) collective-permute-start(f32[2,768]{1,0:T(2,128)S(1)} %meet_rows.1.refs_0_), channel_id=1, source_target_pairs={{0,24},{8,16},{16,8},{24,0},{1,25},{9,17},{17,9},{25,1},{2,26},{10... | collective-permute-start | bytes 18440 | tf_op jit(solution)/shard_map/ppermute | solution.py:328
  61.2 1.8 %collective-permute-done.14.refs_1_ = f32[2,768]{1,0:T(2,128)S(1)} collective-permute-done((f32[2,768]{1,0:T(2,128)S(1)}, f32[2,768]{1,0:T(2,128)S(1)}, u32[]{:S(2)}, u32[]{:S(2)}) %collective-permute-start.14) | collective-permute-done | bytes 6176 | tf_op jit(solution)/shard_map/ppermute | solution.py:328
  63.0 7.9 %weights.1 = (f32[768,256]{1,0:T(8,128)S(1)}, f32[768,256]{1,0:T(8,128)S(1)}, f32[768,256]{1,0:T(8,128)S(1)}, s16[400,256]{1,0:T(8,128)(2,1)S(1)}, s16[400,256]{...) custom-call(f32[2,768]{1,0:T(2,128)S(1)} %meet_rows.1.refs_0_, ...), custom_call_target="tpu_custom_call" | custom-call | flops 1000 | bytes 1000 | tf_op jit(solution)/shard_map/weights/pallas_call | solution.py:379
  71.2 2.9 %collective-permute-start.25 = (s16[400,256]{1,0:T(8,128)(2,1)S(1)}, s16[400,256]{1,0:T(8,128)(2,1)S(1)}, u32[]{:S(2)}, u32[]{:S(2)}) collective-permute-start(s16[400,256]{1,0:T(8,128)(2,1)S(1)} %get-tuple-element.61), channel_id=1, source_target_pairs={{0,192},{64,0},{128,64},{192,128},{1,193},{65,1},{129,65},{193,129... | collective-permute-start | bytes 614408 | tf_op jit(solution)/shard_map/ppermute | solution.py:324
  75.4 1.1 collective-permute-start.20
  76.5 1.8 %collective-permute-start.21 = (s16[2,208,512]{2,1,0:T(8,128)(2,1)S(1)}, s16[2,208,512]{2,1,0:T(8,128)(2,1)S(1)}, u32[]{:S(2)}, u32[]{:S(2)}) collective-permute-start(s16[2,208,512]{2,1,0:T(8,128)(2,1)S(1)} %get-tuple-element.53), channel_id=1, source_target_pairs={{0,4},{4,0},{1,5},{5,1},{2,6},{6,2},{3,7},{7,3},{8,12},{12,8},{9,1... | collective-permute-start | bytes 1277960 | tf_op jit(solution)/shard_map/ppermute | solution.py:328
  78.3 1.3 %collective-permute-done.24.got_a = s16[400,256]{1,0:T(8,128)(2,1)S(1)} collective-permute-done((s16[400,256]{1,0:T(8,128)(2,1)S(1)}, s16[400,256]{1,0:T(8,128)(2,1)S(1)}, u32[]{:S(2)}, u32[]{:S(2)}) %collective-permute-start.24) | collective-permute-done | bytes 204832 | tf_op jit(solution)/shard_map/ppermute | solution.py:324
  80.0 3.2 %collective-permute-start.27 = (s16[784,256]{1,0:T(8,128)(2,1)S(1)}, s16[784,256]{1,0:T(8,128)(2,1)S(1)}, u32[]{:S(2)}, u32[]{:S(2)}) collective-permute-start(s16[784,256]{1,0:T(8,128)(2,1)S(1)} %get-tuple-element.63), channel_id=1, source_target_pairs={{0,192},{64,0},{128,64},{192,128},{1,193},{65,1},{129,65},{193,129... | collective-permute-start | bytes 1204232 | tf_op jit(solution)/shard_map/ppermute | solution.py:324
  83.2 4.1 %collective-permute-done.20.from_x = s16[2,208,512]{2,1,0:T(8,128)(2,1)S(1)} collective-permute-done((s16[2,208,512]{2,1,0:T(8,128)(2,1)S(1)}, s16[2,208,512]{2,1,0:T(8,128)(2,1)S(1)}, u32[]{:S(2)}, u32[]{:S(2)}) %collective-permute-start.20) | collective-permute-done | bytes 426016 | tf_op jit(solution)/shard_map/ppermute | solution.py:328
  88.6 1.3 %collective-permute-start.22 = (s16[208,512]{1,0:T(8,128)(2,1)S(1)}, s16[208,512]{1,0:T(8,128)(2,1)S(1)}, u32[]{:S(2)}, u32[]{:S(2)}) collective-permute-start(s16[208,512]{1,0:T(8,128)(2,1)S(1)} %get-tuple-element.55), channel_id=1, source_target_pairs={{0,2},{2,0},{1,3},{3,1},{4,6},{6,4},{5,7},{7,5},{8,10},{10,8},{9,1... | collective-permute-start | bytes 638984 | tf_op jit(solution)/shard_map/ppermute | solution.py:328
  89.9 1.7 %collective-permute-start.23 = (s16[208,512]{1,0:T(8,128)(2,1)S(1)}, s16[208,512]{1,0:T(8,128)(2,1)S(1)}, u32[]{:S(2)}, u32[]{:S(2)}) collective-permute-start(s16[208,512]{1,0:T(8,128)(2,1)S(1)} %get-tuple-element.56), channel_id=1, source_target_pairs={{0,4},{4,0},{1,5},{5,1},{2,6},{6,2},{3,7},{7,3},{8,12},{12,8},{9,1... | collective-permute-start | bytes 638984 | tf_op jit(solution)/shard_map/ppermute | solution.py:328
  92.4 2.5 %collective-permute-done.22.after_x.from_x = s16[208,512]{1,0:T(8,128)(2,1)S(1)} collective-permute-done((s16[208,512]{1,0:T(8,128)(2,1)S(1)}, s16[208,512]{1,0:T(8,128)(2,1)S(1)}, u32[]{:S(2)}, u32[]{:S(2)}) %collective-permute-start.22) | collective-permute-done | bytes 213024 | tf_op jit(solution)/shard_map/ppermute | solution.py:328
  94.9 1.2 collective-permute-done.23.after_z.from_z
  96.2 20.3 %all_to_all.5.pieces = s16[8,208,128]{2,1,0:T(8,128)(2,1)S(1)} all-to-all(s16[8,208,128]{2,1,0:T(8,128)(2,1)S(1)} %image_code.1), channel_id=1, replica_groups=mesh['y'=4,'xh'=2,'zh'=4,'zl'=2,'xl'=2,'core'=2] {'xh','zh'}, dimensions={0} | all-to-all | bytes 851968 | tf_op jit(solution)/shard_map/all_to_all | solution.py:412
  116.5 1.0 last.1
  (50 shorter events, 12.5 us)
Async XLA Ops:
  0.6 5.9 %collective-permute-start = (bf16[192,128]{1,0:T(8,128)(2,1)}, bf16[192,128]{1,0:T(8,128)(2,1)S(1)}, u32[]{:S(2)}, u32[]{:S(2)}) collective-permute-start(bf16[192,128]{1,0:T(8,128)(2,1)} %image.1), channel_id=1, source_target_pairs={{0,32},{32,0},{1,33},{33,1},{2,34},{34,2},{3,35},{35,3},{4,36},{36... | collective-permute-start | bytes 147464 | tf_op jit(solution)/shard_map/ppermute | solution.py:328
  6.5 0.8 copy-start.1
  7.3 13.6 %collective-permute-start.3 = (bf16[2,192,128]{2,1,0:T(8,128)(2,1)S(1)}, bf16[2,192,128]{2,1,0:T(8,128)(2,1)S(1)}, u32[]{:S(2)}, u32[]{:S(2)}) collective-permute-start(bf16[2,192,128]{2,1,0:T(8,128)(2,1)S(1)} %pair.1.after.both), channel_id=1, source_target_pairs={{0,24},{8,0},{16,8},{24,16},{1,25},{9,1},{17,9},{25,17},{2,26},{10... | collective-permute-start | bytes 294920 | tf_op jit(solution)/shard_map/ppermute | solution.py:324
  13.7 10.5 %collective-permute-start.2 = (bf16[2,192,128]{2,1,0:T(8,128)(2,1)S(1)}, bf16[2,192,128]{2,1,0:T(8,128)(2,1)S(1)}, u32[]{:S(2)}, u32[]{:S(2)}) collective-permute-start(bf16[2,192,128]{2,1,0:T(8,128)(2,1)S(1)} %pair.1.after.both), channel_id=1, source_target_pairs={{0,16},{8,24},{16,0},{24,8},{1,17},{9,25},{17,1},{25,9},{2,18},{10... | collective-permute-start | bytes 294920 | tf_op jit(solution)/shard_map/ppermute | solution.py:324
  14.7 9.5 %collective-permute-start.1 = (bf16[2,192,128]{2,1,0:T(8,128)(2,1)S(1)}, bf16[2,192,128]{2,1,0:T(8,128)(2,1)S(1)}, u32[]{:S(2)}, u32[]{:S(2)}) collective-permute-start(bf16[2,192,128]{2,1,0:T(8,128)(2,1)S(1)} %pair.1.after.both), channel_id=1, source_target_pairs={{0,8},{8,16},{16,24},{24,0},{1,9},{9,17},{17,25},{25,1},{2,10},{10... | collective-permute-start | bytes 294920 | tf_op jit(solution)/shard_map/ppermute | solution.py:324
  17.5 1.0 copy-start
  18.5 0.7 copy-start.2
  19.5 8.9 %collective-permute-start.4 = (bf16[192,1024]{1,0:T(8,128)(2,1)S(1)}, bf16[192,1024]{1,0:T(8,128)(2,1)S(1)}, u32[]{:S(2)}, u32[]{:S(2)}) collective-permute-start(bf16[192,1024]{1,0:T(8,128)(2,1)S(1)} %get-tuple-element.36.keys), channel_id=1, source_target_pairs={{0,2},{2,0},{1,3},{3,1},{4,6},{6,4},{5,7},{7,5},{8,10},{10,8},{9,1... | collective-permute-start | bytes 1179656 | tf_op jit(solution)/shard_map/ppermute | solution.py:328
  24.3 11.5 %collective-permute-start.5 = (bf16[192,1024]{1,0:T(8,128)(2,1)S(1)}, bf16[192,1024]{1,0:T(8,128)(2,1)S(1)}, u32[]{:S(2)}, u32[]{:S(2)}) collective-permute-start(bf16[192,1024]{1,0:T(8,128)(2,1)S(1)} %hold.1.own), channel_id=1, source_target_pairs={{0,4},{4,0},{1,5},{5,1},{2,6},{6,2},{3,7},{7,3},{8,12},{12,8},{9,1... | collective-permute-start | bytes 1179656 | tf_op jit(solution)/shard_map/ppermute | solution.py:328
  25.3 11.9 %collective-permute-start.9 = (bf16[8,192,128]{2,1,0:T(8,128)(2,1)S(1)}, bf16[8,192,128]{2,1,0:T(8,128)(2,1)S(1)}, u32[]{:S(2)}, u32[]{:S(2)}) collective-permute-start(bf16[8,192,128]{2,1,0:T(8,128)(2,1)S(1)} %stack.1.after.refs_2_), channel_id=1, source_target_pairs={{0,192},{64,0},{128,64},{192,128},{1,193},{65,1},{129,65},{193,129... | collective-permute-start | bytes 1179656 | tf_op jit(solution)/shard_map/ppermute | solution.py:324
  28.3 10.9 %collective-permute-start.8 = (bf16[8,192,128]{2,1,0:T(8,128)(2,1)S(1)}, bf16[8,192,128]{2,1,0:T(8,128)(2,1)S(1)}, u32[]{:S(2)}, u32[]{:S(2)}) collective-permute-start(bf16[8,192,128]{2,1,0:T(8,128)(2,1)S(1)} %stack.1.after.refs_2_), channel_id=1, source_target_pairs={{0,64},{64,128},{128,192},{192,0},{1,65},{65,129},{129,193},{193,1... | collective-permute-start | bytes 1179656 | tf_op jit(solution)/shard_map/ppermute | solution.py:324
  28.4 12.9 %collective-permute-start.7 = (bf16[96,1024]{1,0:T(8,128)(2,1)S(1)}, bf16[96,1024]{1,0:T(8,128)(2,1)S(1)}, u32[]{:S(2)}, u32[]{:S(2)}) collective-permute-start(bf16[96,1024]{1,0:T(8,128)(2,1)S(1)} %low.1), channel_id=1, source_target_pairs={{0,4},{4,0},{1,5},{5,1},{2,6},{6,2},{3,7},{7,3},{8,12},{12,8},{9,1... | collective-permute-start | bytes 589832 | tf_op jit(solution)/shard_map/ppermute | solution.py:328
  35.9 5.8 %collective-permute-start.6 = (bf16[96,1024]{1,0:T(8,128)(2,1)S(1)}, bf16[96,1024]{1,0:T(8,128)(2,1)S(1)}, u32[]{:S(2)}, u32[]{:S(2)}) collective-permute-start(bf16[96,1024]{1,0:T(8,128)(2,1)S(1)} %top.1), channel_id=1, source_target_pairs={{0,2},{2,0},{1,3},{3,1},{4,6},{6,4},{5,7},{7,5},{8,10},{10,8},{9,1... | collective-permute-start | bytes 589832 | tf_op jit(solution)/shard_map/ppermute | solution.py:328
  39.2 5.7 %collective-permute-start.12 = (bf16[4,192,128]{2,1,0:T(8,128)(2,1)S(1)}, bf16[4,192,128]{2,1,0:T(8,128)(2,1)S(1)}, u32[]{:S(2)}, u32[]{:S(2)}) collective-permute-start(bf16[4,192,128]{2,1,0:T(8,128)(2,1)S(1)} %get-tuple-element.39), channel_id=1, source_target_pairs={{0,192},{64,0},{128,64},{192,128},{1,193},{65,1},{129,65},{193,129... | collective-permute-start | bytes 589832 | tf_op jit(solution)/shard_map/ppermute | solution.py:324
  40.3 6.9 %collective-permute-start.11 = (bf16[4,192,128]{2,1,0:T(8,128)(2,1)S(1)}, bf16[4,192,128]{2,1,0:T(8,128)(2,1)S(1)}, u32[]{:S(2)}, u32[]{:S(2)}) collective-permute-start(bf16[4,192,128]{2,1,0:T(8,128)(2,1)S(1)} %get-tuple-element.38.after), channel_id=1, source_target_pairs={{0,64},{64,128},{128,192},{192,0},{1,65},{65,129},{129,193},{193,1... | collective-permute-start | bytes 589832 | tf_op jit(solution)/shard_map/ppermute | solution.py:324
  41.7 5.5 %collective-permute-start.10 = (bf16[768,1024]{1,0:T(8,128)(2,1)S(1)}, bf16[768,1024]{1,0:T(8,128)(2,1)S(1)}, u32[]{:S(2)}, u32[]{:S(2)}) collective-permute-start(bf16[768,1024]{1,0:T(8,128)(2,1)S(1)} %join.1.refs_0_.refs_9_), channel_id=1, source_target_pairs={{0,1},{1,0},{2,3},{3,2},{4,5},{5,4},{6,7},{7,6},{8,9},{9,8},{10,11... | collective-permute-start | bytes 4718600 | tf_op jit(solution)/shard_map/ppermute | solution.py:328
  51.9 1.4 %collective-permute-start.15 = (f32[2,1536]{1,0:T(2,128)S(1)}, f32[2,1536]{1,0:T(2,128)S(1)}, u32[]{:S(2)}, u32[]{:S(2)}) collective-permute-start(f32[2,1536]{1,0:T(2,128)S(1)} %get-tuple-element.44.c), channel_id=1, source_target_pairs={{0,1},{1,0},{2,3},{3,2},{4,5},{5,4},{6,7},{7,6},{8,9},{9,8},{10,11... | collective-permute-start | bytes 36872 | tf_op jit(solution)/shard_map/ppermute | solution.py:328
  52.0 4.9 %collective-permute-start.13 = (f32[2,768]{1,0:T(2,128)S(1)}, f32[2,768]{1,0:T(2,128)S(1)}, u32[]{:S(2)}, u32[]{:S(2)}) collective-permute-start(f32[2,768]{1,0:T(2,128)S(1)} %get-tuple-element.43.r), channel_id=1, source_target_pairs={{0,8},{8,0},{16,24},{24,16},{1,9},{9,1},{17,25},{25,17},{2,10},{10... | collective-permute-start | bytes 18440 | tf_op jit(solution)/shard_map/ppermute | solution.py:328
  53.3 9.7 %collective-permute-start.18 = (f32[2,1536]{1,0:T(2,128)S(1)}, f32[2,1536]{1,0:T(2,128)S(1)}, u32[]{:S(2)}, u32[]{:S(2)}) collective-permute-start(f32[2,1536]{1,0:T(2,128)S(1)} %meet.1.refs_2_), channel_id=1, source_target_pairs={{0,6},{2,4},{4,2},{6,0},{1,7},{3,5},{5,3},{7,1},{8,14},{10,12},{12... | collective-permute-start | bytes 36872 | tf_op jit(solution)/shard_map/ppermute | solution.py:376
  55.7 7.3 %collective-permute-start.17 = (f32[2,1536]{1,0:T(2,128)S(1)}, f32[2,1536]{1,0:T(2,128)S(1)}, u32[]{:S(2)}, u32[]{:S(2)}) collective-permute-start(f32[2,1536]{1,0:T(2,128)S(1)} %meet.1.refs_2_), channel_id=1, source_target_pairs={{0,4},{2,6},{4,0},{6,2},{1,5},{3,7},{5,1},{7,3},{8,12},{10,14},{12... | collective-permute-start | bytes 36872 | tf_op jit(solution)/shard_map/ppermute | solution.py:376
  55.9 7.1 %collective-permute-start.16 = (f32[2,1536]{1,0:T(2,128)S(1)}, f32[2,1536]{1,0:T(2,128)S(1)}, u32[]{:S(2)}, u32[]{:S(2)}) collective-permute-start(f32[2,1536]{1,0:T(2,128)S(1)} %meet.1.refs_2_), channel_id=1, source_target_pairs={{0,2},{2,0},{4,6},{6,4},{1,3},{3,1},{5,7},{7,5},{8,10},{10,8},{12,... | collective-permute-start | bytes 36872 | tf_op jit(solution)/shard_map/ppermute | solution.py:376
  56.9 6.0 %collective-permute-start.14 = (f32[2,768]{1,0:T(2,128)S(1)}, f32[2,768]{1,0:T(2,128)S(1)}, u32[]{:S(2)}, u32[]{:S(2)}) collective-permute-start(f32[2,768]{1,0:T(2,128)S(1)} %meet_rows.1.refs_0_), channel_id=1, source_target_pairs={{0,24},{8,16},{16,8},{24,0},{1,25},{9,17},{17,9},{25,1},{2,26},{10... | collective-permute-start | bytes 18440 | tf_op jit(solution)/shard_map/ppermute | solution.py:328
  70.8 3.6 %collective-permute-start.19 = (s16[4,208,1024]{2,1,0:T(8,128)(2,1)S(1)}, s16[4,208,1024]{2,1,0:T(8,128)(2,1)S(1)}, u32[]{:S(2)}, u32[]{:S(2)}) collective-permute-start(s16[4,208,1024]{2,1,0:T(8,128)(2,1)S(1)} %get-tuple-element.48), channel_id=1, source_target_pairs={{0,1},{1,0},{2,3},{3,2},{4,5},{5,4},{6,7},{7,6},{8,9},{9,8},{10,11... | collective-permute-start | bytes 5111816 | tf_op jit(solution)/shard_map/ppermute | solution.py:328
  70.9 8.7 %collective-permute-start.24 = (s16[400,256]{1,0:T(8,128)(2,1)S(1)}, s16[400,256]{1,0:T(8,128)(2,1)S(1)}, u32[]{:S(2)}, u32[]{:S(2)}) collective-permute-start(s16[400,256]{1,0:T(8,128)(2,1)S(1)} %get-tuple-element.60), channel_id=1, source_target_pairs={{0,64},{64,128},{128,192},{192,0},{1,65},{65,129},{129,193},{193,1... | collective-permute-start | bytes 614408 | tf_op jit(solution)/shard_map/ppermute | solution.py:324
  71.2 8.3 %collective-permute-start.25 = (s16[400,256]{1,0:T(8,128)(2,1)S(1)}, s16[400,256]{1,0:T(8,128)(2,1)S(1)}, u32[]{:S(2)}, u32[]{:S(2)}) collective-permute-start(s16[400,256]{1,0:T(8,128)(2,1)S(1)} %get-tuple-element.61), channel_id=1, source_target_pairs={{0,192},{64,0},{128,64},{192,128},{1,193},{65,1},{129,65},{193,129... | collective-permute-start | bytes 614408 | tf_op jit(solution)/shard_map/ppermute | solution.py:324
  75.4 11.9 %collective-permute-start.20 = (s16[2,208,512]{2,1,0:T(8,128)(2,1)S(1)}, s16[2,208,512]{2,1,0:T(8,128)(2,1)S(1)}, u32[]{:S(2)}, u32[]{:S(2)}) collective-permute-start(s16[2,208,512]{2,1,0:T(8,128)(2,1)S(1)} %get-tuple-element.52), channel_id=1, source_target_pairs={{0,2},{2,0},{1,3},{3,1},{4,6},{6,4},{5,7},{7,5},{8,10},{10,8},{9,1... | collective-permute-start | bytes 1277960 | tf_op jit(solution)/shard_map/ppermute | solution.py:328
  76.5 11.7 %collective-permute-start.21 = (s16[2,208,512]{2,1,0:T(8,128)(2,1)S(1)}, s16[2,208,512]{2,1,0:T(8,128)(2,1)S(1)}, u32[]{:S(2)}, u32[]{:S(2)}) collective-permute-start(s16[2,208,512]{2,1,0:T(8,128)(2,1)S(1)} %get-tuple-element.53), channel_id=1, source_target_pairs={{0,4},{4,0},{1,5},{5,1},{2,6},{6,2},{3,7},{7,3},{8,12},{12,8},{9,1... | collective-permute-start | bytes 1277960 | tf_op jit(solution)/shard_map/ppermute | solution.py:328
  79.9 12.2 %collective-permute-start.26 = (s16[784,256]{1,0:T(8,128)(2,1)S(1)}, s16[784,256]{1,0:T(8,128)(2,1)S(1)}, u32[]{:S(2)}, u32[]{:S(2)}) collective-permute-start(s16[784,256]{1,0:T(8,128)(2,1)S(1)} %get-tuple-element.62), channel_id=1, source_target_pairs={{0,64},{64,128},{128,192},{192,0},{1,65},{65,129},{129,193},{193,1... | collective-permute-start | bytes 1204232 | tf_op jit(solution)/shard_map/ppermute | solution.py:324
  80.0 12.1 %collective-permute-start.27 = (s16[784,256]{1,0:T(8,128)(2,1)S(1)}, s16[784,256]{1,0:T(8,128)(2,1)S(1)}, u32[]{:S(2)}, u32[]{:S(2)}) collective-permute-start(s16[784,256]{1,0:T(8,128)(2,1)S(1)} %get-tuple-element.63), channel_id=1, source_target_pairs={{0,192},{64,0},{128,64},{192,128},{1,193},{65,1},{129,65},{193,129... | collective-permute-start | bytes 1204232 | tf_op jit(solution)/shard_map/ppermute | solution.py:324
  88.6 6.3 %collective-permute-start.22 = (s16[208,512]{1,0:T(8,128)(2,1)S(1)}, s16[208,512]{1,0:T(8,128)(2,1)S(1)}, u32[]{:S(2)}, u32[]{:S(2)}) collective-permute-start(s16[208,512]{1,0:T(8,128)(2,1)S(1)} %get-tuple-element.55), channel_id=1, source_target_pairs={{0,2},{2,0},{1,3},{3,1},{4,6},{6,4},{5,7},{7,5},{8,10},{10,8},{9,1... | collective-permute-start | bytes 638984 | tf_op jit(solution)/shard_map/ppermute | solution.py:328
  89.9 6.2 %collective-permute-start.23 = (s16[208,512]{1,0:T(8,128)(2,1)S(1)}, s16[208,512]{1,0:T(8,128)(2,1)S(1)}, u32[]{:S(2)}, u32[]{:S(2)}) collective-permute-start(s16[208,512]{1,0:T(8,128)(2,1)S(1)} %get-tuple-element.56), channel_id=1, source_target_pairs={{0,4},{4,0},{1,5},{5,1},{2,6},{6,2},{3,7},{7,3},{8,12},{12,8},{9,1... | collective-permute-start | bytes 638984 | tf_op jit(solution)/shard_map/ppermute | solution.py:328

commit v11 on v9

--- a/solution.py
+++ b/solution.py
@@ -312,8 +312,8 @@
     out[...] = own[...] + decode(got1[...]) + decode(got3[...])
 
 
-def image_code_kernel(after_x, after_z, total, out):
-    del after_x, after_z
+def image_code_kernel(after, total, out):
+    del after
     rows, width = out.shape[1] - PAD, out.shape[2]
     for xh in range(2):
         for zh in range(4):
@@ -406,8 +406,8 @@
     total = call(image_sum_kernel, shape((n_im, 2 * width), F32), "image_sum", 12, in_specs=[vmem] * 4)(
         own_key, own, q1, q3
     )
-    pieces = call(image_code_kernel, shape((8, rows + PAD, width), I16), "image_code", 12, in_specs=[vmem] * 3)(
-        from_x, from_z, total
+    pieces = call(image_code_kernel, shape((8, rows + PAD, width), I16), "image_code", 12, in_specs=[vmem] * 2)(
+        from_x, total
     )
     pieces = lax.all_to_all(pieces, ("xh", "zh"), 0, 0)
     modality_grad, image_grad = call(

time: 119 us -> 122 us (1.025)
  the two profiles are of different devices: /device:TPU:4 before, /device:TPU:32 now
where the time goes in v11:
time: 122 us
  waiting for transfers between devices  52.7 us (43%)
  starting transfers between devices  48.7 us (40%)
  Pallas kernels  16.9 us (14%)
  local copies, waits for them, and re-layouts  2.53 us (2%)
    ppermute x14, waiting for transfers between devices, flip(): return lax.ppermute(x, axis, [(i, i ^ d) for i in range(n)])  33.9 us
    ppermute x11, starting transfers between devices, shift(): return lax.ppermute(x, axis, [(i, (i + k) % n) for i in range(n)])  21.5 us
    ppermute x14, starting transfers between devices, flip(): return lax.ppermute(x, axis, [(i, i ^ d) for i in range(n)])  15.7 us
    ppermute x11, waiting for transfers between devices, shift(): return lax.ppermute(x, axis, [(i, (i + k) % n) for i in range(n)])  14.7 us
    all_to_all x1, starting transfers between devices, on_device(): pieces = lax.all_to_all(pieces, ('xh', 'zh'), 0, 0)  7.88 us
    pallas_call x1, Pallas kernels, on_device(): call(functools.partial(weights_kernel, scale, tile), outs, 'weights', 36,...  7.84 us
    pallas_call x1, Pallas kernels, on_device(): call(functools.partial(scores_kernel, scale), [shape((n_im, n_ks), F32),...  4.69 us
    all_to_all x1, waiting for transfers between devices, on_device(): pieces = lax.all_to_all(pieces, ('xh', 'zh'), 0, 0)  4.03 us
  transfers between devices with their start and end apart: 29, of which 17 were waited for; matrix products, arithmetic and copies ran while one was open for 0% of the time, Pallas kernels for 2%

profile of v11, /device:TPU:32, one launch (start us, length us, event | category | flops | bytes accessed | tf_op | source)
XLA Modules:
  0.0 121.6 jit_solution(12511650482480577192)
XLA Ops:
  0.6 3.1 %collective-permute-start = (bf16[192,128]{1,0:T(8,128)(2,1)}, bf16[192,128]{1,0:T(8,128)(2,1)S(1)}, u32[]{:S(2)}, u32[]{:S(2)}) collective-permute-start(bf16[192,128]{1,0:T(8,128)(2,1)} %image.1), channel_id=1, source_target_pairs={{0,32},{32,0},{1,33},{33,1},{2,34},{34,2},{3,35},{35,3},{4,36},{36... | collective-permute-start | bytes 147464 | tf_op jit(solution)/shard_map/ppermute | solution.py:328
  3.7 2.8 %collective-permute-done.twin = bf16[192,128]{1,0:T(8,128)(2,1)S(1)} collective-permute-done((bf16[192,128]{1,0:T(8,128)(2,1)}, bf16[192,128]{1,0:T(8,128)(2,1)S(1)}, u32[]{:S(2)}, u32[]{:S(2)}) %collective-permute-start) | collective-permute-done | bytes 49184 | tf_op jit(solution)/shard_map/ppermute | solution.py:328
  7.3 5.5 %collective-permute-start.3 = (bf16[2,192,128]{2,1,0:T(8,128)(2,1)S(1)}, bf16[2,192,128]{2,1,0:T(8,128)(2,1)S(1)}, u32[]{:S(2)}, u32[]{:S(2)}) collective-permute-start(bf16[2,192,128]{2,1,0:T(8,128)(2,1)S(1)} %pair.1.after.both), channel_id=1, source_target_pairs={{0,24},{8,0},{16,8},{24,16},{1,25},{9,1},{17,9},{25,17},{2,26},{10... | collective-permute-start | bytes 294920 | tf_op jit(solution)/shard_map/ppermute | solution.py:324
  12.8 1.4 %collective-permute-start.2 = (bf16[2,192,128]{2,1,0:T(8,128)(2,1)S(1)}, bf16[2,192,128]{2,1,0:T(8,128)(2,1)S(1)}, u32[]{:S(2)}, u32[]{:S(2)}) collective-permute-start(bf16[2,192,128]{2,1,0:T(8,128)(2,1)S(1)} %pair.1.after.both), channel_id=1, source_target_pairs={{0,16},{8,24},{16,0},{24,8},{1,17},{9,25},{17,1},{25,9},{2,18},{10... | collective-permute-start | bytes 294920 | tf_op jit(solution)/shard_map/ppermute | solution.py:324
  14.3 2.4 %collective-permute-start.1 = (bf16[2,192,128]{2,1,0:T(8,128)(2,1)S(1)}, bf16[2,192,128]{2,1,0:T(8,128)(2,1)S(1)}, u32[]{:S(2)}, u32[]{:S(2)}) collective-permute-start(bf16[2,192,128]{2,1,0:T(8,128)(2,1)S(1)} %pair.1.after.both), channel_id=1, source_target_pairs={{0,8},{8,16},{16,24},{24,0},{1,9},{9,17},{17,25},{25,1},{2,10},{10... | collective-permute-start | bytes 294920 | tf_op jit(solution)/shard_map/ppermute | solution.py:324
  18.6 1.5 %collective-permute-start.4 = (bf16[192,1024]{1,0:T(8,128)(2,1)S(1)}, bf16[192,1024]{1,0:T(8,128)(2,1)S(1)}, u32[]{:S(2)}, u32[]{:S(2)}) collective-permute-start(bf16[192,1024]{1,0:T(8,128)(2,1)S(1)} %get-tuple-element.36.keys), channel_id=1, source_target_pairs={{0,2},{2,0},{1,3},{3,1},{4,6},{6,4},{5,7},{7,5},{8,10},{10,8},{9,1... | collective-permute-start | bytes 1179656 | tf_op jit(solution)/shard_map/ppermute | solution.py:328
  20.1 2.7 %collective-permute-done.2.b2 = bf16[2,192,128]{2,1,0:T(8,128)(2,1)S(1)} collective-permute-done((bf16[2,192,128]{2,1,0:T(8,128)(2,1)S(1)}, bf16[2,192,128]{2,1,0:T(8,128)(2,1)S(1)}, u32[]{:S(2)}, u32[]{:S(2)}) %collective-permute-start.2) | collective-permute-done | bytes 98336 | tf_op jit(solution)/shard_map/ppermute | solution.py:324
  22.8 1.3 %collective-permute-done.1.b1 = bf16[2,192,128]{2,1,0:T(8,128)(2,1)S(1)} collective-permute-done((bf16[2,192,128]{2,1,0:T(8,128)(2,1)S(1)}, bf16[2,192,128]{2,1,0:T(8,128)(2,1)S(1)}, u32[]{:S(2)}, u32[]{:S(2)}) %collective-permute-start.1) | collective-permute-done | bytes 98336 | tf_op jit(solution)/shard_map/ppermute | solution.py:324
  24.4 3.1 %collective-permute-start.9 = (bf16[8,192,128]{2,1,0:T(8,128)(2,1)S(1)}, bf16[8,192,128]{2,1,0:T(8,128)(2,1)S(1)}, u32[]{:S(2)}, u32[]{:S(2)}) collective-permute-start(bf16[8,192,128]{2,1,0:T(8,128)(2,1)S(1)} %stack.1.after.refs_2_), channel_id=1, source_target_pairs={{0,192},{64,0},{128,64},{192,128},{1,193},{65,1},{129,65},{193,129... | collective-permute-start | bytes 1179656 | tf_op jit(solution)/shard_map/ppermute | solution.py:324
  27.6 1.1 collective-permute-start.7
  28.6 7.7 %collective-permute-done.5.z = bf16[192,1024]{1,0:T(8,128)(2,1)S(1)} collective-permute-done((bf16[192,1024]{1,0:T(8,128)(2,1)S(1)}, bf16[192,1024]{1,0:T(8,128)(2,1)S(1)}, u32[]{:S(2)}, u32[]{:S(2)}) %collective-permute-start.5) | collective-permute-done | bytes 393248 | tf_op jit(solution)/shard_map/ppermute | solution.py:328
  37.6 2.5 %collective-permute-start.12 = (bf16[4,192,128]{2,1,0:T(8,128)(2,1)S(1)}, bf16[4,192,128]{2,1,0:T(8,128)(2,1)S(1)}, u32[]{:S(2)}, u32[]{:S(2)}) collective-permute-start(bf16[4,192,128]{2,1,0:T(8,128)(2,1)S(1)} %get-tuple-element.39), channel_id=1, source_target_pairs={{0,192},{64,0},{128,64},{192,128},{1,193},{65,1},{129,65},{193,129... | collective-permute-start | bytes 589832 | tf_op jit(solution)/shard_map/ppermute | solution.py:324
  40.1 2.0 %collective-permute-done.6.d_top = bf16[96,1024]{1,0:T(8,128)(2,1)S(1)} collective-permute-done((bf16[96,1024]{1,0:T(8,128)(2,1)S(1)}, bf16[96,1024]{1,0:T(8,128)(2,1)S(1)}, u32[]{:S(2)}, u32[]{:S(2)}) %collective-permute-start.6) | collective-permute-done | bytes 196640 | tf_op jit(solution)/shard_map/ppermute | solution.py:328
  43.4 3.6 %collective-permute-done.11.a = bf16[4,192,128]{2,1,0:T(8,128)(2,1)S(1)} collective-permute-done((bf16[4,192,128]{2,1,0:T(8,128)(2,1)S(1)}, bf16[4,192,128]{2,1,0:T(8,128)(2,1)S(1)}, u32[]{:S(2)}, u32[]{:S(2)}) %collective-permute-start.11) | collective-permute-done | bytes 196640 | tf_op jit(solution)/shard_map/ppermute | solution.py:324
  47.0 4.7 %scores.1 = (f32[768,1536]{1,0:T(8,128)S(1)}, bf16[768,1024]{1,0:T(8,128)(2,1)S(1)}, f32[2,768]{1,0:T(2,128)S(1)}, f32[2,1536]{1,0:T(2,128)S(1)}) custom-call(bf16[768,1024]{1,0:T(8,128)(2,1)S(1)} %join.1.refs_0_.refs_9_, bf16[768,1024]{1,0:T(8,128)(2,1)S(1)} %collective-permute-done.10.refs_1_.refs_10_, bf16[8,192,128]{2,1,0:T(8,128)(2,1)S(1)} %stack.1.after.refs_2_, ...), custom_call_target="tpu_custom_call" | custom-call | flops 1000 | bytes 1000 | tf_op jit(solution)/shard_map/scores/pallas_call | solution.py:366
  51.8 1.8 %collective-permute-start.13 = (f32[2,768]{1,0:T(2,128)S(1)}, f32[2,768]{1,0:T(2,128)S(1)}, u32[]{:S(2)}, u32[]{:S(2)}) collective-permute-start(f32[2,768]{1,0:T(2,128)S(1)} %get-tuple-element.43.r), channel_id=1, source_target_pairs={{0,8},{8,0},{16,24},{24,16},{1,9},{9,1},{17,25},{25,17},{2,10},{10... | collective-permute-start | bytes 18440 | tf_op jit(solution)/shard_map/ppermute | solution.py:328
  54.2 1.5 %collective-permute-start.17 = (f32[2,1536]{1,0:T(2,128)S(1)}, f32[2,1536]{1,0:T(2,128)S(1)}, u32[]{:S(2)}, u32[]{:S(2)}) collective-permute-start(f32[2,1536]{1,0:T(2,128)S(1)} %meet.1.refs_2_), channel_id=1, source_target_pairs={{0,4},{2,6},{4,0},{6,2},{1,5},{3,7},{5,1},{7,3},{8,12},{10,14},{12... | collective-permute-start | bytes 36872 | tf_op jit(solution)/shard_map/ppermute | solution.py:376
  55.8 1.5 %collective-permute-start.16 = (f32[2,1536]{1,0:T(2,128)S(1)}, f32[2,1536]{1,0:T(2,128)S(1)}, u32[]{:S(2)}, u32[]{:S(2)}) collective-permute-start(f32[2,1536]{1,0:T(2,128)S(1)} %meet.1.refs_2_), channel_id=1, source_target_pairs={{0,2},{2,0},{4,6},{6,4},{1,3},{3,1},{5,7},{7,5},{8,10},{10,8},{12,... | collective-permute-start | bytes 36872 | tf_op jit(solution)/shard_map/ppermute | solution.py:376
  57.3 3.8 %collective-permute-start.14 = (f32[2,768]{1,0:T(2,128)S(1)}, f32[2,768]{1,0:T(2,128)S(1)}, u32[]{:S(2)}, u32[]{:S(2)}) collective-permute-start(f32[2,768]{1,0:T(2,128)S(1)} %meet_rows.1.refs_0_), channel_id=1, source_target_pairs={{0,24},{8,16},{16,8},{24,0},{1,25},{9,17},{17,9},{25,1},{2,26},{10... | collective-permute-start | bytes 18440 | tf_op jit(solution)/shard_map/ppermute | solution.py:328
  61.1 2.3 %collective-permute-done.14.refs_1_ = f32[2,768]{1,0:T(2,128)S(1)} collective-permute-done((f32[2,768]{1,0:T(2,128)S(1)}, f32[2,768]{1,0:T(2,128)S(1)}, u32[]{:S(2)}, u32[]{:S(2)}) %collective-permute-start.14) | collective-permute-done | bytes 6176 | tf_op jit(solution)/shard_map/ppermute | solution.py:328
  63.4 7.8 %weights.1 = (f32[768,256]{1,0:T(8,128)S(1)}, f32[768,256]{1,0:T(8,128)S(1)}, f32[768,256]{1,0:T(8,128)S(1)}, s16[400,256]{1,0:T(8,128)(2,1)S(1)}, s16[400,256]{...) custom-call(f32[2,768]{1,0:T(2,128)S(1)} %meet_rows.1.refs_0_, ...), custom_call_target="tpu_custom_call" | custom-call | flops 1000 | bytes 1000 | tf_op jit(solution)/shard_map/weights/pallas_call | solution.py:379
  71.2 3.2 %collective-permute-start.25 = (s16[400,256]{1,0:T(8,128)(2,1)S(1)}, s16[400,256]{1,0:T(8,128)(2,1)S(1)}, u32[]{:S(2)}, u32[]{:S(2)}) collective-permute-start(s16[400,256]{1,0:T(8,128)(2,1)S(1)} %get-tuple-element.61), channel_id=1, source_target_pairs={{0,192},{64,0},{128,64},{192,128},{1,193},{65,1},{129,65},{193,129... | collective-permute-start | bytes 614408 | tf_op jit(solution)/shard_map/ppermute | solution.py:324
  76.8 3.1 %collective-permute-done.24.got_a = s16[400,256]{1,0:T(8,128)(2,1)S(1)} collective-permute-done((s16[400,256]{1,0:T(8,128)(2,1)S(1)}, s16[400,256]{1,0:T(8,128)(2,1)S(1)}, u32[]{:S(2)}, u32[]{:S(2)}) %collective-permute-start.24) | collective-permute-done | bytes 204832 | tf_op jit(solution)/shard_map/ppermute | solution.py:324
  80.4 3.2 %collective-permute-start.27 = (s16[784,256]{1,0:T(8,128)(2,1)S(1)}, s16[784,256]{1,0:T(8,128)(2,1)S(1)}, u32[]{:S(2)}, u32[]{:S(2)}) collective-permute-start(s16[784,256]{1,0:T(8,128)(2,1)S(1)} %get-tuple-element.63), channel_id=1, source_target_pairs={{0,192},{64,0},{128,64},{192,128},{1,193},{65,1},{129,65},{193,129... | collective-permute-start | bytes 1204232 | tf_op jit(solution)/shard_map/ppermute | solution.py:324
  83.6 4.1 %collective-permute-done.20.from_x = s16[2,208,512]{2,1,0:T(8,128)(2,1)S(1)} collective-permute-done((s16[2,208,512]{2,1,0:T(8,128)(2,1)S(1)}, s16[2,208,512]{2,1,0:T(8,128)(2,1)S(1)}, u32[]{:S(2)}, u32[]{:S(2)}) %collective-permute-start.20) | collective-permute-done | bytes 426016 | tf_op jit(solution)/shard_map/ppermute | solution.py:328
  88.3 1.6 %collective-permute-start.22 = (s16[208,512]{1,0:T(8,128)(2,1)S(1)}, s16[208,512]{1,0:T(8,128)(2,1)S(1)}, u32[]{:S(2)}, u32[]{:S(2)}) collective-permute-start(s16[208,512]{1,0:T(8,128)(2,1)S(1)} %get-tuple-element.55), channel_id=1, source_target_pairs={{0,2},{2,0},{1,3},{3,1},{4,6},{6,4},{5,7},{7,5},{8,10},{10,8},{9,1... | collective-permute-start | bytes 638984 | tf_op jit(solution)/shard_map/ppermute | solution.py:328
  89.9 2.5 %collective-permute-done.26.got1 = s16[784,256]{1,0:T(8,128)(2,1)S(1)} collective-permute-done((s16[784,256]{1,0:T(8,128)(2,1)S(1)}, s16[784,256]{1,0:T(8,128)(2,1)S(1)}, u32[]{:S(2)}, u32[]{:S(2)}) %collective-permute-start.26) | collective-permute-done | bytes 401440 | tf_op jit(solution)/shard_map/ppermute | solution.py:324
  92.7 1.9 %collective-permute-done.22.after.from_x = s16[208,512]{1,0:T(8,128)(2,1)S(1)} collective-permute-done((s16[208,512]{1,0:T(8,128)(2,1)S(1)}, s16[208,512]{1,0:T(8,128)(2,1)S(1)}, u32[]{:S(2)}, u32[]{:S(2)}) %collective-permute-start.22) | collective-permute-done | bytes 213024 | tf_op jit(solution)/shard_map/ppermute | solution.py:328
  95.6 7.9 %all-to-all-start = ((s16[8,208,128]{2,1,0:T(8,128)(2,1)}), s16[8,208,128]{2,1,0:T(8,128)(2,1)S(1)}, u32[]{:S(2)}, u32[]{:S(2)}) async-start(s16[8,208,128]{2,1,0:T(8,128)(2,1)} %image_code.1), calls=%async_computation | async-start | bytes 851968 | tf_op jit(solution)/shard_map/all_to_all | solution.py:412
  103.9 12.6 %collective-permute-done.23.from_z = s16[208,512]{1,0:T(8,128)(2,1)S(1)} collective-permute-done((s16[208,512]{1,0:T(8,128)(2,1)S(1)}, s16[208,512]{1,0:T(8,128)(2,1)S(1)}, u32[]{:S(2)}, u32[]{:S(2)}) %collective-permute-start.23) | collective-permute-done | bytes 213024 | tf_op jit(solution)/shard_map/ppermute | solution.py:328
  116.5 4.0 %all-to-all-done.pieces = s16[8,208,128]{2,1,0:T(8,128)(2,1)S(1)} async-done(((s16[8,208,128]{2,1,0:T(8,128)(2,1)}), s16[8,208,128]{2,1,0:T(8,128)(2,1)S(1)}, u32[]{:S(2)}, u32[]{:S(2)}) %all-to-all-start) | async-done | bytes 426016 | tf_op jit(solution)/shard_map/all_to_all | solution.py:412
  120.6 1.0 last.1
  (51 shorter events, 11.5 us)
Async XLA Ops:
  0.6 5.9 %collective-permute-start = (bf16[192,128]{1,0:T(8,128)(2,1)}, bf16[192,128]{1,0:T(8,128)(2,1)S(1)}, u32[]{:S(2)}, u32[]{:S(2)}) collective-permute-start(bf16[192,128]{1,0:T(8,128)(2,1)} %image.1), channel_id=1, source_target_pairs={{0,32},{32,0},{1,33},{33,1},{2,34},{34,2},{3,35},{35,3},{4,36},{36... | collective-permute-start | bytes 147464 | tf_op jit(solution)/shard_map/ppermute | solution.py:328
  6.5 0.8 copy-start.1
  7.3 12.8 %collective-permute-start.3 = (bf16[2,192,128]{2,1,0:T(8,128)(2,1)S(1)}, bf16[2,192,128]{2,1,0:T(8,128)(2,1)S(1)}, u32[]{:S(2)}, u32[]{:S(2)}) collective-permute-start(bf16[2,192,128]{2,1,0:T(8,128)(2,1)S(1)} %pair.1.after.both), channel_id=1, source_target_pairs={{0,24},{8,0},{16,8},{24,16},{1,25},{9,1},{17,9},{25,17},{2,26},{10... | collective-permute-start | bytes 294920 | tf_op jit(solution)/shard_map/ppermute | solution.py:324
  12.8 10.0 %collective-permute-start.2 = (bf16[2,192,128]{2,1,0:T(8,128)(2,1)S(1)}, bf16[2,192,128]{2,1,0:T(8,128)(2,1)S(1)}, u32[]{:S(2)}, u32[]{:S(2)}) collective-permute-start(bf16[2,192,128]{2,1,0:T(8,128)(2,1)S(1)} %pair.1.after.both), channel_id=1, source_target_pairs={{0,16},{8,24},{16,0},{24,8},{1,17},{9,25},{17,1},{25,9},{2,18},{10... | collective-permute-start | bytes 294920 | tf_op jit(solution)/shard_map/ppermute | solution.py:324
  14.3 9.8 %collective-permute-start.1 = (bf16[2,192,128]{2,1,0:T(8,128)(2,1)S(1)}, bf16[2,192,128]{2,1,0:T(8,128)(2,1)S(1)}, u32[]{:S(2)}, u32[]{:S(2)}) collective-permute-start(bf16[2,192,128]{2,1,0:T(8,128)(2,1)S(1)} %pair.1.after.both), channel_id=1, source_target_pairs={{0,8},{8,16},{16,24},{24,0},{1,9},{9,17},{17,25},{25,1},{2,10},{10... | collective-permute-start | bytes 294920 | tf_op jit(solution)/shard_map/ppermute | solution.py:324
  16.6 1.0 copy-start
  17.6 0.7 copy-start.2
  18.6 9.0 %collective-permute-start.4 = (bf16[192,1024]{1,0:T(8,128)(2,1)S(1)}, bf16[192,1024]{1,0:T(8,128)(2,1)S(1)}, u32[]{:S(2)}, u32[]{:S(2)}) collective-permute-start(bf16[192,1024]{1,0:T(8,128)(2,1)S(1)} %get-tuple-element.36.keys), channel_id=1, source_target_pairs={{0,2},{2,0},{1,3},{3,1},{4,6},{6,4},{5,7},{7,5},{8,10},{10,8},{9,1... | collective-permute-start | bytes 1179656 | tf_op jit(solution)/shard_map/ppermute | solution.py:328
  24.2 12.1 %collective-permute-start.5 = (bf16[192,1024]{1,0:T(8,128)(2,1)S(1)}, bf16[192,1024]{1,0:T(8,128)(2,1)S(1)}, u32[]{:S(2)}, u32[]{:S(2)}) collective-permute-start(bf16[192,1024]{1,0:T(8,128)(2,1)S(1)} %hold.1.own), channel_id=1, source_target_pairs={{0,4},{4,0},{1,5},{5,1},{2,6},{6,2},{3,7},{7,3},{8,12},{12,8},{9,1... | collective-permute-start | bytes 1179656 | tf_op jit(solution)/shard_map/ppermute | solution.py:328
  24.4 12.6 %collective-permute-start.9 = (bf16[8,192,128]{2,1,0:T(8,128)(2,1)S(1)}, bf16[8,192,128]{2,1,0:T(8,128)(2,1)S(1)}, u32[]{:S(2)}, u32[]{:S(2)}) collective-permute-start(bf16[8,192,128]{2,1,0:T(8,128)(2,1)S(1)} %stack.1.after.refs_2_), channel_id=1, source_target_pairs={{0,192},{64,0},{128,64},{192,128},{1,193},{65,1},{129,65},{193,129... | collective-permute-start | bytes 1179656 | tf_op jit(solution)/shard_map/ppermute | solution.py:324
  27.5 10.1 %collective-permute-start.8 = (bf16[8,192,128]{2,1,0:T(8,128)(2,1)S(1)}, bf16[8,192,128]{2,1,0:T(8,128)(2,1)S(1)}, u32[]{:S(2)}, u32[]{:S(2)}) collective-permute-start(bf16[8,192,128]{2,1,0:T(8,128)(2,1)S(1)} %stack.1.after.refs_2_), channel_id=1, source_target_pairs={{0,64},{64,128},{128,192},{192,0},{1,65},{65,129},{129,193},{193,1... | collective-permute-start | bytes 1179656 | tf_op jit(solution)/shard_map/ppermute | solution.py:324
  27.6 12.6 %collective-permute-start.7 = (bf16[96,1024]{1,0:T(8,128)(2,1)S(1)}, bf16[96,1024]{1,0:T(8,128)(2,1)S(1)}, u32[]{:S(2)}, u32[]{:S(2)}) collective-permute-start(bf16[96,1024]{1,0:T(8,128)(2,1)S(1)} %low.1), channel_id=1, source_target_pairs={{0,4},{4,0},{1,5},{5,1},{2,6},{6,2},{3,7},{7,3},{8,12},{12,8},{9,1... | collective-permute-start | bytes 589832 | tf_op jit(solution)/shard_map/ppermute | solution.py:328
  36.3 5.8 %collective-permute-start.6 = (bf16[96,1024]{1,0:T(8,128)(2,1)S(1)}, bf16[96,1024]{1,0:T(8,128)(2,1)S(1)}, u32[]{:S(2)}, u32[]{:S(2)}) collective-permute-start(bf16[96,1024]{1,0:T(8,128)(2,1)S(1)} %top.1), channel_id=1, source_target_pairs={{0,2},{2,0},{1,3},{3,1},{4,6},{6,4},{5,7},{7,5},{8,10},{10,8},{9,1... | collective-permute-start | bytes 589832 | tf_op jit(solution)/shard_map/ppermute | solution.py:328
  37.6 5.7 %collective-permute-start.12 = (bf16[4,192,128]{2,1,0:T(8,128)(2,1)S(1)}, bf16[4,192,128]{2,1,0:T(8,128)(2,1)S(1)}, u32[]{:S(2)}, u32[]{:S(2)}) collective-permute-start(bf16[4,192,128]{2,1,0:T(8,128)(2,1)S(1)} %get-tuple-element.39), channel_id=1, source_target_pairs={{0,192},{64,0},{128,64},{192,128},{1,193},{65,1},{129,65},{193,129... | collective-permute-start | bytes 589832 | tf_op jit(solution)/shard_map/ppermute | solution.py:324
  40.1 6.9 %collective-permute-start.11 = (bf16[4,192,128]{2,1,0:T(8,128)(2,1)S(1)}, bf16[4,192,128]{2,1,0:T(8,128)(2,1)S(1)}, u32[]{:S(2)}, u32[]{:S(2)}) collective-permute-start(bf16[4,192,128]{2,1,0:T(8,128)(2,1)S(1)} %get-tuple-element.38.after), channel_id=1, source_target_pairs={{0,64},{64,128},{128,192},{192,0},{1,65},{65,129},{129,193},{193,1... | collective-permute-start | bytes 589832 | tf_op jit(solution)/shard_map/ppermute | solution.py:324
  42.2 4.8 %collective-permute-start.10 = (bf16[768,1024]{1,0:T(8,128)(2,1)S(1)}, bf16[768,1024]{1,0:T(8,128)(2,1)S(1)}, u32[]{:S(2)}, u32[]{:S(2)}) collective-permute-start(bf16[768,1024]{1,0:T(8,128)(2,1)S(1)} %join.1.refs_0_.refs_9_), channel_id=1, source_target_pairs={{0,1},{1,0},{2,3},{3,2},{4,5},{5,4},{6,7},{7,6},{8,9},{9,8},{10,11... | collective-permute-start | bytes 4718600 | tf_op jit(solution)/shard_map/ppermute | solution.py:328
  51.7 1.9 %collective-permute-start.15 = (f32[2,1536]{1,0:T(2,128)S(1)}, f32[2,1536]{1,0:T(2,128)S(1)}, u32[]{:S(2)}, u32[]{:S(2)}) collective-permute-start(f32[2,1536]{1,0:T(2,128)S(1)} %get-tuple-element.44.c), channel_id=1, source_target_pairs={{0,1},{1,0},{2,3},{3,2},{4,5},{5,4},{6,7},{7,6},{8,9},{9,8},{10,11... | collective-permute-start | bytes 36872 | tf_op jit(solution)/shard_map/ppermute | solution.py:328
  51.8 5.4 %collective-permute-start.13 = (f32[2,768]{1,0:T(2,128)S(1)}, f32[2,768]{1,0:T(2,128)S(1)}, u32[]{:S(2)}, u32[]{:S(2)}) collective-permute-start(f32[2,768]{1,0:T(2,128)S(1)} %get-tuple-element.43.r), channel_id=1, source_target_pairs={{0,8},{8,0},{16,24},{24,16},{1,9},{9,1},{17,25},{25,17},{2,10},{10... | collective-permute-start | bytes 18440 | tf_op jit(solution)/shard_map/ppermute | solution.py:328
  53.7 9.7 %collective-permute-start.18 = (f32[2,1536]{1,0:T(2,128)S(1)}, f32[2,1536]{1,0:T(2,128)S(1)}, u32[]{:S(2)}, u32[]{:S(2)}) collective-permute-start(f32[2,1536]{1,0:T(2,128)S(1)} %meet.1.refs_2_), channel_id=1, source_target_pairs={{0,6},{2,4},{4,2},{6,0},{1,7},{3,5},{5,3},{7,1},{8,14},{10,12},{12... | collective-permute-start | bytes 36872 | tf_op jit(solution)/shard_map/ppermute | solution.py:376
  54.2 9.1 %collective-permute-start.17 = (f32[2,1536]{1,0:T(2,128)S(1)}, f32[2,1536]{1,0:T(2,128)S(1)}, u32[]{:S(2)}, u32[]{:S(2)}) collective-permute-start(f32[2,1536]{1,0:T(2,128)S(1)} %meet.1.refs_2_), channel_id=1, source_target_pairs={{0,4},{2,6},{4,0},{6,2},{1,5},{3,7},{5,1},{7,3},{8,12},{10,14},{12... | collective-permute-start | bytes 36872 | tf_op jit(solution)/shard_map/ppermute | solution.py:376
  55.8 7.6 %collective-permute-start.16 = (f32[2,1536]{1,0:T(2,128)S(1)}, f32[2,1536]{1,0:T(2,128)S(1)}, u32[]{:S(2)}, u32[]{:S(2)}) collective-permute-start(f32[2,1536]{1,0:T(2,128)S(1)} %meet.1.refs_2_), channel_id=1, source_target_pairs={{0,2},{2,0},{4,6},{6,4},{1,3},{3,1},{5,7},{7,5},{8,10},{10,8},{12,... | collective-permute-start | bytes 36872 | tf_op jit(solution)/shard_map/ppermute | solution.py:376
  57.3 6.0 %collective-permute-start.14 = (f32[2,768]{1,0:T(2,128)S(1)}, f32[2,768]{1,0:T(2,128)S(1)}, u32[]{:S(2)}, u32[]{:S(2)}) collective-permute-start(f32[2,768]{1,0:T(2,128)S(1)} %meet_rows.1.refs_0_), channel_id=1, source_target_pairs={{0,24},{8,16},{16,8},{24,0},{1,25},{9,17},{17,9},{25,1},{2,26},{10... | collective-permute-start | bytes 18440 | tf_op jit(solution)/shard_map/ppermute | solution.py:328
  71.2 3.6 %collective-permute-start.19 = (s16[4,208,1024]{2,1,0:T(8,128)(2,1)S(1)}, s16[4,208,1024]{2,1,0:T(8,128)(2,1)S(1)}, u32[]{:S(2)}, u32[]{:S(2)}) collective-permute-start(s16[4,208,1024]{2,1,0:T(8,128)(2,1)S(1)} %get-tuple-element.48), channel_id=1, source_target_pairs={{0,1},{1,0},{2,3},{3,2},{4,5},{5,4},{6,7},{7,6},{8,9},{9,8},{10,11... | collective-permute-start | bytes 5111816 | tf_op jit(solution)/shard_map/ppermute | solution.py:328
  71.2 8.7 %collective-permute-start.24 = (s16[400,256]{1,0:T(8,128)(2,1)S(1)}, s16[400,256]{1,0:T(8,128)(2,1)S(1)}, u32[]{:S(2)}, u32[]{:S(2)}) collective-permute-start(s16[400,256]{1,0:T(8,128)(2,1)S(1)} %get-tuple-element.60), channel_id=1, source_target_pairs={{0,64},{64,128},{128,192},{192,0},{1,65},{65,129},{129,193},{193,1... | collective-permute-start | bytes 614408 | tf_op jit(solution)/shard_map/ppermute | solution.py:324
  71.2 8.7 %collective-permute-start.25 = (s16[400,256]{1,0:T(8,128)(2,1)S(1)}, s16[400,256]{1,0:T(8,128)(2,1)S(1)}, u32[]{:S(2)}, u32[]{:S(2)}) collective-permute-start(s16[400,256]{1,0:T(8,128)(2,1)S(1)} %get-tuple-element.61), channel_id=1, source_target_pairs={{0,192},{64,0},{128,64},{192,128},{1,193},{65,1},{129,65},{193,129... | collective-permute-start | bytes 614408 | tf_op jit(solution)/shard_map/ppermute | solution.py:324
  75.7 11.9 %collective-permute-start.20 = (s16[2,208,512]{2,1,0:T(8,128)(2,1)S(1)}, s16[2,208,512]{2,1,0:T(8,128)(2,1)S(1)}, u32[]{:S(2)}, u32[]{:S(2)}) collective-permute-start(s16[2,208,512]{2,1,0:T(8,128)(2,1)S(1)} %get-tuple-element.52), channel_id=1, source_target_pairs={{0,2},{2,0},{1,3},{3,1},{4,6},{6,4},{5,7},{7,5},{8,10},{10,8},{9,1... | collective-permute-start | bytes 1277960 | tf_op jit(solution)/shard_map/ppermute | solution.py:328
  76.3 11.6 %collective-permute-start.21 = (s16[2,208,512]{2,1,0:T(8,128)(2,1)S(1)}, s16[2,208,512]{2,1,0:T(8,128)(2,1)S(1)}, u32[]{:S(2)}, u32[]{:S(2)}) collective-permute-start(s16[2,208,512]{2,1,0:T(8,128)(2,1)S(1)} %get-tuple-element.53), channel_id=1, source_target_pairs={{0,4},{4,0},{1,5},{5,1},{2,6},{6,2},{3,7},{7,3},{8,12},{12,8},{9,1... | collective-permute-start | bytes 1277960 | tf_op jit(solution)/shard_map/ppermute | solution.py:328
  80.3 12.2 %collective-permute-start.26 = (s16[784,256]{1,0:T(8,128)(2,1)S(1)}, s16[784,256]{1,0:T(8,128)(2,1)S(1)}, u32[]{:S(2)}, u32[]{:S(2)}) collective-permute-start(s16[784,256]{1,0:T(8,128)(2,1)S(1)} %get-tuple-element.62), channel_id=1, source_target_pairs={{0,64},{64,128},{128,192},{192,0},{1,65},{65,129},{129,193},{193,1... | collective-permute-start | bytes 1204232 | tf_op jit(solution)/shard_map/ppermute | solution.py:324
  80.4 12.1 %collective-permute-start.27 = (s16[784,256]{1,0:T(8,128)(2,1)S(1)}, s16[784,256]{1,0:T(8,128)(2,1)S(1)}, u32[]{:S(2)}, u32[]{:S(2)}) collective-permute-start(s16[784,256]{1,0:T(8,128)(2,1)S(1)} %get-tuple-element.63), channel_id=1, source_target_pairs={{0,192},{64,0},{128,64},{192,128},{1,193},{65,1},{129,65},{193,129... | collective-permute-start | bytes 1204232 | tf_op jit(solution)/shard_map/ppermute | solution.py:324
  88.3 6.3 %collective-permute-start.22 = (s16[208,512]{1,0:T(8,128)(2,1)S(1)}, s16[208,512]{1,0:T(8,128)(2,1)S(1)}, u32[]{:S(2)}, u32[]{:S(2)}) collective-permute-start(s16[208,512]{1,0:T(8,128)(2,1)S(1)} %get-tuple-element.55), channel_id=1, source_target_pairs={{0,2},{2,0},{1,3},{3,1},{4,6},{6,4},{5,7},{7,5},{8,10},{10,8},{9,1... | collective-permute-start | bytes 638984 | tf_op jit(solution)/shard_map/ppermute | solution.py:328
  95.6 25.0 %all-to-all-start = ((s16[8,208,128]{2,1,0:T(8,128)(2,1)}), s16[8,208,128]{2,1,0:T(8,128)(2,1)S(1)}, u32[]{:S(2)}, u32[]{:S(2)}) async-start(s16[8,208,128]{2,1,0:T(8,128)(2,1)} %image_code.1), calls=%async_computation | async-start | bytes 851968 | tf_op jit(solution)/shard_map/all_to_all | solution.py:412
  103.4 13.1 %collective-permute-start.23 = (s16[208,512]{1,0:T(8,128)(2,1)S(1)}, s16[208,512]{1,0:T(8,128)(2,1)S(1)}, u32[]{:S(2)}, u32[]{:S(2)}) collective-permute-start(s16[208,512]{1,0:T(8,128)(2,1)S(1)} %get-tuple-element.56), channel_id=1, source_target_pairs={{0,4},{4,0},{1,5},{5,1},{2,6},{6,2},{3,7},{7,3},{8,12},{12,8},{9,1... | collective-permute-start | bytes 638984 | tf_op jit(solution)/shard_map/ppermute | solution.py:328
